TPU v7x, 128 devices: a whole 4x4x4 slice. The times are simulated.
128 devices in a mesh: dp: 32 (over x, y, core), mp: 4 (over z).
Axes of the slice: x: 4, y: 4, z: 4, core: 2. Of those that a mesh axis runs over, the one named last changes fastest.
Arguments:
- frames: bfloat16 [49152, 1536], P('dp'), may hold values from -6 to 6
- grad_out: bfloat16 [49152, 1536], P('dp'), may hold values from -6 to 6
- w_in: bfloat16 [1536, 2, 1536], P(None, None, 'mp'), may hold values from -0.15625 to 0.15625
- conv_kernel: float32 [31, 1536], P(None, 'mp'), may hold values from -1 to 1
- conv_bias: float32 [1536], P('mp'), may hold values from -3 to 3
- w_out: bfloat16 [1536, 1536], P('mp'), may hold values from -0.15625 to 0.15625
- seg_lengths: int32 [32, 32], P('dp'), may hold values from 24 to 72, as said below
- seg_owner: int32 [32, 32], P('dp'), may hold values from 0 to 31, as said below
- slot_device: int32 [32, 32], P('dp'), may hold values from 0 to 31, as said below
Outputs:
- dx_frames: bfloat16 [1024, 72, 1536], P('dp', None, 'mp')
- grad_w_in: float32 [1536, 2, 1536], P('dp', None, 'mp')
- grad_w_out: float32 [1536, 1536], P('mp', 'dp')
- grad_kernel: float32 [31, 1536], P(None, 'mp')
- grad_bias: float32 [1536], P('mp')
Inputs may be any that keep to these rules, and one draw needn't show every extreme that they name: `seg_lengths`: each row sums to 1536, and every row holds at least one length 72. `seg_owner`: each row is a permutation: every pack holds exactly one utterance of each owner. `slot_device`: each row is a permutation: owner o's utterance u is packed on pack slot_device[o, u].
All inputs are finite; a program needn't handle non-finite values.
Results may differ from a plain program's by a relative error of at most 0.0049.
Values may be sent and summed in bfloat16 or wider, within the bound.
No kernel may reach another device: no remote copies, remote signals or barrier semaphores. Data moves between devices by JAX's collectives and lax.ppermute only.
A program may use at most 128 MiB of HBM per device.

v0:
```python
import math

import jax
import jax.numpy as jnp
from jax import lax
from jax.sharding import PartitionSpec as P

TAPS = 31
MAXLEN = 72


def segment_ids(lengths, rows):
    seg_ends = jnp.cumsum(lengths)
    position = jnp.arange(rows, dtype=jnp.int32)
    return jnp.sum((position[:, None] >= seg_ends[None, :]).astype(jnp.int32), axis=1)


def padded_pair(signal, segment):
    reach = (TAPS - 1) // 2
    padded = jnp.pad(signal, ((reach, reach), (0, 0)))
    padded_segment = jnp.pad(segment, (reach, reach), constant_values=-1)
    return (padded, padded_segment)


def shifted(padded, padded_segment, segment, offset):
    reach = (TAPS - 1) // 2
    rows = segment.shape[0]
    piece = padded[reach + offset : reach + offset + rows]
    keep = padded_segment[reach + offset : reach + offset + rows] == segment
    return jnp.where(keep[:, None], piece, jnp.zeros((), piece.dtype))


def depthwise(signal, segment, kernel, direction):
    reach = (TAPS - 1) // 2
    padded, padded_segment = padded_pair(signal, segment)
    total = jnp.zeros_like(signal)
    for tap_index in range(TAPS):
        total = total + kernel[tap_index] * shifted(
            padded, padded_segment, segment, direction * (tap_index - reach)
        )
    return total


def kernel_terms(grad_conv, gated, segment):
    reach = (TAPS - 1) // 2
    padded, padded_segment = padded_pair(gated, segment)
    terms = []
    for tap_index in range(TAPS):
        terms.append(
            jnp.sum(grad_conv * shifted(padded, padded_segment, segment, tap_index - reach), axis=0)
        )
    return jnp.stack(terms)


def on_device(
    frames, grad_out, w_in, conv_kernel, conv_bias, w_out, seg_lengths, seg_owner, slot_device
):
    count_dev = lax.axis_size("dp")
    rows = frames.shape[0]
    width = frames.shape[1]
    channels = w_in.shape[2]
    lengths = seg_lengths[0]
    segment = segment_ids(lengths, rows)
    w_flat = w_in.reshape(width, 2 * channels)
    projected = jnp.dot(frames, w_flat, preferred_element_type=jnp.float32)
    value = projected[:, :channels]
    gate = projected[:, channels:]
    gate_sig = jax.nn.sigmoid(gate)
    gated = value * gate_sig
    conv_out = depthwise(gated, segment, conv_kernel, 1) + conv_bias
    conv_sig = jax.nn.sigmoid(conv_out)
    activated = (conv_out * conv_sig).astype(jnp.bfloat16)
    grad_swish = lax.dot_general(
        grad_out, w_out, (((1,), (1,)), ((), ())), preferred_element_type=jnp.float32
    )
    grad_conv = grad_swish * conv_sig * (1.0 + conv_out * (1.0 - conv_sig))
    grad_glu = depthwise(grad_conv, segment, conv_kernel, -1)
    grad_proj = jnp.concatenate(
        [grad_glu * gate_sig, grad_glu * value * gate_sig * (1.0 - gate_sig)], axis=1
    ).astype(jnp.bfloat16)
    scale = 1.0 / math.sqrt(rows * count_dev)
    partial_rows = lax.dot_general(
        grad_proj, w_flat, (((1,), (1,)), ((), ())), preferred_element_type=jnp.float32
    )
    grad_rows = lax.psum_scatter(partial_rows, "mp", scatter_dimension=1, tiled=True).astype(
        jnp.bfloat16
    )
    owners = jnp.arange(count_dev, dtype=jnp.int32)
    starts = jnp.cumsum(lengths) - lengths
    match = (seg_owner[0][:, None] == owners[None, :]).astype(jnp.int32)
    owner_start = jnp.sum(match * starts[:, None], axis=0)
    owner_length = jnp.sum(match * lengths[:, None], axis=0)
    offsets = jnp.arange(MAXLEN, dtype=jnp.int32)
    row_index = owner_start[:, None] + offsets[None, :]
    valid = offsets[None, :] < owner_length[:, None]
    picked = jnp.take(grad_rows, jnp.where(valid, row_index, 0).reshape(-1), axis=0).reshape(
        count_dev, MAXLEN, channels
    )
    outgoing = jnp.where(valid[:, :, None], picked, jnp.zeros((), picked.dtype))
    received = lax.all_to_all(outgoing, "dp", split_axis=0, concat_axis=0, tiled=True)
    dx_frames = jnp.take(received, slot_device[0], axis=0)
    term = lax.dot_general(
        frames, grad_proj, (((0,), (0,)), ((), ())), preferred_element_type=jnp.float32
    )
    grad_w_in = (
        lax.psum_scatter(
            term.reshape(lax.axis_size("dp") * (width // count_dev), 2, channels),
            "dp",
            scatter_dimension=0,
            tiled=True,
        )
        * scale
    )
    out_term = lax.dot_general(
        activated, grad_out, (((0,), (0,)), ((), ())), preferred_element_type=jnp.float32
    )
    grad_w_out = lax.psum_scatter(out_term, "dp", scatter_dimension=1, tiled=True) * scale
    kernel_term = kernel_terms(grad_conv, gated, segment)
    bias_term = jnp.sum(grad_conv, axis=0)
    grad_kernel, grad_bias = lax.psum((kernel_term, bias_term), "dp")
    return (dx_frames, grad_w_in, grad_w_out, grad_kernel * scale, grad_bias * scale)


def solution(mesh):
    return jax.shard_map(
        on_device,
        mesh=mesh,
        in_specs=(
            P("dp", None),
            P("dp", None),
            P(None, None, "mp"),
            P(None, "mp"),
            P("mp"),
            P("mp", None),
            P("dp", None),
            P("dp", None),
            P("dp", None),
        ),
        out_specs=(P("dp", None, "mp"), P("dp", None, "mp"), P("mp", "dp"), P(None, "mp"), P("mp")),
        check_vma=False,
    )
```

profile of v0, /device:TPU:0, one launch (start us, length us, event | category | flops | bytes accessed | tf_op | source)
XLA Modules:
  0.0 380.9 jit_solution(8863421729060110262)
XLA Ops:
  8.1 0.8 copy.20
  8.9 0.1 reduce-window.7
  8.9 0.1 reduce
  9.1 0.1 convert_reduce_fusion
  9.2 0.7 slice_compare_fusion.26
  9.8 0.7 slice_compare_fusion.13
  10.5 0.7 slice_compare_fusion.29
  11.2 0.7 slice_compare_fusion
  11.9 1.7 slice_reduce_fusion.29
  13.6 1.9 slice_reduce_fusion.30
  15.5 2.3 copy.22
  17.8 1.4 copy-done.3
  19.2 3.9 %fusion.42 = f32[1536,768]{1,0:T(8,128)S(1)} fusion(bf16[1536,1536]{1,0:T(8,128)(2,1)S(1)} %copy-done.61, bf16[1536,768]{1,0:T(8,128)(2,1)S(1)} %bitcast.27), kind=kOutput, calls=%fused_computation.208 | convolution fusion | flops 3623878656 | bytes 11796480 | tf_op jit(solution)/shard_map/dot_general | solution.py:65
  23.1 0.6 slice_multiply_fusion
  23.7 1.5 copy-done.2
  25.2 18.3 %add_add_fusion = f32[1536,384]{1,0:T(8,128)} fusion(f32[1536,384]{1,0:T(8,128)S(1)} %slice_multiply_fusion, f32[384]{0:T(512)} %param.13, f32[384]{0:T(512)} %get-tuple-element.66, f32[384]{0:T(512)} %get-tuple-element.67, f32[384]{0:T(512)} %get-tuple-element.38, f32[384]{0:T(512)} %get-tuple-element.39, f32[384]{0:T(512)} %get-tuple-element.40, ...), kind=kLoop, calls=%fused_computation.84 | loop fusion | flops 54263808 | bytes 4813824 | tf_op jit(solution)/shard_map/add | solution.py:70
  43.5 8.2 %multiply_reduce_fusion.27 = (f32[384]{0:T(512)}, f32[384]{0:T(512)}, f32[384]{0:T(512)}, f32[384]{0:T(512)}, f32[1536,384]{1,0:T(8,128)}) fusion(pred[1536]{0:T(1024)(128)(4,1)} %get-tuple-element.100, f32[1536,384]{1,0:T(8,128)S(1)} %slice_multiply_fusion, pred[1536]{0:T(1024)(128)(4,1)} %get-tuple-element.101, pred[1536]{0:T(1024)(128)(4,1)} %get-tuple-element.102, ...), kind=kOutput, calls=%fused_computation.36 | convolution fusion | flops 1823734272 | bytes 12988416 | tf_op jit(solution)/shard_map/dot_general | solution.py:73
  51.7 46.1 %multiply_convert_fusion.2 = (bf16[1536,384]{1,0:T(8,128)(2,1)S(1)}, f32[1536,384]{1,0:T(8,128)}) fusion(f32[1536,768]{1,0:T(8,128)} %copy-done.2, pred[1536]{0:T(1024)(128)(4,1)} %get-tuple-element.103, f32[384]{0:T(512)} %get-tuple-element.66, pred[1536]{0:T(1024)(128)(4,1)} %get-tuple-element.102, f32[384]{0:T(512)} %get-tuple-element.67, ...), kind=kLoop, calls=%fused_computation.42 | loop fusion | flops 56623104 | bytes 8351232 | tf_op jit(solution)/shard_map/convert
  97.8 3.9 %multiply_convert_fusion.1 = bf16[1536,384]{1,0:T(8,128)(2,1)S(1)} fusion(f32[1536,384]{1,0:T(8,128)} %get-tuple-element.73, f32[1536,768]{1,0:T(8,128)} %copy-done.2), kind=kLoop, calls=%fused_computation.41 | loop fusion | flops 4718592 | bytes 8257536 | tf_op jit(solution)/shard_map/convert.1
  101.7 1.0 copy-done.5
  102.7 6.5 %fusion.34 = f32[1536,1536]{1,0:T(8,128)} fusion(bf16[1536,768]{1,0:T(8,128)(2,1)S(1)} %bitcast.28, bf16[1536,384]{1,0:T(8,128)(2,1)S(1)} %multiply_convert_fusion.1, bf16[1536,384]{1,0:T(8,128)(2,1)S(1)} %get-tuple-element.72), kind=kOutput, calls=%fused_computation.119 | convolution fusion | flops 3628597248 | bytes 14155776 | tf_op jit(solution)/shard_map/dot_general | solution.py:82
  109.2 0.0 all-reduce.7.cloned.1.call-start
  109.3 8.7 %fusion.33 = f32[768,1536]{1,0:T(8,128)} fusion(bf16[1536,1536]{1,0:T(8,128)(2,1)} %param.9, bf16[1536,384]{1,0:T(8,128)(2,1)} %copy-done.5, bf16[1536,384]{1,0:T(8,128)(2,1)S(1)} %get-tuple-element.72), kind=kOutput, calls=%fused_computation.118 | convolution fusion | flops 3628597248 | bytes 11796480 | tf_op jit(solution)/shard_map/dot_general | solution.py:102
  118.0 8.2 %copy.21 = f32[1536,2,384]{2,1,0:T(2,128)} copy(f32[1536,2,384]{0,2,1:T(8,128)} %bitcast.25) | data formatting | bytes 9437184 | tf_op jit(solution)/shard_map/reshape | solution.py:107
  126.3 0.3 reduce-scatter.5.cloned.1.call-start
  126.5 7.3 %fusion.35 = f32[384,1536]{0,1:T(8,128)} fusion(bf16[1536,1536]{1,0:T(8,128)(2,1)} %param.10, f32[1536,384]{1,0:T(8,128)} %add_add_fusion), kind=kOutput, calls=%fused_computation.120 | convolution fusion | flops 1814888448 | bytes 9437184 | tf_op jit(solution)/shard_map/dot_general | solution.py:114
  133.9 0.5 copy-done.53
  134.5 0.1 select_reduce_fusion.1
  134.6 0.7 iota_compare_fusion.2
  135.3 0.1 add_select_fusion
  135.5 6.8 %multiply_reduce_fusion = (f32[384]{0:T(512)}, f32[384]{0:T(512)}, f32[384]{0:T(512)}, f32[384]{0:T(512)}, f32[384]{0:T(512)}, /*index=5*/f32[384]{0:T(512)}, f32[384]{0:T(512)}, f32[384]{0:T(512)}, f32[384]{0:T(512)}) fusion(f32[1536,384]{1,0:T(8,128)} %get-tuple-element.106, pred[1536]{0:T(1024)(128)(4,1)S(1)} %copy-done.25, ...), kind=kLoop, calls=%fused_computation.9 | loop fusion | flops 15921792 | bytes 4746240 | tf_op jit(solution)/shard_map/reduce_sum | solution.py:50
  142.3 0.1 select_n.341
  142.5 6.7 %multiply_reduce_fusion.9 = (f32[384]{0:T(512)}, f32[384]{0:T(512)}, f32[384]{0:T(512)}, f32[384]{0:T(512)}, f32[384]{0:T(512)}, /*index=5*/f32[384]{0:T(512)}, ...) fusion(f32[1536,384]{1,0:T(8,128)} %get-tuple-element.106, pred[1536]{0:T(1024)(128)(4,1)S(1)} %copy-done.24, ...), kind=kLoop, calls=%fused_computation.18 | loop fusion | flops 15921408 | bytes 4746240 | tf_op jit(solution)/shard_map/reduce_sum | solution.py:50
  149.2 51.9 %reduce-scatter.3.cloned.1.call-done = f32[1536,384]{1,0:T(8,128)} async-done(((f32[1536,1536]{1,0:T(8,128)}), f32[1536,384]{1,0:T(8,128)}) %reduce-scatter.3.cloned.1.call-update) | async-done | bytes 2359312 | tf_op jit(solution)/shard_map/reduce_scatter | solution.py:85
  201.1 1.8 convert_element_type.16
  202.9 7.3 %gather_fusion = bf16[2304,384]{1,0:T(8,128)(2,1)} fusion(bf16[1536,384]{1,0:T(8,128)(2,1)S(1)} %convert_element_type.16, s32[3072]{0:T(1024)S(1)} %pad_clamp_fusion), kind=kCustom, calls=%fused_computation | custom fusion | bytes 3548160 | tf_op jit(solution)/shard_map/jit(_take)/gather | solution.py:96
  210.2 3.9 %select_select_fusion = bf16[32,72,384]{2,1,0:T(8,128)(2,1)} fusion(bf16[32,72,384]{2,1,0:T(8,128)(2,1)} %bitcast.24, pred[32,72]{1,0:T(8,128)(4,1)} %get-tuple-element.105, pred[32,72]{1,0:T(8,128)(4,1)} %get-tuple-element.104), kind=kLoop, calls=%fused_computation.116 | loop fusion | flops 1769472 | bytes 3543552 | tf_op jit(solution)/shard_map/jit(_where)/select_n | solution.py:99
  214.2 7.2 %all-to-all-start = ((bf16[32,72,384]{2,1,0:T(8,128)(2,1)}), bf16[32,72,384]{2,1,0:T(8,128)(2,1)}, u32[]{:S(2)}, u32[]{:S(2)}) async-start(bf16[32,72,384]{2,1,0:T(8,128)(2,1)} %select_select_fusion), calls=%async_computation.1 | async-start | bytes 3538944 | tf_op jit(solution)/shard_map/all_to_all | solution.py:100
  221.8 6.2 %multiply_reduce_fusion.18 = (f32[384]{0:T(512)S(1)}, f32[384]{0:T(512)S(1)}, f32[384]{0:T(512)S(1)}, f32[384]{0:T(512)S(1)}, f32[384]{0:T(512)S(1)}, /*index=5*...) fusion(f32[1536,384]{1,0:T(8,128)} %get-tuple-element.106, ...), kind=kLoop, calls=%fused_computation.27 | loop fusion | flops 15921792 | bytes 4746240 | tf_op jit(solution)/shard_map/reduce_sum | solution.py:50
  228.6 0.6 dynamic-slice
  229.8 0.1 stack.127
  230.0 135.1 %all-reduce.4 = (f32[31,384]{1,0:T(8,128)S(1)}, f32[384]{0:T(512)S(1)}) all-reduce(f32[31,384]{1,0:T(8,128)S(1)} %stack.127, f32[384]{0:T(512)S(1)} %copy-done.34), channel_id=1, replica_groups=mesh['dp'=32,'mp'=4] {'dp'}, use_global_device_ids=true, to_apply=%region_38.39 | all-reduce | flops 12288 | bytes 98304 | tf_op jit(solution)/shard_map/psum | solution.py:120
  365.1 0.6 broadcast_multiply_fusion.2
  365.6 0.6 broadcast_multiply_fusion.1
  366.3 1.6 dynamic-slice_multiply_fusion
  367.9 1.5 broadcast_multiply_fusion
  369.4 2.5 gather_fusion.1
  372.0 1.5 broadcast_select_fusion
  (168 shorter events, 0.5 us)
Async XLA Ops:
  8.0 35.5 %copy-start = (bf16[384,1536]{1,0:T(8,128)(2,1)S(1)}, bf16[384,1536]{1,0:T(8,128)(2,1)}, u32[]{:S(2)}) copy-start(bf16[384,1536]{1,0:T(8,128)(2,1)} %param.14) | copy-start | bytes 3538948
  8.0 193.1 %reduce-scatter.3.cloned.1.call-start = ((), (), s32[]{:S(2)}) async-start(), calls=%async_computation.3 | async-start | bytes 11796480 | tf_op jit(solution)/shard_map/reduce_scatter | solution.py:85
  10.5 41.1 %copy-start.6 = (pred[1536]{0:T(1024)(128)(4,1)}, pred[1536]{0:T(1024)(128)(4,1)S(1)}, u32[]{:S(2)}) copy-start(pred[1536]{0:T(1024)(128)(4,1)S(1)} %get-tuple-element.91) | copy-start | bytes 4612
  11.9 39.7 %copy-start.8 = (pred[1536]{0:T(1024)(128)(4,1)}, pred[1536]{0:T(1024)(128)(4,1)S(1)}, u32[]{:S(2)}) copy-start(pred[1536]{0:T(1024)(128)(4,1)S(1)} %get-tuple-element.93) | copy-start | bytes 4612
  11.9 39.7 %copy-start.10 = (pred[1536]{0:T(1024)(128)(4,1)}, pred[1536]{0:T(1024)(128)(4,1)S(1)}, u32[]{:S(2)}) copy-start(pred[1536]{0:T(1024)(128)(4,1)S(1)} %get-tuple-element.94) | copy-start | bytes 4612
  109.2 257.0 %all-reduce.7.cloned.1.call-start = ((), (), s32[]{:S(2)}) async-start(), calls=%async_computation.5 | async-start | bytes 9437184
  126.3 241.7 %reduce-scatter.5.cloned.1.call-start = ((), (), s32[]{:S(2)}) async-start(), calls=%async_computation.4 | async-start | bytes 2433024 | tf_op jit(solution)/shard_map/reduce_scatter | solution.py:117
  135.4 7.0 %copy-start.17 = (pred[1536]{0:T(1024)(128)(4,1)S(1)}, pred[1536]{0:T(1024)(128)(4,1)}, u32[]{:S(2)}) copy-start(pred[1536]{0:T(1024)(128)(4,1)} %get-tuple-element.83) | copy-start | bytes 4612
  135.4 7.0 %copy-start.18 = (pred[1536]{0:T(1024)(128)(4,1)S(1)}, pred[1536]{0:T(1024)(128)(4,1)}, u32[]{:S(2)}) copy-start(pred[1536]{0:T(1024)(128)(4,1)} %get-tuple-element.84) | copy-start | bytes 4612
  135.5 7.0 %copy-start.19 = (pred[1536]{0:T(1024)(128)(4,1)S(1)}, pred[1536]{0:T(1024)(128)(4,1)}, u32[]{:S(2)}) copy-start(pred[1536]{0:T(1024)(128)(4,1)} %get-tuple-element.85) | copy-start | bytes 4612
  135.5 7.0 %copy-start.20 = (pred[1536]{0:T(1024)(128)(4,1)S(1)}, pred[1536]{0:T(1024)(128)(4,1)}, u32[]{:S(2)}) copy-start(pred[1536]{0:T(1024)(128)(4,1)} %get-tuple-element.86) | copy-start | bytes 4612
  135.5 7.0 %copy-start.21 = (pred[1536]{0:T(1024)(128)(4,1)S(1)}, pred[1536]{0:T(1024)(128)(4,1)}, u32[]{:S(2)}) copy-start(pred[1536]{0:T(1024)(128)(4,1)} %get-tuple-element.87) | copy-start | bytes 4612
  135.5 7.0 %copy-start.22 = (pred[1536]{0:T(1024)(128)(4,1)S(1)}, pred[1536]{0:T(1024)(128)(4,1)}, u32[]{:S(2)}) copy-start(pred[1536]{0:T(1024)(128)(4,1)} %get-tuple-element.88) | copy-start | bytes 4612
  135.5 7.0 %copy-start.23 = (pred[1536]{0:T(1024)(128)(4,1)S(1)}, pred[1536]{0:T(1024)(128)(4,1)}, u32[]{:S(2)}) copy-start(pred[1536]{0:T(1024)(128)(4,1)} %get-tuple-element.89) | copy-start | bytes 4612
  135.5 7.0 %copy-start.24 = (pred[1536]{0:T(1024)(128)(4,1)S(1)}, pred[1536]{0:T(1024)(128)(4,1)}, u32[]{:S(2)}) copy-start(pred[1536]{0:T(1024)(128)(4,1)} %get-tuple-element.82) | copy-start | bytes 4612
  214.2 7.3 %copy-start.7 = (pred[1536]{0:T(1024)(128)(4,1)S(1)}, pred[1536]{0:T(1024)(128)(4,1)}, u32[]{:S(2)}) copy-start(pred[1536]{0:T(1024)(128)(4,1)} %copy-done.6) | copy-start | bytes 4612
  214.2 7.3 %copy-start.9 = (pred[1536]{0:T(1024)(128)(4,1)S(1)}, pred[1536]{0:T(1024)(128)(4,1)}, u32[]{:S(2)}) copy-start(pred[1536]{0:T(1024)(128)(4,1)} %copy-done.8) | copy-start | bytes 4612
  214.2 7.3 %copy-start.11 = (pred[1536]{0:T(1024)(128)(4,1)S(1)}, pred[1536]{0:T(1024)(128)(4,1)}, u32[]{:S(2)}) copy-start(pred[1536]{0:T(1024)(128)(4,1)} %copy-done.10) | copy-start | bytes 4612
  214.2 7.3 %copy-start.12 = (pred[1536]{0:T(1024)(128)(4,1)S(1)}, pred[1536]{0:T(1024)(128)(4,1)}, u32[]{:S(2)}) copy-start(pred[1536]{0:T(1024)(128)(4,1)} %get-tuple-element.95) | copy-start | bytes 4612
  214.2 7.3 %copy-start.13 = (pred[1536]{0:T(1024)(128)(4,1)S(1)}, pred[1536]{0:T(1024)(128)(4,1)}, u32[]{:S(2)}) copy-start(pred[1536]{0:T(1024)(128)(4,1)} %get-tuple-element.96) | copy-start | bytes 4612
  214.2 7.3 %copy-start.14 = (pred[1536]{0:T(1024)(128)(4,1)S(1)}, pred[1536]{0:T(1024)(128)(4,1)}, u32[]{:S(2)}) copy-start(pred[1536]{0:T(1024)(128)(4,1)} %get-tuple-element.97) | copy-start | bytes 4612
  214.2 7.3 %copy-start.15 = (pred[1536]{0:T(1024)(128)(4,1)S(1)}, pred[1536]{0:T(1024)(128)(4,1)}, u32[]{:S(2)}) copy-start(pred[1536]{0:T(1024)(128)(4,1)} %get-tuple-element.98) | copy-start | bytes 4612
  214.2 7.3 %copy-start.16 = (pred[1536]{0:T(1024)(128)(4,1)S(1)}, pred[1536]{0:T(1024)(128)(4,1)}, u32[]{:S(2)}) copy-start(pred[1536]{0:T(1024)(128)(4,1)} %get-tuple-element.99) | copy-start | bytes 4612
  214.2 155.2 %all-to-all-start = ((bf16[32,72,384]{2,1,0:T(8,128)(2,1)}), bf16[32,72,384]{2,1,0:T(8,128)(2,1)}, u32[]{:S(2)}, u32[]{:S(2)}) async-start(bf16[32,72,384]{2,1,0:T(8,128)(2,1)} %select_select_fusion), calls=%async_computation.1 | async-start | bytes 3538944 | tf_op jit(solution)/shard_map/all_to_all | solution.py:100
  221.5 6.5 %copy-start.58 = (f32[384]{0:T(512)S(1)}, f32[384]{0:T(512)}, u32[]{:S(2)}) copy-start(f32[384]{0:T(512)} %get-tuple-element.33) | copy-start | bytes 4612
  221.5 6.5 %copy-start.57 = (f32[384]{0:T(512)S(1)}, f32[384]{0:T(512)}, u32[]{:S(2)}) copy-start(f32[384]{0:T(512)} %get-tuple-element.34) | copy-start | bytes 4612
  221.5 6.5 %copy-start.56 = (f32[384]{0:T(512)S(1)}, f32[384]{0:T(512)}, u32[]{:S(2)}) copy-start(f32[384]{0:T(512)} %get-tuple-element.35) | copy-start | bytes 4612
  221.6 6.5 %copy-start.51 = (f32[384]{0:T(512)S(1)}, f32[384]{0:T(512)}, u32[]{:S(2)}) copy-start(f32[384]{0:T(512)} %get-tuple-element.5) | copy-start | bytes 4612
  221.6 6.5 %copy-start.50 = (f32[384]{0:T(512)S(1)}, f32[384]{0:T(512)}, u32[]{:S(2)}) copy-start(f32[384]{0:T(512)} %get-tuple-element.6) | copy-start | bytes 4612
  221.6 6.6 %copy-start.49 = (f32[384]{0:T(512)S(1)}, f32[384]{0:T(512)}, u32[]{:S(2)}) copy-start(f32[384]{0:T(512)} %get-tuple-element.7) | copy-start | bytes 4612
  221.6 6.6 %copy-start.48 = (f32[384]{0:T(512)S(1)}, f32[384]{0:T(512)}, u32[]{:S(2)}) copy-start(f32[384]{0:T(512)} %get-tuple-element.8) | copy-start | bytes 4612
  221.6 6.6 %copy-start.47 = (f32[384]{0:T(512)S(1)}, f32[384]{0:T(512)}, u32[]{:S(2)}) copy-start(f32[384]{0:T(512)} %get-tuple-element.9) | copy-start | bytes 4612
  221.6 6.6 %copy-start.46 = (f32[384]{0:T(512)S(1)}, f32[384]{0:T(512)}, u32[]{:S(2)}) copy-start(f32[384]{0:T(512)} %get-tuple-element.10) | copy-start | bytes 4612
  221.6 6.6 %copy-start.45 = (f32[384]{0:T(512)S(1)}, f32[384]{0:T(512)}, u32[]{:S(2)}) copy-start(f32[384]{0:T(512)} %get-tuple-element.11) | copy-start | bytes 4612
  221.6 6.6 %copy-start.44 = (f32[384]{0:T(512)S(1)}, f32[384]{0:T(512)}, u32[]{:S(2)}) copy-start(f32[384]{0:T(512)} %get-tuple-element.12) | copy-start | bytes 4612
  221.6 6.6 %copy-start.43 = (f32[384]{0:T(512)S(1)}, f32[384]{0:T(512)}, u32[]{:S(2)}) copy-start(f32[384]{0:T(512)} %get-tuple-element.13) | copy-start | bytes 4612
  221.6 6.6 %copy-start.52 = (f32[384]{0:T(512)S(1)}, f32[384]{0:T(512)}, u32[]{:S(2)}) copy-start(f32[384]{0:T(512)} %get-tuple-element.14) | copy-start | bytes 4612
  221.7 6.7 %copy-start.42 = (f32[384]{0:T(512)S(1)}, f32[384]{0:T(512)}, u32[]{:S(2)}) copy-start(f32[384]{0:T(512)} %get-tuple-element.15) | copy-start | bytes 4612
  221.7 6.8 %copy-start.41 = (f32[384]{0:T(512)S(1)}, f32[384]{0:T(512)}, u32[]{:S(2)}) copy-start(f32[384]{0:T(512)} %get-tuple-element.16) | copy-start | bytes 4612
  221.7 6.8 %copy-start.40 = (f32[384]{0:T(512)S(1)}, f32[384]{0:T(512)}, u32[]{:S(2)}) copy-start(f32[384]{0:T(512)} %get-tuple-element.17) | copy-start | bytes 4612
  221.7 6.8 %copy-start.39 = (f32[384]{0:T(512)S(1)}, f32[384]{0:T(512)}, u32[]{:S(2)}) copy-start(f32[384]{0:T(512)} %get-tuple-element.18) | copy-start | bytes 4612
  221.7 6.8 %copy-start.38 = (f32[384]{0:T(512)S(1)}, f32[384]{0:T(512)}, u32[]{:S(2)}) copy-start(f32[384]{0:T(512)} %get-tuple-element.19) | copy-start | bytes 4612
  221.7 6.8 %copy-start.37 = (f32[384]{0:T(512)S(1)}, f32[384]{0:T(512)}, u32[]{:S(2)}) copy-start(f32[384]{0:T(512)} %get-tuple-element.20) | copy-start | bytes 4612
  221.7 6.8 %copy-start.36 = (f32[384]{0:T(512)S(1)}, f32[384]{0:T(512)}, u32[]{:S(2)}) copy-start(f32[384]{0:T(512)} %get-tuple-element.21) | copy-start | bytes 4612
  221.7 6.8 %copy-start.35 = (f32[384]{0:T(512)S(1)}, f32[384]{0:T(512)}, u32[]{:S(2)}) copy-start(f32[384]{0:T(512)} %get-tuple-element.22) | copy-start | bytes 4612
  221.7 6.8 %copy-start.63 = (u32[128]{0:T(128)S(1)}, u32[128]{0:T(128)}, u32[]{:S(2)}) copy-start(u32[128]{0:T(128)} %constant.63) | copy-start | bytes 1540
  221.8 8.2 %copy-start.34 = (f32[384]{0:T(512)S(1)}, f32[384]{0:T(512)}, u32[]{:S(2)}) copy-start(f32[384]{0:T(512)} %get-tuple-element.36) | copy-start | bytes 4612
  221.8 143.3 %copy-start.62 = (s32[1,32]{1,0:T(1,128)S(1)}, s32[1,32]{1,0:T(1,128)}, u32[]{:S(2)}) copy-start(s32[1,32]{1,0:T(1,128)} %param.17) | copy-start | bytes 388
  (20 other events, 45.8 us)
Sparse Core Ops, SparseCore 0:
  109.3 91.6 reduce-scatter.2
  205.1 79.5 reduce-scatter.4
Sparse Core Ops, SparseCore 1:
  126.3 131.8 all-reduce.6
where the time goes:
time: 382 us; the launch traced here: 381 us
  blocking collectives  135 us (35%)
  other arithmetic  104 us (27%)
  waiting for transfers between devices  51.9 us (14%)
  matrix products  34.6 us (9%)
  local copies, waits for them, and re-layouts  30.4 us (8%)
  between operations  17.3 us (5%)
  starting transfers between devices  7.54 us (2%)
    psum x1, blocking collectives, on_device(): grad_kernel, grad_bias = lax.psum((kernel_term, bias_term), 'dp')  135 us
    reduce_scatter x1, waiting for transfers between devices, on_device(): lax.psum_scatter(partial_rows, 'mp', scatter_dimension=1, tiled=True)  51.9 us
    another operation x4, other arithmetic  50.2 us
    reduce_sum x3, other arithmetic, kernel_terms(): jnp.sum(grad_conv * shifted(padded, padded_segment, segment, tap_index -...  19.7 us
    add x1, other arithmetic, on_device(): conv_out = depthwise(gated, segment, conv_kernel, 1) + conv_bias  18.3 us
    dot_general x1, matrix products, on_device(): lax.dot_general(frames, grad_proj, (((0,), (0,)), ((), ())), preferred_el...  8.71 us
    reshape x1, local copies, waits for them, and re-layouts, on_device(): term.reshape(lax.axis_size('dp') * (width // count_dev), 2, channels)  8.25 us
    dot_general x1, matrix products, on_device(): lax.dot_general(grad_out, w_out, (((1,), (1,)), ((), ())), preferred_elem...  8.15 us
  transfers between devices with their start and end apart: 4, of which 1 were waited for; matrix products, arithmetic and copies ran while one was open for 17% of the time, Pallas kernels for 0%

commit v1 on v0

v1 whole, which is shorter than its diff:
```python
import math
import numpy as np
import jax, jax.numpy as jnp
from jax import lax
from jax.sharding import PartitionSpec as P
from jax.experimental import pallas as pl
from jax.experimental.pallas import tpu as pltpu

TAPS = 31
MAXLEN = 72
REACH = 15
WIN = 80
POINTS = 95
HALF = 48
FREQ = 2 * HALF
SEGS = 32
BLOCK = 256


def tables():
    f = np.arange(HALF)[:, None].astype(np.float64)
    w = np.where(f == 0, 1.0 / POINTS, 2.0 / POINTS)
    r = np.arange(WIN)[None, :]
    ang = 2 * np.pi * ((f * r) % POINTS) / POINTS
    fwd = np.concatenate([np.cos(ang), np.sin(ang)], 0)
    inv = np.concatenate([w * np.cos(ang), w * np.sin(ang)], 0).T
    t = np.arange(TAPS + 1)[None, :] - REACH
    tang = 2 * np.pi * ((f * t) % POINTS) / POINTS
    taps = np.concatenate([np.cos(tang), np.sin(tang)], 0)
    back = np.concatenate([w * np.cos(tang), -w * np.sin(tang)], 0).T
    taps[:, TAPS:] = 0
    back[TAPS:] = 0
    def split(table):
        high = table.astype(jnp.bfloat16).astype(np.float32)
        low = (table - high).astype(jnp.bfloat16).astype(np.float32)
        return np.concatenate([high, low, high], 1)

    return (
        jnp.asarray(split(fwd), jnp.float32),
        jnp.asarray(split(inv), jnp.bfloat16),
        jnp.asarray(taps, jnp.float32),
        jnp.asarray(back, jnp.float32),
    )


def pack_kernel(
    len_ref, frames_hbm, gout_hbm, w_ref, wout_ref, taps_ref, bias_ref,
    fwd_ref, inv_ref, tap_table_ref, back_table_ref,
    gp_ref, act_ref, kb_ref,
    fr, go, gsig, gated, gsw, conv, gc, spec, kf, acc, f_sem, g_sem,
):
    rows = frames_hbm.shape[0]
    ch = wout_ref.shape[0]
    blocks = rows // BLOCK

    def copy(hbm, vmem, sem, i):
        at = pl.ds(pl.multiple_of(i * BLOCK, BLOCK), BLOCK)
        return pltpu.make_async_copy(hbm.at[at], vmem.at[at], sem.at[i])

    for i in range(blocks):
        copy(frames_hbm, fr, f_sem, i).start()
        copy(gout_hbm, go, g_sem, i).start()

    tail = pl.ds(rows, WIN)
    gated[tail, :] = jnp.zeros((WIN, ch), jnp.float32)
    gc[tail, :] = jnp.zeros((WIN, ch), jnp.float32)
    kf[...] = jnp.dot(
        tap_table_ref[...], taps_ref[...],
        precision=lax.Precision.HIGHEST, preferred_element_type=jnp.float32,
    )
    acc[...] = jnp.zeros_like(acc)

    def project(i, carry):
        at = pl.ds(pl.multiple_of(i * BLOCK, BLOCK), BLOCK)
        copy(frames_hbm, fr, f_sem, i).wait()
        both = jnp.dot(fr[at, :], w_ref[...], preferred_element_type=jnp.float32)
        sig = jax.nn.sigmoid(both[:, ch:])
        g = both[:, :ch] * sig
        gsig[at, :] = sig
        gated[at, :] = g
        copy(gout_hbm, go, g_sem, i).wait()
        gsw[at, :] = lax.dot_general(
            go[at, :], wout_ref[...], (((1,), (1,)), ((), ())), preferred_element_type=jnp.float32
        )
        return carry

    lax.fori_loop(0, blocks, project, 0)

    lane = lax.rem(lax.broadcasted_iota(jnp.int32, (FREQ, 3 * WIN), 1), WIN)
    row16 = lax.broadcasted_iota(jnp.int32, (8, ch), 0)
    bias = bias_ref[...]

    def pieces(x):
        high = x.astype(jnp.bfloat16)
        low = (x - high.astype(jnp.float32)).astype(jnp.bfloat16)
        return jnp.concatenate([high, high, low], 0)

    def place(start):
        base = pl.multiple_of(lax.div(start, 8) * 8, 8)
        return base, start - base

    def spectrum(src, base, off, length):
        masked = jnp.where((lane >= off) & (lane < off + length), fwd_ref[...], 0.0)
        return jnp.dot(
            masked.astype(jnp.bfloat16), pieces(src[pl.ds(base, WIN), :]),
            preferred_element_type=jnp.float32,
        )

    def put(real, imag, base, off, shift):
        out = jnp.dot(
            inv_ref[...],
            pieces(jnp.concatenate([real, imag], 0)),
            preferred_element_type=jnp.float32,
        )
        if shift is not None:
            out = out + shift
        head = pl.ds(base, 8)
        conv[head, :] = jnp.where(row16 >= off, out[:8], conv[head, :])
        conv[pl.ds(base + 8, WIN - 8), :] = out[8:]

    def forward(k, start):
        length = len_ref[0, k]
        base, off = place(start)
        s = spectrum(gated, base, off, length)
        spec[k] = s
        gr, gi = s[:HALF], s[HALF:]
        kc, ks = kf[:HALF], kf[HALF:]
        put(kc * gr + ks * gi, kc * gi - ks * gr, base, off, bias)
        return start + length

    lax.fori_loop(0, SEGS, forward, 0)

    def swish(i, total):
        at = pl.ds(pl.multiple_of(i * BLOCK, BLOCK), BLOCK)
        c = conv[at, :]
        sig = jax.nn.sigmoid(c)
        act_ref[at, :] = (c * sig).astype(jnp.bfloat16)
        g = gsw[at, :] * sig * (1.0 + c * (1.0 - sig))
        gc[at, :] = g
        return total + jnp.sum(g.reshape(BLOCK // 8, 8, ch), axis=0)

    bias_sum = lax.fori_loop(0, blocks, swish, jnp.zeros((8, ch), jnp.float32))

    def backward(k, start):
        length = len_ref[0, k]
        base, off = place(start)
        s = spectrum(gc, base, off, length)
        cr, ci = s[:HALF], s[HALF:]
        g = spec[k]
        gr, gi = g[:HALF], g[HALF:]
        kc, ks = kf[:HALF], kf[HALF:]
        put(kc * cr - ks * ci, kc * ci + ks * cr, base, off, None)
        acc[:HALF, :] += gr * cr + gi * ci
        acc[HALF:, :] += gr * ci - gi * cr
        return start + length

    lax.fori_loop(0, SEGS, backward, 0)

    def project_back(i, carry):
        at = pl.ds(pl.multiple_of(i * BLOCK, BLOCK), BLOCK)
        g = conv[at, :]
        sig = gsig[at, :]
        gp_ref[at, :ch] = (g * sig).astype(jnp.bfloat16)
        gp_ref[at, ch:] = (g * gated[at, :] * (1.0 - sig)).astype(jnp.bfloat16)
        return carry

    lax.fori_loop(0, blocks, project_back, 0)

    taps_grad = jnp.dot(
        back_table_ref[...], acc[...],
        precision=lax.Precision.HIGHEST, preferred_element_type=jnp.float32,
    )
    which = lax.broadcasted_iota(jnp.int32, (TAPS + 1, ch), 0)
    kb_ref[...] = jnp.where(which < TAPS, taps_grad, jnp.sum(bias_sum, axis=0, keepdims=True))


def pack_call(lengths, frames, grad_out, w_flat, w_out, conv_kernel, conv_bias):
    rows, width = frames.shape
    ch = w_out.shape[0]
    fwd, inv, tap_table, back_table = tables()
    taps = jnp.concatenate([conv_kernel, jnp.zeros((1, ch), jnp.float32)], 0)
    vm = pl.BlockSpec(memory_space=pltpu.VMEM)
    blocks = rows // BLOCK
    f32, bf = jnp.float32, jnp.bfloat16
    return pl.pallas_call(
        pack_kernel,
        out_shape=(
            jax.ShapeDtypeStruct((rows, 2 * ch), bf),
            jax.ShapeDtypeStruct((rows, ch), bf),
            jax.ShapeDtypeStruct((TAPS + 1, ch), f32),
        ),
        in_specs=[
            pl.BlockSpec(memory_space=pltpu.SMEM),
            pl.BlockSpec(memory_space=pl.ANY),
            pl.BlockSpec(memory_space=pl.ANY),
        ] + [vm] * 8,
        out_specs=(vm, vm, vm),
        scratch_shapes=[
            pltpu.VMEM((rows, width), bf),
            pltpu.VMEM((rows, width), bf),
            pltpu.VMEM((rows, ch), f32),
            pltpu.VMEM((rows + WIN, ch), f32),
            pltpu.VMEM((rows, ch), f32),
            pltpu.VMEM((rows + WIN, ch), f32),
            pltpu.VMEM((rows + WIN, ch), f32),
            pltpu.VMEM((SEGS, FREQ, ch), f32),
            pltpu.VMEM((FREQ, ch), f32),
            pltpu.VMEM((FREQ, ch), f32),
            pltpu.SemaphoreType.DMA((blocks,)),
            pltpu.SemaphoreType.DMA((blocks,)),
        ],
        compiler_params=pltpu.CompilerParams(vmem_limit_bytes=56 * 1024 * 1024),
        cost_estimate=pl.CostEstimate(flops=8 * 10**9, bytes_accessed=18 * 10**6, transcendentals=0),
    )(lengths, frames, grad_out, w_flat, w_out, taps, conv_bias.reshape(1, ch), fwd, inv, tap_table, back_table)


def pick_kernel(len_ref, owner_ref, keep_a, keep_b, first_a, first_b, last_a, last_b, out_ref, held):
    half, ch = last_a.shape
    rows = 2 * half
    for at, keep, first, last in ((0, keep_a, first_a, last_a), (half, keep_b, first_b, last_b)):
        total = keep[:, :ch] + first[:, :ch].astype(jnp.float32) + last[...].astype(jnp.float32)
        held[pl.ds(at, half), :] = total.astype(jnp.bfloat16).astype(jnp.float32)
    held[pl.ds(rows, WIN), :] = jnp.zeros((WIN, ch), jnp.float32)
    row = lax.broadcasted_iota(jnp.int32, (MAXLEN, WIN), 0)
    lane = lax.broadcasted_iota(jnp.int32, (MAXLEN, WIN), 1)

    def pick(k, start):
        length = len_ref[0, k]
        base = pl.multiple_of(lax.div(start, 8) * 8, 8)
        hot = ((lane == row + (start - base)) & (row < length)).astype(jnp.float32)
        out_ref[owner_ref[0, k]] = jnp.dot(
            hot.astype(jnp.bfloat16), held[pl.ds(base, WIN), :].astype(jnp.bfloat16),
            preferred_element_type=jnp.float32,
        ).astype(jnp.bfloat16)
        return start + length

    lax.fori_loop(0, SEGS, pick, 0)


def pick_call(lengths, owners, *parts):
    half, ch = parts[-1].shape
    vm = pl.BlockSpec(memory_space=pltpu.VMEM)
    sm = pl.BlockSpec(memory_space=pltpu.SMEM)
    return pl.pallas_call(
        pick_kernel,
        out_shape=jax.ShapeDtypeStruct((SEGS, MAXLEN, ch), jnp.bfloat16),
        in_specs=[sm, sm] + [vm] * 6,
        out_specs=vm,
        scratch_shapes=[pltpu.VMEM((2 * half + WIN, ch), jnp.float32)],
        compiler_params=pltpu.CompilerParams(vmem_limit_bytes=40 * 1024 * 1024),
        cost_estimate=pl.CostEstimate(flops=10**9, bytes_accessed=10**7, transcendentals=0),
    )(lengths, owners, *parts)


def order_kernel(slot_ref, src, dst, sem):
    def copy(u):
        return pltpu.make_async_copy(src.at[slot_ref[0, u]], dst.at[u], sem.at[u])

    for u in range(SEGS):
        copy(u).start()
    for u in range(SEGS):
        copy(u).wait()


def order_call(slots, received):
    return pl.pallas_call(
        order_kernel,
        out_shape=jax.ShapeDtypeStruct(received.shape, received.dtype),
        in_specs=[pl.BlockSpec(memory_space=pltpu.SMEM), pl.BlockSpec(memory_space=pl.ANY)],
        out_specs=pl.BlockSpec(memory_space=pl.ANY),
        scratch_shapes=[pltpu.SemaphoreType.DMA((SEGS,))],
        cost_estimate=pl.CostEstimate(flops=0, bytes_accessed=4 * 10**6, transcendentals=0),
    )(slots, received)


def on_device(
    frames, grad_out, w_in, conv_kernel, conv_bias, w_out, seg_lengths, seg_owner, slot_device
):
    f32, bf = jnp.float32, jnp.bfloat16
    count_dev = lax.axis_size("dp")
    rows, width = frames.shape
    ch = w_out.shape[0]
    half = rows // 2
    scale = 1.0 / math.sqrt(rows * count_dev)
    w_flat = w_in.reshape(width, 2 * ch)
    grad_proj, activated, small = pack_call(
        seg_lengths, frames, grad_out, w_flat, w_out, conv_kernel, conv_bias
    )
    small_all = lax.all_gather(small, "dp", axis=0)

    mine = lax.axis_index("mp")
    near, far = mine ^ 1, 3 - mine
    other = 3 - near
    blocks = w_flat.reshape(4, ch, 2 * ch)

    def weights(a, b):
        return jnp.concatenate(
            [lax.dynamic_index_in_dim(blocks, a, 0, False), lax.dynamic_index_in_dim(blocks, b, 0, False)], 0
        )

    def part(rows_of, w):
        return lax.dot_general(rows_of, w, (((1,), (1,)), ((), ())), preferred_element_type=f32)

    pair = [(i, i ^ 1) for i in range(4)]
    cross = [(i, 3 - i) for i in range(4)]
    top, low = grad_proj[:half], grad_proj[half:]
    w_send = weights(near, other)
    first_a = lax.ppermute(part(top, w_send).astype(bf), "mp", pair)
    first_b = lax.ppermute(part(low, weights(far, other)).astype(bf), "mp", cross)
    keep_a = part(top, weights(mine, far))
    keep_b = part(low, weights(mine, near))
    last_a = lax.ppermute((keep_a[:, ch:] + first_a[:, ch:].astype(f32)).astype(bf), "mp", cross)
    last_b = lax.ppermute((keep_b[:, ch:] + first_b[:, ch:].astype(f32)).astype(bf), "mp", pair)
    outgoing = pick_call(seg_lengths, seg_owner, keep_a, keep_b, first_a, first_b, last_a, last_b)
    received = lax.all_to_all(outgoing, "dp", split_axis=0, concat_axis=0, tiled=True)
    dx_frames = order_call(slot_device, received)

    tn = (((0,), (0,)), ((), ()))
    term = lax.dot_general(frames, grad_proj, tn, preferred_element_type=f32).astype(bf)
    out_term = lax.dot_general(grad_out, activated, tn, preferred_element_type=f32).astype(bf)
    deep = width // count_dev
    terms = jnp.concatenate([term, out_term], 1).reshape(count_dev, deep, 3 * ch)
    terms = lax.all_to_all(terms, "dp", split_axis=0, concat_axis=0, tiled=True)
    sums = jnp.sum(terms.astype(f32), axis=0) * scale
    small_sum = jnp.sum(small_all, axis=0) * scale
    return (
        dx_frames,
        sums[:, : 2 * ch].reshape(deep, 2, ch),
        sums[:, 2 * ch :].T,
        small_sum[:TAPS],
        small_sum[TAPS],
    )

def solution(mesh):
    return jax.shard_map(
        on_device,
        mesh=mesh,
        in_specs=(
            P("dp", None),
            P("dp", None),
            P(None, None, "mp"),
            P(None, "mp"),
            P("mp"),
            P("mp", None),
            P("dp", None),
            P("dp", None),
            P("dp", None),
        ),
        out_specs=(P("dp", None, "mp"), P("dp", None, "mp"), P("mp", "dp"), P(None, "mp"), P("mp")),
        check_vma=False,
    )
```

time: 382 us -> 235 us (0.62)
  blocking collectives: 135 us -> 0 us
  Pallas kernels: 0 us -> 103 us
  other arithmetic: 104 us -> 3.93 us
  matrix products: 34.6 us -> 12.1 us
  starting transfers between devices: 7.54 us -> 19.4 us
  local copies, waits for them, and re-layouts: 30.4 us -> 20.9 us
  waiting for transfers between devices: 51.9 us -> 60.7 us
    psum x1 -> x0, blocking collectives: 135 us -> none  [on_device(): grad_kernel, grad_bias = lax.psum((kernel_term, bias_term), 'dp')]
    pallas_call x0 -> x3, Pallas kernels: none -> 103 us  [the longest x1 55.7 us: order_call(): pl.pallas_call(order_kernel, out_shape=jax.ShapeDtypeStruct(received.shap...]
    reduce_scatter x2 -> x0, waiting for transfers between devices: 51.9 us -> none  [the longest x1 51.9 us: on_device(): lax.psum_scatter(partial_rows, 'mp', scatter_dimension=1, tiled=True)]
    another operation x4 -> x0, other arithmetic: 50.2 us -> none
    ppermute x0 -> x4, waiting for transfers between devices: none -> 40.8 us  [the longest x1 22.7 us: on_device(): lax.ppermute(part(low, weights(far, other)).astype(bf), 'mp', cross)]
    dot_general x5 -> x6, matrix products: 34.6 us -> 12.1 us  [the longest x4 4.48 us: part(): lax.dot_general(rows_of, w, (((1,), (1,)), ((), ())), preferred_element_t...]
    all_to_all x1, waiting for transfers between devices: 0.01 us -> 19.2 us  [on_device(): lax.all_to_all(outgoing, 'dp', split_axis=0, concat_axis=0, tiled=True)]
    add x1 -> x0, other arithmetic: 18.3 us -> none  [on_device(): conv_out = depthwise(gated, segment, conv_kernel, 1) + conv_bias]
  transfers between devices with their start and end apart: 4 -> 7, of which waited for: 1 -> 5; matrix products, arithmetic and copies ran while one was open for 17% -> 8% of each run, Pallas kernels for 0% -> 3%
where the time goes in v1:
time: 235 us; the launch traced here: 234 us
  Pallas kernels  103 us (44%)
  waiting for transfers between devices  60.7 us (26%)
  local copies, waits for them, and re-layouts  20.9 us (9%)
  starting transfers between devices  19.4 us (8%)
  between operations  14.3 us (6%)
  matrix products  12.1 us (5%)
  other arithmetic  3.93 us (2%)
    pallas_call x1, Pallas kernels, order_call(): pl.pallas_call(order_kernel, out_shape=jax.ShapeDtypeStruct(received.shap...  55.7 us
    pallas_call x1, Pallas kernels, pack_call(): pl.pallas_call(pack_kernel, out_shape=(jax.ShapeDtypeStruct((rows, 2 * ch...  40.1 us
    ppermute x1, waiting for transfers between devices, on_device(): lax.ppermute(part(low, weights(far, other)).astype(bf), 'mp', cross)  22.7 us
    all_to_all x1, waiting for transfers between devices, on_device(): lax.all_to_all(outgoing, 'dp', split_axis=0, concat_axis=0, tiled=True)  19.2 us
    ppermute x1, waiting for transfers between devices, on_device(): lax.ppermute((keep_b[:, ch:] + first_b[:, ch:].astype(f32)).astype(bf), '...  12.1 us
    all_to_all x1, starting transfers between devices, on_device(): terms = lax.all_to_all(terms, 'dp', split_axis=0, concat_axis=0, tiled=True)  7.41 us
    pallas_call x1, Pallas kernels, pick_call(): pl.pallas_call(pick_kernel, out_shape=jax.ShapeDtypeStruct((SEGS, MAXLEN,...  7.26 us
    all_to_all x1, starting transfers between devices, on_device(): lax.all_to_all(outgoing, 'dp', split_axis=0, concat_axis=0, tiled=True)  7.23 us
  transfers between devices with their start and end apart: 7, of which 5 were waited for; matrix products, arithmetic and copies ran while one was open for 8% of the time, Pallas kernels for 3%

profile of v1, /device:TPU:0, one launch (start us, length us, event | category | flops | bytes accessed | tf_op | source)
XLA Modules:
  0.0 234.3 jit_solution(3248556290393329650)
XLA Ops:
  7.2 1.2 reshape.23.bias_ref
  8.4 3.7 %copy.19 = bf16[192,8,2,384]{3,1,2,0:T(8,128)(2,1)} copy(bf16[192,8,2,384]{3,2,1,0:T(2,128)(2,1)} %bitcast.24) | data formatting | bytes 4718592
  12.1 0.0 copy-done.3
  12.1 0.6 concatenate.18.taps_ref
  12.8 40.1 %shard_map.164 = (bf16[1536,768]{1,0:T(8,128)(2,1)}, bf16[1536,384]{1,0:T(8,128)(2,1)}, f32[32,384]{1,0:T(8,128)}) custom-call(s32[1,32]{1,0:T(1,128)} %len_ref.3, bf16[1536,1536]{1,0:T(8,128)(2,1)} %frames_hbm.1, bf16[1536,1536]{1,0:T(8,128)(2,1)} %gout_hbm.1, bf16[1536,768]{1,0:T(8,128)(2,1)} %bitcast.25, bf16[384,1536]{1,0:T(8,128)(2,1)} %wout_ref.1, ...), custom_call_target="tpu_custom_call" | custom-call | flops 8000000000 | bytes 18000000 | tf_op jit(solution)/shard_map/pallas_call | solution.py:185
  52.9 0.0 slice-done
  52.9 0.0 slice-done.1
  52.9 0.0 copy-start.4
  52.9 0.0 copy-start.5
  52.9 3.4 %fusion.1 = bf16[1536,384]{0,1:T(8,128)(2,1)S(1)} fusion(bf16[1536,384]{1,0:T(8,128)(2,1)} %get-tuple-element.9, bf16[1536,1536]{1,0:T(8,128)(2,1)S(1)} %bitcast.29), kind=kOutput, calls=%fused_computation.5 | convolution fusion | flops 1812529152 | bytes 7077888 | tf_op jit(solution)/shard_map/dot_general | solution.py:320
  56.4 4.2 %fusion = bf16[1536,768]{0,1:T(8,128)(2,1)S(1)} fusion(bf16[1536,768]{1,0:T(8,128)(2,1)S(1)} %copy-done.5, bf16[1536,1536]{1,0:T(8,128)(2,1)S(1)} %copy-done.4), kind=kOutput, calls=%fused_computation.3 | convolution fusion | flops 3625058304 | bytes 9437184 | tf_op jit(solution)/shard_map/dot_general | solution.py:319
  60.6 0.2 pad_maximum_fusion
  60.8 3.8 %copy.18 = bf16[1536,1152]{1,0:T(8,128)(2,1)} copy(bf16[1536,1152]{0,1:T(8,128)(2,1)S(1)} %pad_maximum_fusion) | data formatting | bytes 7077888 | tf_op jit(solution)/shard_map/concatenate | solution.py:322
  64.7 7.4 %all-to-all-start.1 = ((bf16[32,48,1152]{2,1,0:T(8,128)(2,1)}), bf16[32,48,1152]{2,1,0:T(8,128)(2,1)S(1)}, u32[]{:S(2)}, u32[]{:S(2)}) async-start(bf16[32,48,1152]{2,1,0:T(8,128)(2,1)} %bitcast.23), calls=%async_computation.1 | async-start | bytes 7077888 | tf_op jit(solution)/shard_map/all_to_all | solution.py:323
  72.1 0.0 all-gather.3.cloned.1.call-start
  72.1 0.7 all-gather.3.cloned.1.call-update
  72.8 6.5 %reshape_reshape.3 = bf16[4,384,768]{2,1,0:T(8,128)(2,1)} reshape(bf16[1536,2,384]{2,1,0:T(2,128)(2,1)} %param.15) | data formatting | bytes 4718592 | tf_op jit(solution)/shard_map/reshape;reshape | solution.py:294
  79.3 1.9 dynamic-slice_bitcast_fusion
  81.2 0.5 copy-done.6
  81.7 1.1 convolution_convert_fusion.2
  82.8 4.1 %collective-permute-start.1 = (bf16[768,768]{1,0:T(8,128)(2,1)S(1)}, bf16[768,768]{1,0:T(8,128)(2,1)S(1)}, u32[]{:S(2)}, u32[]{:S(2)}) collective-permute-start(bf16[768,768]{1,0:T(8,128)(2,1)S(1)} %convolution_convert_fusion.2), channel_id=1, source_target_pairs={{0,3},{1,2},{2,1},{3,0},{4,7},{5,6},{6,5},{7,4},{8,11},{9,10},{10,... | collective-permute-start | bytes 3538952 | tf_op jit(solution)/shard_map/ppermute | solution.py:309
  86.9 1.1 convolution_convert_fusion.3
  88.0 0.3 collective-permute-start
  88.3 1.1 fusion.3.keep_b
  89.4 1.1 fusion.2.keep_a
  90.5 0.0 copy-start
  90.6 0.0 copy-start.1
  90.6 22.7 %collective-permute-done.1.first_b = bf16[768,768]{1,0:T(8,128)(2,1)S(1)} collective-permute-done((bf16[768,768]{1,0:T(8,128)(2,1)S(1)}, bf16[768,768]{1,0:T(8,128)(2,1)S(1)}, u32[]{:S(2)}, u32[]{:S(2)}) %collective-permute-start.1) | collective-permute-done | bytes 1179680 | tf_op jit(solution)/shard_map/ppermute | solution.py:309
  113.3 0.1 fusion.4
  113.4 0.1 collective-permute-start.3
  113.5 2.8 %collective-permute-done.first_a = bf16[768,768]{1,0:T(8,128)(2,1)S(1)} collective-permute-done((bf16[768,768]{1,0:T(8,128)(2,1)S(1)}, bf16[768,768]{1,0:T(8,128)(2,1)S(1)}, u32[]{:S(2)}, u32[]{:S(2)}) %collective-permute-start) | collective-permute-done | bytes 1179680 | tf_op jit(solution)/shard_map/ppermute | solution.py:308
  116.3 0.1 fusion.5
  116.5 0.2 collective-permute-start.2
  116.7 12.1 %collective-permute-done.3.last_b = bf16[768,384]{1,0:T(8,128)(2,1)S(1)} collective-permute-done((bf16[768,384]{1,0:T(8,128)(2,1)S(1)}, bf16[768,384]{1,0:T(8,128)(2,1)S(1)}, u32[]{:S(2)}, u32[]{:S(2)}) %collective-permute-start.3) | collective-permute-done | bytes 589856 | tf_op jit(solution)/shard_map/ppermute | solution.py:313
  128.8 3.2 %collective-permute-done.2.last_a = bf16[768,384]{1,0:T(8,128)(2,1)S(1)} collective-permute-done((bf16[768,384]{1,0:T(8,128)(2,1)S(1)}, bf16[768,384]{1,0:T(8,128)(2,1)S(1)}, u32[]{:S(2)}, u32[]{:S(2)}) %collective-permute-start.2) | collective-permute-done | bytes 589856 | tf_op jit(solution)/shard_map/ppermute | solution.py:312
  132.0 7.3 %shard_map.165 = bf16[32,72,384]{2,1,0:T(8,128)(2,1)} custom-call(s32[1,32]{1,0:T(1,128)S(1)} %copy-done, s32[1,32]{1,0:T(1,128)S(1)} %copy-done.1, f32[768,768]{1,0:T(8,128)S(1)} %fusion.2.keep_a, f32[768,768]{1,0:T(8,128)S(1)} %fusion.3.keep_b, bf16[768,768]{1,0:T(8,128)(2,1)S(1)} %collective-permute-done.first_a, ...), custom_call_target="tpu_custom_call" | custom-call | flops 1000000000 | bytes 10000000 | tf_op jit(solution)/shard_map/pallas_call | solution.py:244
  139.2 0.0 all-to-all-done.1
  139.2 7.2 %all-to-all-start = ((bf16[32,72,384]{2,1,0:T(8,128)(2,1)}), bf16[32,72,384]{2,1,0:T(8,128)(2,1)}, u32[]{:S(2)}, u32[]{:S(2)}) async-start(bf16[32,72,384]{2,1,0:T(8,128)(2,1)} %shard_map.165), calls=%async_computation | async-start | bytes 3538944 | tf_op jit(solution)/shard_map/all_to_all | solution.py:315
  146.4 0.0 all-gather.3.cloned.1.call-done
  146.5 2.1 reduce_sum.19
  148.6 0.8 broadcast_multiply_fusion.1
  149.4 0.6 copy-done.2
  150.0 0.6 slice_reduce_fusion
  150.6 0.5 convert_reduce_fusion
  151.2 0.7 reshape.25
  151.9 0.6 slice_bitcast_fusion
  152.6 19.2 %all-to-all-done.src = bf16[32,72,384]{2,1,0:T(8,128)(2,1)} async-done(((bf16[32,72,384]{2,1,0:T(8,128)(2,1)}), bf16[32,72,384]{2,1,0:T(8,128)(2,1)}, u32[]{:S(2)}, u32[]{:S(2)}) %all-to-all-start) | async-done | bytes 1769504 | tf_op jit(solution)/shard_map/all_to_all | solution.py:315
  171.7 55.7 %shard_map.166 = bf16[32,72,384]{2,1,0:T(8,128)(2,1)} custom-call(s32[1,32]{1,0:T(1,128)} %slot_ref.1, bf16[32,72,384]{2,1,0:T(8,128)(2,1)} %all-to-all-done.src), custom_call_target="tpu_custom_call" | custom-call | bytes 4000000 | tf_op jit(solution)/shard_map/pallas_call | solution.py:266
  (12 shorter events, 0.1 us)
Async XLA Ops:
  8.4 3.7 %copy-start.3 = (f32[31,384]{1,0:T(8,128)S(1)}, f32[31,384]{1,0:T(8,128)}, u32[]{:S(2)}) copy-start(f32[31,384]{1,0:T(8,128)} %param.16) | copy-start | bytes 142852
  8.4 44.5 %slice-start = ((s8[4718592]{0:T(1024)(128)(4,1)}), s8[4194304]{0:T(1024)(128)(4,1)S(1)}, s32[]{:S(2)}) async-start(s8[4718592]{0:T(1024)(128)(4,1)} %bitcast.28), calls=%async_computation.3 | async-start | bytes 8388608
  12.8 40.2 %slice-start.1 = ((s8[4718592]{0:T(1024)(128)(4,1)}), s8[524288]{0:T(1024)(128)(4,1)S(1)}, s32[]{:S(2)}) async-start(s8[4718592]{0:T(1024)(128)(4,1)} %bitcast.28), calls=%async_computation.4 | async-start | bytes 1048576
  52.9 3.5 %copy-start.4 = (bf16[1536,1536]{1,0:T(8,128)(2,1)S(1)}, bf16[1536,1536]{1,0:T(8,128)(2,1)}, u32[]{:S(2)}) copy-start(bf16[1536,1536]{1,0:T(8,128)(2,1)} %frames_hbm.1) | copy-start | bytes 14155780
  52.9 3.5 %copy-start.5 = (bf16[1536,768]{1,0:T(8,128)(2,1)S(1)}, bf16[1536,768]{1,0:T(8,128)(2,1)}, u32[]{:S(2)}) copy-start(bf16[1536,768]{1,0:T(8,128)(2,1)} %get-tuple-element.8) | copy-start | bytes 7077892
  64.7 74.6 %all-to-all-start.1 = ((bf16[32,48,1152]{2,1,0:T(8,128)(2,1)}), bf16[32,48,1152]{2,1,0:T(8,128)(2,1)S(1)}, u32[]{:S(2)}, u32[]{:S(2)}) async-start(bf16[32,48,1152]{2,1,0:T(8,128)(2,1)} %bitcast.23), calls=%async_computation.1 | async-start | bytes 7077888 | tf_op jit(solution)/shard_map/all_to_all | solution.py:323
  72.1 74.4 %all-gather.3.cloned.1.call-start = ((), (), s32[]{:S(2)}) async-start(), calls=%async_computation.2 | async-start | bytes 1622016 | tf_op jit(solution)/shard_map/all_gather | solution.py:289
  79.3 2.4 %copy-start.6 = (bf16[1536,768]{1,0:T(8,128)(2,1)S(1)}, bf16[1536,768]{1,0:T(8,128)(2,1)}, u32[]{:S(2)}) copy-start(bf16[1536,768]{1,0:T(8,128)(2,1)} %get-tuple-element.8) | copy-start | bytes 7077892
  82.8 30.5 %collective-permute-start.1 = (bf16[768,768]{1,0:T(8,128)(2,1)S(1)}, bf16[768,768]{1,0:T(8,128)(2,1)S(1)}, u32[]{:S(2)}, u32[]{:S(2)}) collective-permute-start(bf16[768,768]{1,0:T(8,128)(2,1)S(1)} %convolution_convert_fusion.2), channel_id=1, source_target_pairs={{0,3},{1,2},{2,1},{3,0},{4,7},{5,6},{6,5},{7,4},{8,11},{9,10},{10,... | collective-permute-start | bytes 3538952 | tf_op jit(solution)/shard_map/ppermute | solution.py:309
  88.0 28.3 %collective-permute-start = (bf16[768,768]{1,0:T(8,128)(2,1)S(1)}, bf16[768,768]{1,0:T(8,128)(2,1)S(1)}, u32[]{:S(2)}, u32[]{:S(2)}) collective-permute-start(bf16[768,768]{1,0:T(8,128)(2,1)S(1)} %convolution_convert_fusion.3), channel_id=1, source_target_pairs={{0,1},{1,0},{2,3},{3,2},{4,5},{5,4},{6,7},{7,6},{8,9},{9,8},{10,11... | collective-permute-start | bytes 3538952 | tf_op jit(solution)/shard_map/ppermute | solution.py:308
  90.5 41.4 %copy-start = (s32[1,32]{1,0:T(1,128)S(1)}, s32[1,32]{1,0:T(1,128)}, u32[]{:S(2)}) copy-start(s32[1,32]{1,0:T(1,128)} %len_ref.3) | copy-start | bytes 388
  90.6 41.4 %copy-start.1 = (s32[1,32]{1,0:T(1,128)S(1)}, s32[1,32]{1,0:T(1,128)}, u32[]{:S(2)}) copy-start(s32[1,32]{1,0:T(1,128)} %owner_ref.1) | copy-start | bytes 388
  113.4 15.4 %collective-permute-start.3 = (bf16[768,384]{1,0:T(8,128)(2,1)S(1)}, bf16[768,384]{1,0:T(8,128)(2,1)S(1)}, u32[]{:S(2)}, u32[]{:S(2)}) collective-permute-start(bf16[768,384]{1,0:T(8,128)(2,1)S(1)} %fusion.4), channel_id=1, source_target_pairs={{0,1},{1,0},{2,3},{3,2},{4,5},{5,4},{6,7},{7,6},{8,9},{9,8},{10,11... | collective-permute-start | bytes 1769480 | tf_op jit(solution)/shard_map/ppermute | solution.py:313
  116.5 15.5 %collective-permute-start.2 = (bf16[768,384]{1,0:T(8,128)(2,1)S(1)}, bf16[768,384]{1,0:T(8,128)(2,1)S(1)}, u32[]{:S(2)}, u32[]{:S(2)}) collective-permute-start(bf16[768,384]{1,0:T(8,128)(2,1)S(1)} %fusion.5), channel_id=1, source_target_pairs={{0,3},{1,2},{2,1},{3,0},{4,7},{5,6},{6,5},{7,4},{8,11},{9,10},{10,... | collective-permute-start | bytes 1769480 | tf_op jit(solution)/shard_map/ppermute | solution.py:312
  139.2 32.5 %all-to-all-start = ((bf16[32,72,384]{2,1,0:T(8,128)(2,1)}), bf16[32,72,384]{2,1,0:T(8,128)(2,1)}, u32[]{:S(2)}, u32[]{:S(2)}) async-start(bf16[32,72,384]{2,1,0:T(8,128)(2,1)} %shard_map.165), calls=%async_computation | async-start | bytes 3538944 | tf_op jit(solution)/shard_map/all_to_all | solution.py:315
  149.4 0.6 copy-start.2
Sparse Core Ops, SparseCore 0:
  75.7 61.7 all-gather.2

commit v2 on v0

v2 whole, which is shorter than its diff:
```python
import math

import jax
import jax.numpy as jnp
import numpy as np
from jax import lax
from jax.experimental import pallas as pl
from jax.experimental.pallas import tpu as pltpu
from jax.sharding import PartitionSpec as P

TAPS = 31
MAXLEN = 72
REACH = 15
WIN = 80
POINTS = 95
HALF = 48
FREQ = 2 * HALF
MARGIN = 96
SEGS = 32
GROUP = 4
MIB = 1024 * 1024
F32, BF16 = jnp.float32, jnp.bfloat16
NT = (((1,), (1,)), ((), ()))
TN = (((0,), (0,)), ((), ()))


def tables():
    f = np.arange(HALF)[:, None].astype(np.float64)
    w = np.where(f == 0, 1.0 / POINTS, 2.0 / POINTS)
    ang = 2 * np.pi * ((f * np.arange(WIN)[None, :]) % POINTS) / POINTS
    fwd = np.concatenate([np.cos(ang), np.sin(ang)], 0)
    inv = np.concatenate([w * np.cos(ang), w * np.sin(ang)], 0).T
    tang = 2 * np.pi * ((f * (np.arange(TAPS)[None, :] - REACH)) % POINTS) / POINTS
    taps = np.concatenate([np.cos(tang), np.sin(tang)], 0)
    back = np.concatenate([w * np.cos(tang), -w * np.sin(tang)], 0).T

    def split(table):
        high = table.astype(BF16).astype(np.float32)
        low = (table - high).astype(BF16).astype(np.float32)
        return np.concatenate([high, low, high], 1)

    return (
        jnp.asarray(split(fwd), F32),
        jnp.asarray(split(inv), BF16),
        jnp.asarray(taps, F32),
        jnp.asarray(back, F32),
    )


def aligned(start, rows):
    base = pl.multiple_of(lax.div(start, rows) * rows, rows)
    return base, start - base


def pieces(x):
    high = x.astype(BF16)
    low = (x - high.astype(F32)).astype(BF16)
    return jnp.concatenate([high, high, low], 0)


def chunk_kernel(first, rows, load, last, halves, *refs):
    (len_ref, frames_hbm, gout_hbm, w_ref, wout_ref, taps_ref, bias_ref,
     fwd_ref, inv_ref, tap_table_ref, back_table_ref) = refs[:11]
    refs = refs[11:]
    if first:
        gp_prev, act_prev, sum_prev = refs[:3]
        refs = refs[3:]
    gp_ref, act_ref, sum_ref = refs[:3]
    outs = refs[3 : 3 + len(halves)]
    fr, go, gsig, gated, gsw, conv, gc, spec, kf, acc, f_sem, g_sem = refs[3 + len(halves) :]
    ch = wout_ref.shape[0]
    blocks = 3
    block = load // blocks

    def copy(hbm, vmem, sem, i):
        src = pl.ds(pl.multiple_of(first + i * block, 16), block)
        dst = pl.ds(pl.multiple_of(i * block, 16), block)
        return pltpu.make_async_copy(hbm.at[src], vmem.at[dst], sem.at[i])

    for i in range(blocks):
        copy(frames_hbm, fr, f_sem, i).start()
        copy(gout_hbm, go, g_sem, i).start()

    tail = pl.ds(load, WIN)
    gated[tail, :] = jnp.zeros((WIN, ch), F32)
    gc[tail, :] = jnp.zeros((WIN, ch), F32)
    conv[...] = jnp.zeros_like(conv)
    kf[...] = jnp.dot(
        tap_table_ref[...], taps_ref[...],
        precision=lax.Precision.HIGHEST, preferred_element_type=F32,
    )
    acc[...] = sum_prev[...] if first else jnp.zeros_like(acc)

    def before(state):
        return state[1] < first

    def skip(state):
        return state[0] + 1, state[1] + len_ref[0, state[0]]

    k0, s0 = lax.while_loop(before, skip, (jnp.int32(0), jnp.int32(0)))
    s0 = s0 - first

    def project(i, carry):
        at = pl.ds(pl.multiple_of(i * block, 16), block)
        copy(frames_hbm, fr, f_sem, i).wait()
        both = jnp.dot(fr[at, :], w_ref[...], preferred_element_type=F32)
        sig = jax.nn.sigmoid(both[:, ch:])
        gsig[at, :] = sig
        gated[at, :] = both[:, :ch] * sig
        copy(gout_hbm, go, g_sem, i).wait()
        gsw[at, :] = lax.dot_general(go[at, :], wout_ref[...], NT, preferred_element_type=F32)
        return carry

    lax.fori_loop(0, blocks, project, 0)

    lane = lax.rem(lax.broadcasted_iota(jnp.int32, (FREQ, 3 * WIN), 1), WIN)
    row8 = lax.broadcasted_iota(jnp.int32, (8, ch), 0)

    def spectrum(src, base, off, length):
        masked = jnp.where((lane >= off) & (lane < off + length), fwd_ref[...], 0.0)
        return jnp.dot(
            masked.astype(BF16), pieces(src[pl.ds(base, WIN), :]), preferred_element_type=F32
        )

    def inverse(real, imag):
        return jnp.dot(
            inv_ref[...], pieces(jnp.concatenate([real, imag], 0)), preferred_element_type=F32
        )

    def put(out, base, off):
        head = pl.ds(base, 8)
        conv[head, :] = jnp.where(row8 >= off, out[:8], conv[head, :])
        conv[pl.ds(base + 8, WIN - 8), :] = out[8:]

    def group_of(start, k):
        places = []
        for j in range(GROUP):
            live = (start < rows) & (k + j < SEGS)
            length = jnp.where(live, len_ref[0, jnp.minimum(k + j, SEGS - 1)], 0)
            base, off = aligned(jnp.where(live, start, load), 8)
            places.append((base, off, length))
            start = start + length
        return places, start

    def more(state):
        return (state[1] < rows) & (state[0] < SEGS)

    def forward(state):
        k, start = state
        places, start = group_of(start, k)
        results = []
        kc, ks = kf[:HALF], kf[HALF:]
        for j, (base, off, length) in enumerate(places):
            s = spectrum(gated, base, off, length)
            spec[k - k0 + j] = s
            gr, gi = s[:HALF], s[HALF:]
            results.append(inverse(kc * gr + ks * gi, kc * gi - ks * gr))
        for (base, off, length), out in zip(places, results):
            put(out, base, off)
        return k + GROUP, start

    lax.while_loop(more, forward, (k0, s0))

    bias = bias_ref[...]

    def swish(i, carry):
        at = pl.ds(pl.multiple_of(i * block, 16), block)
        c = conv[at, :] + bias
        sig = jax.nn.sigmoid(c)
        act_ref[at, :] = (c * sig).astype(BF16)
        gc[at, :] = gsw[at, :] * sig * (1.0 + c * (1.0 - sig))
        return carry

    lax.fori_loop(0, blocks, swish, 0)

    def backward(state):
        k, start = state
        places, start = group_of(start, k)
        results = []
        kc, ks = kf[:HALF], kf[HALF:]
        real = jnp.zeros((HALF, ch), F32)
        imag = jnp.zeros((HALF, ch), F32)
        plain = jnp.zeros((8, ch), F32)
        for j, (base, off, length) in enumerate(places):
            s = spectrum(gc, base, off, length)
            cr, ci = s[:HALF], s[HALF:]
            g = spec[k - k0 + j]
            gr, gi = g[:HALF], g[HALF:]
            results.append(inverse(kc * cr - ks * ci, kc * ci + ks * cr))
            real += gr * cr + gi * ci
            imag += gr * ci - gi * cr
            plain += s[:8]
        acc[:HALF, :] += real
        acc[HALF:FREQ, :] += imag
        acc[FREQ:, :] += plain
        for (base, off, length), out in zip(places, results):
            put(out, base, off)
        return k + GROUP, start

    lax.while_loop(more, backward, (k0, s0))

    def project_back(i, carry):
        at = pl.ds(pl.multiple_of(i * block, 16), block)
        g = conv[at, :]
        sig = gsig[at, :]
        gp_ref[at, :ch] = (g * sig).astype(BF16)
        gp_ref[at, ch:] = (g * gated[at, :] * (1.0 - sig)).astype(BF16)
        return carry

    lax.fori_loop(0, blocks, project_back, 0)

    if first:
        head = pl.ds(0, MARGIN)
        from_prev = lax.broadcasted_iota(jnp.int32, (MARGIN, 1), 0) < s0
        gp_ref[head, :] = jnp.where(
            from_prev, gp_prev[...].astype(F32), gp_ref[head, :].astype(F32)
        ).astype(BF16)
        act_ref[head, :] = jnp.where(
            from_prev, act_prev[...].astype(F32), act_ref[head, :].astype(F32)
        ).astype(BF16)

    mine = lax.axis_index("mp")
    for out, (start, size, picks) in zip(outs, halves):
        for j, pick in enumerate(picks):
            at = pl.ds(pl.multiple_of(pick(mine) * ch, ch), ch)
            out[:, j * ch : (j + 1) * ch] = lax.dot_general(
                gp_ref[start : start + size, :], w_ref[at, :], NT, preferred_element_type=F32
            ).astype(out.dtype)

    if last:
        taps_grad = jnp.dot(
            back_table_ref[...], acc[:FREQ, :],
            precision=lax.Precision.HIGHEST, preferred_element_type=F32,
        )
        sum_ref[:TAPS, :] = taps_grad
        sum_ref[TAPS:, :] = acc[FREQ : FREQ + 1, :]
    else:
        sum_ref[...] = acc[...]


def chunk_call(first, rows, halves, prev, lengths, frames, grad_out, w_flat, w_out, taps, bias, consts):
    total, width = frames.shape
    ch = w_out.shape[0]
    last = first + rows == total
    load = rows if last else rows + MARGIN
    vm = pl.BlockSpec(memory_space=pltpu.VMEM)
    hbm = pl.BlockSpec(memory_space=pl.ANY)
    sm = pl.BlockSpec(memory_space=pltpu.SMEM)
    operands = [lengths, frames, grad_out, w_flat, w_out, taps, bias, *consts]
    specs = [sm, hbm, hbm] + [vm] * 8
    if first:
        gp_prev, act_prev, sum_prev = prev
        at = gp_prev.shape[0] - MARGIN
        operands += [gp_prev[at:], act_prev[at:], sum_prev]
        specs += [vm] * 3

    def body(*refs):
        chunk_kernel(first, rows, load, last, [h[:3] for h in halves], *refs)

    out_shape = [
        jax.ShapeDtypeStruct((load, 2 * ch), BF16),
        jax.ShapeDtypeStruct((load, ch), BF16),
        jax.ShapeDtypeStruct((TAPS + 1 if last else FREQ + 8, ch), F32),
    ] + [jax.ShapeDtypeStruct((size, len(picks) * ch), dtype) for _, size, picks, dtype in halves]
    return pl.pallas_call(
        body,
        out_shape=out_shape,
        in_specs=specs,
        out_specs=[vm] * len(out_shape),
        scratch_shapes=[
            pltpu.VMEM((load, width), BF16),
            pltpu.VMEM((load, width), BF16),
            pltpu.VMEM((load, ch), F32),
            pltpu.VMEM((load + WIN, ch), F32),
            pltpu.VMEM((load, ch), F32),
            pltpu.VMEM((load + WIN, ch), F32),
            pltpu.VMEM((load + WIN, ch), F32),
            pltpu.VMEM((SEGS + GROUP, FREQ, ch), F32),
            pltpu.VMEM((FREQ, ch), F32),
            pltpu.VMEM((FREQ + 8, ch), F32),
            pltpu.SemaphoreType.DMA((3,)),
            pltpu.SemaphoreType.DMA((3,)),
        ],
        compiler_params=pltpu.CompilerParams(vmem_limit_bytes=48 * MIB),
        cost_estimate=pl.CostEstimate(flops=2 * 10**10, bytes_accessed=2 * 10**7, transcendentals=0),
        name="chunk%d" % first,
    )(*operands)


def pick_kernel(
    len_ref, owner_ref, keep0, near0, far0, back0, keep_a, keep_b, first_a, first_b, last_a, last_b,
    out_ref, held,
):
    rows0, ch = keep0.shape
    half = last_a.shape[0]
    rows = rows0 + 2 * half
    held[pl.ds(0, rows0), :] = (
        keep0[...] + near0[...].astype(F32) + far0[...].astype(F32) + back0[...].astype(F32)
    ).astype(BF16)
    for at, keep, one, two in ((rows0, keep_a, first_a, last_a), (rows0 + half, keep_b, first_b, last_b)):
        held[pl.ds(at, half), :] = (
            keep[:, :ch] + one[:, :ch].astype(F32) + two[...].astype(F32)
        ).astype(BF16)
    held[pl.ds(rows, MARGIN), :] = jnp.zeros((MARGIN, ch), BF16)
    row = lax.broadcasted_iota(jnp.int32, (MAXLEN, MARGIN), 0)
    lane = lax.broadcasted_iota(jnp.int32, (MAXLEN, MARGIN), 1)

    def pick(i, start):
        for j in range(GROUP):
            k = i * GROUP + j
            length = len_ref[0, k]
            base, off = aligned(start, 16)
            hot = jnp.where((lane == row + off) & (row < length), 1.0, 0.0).astype(BF16)
            out_ref[owner_ref[0, k]] = jnp.dot(
                hot, held[pl.ds(base, MARGIN), :], preferred_element_type=F32
            ).astype(BF16)
            start = start + length
        return start

    lax.fori_loop(0, SEGS // GROUP, pick, jnp.int32(0))


def pick_call(lengths, owners, rows, *parts):
    ch = parts[-1].shape[1]
    vm = pl.BlockSpec(memory_space=pltpu.VMEM)
    sm = pl.BlockSpec(memory_space=pltpu.SMEM)
    return pl.pallas_call(
        pick_kernel,
        out_shape=jax.ShapeDtypeStruct((SEGS, MAXLEN, ch), BF16),
        in_specs=[sm, sm] + [vm] * len(parts),
        out_specs=vm,
        scratch_shapes=[pltpu.VMEM((rows + MARGIN, ch), BF16)],
        compiler_params=pltpu.CompilerParams(vmem_limit_bytes=40 * MIB),
        cost_estimate=pl.CostEstimate(flops=10**9, bytes_accessed=10**7, transcendentals=0),
        name="pick",
    )(lengths, owners, *parts)


def order_kernel(slot_ref, src, dst, sem):
    def copy(u):
        return pltpu.make_async_copy(src.at[slot_ref[0, u]], dst.at[u], sem.at[u])

    for u in range(SEGS):
        copy(u).start()
    for u in range(SEGS):
        copy(u).wait()


def order_call(slots, received):
    return pl.pallas_call(
        order_kernel,
        out_shape=jax.ShapeDtypeStruct(received.shape, received.dtype),
        in_specs=[pl.BlockSpec(memory_space=pltpu.SMEM), pl.BlockSpec(memory_space=pltpu.VMEM)],
        out_specs=pl.BlockSpec(memory_space=pl.ANY),
        scratch_shapes=[pltpu.SemaphoreType.DMA((SEGS,))],
        compiler_params=pltpu.CompilerParams(vmem_limit_bytes=16 * MIB),
        cost_estimate=pl.CostEstimate(flops=0, bytes_accessed=4 * 10**6, transcendentals=0),
        name="order",
    )(slots, received)


def weight_kernel(deep, frames_ref, gout_ref, gp0, gp1, act0, act1, keep_ref, send_ref, held):
    core = lax.rem(lax.axis_index("dp"), 2)
    total, cols = frames_ref.shape
    rows1 = gp1.shape[0]
    rows0 = total - rows1
    wide = gp0.shape[1]

    def both(left, right0, right1):
        one = lax.dot_general(left[:rows0, :], right0[:rows0, :], TN, preferred_element_type=F32)
        return one + lax.dot_general(left[rows0:, :], right1[...], TN, preferred_element_type=F32)

    held[:, :wide] = both(frames_ref, gp0, gp1)
    held[:, wide:] = both(gout_ref, act0, act1)
    for j in range(cols // (2 * deep)):
        own = pl.ds(pl.multiple_of((2 * j + core) * deep, 16), deep)
        other = pl.ds(pl.multiple_of((2 * j + 1 - core) * deep, 16), deep)
        keep_ref[j] = held[own, :]
        send_ref[j] = held[other, :].astype(BF16)


def weight_call(deep, frames, grad_out, gp0, gp1, act0, act1):
    total, width = frames.shape
    wide = gp0.shape[1] + act0.shape[1]
    cols = width // 4
    pairs = width // (2 * deep)
    vm = pl.BlockSpec(memory_space=pltpu.VMEM)
    tall = pl.BlockSpec((total, cols), lambda i: (0, i))
    out = pl.BlockSpec((pairs // 4, deep, wide), lambda i: (i, 0, 0))
    return pl.pallas_call(
        lambda *refs: weight_kernel(deep, *refs),
        grid=(4,),
        out_shape=(
            jax.ShapeDtypeStruct((pairs, deep, wide), F32),
            jax.ShapeDtypeStruct((pairs, deep, wide), BF16),
        ),
        in_specs=[tall, tall, vm, vm, vm, vm],
        out_specs=(out, out),
        scratch_shapes=[pltpu.VMEM((cols, wide), F32)],
        compiler_params=pltpu.CompilerParams(vmem_limit_bytes=48 * MIB),
        cost_estimate=pl.CostEstimate(flops=11 * 10**9, bytes_accessed=2 * 10**7, transcendentals=0),
        name="weight",
    )(frames, grad_out, gp0, gp1, act0, act1)


def on_device(
    frames, grad_out, w_in, conv_kernel, conv_bias, w_out, seg_lengths, seg_owner, slot_device
):
    count_dev = lax.axis_size("dp")
    rows, width = frames.shape
    ch = w_out.shape[0]
    scale = 1.0 / math.sqrt(rows * count_dev)
    deep = width // count_dev
    w_flat = w_in.reshape(width, 2 * ch)
    consts = tables()
    shared = (seg_lengths, frames, grad_out, w_flat, w_out, conv_kernel, conv_bias.reshape(1, ch), consts)
    half = rows // 2
    quarter = half // 2

    def turn(d):
        return lambda m: lax.rem(m + d, 4)

    def mine(m):
        return m

    def near(m):
        return m ^ 1

    def far(m):
        return 3 - m

    def other(m):
        return 3 - (m ^ 1)

    gp0, act0, sum0, keep0, near0, far0, back0 = chunk_call(
        0, half,
        [(0, half, [turn(d)], F32 if d == 0 else BF16) for d in range(4)],
        None, *shared,
    )

    def ring(d):
        return [(i, (i + d) % 4) for i in range(4)]

    far0 = lax.ppermute(far0, "mp", ring(2))
    near0 = lax.ppermute(near0, "mp", ring(1))
    back0 = lax.ppermute(back0, "mp", ring(3))

    gp1, act1, small, send_a, send_b, keep_a, keep_b = chunk_call(
        half, half,
        [
            (0, quarter, [near, other], BF16),
            (quarter, quarter, [far, other], BF16),
            (0, quarter, [mine, far], F32),
            (quarter, quarter, [mine, near], F32),
        ],
        (gp0, act0, sum0), *shared,
    )
    pair = [(i, i ^ 1) for i in range(4)]
    cross = [(i, 3 - i) for i in range(4)]
    first_a = lax.ppermute(send_a, "mp", pair)
    first_b = lax.ppermute(send_b, "mp", cross)
    small_all = lax.all_gather(small, "dp", axis=0)
    last_a = lax.ppermute((keep_a[:, ch:] + first_a[:, ch:].astype(F32)).astype(BF16), "mp", cross)
    last_b = lax.ppermute((keep_b[:, ch:] + first_b[:, ch:].astype(F32)).astype(BF16), "mp", pair)
    outgoing = pick_call(
        seg_lengths, seg_owner, rows,
        keep0, near0, far0, back0, keep_a, keep_b, first_a, first_b, last_a, last_b,
    )
    received = lax.all_to_all(outgoing, "dp", split_axis=0, concat_axis=0, tiled=True)
    dx_frames = order_call(slot_device, received)

    keep, send = weight_call(deep, frames, grad_out, gp0, gp1, act0, act1)
    got = lax.ppermute(send, "dp", [(i, i ^ 1) for i in range(count_dev)])
    terms = (keep + got.astype(F32)).astype(BF16)
    cores = [[2 * i + c for i in range(count_dev // 2)] for c in range(2)]
    terms = lax.all_to_all(
        terms, "dp", split_axis=0, concat_axis=0, axis_index_groups=cores, tiled=True
    )
    sums = jnp.sum(terms.astype(F32), axis=0) * scale
    small_sum = jnp.sum(small_all, axis=0) * scale
    return (
        dx_frames,
        sums[:, : 2 * ch].reshape(deep, 2, ch),
        sums[:, 2 * ch :].T,
        small_sum[:TAPS],
        small_sum[TAPS],
    )


def solution(mesh):
    return jax.shard_map(
        on_device,
        mesh=mesh,
        in_specs=(
            P("dp", None),
            P("dp", None),
            P(None, None, "mp"),
            P(None, "mp"),
            P("mp"),
            P("mp", None),
            P("dp", None),
            P("dp", None),
            P("dp", None),
        ),
        out_specs=(P("dp", None, "mp"), P("dp", None, "mp"), P("mp", "dp"), P(None, "mp"), P("mp")),
        check_vma=False,
    )
```

time: 382 us -> 173 us (0.45)
  blocking collectives: 135 us -> 0 us
  other arithmetic: 104 us -> 7.47 us
  Pallas kernels: 0 us -> 62 us
  matrix products: 34.6 us -> 0 us
  local copies, waits for them, and re-layouts: 30.4 us -> 12.1 us
  starting transfers between devices: 7.54 us -> 20 us
  waiting for transfers between devices: 51.9 us -> 56.5 us
    psum x1 -> x0, blocking collectives: 135 us -> none  [on_device(): grad_kernel, grad_bias = lax.psum((kernel_term, bias_term), 'dp')]
    pallas_call x0 -> x5, Pallas kernels: none -> 62 us  [the longest x2 44 us: chunk_call(): pl.pallas_call(body, out_shape=out_shape, in_specs=specs, out_specs=[vm]...]
    reduce_scatter x2 -> x0, waiting for transfers between devices: 51.9 us -> none  [the longest x1 51.9 us: on_device(): lax.psum_scatter(partial_rows, 'mp', scatter_dimension=1, tiled=True)]
    another operation x4 -> x0, other arithmetic: 50.2 us -> none
    dot_general x5 -> x0, matrix products: 34.6 us -> none  [the longest x1 8.71 us: on_device(): lax.dot_general(frames, grad_proj, (((0,), (0,)), ((), ())), preferred_el...]
    all_to_all x1, waiting for transfers between devices: 0.01 us -> 22.4 us  [on_device(): lax.all_to_all(outgoing, 'dp', split_axis=0, concat_axis=0, tiled=True)]
    all_to_all x0 -> x1, waiting for transfers between devices: none -> 21.6 us  [on_device(): lax.all_to_all(terms, 'dp', split_axis=0, concat_axis=0, axis_index_group...]
    add x1 -> x0, other arithmetic: 18.3 us -> none  [on_device(): conv_out = depthwise(gated, segment, conv_kernel, 1) + conv_bias]
  transfers between devices with their start and end apart: 4 -> 11, of which waited for: 1 -> 6; matrix products, arithmetic and copies ran while one was open for 17% -> 5% of each run, Pallas kernels for 0% -> 22%
where the time goes in v2:
time: 173 us; the launch traced here: 172 us
  Pallas kernels  62 us (36%)
  waiting for transfers between devices  56.5 us (33%)
  starting transfers between devices  20 us (12%)
  between operations  14.3 us (8%)
  local copies, waits for them, and re-layouts  12.1 us (7%)
  other arithmetic  7.47 us (4%)
    pallas_call x2, Pallas kernels, chunk_call(): pl.pallas_call(body, out_shape=out_shape, in_specs=specs, out_specs=[vm]...  44 us
    all_to_all x1, waiting for transfers between devices, on_device(): lax.all_to_all(outgoing, 'dp', split_axis=0, concat_axis=0, tiled=True)  22.4 us
    all_to_all x1, waiting for transfers between devices, on_device(): lax.all_to_all(terms, 'dp', split_axis=0, concat_axis=0, axis_index_group...  21.6 us
    pallas_call x1, Pallas kernels, weight_call(): pl.pallas_call(lambda *refs: weight_kernel(deep, *refs), grid=(4,), out_s...  11 us
    unnamed x33, local copies, waits for them, and re-layouts  8.51 us
    ppermute x1, waiting for transfers between devices, on_device(): lax.ppermute((keep_a[:, ch:] + first_a[:, ch:].astype(F32)).astype(BF16),...  7.89 us
    all_to_all x1, starting transfers between devices, on_device(): lax.all_to_all(outgoing, 'dp', split_axis=0, concat_axis=0, tiled=True)  7.4 us
    pallas_call x1, Pallas kernels, pick_call(): pl.pallas_call(pick_kernel, out_shape=jax.ShapeDtypeStruct((SEGS, MAXLEN,...  4.97 us
  transfers between devices with their start and end apart: 11, of which 6 were waited for; matrix products, arithmetic and copies ran while one was open for 5% of the time, Pallas kernels for 22%

profile of v2, /device:TPU:0, one launch (start us, length us, event | category | flops | bytes accessed | tf_op | source)
XLA Modules:
  0.0 172.4 jit_solution(11282863106667906821)
XLA Ops:
  7.2 0.0 all-gather.3.cloned.1.call-start
  7.2 0.7 reshape.20.refs_6_
  7.9 0.0 copy-start.12
  7.9 0.0 copy-start.13
  7.9 0.0 copy-start.14
  7.9 3.7 %copy.18 = bf16[192,8,2,384]{3,1,2,0:T(8,128)(2,1)} copy(bf16[192,8,2,384]{3,2,1,0:T(2,128)(2,1)} %bitcast.6) | data formatting | bytes 4718592
  11.7 23.4 %chunk0.1 = (bf16[864,768]{1,0:T(8,128)(2,1)}, bf16[864,384]{1,0:T(8,128)(2,1)S(1)}, f32[104,384]{1,0:T(8,128)S(1)}, f32[768,384]{1,0:T(8,128)S(1)}, bf16[768,38...) custom-call(s32[1,32]{1,0:T(1,128)S(1)} %copy-done.6, bf16[1536,1536]{1,0:T(8,128)(2,1)} %refs_0_.5, ...), custom_call_target="tpu_custom_call" | custom-call | flops 20000000000 | bytes 20000000 | tf_op jit(solution)/shard_map/chunk0/pallas_call | solution.py:265
  35.0 1.0 copy-done
  36.1 2.0 %collective-permute-start = (bf16[768,384]{1,0:T(8,128)(2,1)S(1)}, bf16[768,384]{1,0:T(8,128)(2,1)S(1)}, u32[]{:S(2)}, u32[]{:S(2)}) collective-permute-start(bf16[768,384]{1,0:T(8,128)(2,1)S(1)} %get-tuple-element.22), channel_id=1, source_target_pairs={{0,1},{1,2},{2,3},{3,0},{4,5},{5,6},{6,7},{7,4},{8,9},{9,10},{10,1... | collective-permute-start | bytes 1769480 | tf_op jit(solution)/shard_map/ppermute | solution.py:445
  38.0 3.6 %collective-permute-start.1 = (bf16[768,384]{1,0:T(8,128)(2,1)}, bf16[768,384]{1,0:T(8,128)(2,1)}, u32[]{:S(2)}, u32[]{:S(2)}) collective-permute-start(bf16[768,384]{1,0:T(8,128)(2,1)} %get-tuple-element.23), channel_id=1, source_target_pairs={{0,2},{1,3},{2,0},{3,1},{4,6},{5,7},{6,4},{7,5},{8,10},{9,11},{10,... | collective-permute-start | bytes 1769480 | tf_op jit(solution)/shard_map/ppermute | solution.py:444
  41.6 1.0 collective-permute-start.2
  42.6 0.9 slice.30.refs_11_
  43.6 0.0 copy-start.5
  43.6 20.7 %chunk768.1 = (bf16[768,768]{1,0:T(8,128)(2,1)S(1)}, bf16[768,384]{1,0:T(8,128)(2,1)S(1)}, f32[32,384]{1,0:T(8,128)S(1)}, bf16[384,768]{1,0:T(8,128)(2,1)S(1)}, ...) custom-call(s32[1,32]{1,0:T(1,128)S(1)} %copy-done.6, bf16[1536,1536]{1,0:T(8,128)(2,1)} %refs_0_.5, ...), custom_call_target="tpu_custom_call" | custom-call | flops 20000000000 | bytes 20000000 | tf_op jit(solution)/shard_map/chunk768/pallas_call | solution.py:265
  64.2 0.0 copy-start.4
  64.3 0.6 copy-done.4
  64.9 1.0 collective-permute-start.3
  65.9 0.0 collective-permute-start.4
  65.9 11.0 %weight.1 = (f32[16,48,1152]{2,1,0:T(8,128)}, bf16[16,48,1152]{2,1,0:T(8,128)(2,1)}) custom-call(bf16[1536,1536]{1,0:T(8,128)(2,1)} %refs_0_.5, bf16[1536,1536]{1,0:T(8,128)(2,1)} %refs_1_.5, bf16[864,768]{1,0:T(8,128)(2,1)S(1)} %copy-done.5, bf16[768,768]{1,0:T(8,128)(2,1)S(1)} %get-tuple-element.32.refs_3_, ...), custom_call_target="tpu_custom_call" | custom-call | flops 11000000512 | bytes 20000000 | tf_op jit(solution)/shard_map/weight/pallas_call | solution.py:390
  77.0 2.2 %collective-permute-done.3.first_a = bf16[384,768]{1,0:T(8,128)(2,1)S(1)} collective-permute-done((bf16[384,768]{1,0:T(8,128)(2,1)S(1)}, bf16[384,768]{1,0:T(8,128)(2,1)S(1)}, u32[]{:S(2)}, u32[]{:S(2)}) %collective-permute-start.3) | collective-permute-done | bytes 589856 | tf_op jit(solution)/shard_map/ppermute | solution.py:460
  79.1 0.0 collective-permute-start.7
  79.1 0.8 add_convert_fusion.2
  79.9 1.1 collective-permute-done.4.first_b
  81.1 0.3 collective-permute-start.5
  81.3 0.8 add_convert_fusion.1
  82.1 0.0 collective-permute-done.near0
  82.1 0.8 copy-done.2
  82.9 0.0 collective-permute-start.6
  82.9 0.0 all-gather.3.cloned.1.call-update
  83.0 0.0 collective-permute-done.1.far0
  83.0 7.9 %collective-permute-done.5.last_a = bf16[384,384]{1,0:T(8,128)(2,1)} collective-permute-done((bf16[384,384]{1,0:T(8,128)(2,1)}, bf16[384,384]{1,0:T(8,128)(2,1)}, u32[]{:S(2)}, u32[]{:S(2)}) %collective-permute-start.5) | collective-permute-done | bytes 294944 | tf_op jit(solution)/shard_map/ppermute | solution.py:463
  90.9 1.3 collective-permute-done.6.last_b
  92.1 1.3 copy-done.1
  93.4 1.1 copy-done.3
  94.5 5.0 %pick.1 = bf16[32,72,384]{2,1,0:T(8,128)(2,1)} custom-call(s32[1,32]{1,0:T(1,128)S(1)} %copy-done.6, s32[1,32]{1,0:T(1,128)S(1)} %copy-done.7, f32[768,384]{1,0:T(8,128)S(1)} %copy-done.1, bf16[768,384]{1,0:T(8,128)(2,1)S(1)} %copy-done.3, bf16[768,384]{1,0:T(8,128)(2,1)} %collective-permute-done.1.far0, bf16[768,384]{1,0:T(8,128)(2,1)} %collective-permute-done.2.back0, ...), custom_call_target="tpu_custom_call" | custom-call | flops 1000000000 | bytes 10000000 | tf_op jit(solution)/shard_map/pick/pallas_call | solution.py:327
  99.4 7.4 %all-to-all-start = ((bf16[32,72,384]{2,1,0:T(8,128)(2,1)}), bf16[32,72,384]{2,1,0:T(8,128)(2,1)S(1)}, u32[]{:S(2)}, u32[]{:S(2)}) async-start(bf16[32,72,384]{2,1,0:T(8,128)(2,1)} %pick.1), calls=%async_computation | async-start | bytes 3538944 | tf_op jit(solution)/shard_map/all_to_all | solution.py:469
  106.8 4.1 %add_convert_fusion = bf16[16,48,1152]{2,1,0:T(8,128)(2,1)} fusion(f32[16,48,1152]{2,1,0:T(8,128)} %get-tuple-element.34, bf16[16,48,1152]{2,1,0:T(8,128)(2,1)} %collective-permute-done.7), kind=kLoop, calls=%fused_computation.1 | loop fusion | flops 2654208 | bytes 7077888 | tf_op jit(solution)/shard_map/convert_element_type | solution.py:474
  111.0 22.4 %all-to-all-done.src = bf16[32,72,384]{2,1,0:T(8,128)(2,1)S(1)} async-done(((bf16[32,72,384]{2,1,0:T(8,128)(2,1)}), bf16[32,72,384]{2,1,0:T(8,128)(2,1)S(1)}, u32[]{:S(2)}, u32[]{:S(2)}) %all-to-all-start) | async-done | bytes 1769504 | tf_op jit(solution)/shard_map/all_to_all | solution.py:469
  133.4 4.6 %all-to-all-start.1 = ((bf16[16,48,1152]{2,1,0:T(8,128)(2,1)}), bf16[16,48,1152]{2,1,0:T(8,128)(2,1)S(1)}, u32[]{:S(2)}, u32[]{:S(2)}) async-start(bf16[16,48,1152]{2,1,0:T(8,128)(2,1)} %add_convert_fusion), calls=%async_computation.1 | async-start | bytes 3538944 | tf_op jit(solution)/shard_map/all_to_all | solution.py:476
  138.0 2.0 %order.1 = bf16[32,72,384]{2,1,0:T(8,128)(2,1)} custom-call(s32[1,32]{1,0:T(1,128)S(1)} %copy-done.8, bf16[32,72,384]{2,1,0:T(8,128)(2,1)S(1)} %all-to-all-done.src), custom_call_target="tpu_custom_call" | custom-call | bytes 4000000 | tf_op jit(solution)/shard_map/order/pallas_call | solution.py:350
  140.0 0.0 all-gather.3.cloned.1.call-done
  140.1 1.5 reduce_sum.19
  141.6 0.0 copy-start.15
  141.6 0.6 slice_reduce_fusion
  142.2 21.6 %all-to-all-done.1 = bf16[16,48,1152]{2,1,0:T(8,128)(2,1)S(1)} async-done(((bf16[16,48,1152]{2,1,0:T(8,128)(2,1)}), bf16[16,48,1152]{2,1,0:T(8,128)(2,1)S(1)}, u32[]{:S(2)}, u32[]{:S(2)}) %all-to-all-start.1) | async-done | bytes 1769504 | tf_op jit(solution)/shard_map/all_to_all | solution.py:476
  163.8 0.3 convert_reduce_fusion
  164.1 0.6 slice_bitcast_fusion
  164.8 0.7 reshape.21
  (27 shorter events, 0.1 us)
Async XLA Ops:
  7.2 132.9 %all-gather.3.cloned.1.call-start = ((), (), s32[]{:S(2)}) async-start(), calls=%async_computation.2 | async-start | bytes 1622016 | tf_op jit(solution)/shard_map/all_gather | solution.py:462
  7.9 3.7 %copy-start.6 = (s32[1,32]{1,0:T(1,128)S(1)}, s32[1,32]{1,0:T(1,128)}, u32[]{:S(2)}) copy-start(s32[1,32]{1,0:T(1,128)} %len_ref.1) | copy-start | bytes 388
  7.9 3.7 %copy-start.9 = (bf16[384,1536]{1,0:T(8,128)(2,1)S(1)}, bf16[384,1536]{1,0:T(8,128)(2,1)}, u32[]{:S(2)}) copy-start(bf16[384,1536]{1,0:T(8,128)(2,1)} %refs_4_.3) | copy-start | bytes 3538948
  7.9 3.7 %copy-start.10 = (f32[31,384]{1,0:T(8,128)S(1)}, f32[31,384]{1,0:T(8,128)}, u32[]{:S(2)}) copy-start(f32[31,384]{1,0:T(8,128)} %refs_5_.3) | copy-start | bytes 142852
  7.9 3.7 %copy-start.11 = (f32[96,240]{1,0:T(8,128)S(1)}, f32[96,240]{1,0:T(8,128)}, u32[]{:S(2)}) copy-start(f32[96,240]{1,0:T(8,128)} %constant.5.clone.refs_7_) | copy-start | bytes 276484
  7.9 3.7 %copy-start.12 = (bf16[80,288]{1,0:T(8,128)(2,1)S(1)}, bf16[80,288]{1,0:T(8,128)(2,1)}, u32[]{:S(2)}) copy-start(bf16[80,288]{1,0:T(8,128)(2,1)} %constant.14.clone.refs_8_) | copy-start | bytes 138244
  7.9 3.7 %copy-start.13 = (f32[96,31]{1,0:T(8,128)S(1)}, f32[96,31]{1,0:T(8,128)}, u32[]{:S(2)}) copy-start(f32[96,31]{1,0:T(8,128)} %constant.15.clone.refs_9_) | copy-start | bytes 35716
  7.9 3.7 %copy-start.14 = (f32[31,96]{1,0:T(8,128)S(1)}, f32[31,96]{1,0:T(8,128)}, u32[]{:S(2)}) copy-start(f32[31,96]{1,0:T(8,128)} %constant.16.clone.refs_10_) | copy-start | bytes 35716
  35.0 1.0 copy-start
  36.1 46.1 %collective-permute-start = (bf16[768,384]{1,0:T(8,128)(2,1)S(1)}, bf16[768,384]{1,0:T(8,128)(2,1)S(1)}, u32[]{:S(2)}, u32[]{:S(2)}) collective-permute-start(bf16[768,384]{1,0:T(8,128)(2,1)S(1)} %get-tuple-element.22), channel_id=1, source_target_pairs={{0,1},{1,2},{2,3},{3,0},{4,5},{5,6},{6,7},{7,4},{8,9},{9,10},{10,1... | collective-permute-start | bytes 1769480 | tf_op jit(solution)/shard_map/ppermute | solution.py:445
  38.0 44.9 %collective-permute-start.1 = (bf16[768,384]{1,0:T(8,128)(2,1)}, bf16[768,384]{1,0:T(8,128)(2,1)}, u32[]{:S(2)}, u32[]{:S(2)}) collective-permute-start(bf16[768,384]{1,0:T(8,128)(2,1)} %get-tuple-element.23), channel_id=1, source_target_pairs={{0,2},{1,3},{2,0},{3,1},{4,6},{5,7},{6,4},{7,5},{8,10},{9,11},{10,... | collective-permute-start | bytes 1769480 | tf_op jit(solution)/shard_map/ppermute | solution.py:444
  41.6 41.4 %collective-permute-start.2 = (bf16[768,384]{1,0:T(8,128)(2,1)}, bf16[768,384]{1,0:T(8,128)(2,1)}, u32[]{:S(2)}, u32[]{:S(2)}) collective-permute-start(bf16[768,384]{1,0:T(8,128)(2,1)} %get-tuple-element.24), channel_id=1, source_target_pairs={{0,3},{1,0},{2,1},{3,2},{4,7},{5,4},{6,5},{7,6},{8,11},{9,8},{10,9... | collective-permute-start | bytes 1769480 | tf_op jit(solution)/shard_map/ppermute | solution.py:446
  43.6 22.3 %copy-start.5 = (bf16[864,768]{1,0:T(8,128)(2,1)S(1)}, bf16[864,768]{1,0:T(8,128)(2,1)}, u32[]{:S(2)}) copy-start(bf16[864,768]{1,0:T(8,128)(2,1)} %get-tuple-element.25.refs_2_) | copy-start | bytes 3981316
  64.2 0.6 copy-start.4
  64.9 14.2 %collective-permute-start.3 = (bf16[384,768]{1,0:T(8,128)(2,1)S(1)}, bf16[384,768]{1,0:T(8,128)(2,1)S(1)}, u32[]{:S(2)}, u32[]{:S(2)}) collective-permute-start(bf16[384,768]{1,0:T(8,128)(2,1)S(1)} %get-tuple-element.30), channel_id=1, source_target_pairs={{0,1},{1,0},{2,3},{3,2},{4,5},{5,4},{6,7},{7,6},{8,9},{9,8},{10,11... | collective-permute-start | bytes 1769480 | tf_op jit(solution)/shard_map/ppermute | solution.py:460
  65.9 15.2 %collective-permute-start.4 = (bf16[384,768]{1,0:T(8,128)(2,1)S(1)}, bf16[384,768]{1,0:T(8,128)(2,1)S(1)}, u32[]{:S(2)}, u32[]{:S(2)}) collective-permute-start(bf16[384,768]{1,0:T(8,128)(2,1)S(1)} %get-tuple-element.31), channel_id=1, source_target_pairs={{0,3},{1,2},{2,1},{3,0},{4,7},{5,6},{6,5},{7,4},{8,11},{9,10},{10,... | collective-permute-start | bytes 1769480 | tf_op jit(solution)/shard_map/ppermute | solution.py:461
  77.0 15.2 %copy-start.7 = (s32[1,32]{1,0:T(1,128)S(1)}, s32[1,32]{1,0:T(1,128)}, u32[]{:S(2)}) copy-start(s32[1,32]{1,0:T(1,128)} %owner_ref.1) | copy-start | bytes 388
  79.1 27.7 %collective-permute-start.7 = (bf16[16,48,1152]{2,1,0:T(8,128)(2,1)}, bf16[16,48,1152]{2,1,0:T(8,128)(2,1)}, u32[]{:S(2)}, u32[]{:S(2)}) collective-permute-start(bf16[16,48,1152]{2,1,0:T(8,128)(2,1)} %get-tuple-element.35), channel_id=1, source_target_pairs={{0,4},{4,0},{8,12},{12,8},{16,20},{20,16},{24,28},{28,24},{32,36},... | collective-permute-start | bytes 5308424 | tf_op jit(solution)/shard_map/ppermute | solution.py:473
  81.1 9.8 %collective-permute-start.5 = (bf16[384,384]{1,0:T(8,128)(2,1)}, bf16[384,384]{1,0:T(8,128)(2,1)}, u32[]{:S(2)}, u32[]{:S(2)}) collective-permute-start(bf16[384,384]{1,0:T(8,128)(2,1)} %add_convert_fusion.2), channel_id=1, source_target_pairs={{0,3},{1,2},{2,1},{3,0},{4,7},{5,6},{6,5},{7,4},{8,11},{9,10},{10,... | collective-permute-start | bytes 884744 | tf_op jit(solution)/shard_map/ppermute | solution.py:463
  82.1 0.8 copy-start.2
  82.9 9.2 %collective-permute-start.6 = (bf16[384,384]{1,0:T(8,128)(2,1)}, bf16[384,384]{1,0:T(8,128)(2,1)}, u32[]{:S(2)}, u32[]{:S(2)}) collective-permute-start(bf16[384,384]{1,0:T(8,128)(2,1)} %add_convert_fusion.1), channel_id=1, source_target_pairs={{0,1},{1,0},{2,3},{3,2},{4,5},{5,4},{6,7},{7,6},{8,9},{9,8},{10,11... | collective-permute-start | bytes 884744 | tf_op jit(solution)/shard_map/ppermute | solution.py:464
  92.1 1.3 copy-start.1
  93.4 1.1 copy-start.3
  99.4 33.9 %all-to-all-start = ((bf16[32,72,384]{2,1,0:T(8,128)(2,1)}), bf16[32,72,384]{2,1,0:T(8,128)(2,1)S(1)}, u32[]{:S(2)}, u32[]{:S(2)}) async-start(bf16[32,72,384]{2,1,0:T(8,128)(2,1)} %pick.1), calls=%async_computation | async-start | bytes 3538944 | tf_op jit(solution)/shard_map/all_to_all | solution.py:469
  111.0 27.0 %copy-start.8 = (s32[1,32]{1,0:T(1,128)S(1)}, s32[1,32]{1,0:T(1,128)}, u32[]{:S(2)}) copy-start(s32[1,32]{1,0:T(1,128)} %slot_ref.1) | copy-start | bytes 388
  133.4 30.5 %all-to-all-start.1 = ((bf16[16,48,1152]{2,1,0:T(8,128)(2,1)}), bf16[16,48,1152]{2,1,0:T(8,128)(2,1)S(1)}, u32[]{:S(2)}, u32[]{:S(2)}) async-start(bf16[16,48,1152]{2,1,0:T(8,128)(2,1)} %add_convert_fusion), calls=%async_computation.1 | async-start | bytes 3538944 | tf_op jit(solution)/shard_map/all_to_all | solution.py:476
  141.6 23.9 %copy-start.15 = (f32[32,384]{1,0:T(8,128)}, f32[32,384]{1,0:T(8,128)S(1)}, u32[]{:S(2)}) copy-start(f32[32,384]{1,0:T(8,128)S(1)} %broadcast_multiply_fusion.1) | copy-start | bytes 147460
Sparse Core Ops, SparseCore 0:
  83.1 55.2 all-gather.2

commit v3 on v2

--- a/solution.py
+++ b/solution.py
@@ -19,6 +19,8 @@
 SEGS = 32
 GROUP = 4
 MIB = 1024 * 1024
+TINY = pl.CostEstimate(flops=10**6, bytes_accessed=10**5, transcendentals=0)
+LONG = pl.CostEstimate(flops=10**6, bytes_accessed=6 * 10**7, transcendentals=0)
 F32, BF16 = jnp.float32, jnp.bfloat16
 NT = (((1,), (1,)), ((), ()))
 TN = (((0,), (0,)), ((), ()))
@@ -287,20 +289,23 @@
     )(*operands)
 
 
-def pick_kernel(
-    len_ref, owner_ref, keep0, near0, far0, back0, keep_a, keep_b, first_a, first_b, last_a, last_b,
-    out_ref, held,
-):
-    rows0, ch = keep0.shape
+def fold_kernel(keep0, near0, far0, back0, keep_a, keep_b, first_a, first_b, held_ref, part_ref, out_a, out_b):
+    half, ch = out_a.shape
+    held_ref[...] = (
+        keep0[...] + near0[...].astype(F32) + far0[...].astype(F32) + back0[...].astype(F32)
+    ).astype(BF16)
+    for at, keep, one, out in ((0, keep_a, first_a, out_a), (half, keep_b, first_b, out_b)):
+        out[...] = (keep[:, ch:] + one[:, ch:].astype(F32)).astype(BF16)
+        part_ref[at : at + half, :] = keep[:, :ch] + one[:, :ch].astype(F32)
+
+
+def pick_kernel(len_ref, owner_ref, held0, part, last_a, last_b, out_ref, held):
+    rows0, ch = held0.shape
     half = last_a.shape[0]
     rows = rows0 + 2 * half
-    held[pl.ds(0, rows0), :] = (
-        keep0[...] + near0[...].astype(F32) + far0[...].astype(F32) + back0[...].astype(F32)
-    ).astype(BF16)
-    for at, keep, one, two in ((rows0, keep_a, first_a, last_a), (rows0 + half, keep_b, first_b, last_b)):
-        held[pl.ds(at, half), :] = (
-            keep[:, :ch] + one[:, :ch].astype(F32) + two[...].astype(F32)
-        ).astype(BF16)
+    held[pl.ds(0, rows0), :] = held0[...]
+    for at, two in ((0, last_a), (half, last_b)):
+        held[pl.ds(rows0 + at, half), :] = (part[at : at + half, :] + two[...].astype(F32)).astype(BF16)
     held[pl.ds(rows, MARGIN), :] = jnp.zeros((MARGIN, ch), BF16)
     row = lax.broadcasted_iota(jnp.int32, (MAXLEN, MARGIN), 0)
     lane = lax.broadcasted_iota(jnp.int32, (MAXLEN, MARGIN), 1)
@@ -331,7 +336,7 @@
         out_specs=vm,
         scratch_shapes=[pltpu.VMEM((rows + MARGIN, ch), BF16)],
         compiler_params=pltpu.CompilerParams(vmem_limit_bytes=40 * MIB),
-        cost_estimate=pl.CostEstimate(flops=10**9, bytes_accessed=10**7, transcendentals=0),
+        cost_estimate=TINY,
         name="pick",
     )(lengths, owners, *parts)
 
@@ -354,12 +359,13 @@
         out_specs=pl.BlockSpec(memory_space=pl.ANY),
         scratch_shapes=[pltpu.SemaphoreType.DMA((SEGS,))],
         compiler_params=pltpu.CompilerParams(vmem_limit_bytes=16 * MIB),
-        cost_estimate=pl.CostEstimate(flops=0, bytes_accessed=4 * 10**6, transcendentals=0),
+        cost_estimate=TINY,
         name="order",
     )(slots, received)
 
 
 def weight_kernel(deep, frames_ref, gout_ref, gp0, gp1, act0, act1, keep_ref, send_ref, held):
+    step = pl.program_id(0) * 4
     core = lax.rem(lax.axis_index("dp"), 2)
     total, cols = frames_ref.shape
     rows1 = gp1.shape[0]
@@ -375,8 +381,8 @@
     for j in range(cols // (2 * deep)):
         own = pl.ds(pl.multiple_of((2 * j + core) * deep, 16), deep)
         other = pl.ds(pl.multiple_of((2 * j + 1 - core) * deep, 16), deep)
-        keep_ref[j] = held[own, :]
-        send_ref[j] = held[other, :].astype(BF16)
+        keep_ref[step + j] = held[own, :]
+        send_ref[step + j] = held[other, :].astype(BF16)
 
 
 def weight_call(deep, frames, grad_out, gp0, gp1, act0, act1):
@@ -386,7 +392,6 @@
     pairs = width // (2 * deep)
     vm = pl.BlockSpec(memory_space=pltpu.VMEM)
     tall = pl.BlockSpec((total, cols), lambda i: (0, i))
-    out = pl.BlockSpec((pairs // 4, deep, wide), lambda i: (i, 0, 0))
     return pl.pallas_call(
         lambda *refs: weight_kernel(deep, *refs),
         grid=(4,),
@@ -395,12 +400,140 @@
             jax.ShapeDtypeStruct((pairs, deep, wide), BF16),
         ),
         in_specs=[tall, tall, vm, vm, vm, vm],
-        out_specs=(out, out),
+        out_specs=(vm, vm),
         scratch_shapes=[pltpu.VMEM((cols, wide), F32)],
         compiler_params=pltpu.CompilerParams(vmem_limit_bytes=48 * MIB),
         cost_estimate=pl.CostEstimate(flops=11 * 10**9, bytes_accessed=2 * 10**7, transcendentals=0),
         name="weight",
     )(frames, grad_out, gp0, gp1, act0, act1)
+
+
+CUT = 640
+
+
+def put_small(out, at, x):
+    taps, ch = x.shape
+    high = x.astype(BF16)
+    for j, part in enumerate((high, (x - high.astype(F32)).astype(BF16))):
+        out[at + j] = jnp.zeros(out.shape[1:], out.dtype)
+        out[at + j, :taps, :ch] = part
+
+
+def get_small(ref, at, shape):
+    taps, ch = shape
+    return ref[at, :taps, :ch].astype(F32) + ref[at + 1, :taps, :ch].astype(F32)
+
+
+def places():
+    dp = lax.axis_index("dp")
+    return lax.div(dp, 8), lax.rem(lax.div(dp, 2), 4)
+
+
+def near(v):
+    return v ^ 1
+
+
+def far(v):
+    return 3 - v
+
+
+def both_ways():
+    dp = lax.axis_index("dp")
+    x, y = lax.div(dp, 8), lax.rem(lax.div(dp, 2), 4)
+    return (slice(0, CUT), x, y, True), (slice(CUT, None), y, x, False)
+
+
+def core_sum_kernel(keep, got, small, small_got, *outs):
+    small_total = small[...] + small_got[...]
+    outs[4][...] = small_total
+    for i, (cols, a, b, x_first) in enumerate(both_ways()):
+        for j in range(4):
+            for where, out, slot in ((a, outs[i], 0), (far(a), outs[i], 4), (near(a), outs[2 + i], 0), (far(near(a)), outs[2 + i], 4)):
+                at = where * 4 + j if x_first else j * 4 + where
+                total = keep[at, :, cols] + got[at, :, cols].astype(F32)
+                out[slot + j] = total.astype(out.dtype)
+    put_small(outs[3], 8, small_total)
+
+
+def half_sum_kernel(own_x, own_y, small, got_x, got_y, *outs):
+    small_total = small[...] + get_small(got_y, 8, small.shape)
+    outs[4][...] = small_total
+    for i, ((cols, a, b, x_first), own, got) in enumerate(zip(both_ways(), (own_x, own_y), (got_x, got_y))):
+        for s in range(2):
+            for j, where in enumerate((b, far(b))):
+                at = 4 * s + where
+                outs[i][2 * s + j] = own[at] + got[at].astype(F32)
+            for j, where in enumerate((near(b), far(near(b)))):
+                at = 4 * s + where
+                outs[2 + i][2 * s + j] = (own[at] + got[at].astype(F32)).astype(BF16)
+    put_small(outs[3], 4, small_total)
+
+
+def square_sum_kernel(own_x, own_y, small, got_x, got_y, own_ref, small_out, *outs):
+    taps, ch = small.shape
+    small_total = small[...] + get_small(got_y, 4, small.shape)
+    small_out[...] = small_total
+    high = small_total.astype(BF16)
+    low = (small_total - high.astype(F32)).astype(BF16)
+    for out, at_x, at_y in ((own_ref, 0, 0), (outs[0], 2, 1), (outs[1], 1, 2), (outs[2], 3, 3)):
+        out[:, :CUT] = (own_x[at_x] + got_x[at_x].astype(F32)).astype(out.dtype)
+        out[:, CUT : 3 * ch] = (own_y[at_y] + got_y[at_y].astype(F32)).astype(out.dtype)
+    for out in outs:
+        out[:, 3 * ch :] = jnp.zeros((out.shape[0], 2 * ch), BF16)
+        out[:taps, 3 * ch : 4 * ch] = high
+        out[:taps, 4 * ch :] = low
+
+
+def last_sum_kernel(scale, own, small, r1, r2, r3, w_out, small_out):
+    taps, ch = small.shape
+    total, small_total = own[...], small[...]
+    for r in (r1, r2, r3):
+        total = total + r[:, : 3 * ch].astype(F32)
+        small_total = small_total + r[:taps, 3 * ch : 4 * ch].astype(F32) + r[:taps, 4 * ch :].astype(F32)
+    w_out[...] = total * scale
+    small_out[...] = small_total * scale
+
+
+def sum_call(kernel, name, cost, out_shape, *operands):
+    vm = pl.BlockSpec(memory_space=pltpu.VMEM)
+    return pl.pallas_call(
+        kernel,
+        out_shape=out_shape,
+        in_specs=[vm] * len(operands),
+        out_specs=[vm] * len(out_shape),
+        compiler_params=pltpu.CompilerParams(vmem_limit_bytes=32 * MIB),
+        cost_estimate=cost,
+        name=name,
+    )(*operands)
+
+
+def halves(n, deep, wide, small):
+    return [
+        jax.ShapeDtypeStruct((n, deep, CUT), F32),
+        jax.ShapeDtypeStruct((n, deep, wide - CUT), F32),
+        jax.ShapeDtypeStruct((n, deep, CUT), BF16),
+        jax.ShapeDtypeStruct((n + 2, deep, wide - CUT), BF16),
+        jax.ShapeDtypeStruct(small.shape, F32),
+    ]
+
+
+def move(array, fx=None, fy=None):
+    def to(i):
+        x, y, c = i // 8, i // 2 % 4, i % 2
+        if fx is None and fy is None:
+            c ^= 1
+        return ((fx(x) if fx else x) * 4 + (fy(y) if fy else y)) * 2 + c
+
+    return lax.ppermute(array, "dp", [(i, to(i)) for i in range(lax.axis_size("dp"))])
+
+
+def together(live, stage, *operands):
+    shapes = jax.eval_shape(stage, *operands)
+
+    def never(*_):
+        return jax.tree.map(lambda s: jnp.zeros(s.shape, s.dtype), shapes)
+
+    return lax.cond(live, stage, never, *operands)
 
 
 def on_device(
@@ -418,19 +551,13 @@
     quarter = half // 2
 
     def turn(d):
-        return lambda m: lax.rem(m + d, 4)
+        return lambda m: (m + d) % 4
 
     def mine(m):
         return m
 
-    def near(m):
-        return m ^ 1
-
-    def far(m):
-        return 3 - m
-
     def other(m):
-        return 3 - (m ^ 1)
+        return far(near(m))
 
     gp0, act0, sum0, keep0, near0, far0, back0 = chunk_call(
         0, half,
@@ -441,43 +568,92 @@
     def ring(d):
         return [(i, (i + d) % 4) for i in range(4)]
 
-    far0 = lax.ppermute(far0, "mp", ring(2))
-    near0 = lax.ppermute(near0, "mp", ring(1))
-    back0 = lax.ppermute(back0, "mp", ring(3))
-
-    gp1, act1, small, send_a, send_b, keep_a, keep_b = chunk_call(
-        half, half,
-        [
-            (0, quarter, [near, other], BF16),
-            (quarter, quarter, [far, other], BF16),
-            (0, quarter, [mine, far], F32),
-            (quarter, quarter, [mine, near], F32),
-        ],
-        (gp0, act0, sum0), *shared,
+    live = seg_lengths[0, 0] > 0
+
+    def zeroth_stage(near0, far0, back0, gp0, act0, sum0, *shared):
+        shared = shared[:7] + (shared[7:],)
+        return (
+            lax.ppermute(near0, "mp", ring(1)),
+            lax.ppermute(far0, "mp", ring(2)),
+            lax.ppermute(back0, "mp", ring(3)),
+            *chunk_call(
+                half, half,
+                [
+                    (0, quarter, [near, other], BF16),
+                    (quarter, quarter, [far, other], BF16),
+                    (0, quarter, [mine, far], F32),
+                    (quarter, quarter, [mine, near], F32),
+                ],
+                (gp0, act0, sum0), *shared,
+            ),
+        )
+
+    near0, far0, back0, gp1, act1, small, send_a, send_b, keep_a, keep_b = together(
+        live, zeroth_stage, near0, far0, back0, gp0, act0, sum0, *shared[:7], *consts
     )
     pair = [(i, i ^ 1) for i in range(4)]
     cross = [(i, 3 - i) for i in range(4)]
     first_a = lax.ppermute(send_a, "mp", pair)
     first_b = lax.ppermute(send_b, "mp", cross)
-    small_all = lax.all_gather(small, "dp", axis=0)
-    last_a = lax.ppermute((keep_a[:, ch:] + first_a[:, ch:].astype(F32)).astype(BF16), "mp", cross)
-    last_b = lax.ppermute((keep_b[:, ch:] + first_b[:, ch:].astype(F32)).astype(BF16), "mp", pair)
-    outgoing = pick_call(
-        seg_lengths, seg_owner, rows,
-        keep0, near0, far0, back0, keep_a, keep_b, first_a, first_b, last_a, last_b,
+    def first_stage(frames, grad_out, gp0, gp1, act0, act1, small, send_a, send_b):
+        first_a = lax.ppermute(send_a, "mp", pair)
+        first_b = lax.ppermute(send_b, "mp", cross)
+        small_got = move(small)
+        return first_a, first_b, small_got, *weight_call(deep, frames, grad_out, gp0, gp1, act0, act1)
+
+    def second_stage(send_a, send_b, send_x, send_y):
+        return (
+            lax.ppermute(send_a, "mp", cross),
+            lax.ppermute(send_b, "mp", pair),
+            move(send_x, fx=near),
+            move(send_y, fy=near),
+        )
+
+    def third_stage(lengths, owners, held0, part, last_a, last_b, send_x, send_y):
+        return (
+            move(send_x, fy=near),
+            move(send_y, fx=near),
+            pick_call(lengths, owners, rows, held0, part, last_a, last_b),
+        )
+
+    first_a, first_b, small_got, keep, send = together(
+        live, first_stage, frames, grad_out, gp0, gp1, act0, act1, small, send_a, send_b
+    )
+    got = move(send)
+    held0, part, send_a, send_b = sum_call(
+        fold_kernel, "fold", LONG,
+        [
+            jax.ShapeDtypeStruct((half, ch), BF16),
+            jax.ShapeDtypeStruct((half, ch), F32),
+            jax.ShapeDtypeStruct((quarter, ch), BF16),
+            jax.ShapeDtypeStruct((quarter, ch), BF16),
+        ],
+        keep0, near0, far0, back0, keep_a, keep_b, first_a, first_b,
+    )
+    own_x, own_y, send_x, send_y, small = sum_call(
+        core_sum_kernel, "core_sum", TINY, halves(8, deep, 3 * ch, small), keep, got, small, small_got
+    )
+    last_a, last_b, got_x, got_y = together(live, second_stage, send_a, send_b, send_x, send_y)
+    own_x, own_y, send_x, send_y, small = sum_call(
+        half_sum_kernel, "half_sum", TINY, halves(4, deep, 3 * ch, small), own_x, own_y, small, got_x, got_y
+    )
+    got_x, got_y, outgoing = together(
+        live, third_stage, seg_lengths, seg_owner, held0, part, last_a, last_b, send_x, send_y
     )
     received = lax.all_to_all(outgoing, "dp", split_axis=0, concat_axis=0, tiled=True)
     dx_frames = order_call(slot_device, received)
-
-    keep, send = weight_call(deep, frames, grad_out, gp0, gp1, act0, act1)
-    got = lax.ppermute(send, "dp", [(i, i ^ 1) for i in range(count_dev)])
-    terms = (keep + got.astype(F32)).astype(BF16)
-    cores = [[2 * i + c for i in range(count_dev // 2)] for c in range(2)]
-    terms = lax.all_to_all(
-        terms, "dp", split_axis=0, concat_axis=0, axis_index_groups=cores, tiled=True
-    )
-    sums = jnp.sum(terms.astype(F32), axis=0) * scale
-    small_sum = jnp.sum(small_all, axis=0) * scale
+    wide = 3 * ch
+    own, small, *sends = sum_call(
+        square_sum_kernel, "square_sum", TINY,
+        [jax.ShapeDtypeStruct((deep, wide), F32), jax.ShapeDtypeStruct(small.shape, F32)]
+        + [jax.ShapeDtypeStruct((deep, wide + 2 * ch), BF16)] * 3,
+        own_x, own_y, small, got_x, got_y,
+    )
+    sums, small_sum = sum_call(
+        lambda *refs: last_sum_kernel(scale, *refs), "last_sum", TINY,
+        [jax.ShapeDtypeStruct((deep, wide), F32), jax.ShapeDtypeStruct(small.shape, F32)],
+        own, small, move(sends[0], fx=far), move(sends[1], fy=far), move(sends[2], fx=far, fy=far),
+    )
     return (
         dx_frames,
         sums[:, : 2 * ch].reshape(deep, 2, ch),

time: 173 us -> 154 us (0.89)
  between operations: 14.3 us -> 1.6 us
  waiting for transfers between devices: 56.5 us -> 44.5 us
  starting transfers between devices: 20 us -> 30.1 us
  other arithmetic: 7.47 us -> 0.01 us
  Pallas kernels: 62 us -> 67.4 us
  local copies, waits for them, and re-layouts: 12.1 us -> 8.37 us
    ppermute x8 -> x16, waiting for transfers between devices: 12.4 us -> 44.5 us  [the longest x9 29.6 us: move(): lax.ppermute(array, 'dp', [(i, to(i)) for i in range(lax.axis_size('dp'))])]
    all_to_all x1, waiting for transfers between devices: 22.4 us -> 0.01 us  [on_device(): lax.all_to_all(outgoing, 'dp', split_axis=0, concat_axis=0, tiled=True)]
    all_to_all x1 -> x0, waiting for transfers between devices: 21.6 us -> none  [on_device(): lax.all_to_all(terms, 'dp', split_axis=0, concat_axis=0, axis_index_group...]
    ppermute x8 -> x16, starting transfers between devices: 7.9 us -> 24.5 us  [the longest x9 13.5 us: move(): lax.ppermute(array, 'dp', [(i, to(i)) for i in range(lax.axis_size('dp'))])]
    pallas_call x0 -> x5, Pallas kernels: none -> 7.84 us  [sum_call(): pl.pallas_call(kernel, out_shape=out_shape, in_specs=[vm] * len(operands)...]
    convert_element_type x3 -> x0, other arithmetic: 5.69 us -> none  [the longest x1 4.11 us: on_device(): terms = (keep + got.astype(F32)).astype(BF16)]
    all_to_all x1 -> x0, starting transfers between devices: 4.62 us -> none  [on_device(): lax.all_to_all(terms, 'dp', split_axis=0, concat_axis=0, axis_index_group...]
    unnamed x33 -> x29, local copies, waits for them, and re-layouts: 8.51 us -> 4.06 us
  transfers between devices with their start and end apart: 11 -> 17, of which waited for: 6 -> 11; matrix products, arithmetic and copies ran while one was open for 5% -> 2% of each run, Pallas kernels for 22% -> 28%
where the time goes in v3:
time: 154 us; the launch traced here: 152 us
  Pallas kernels  67.4 us (44%)
  waiting for transfers between devices  44.5 us (29%)
  starting transfers between devices  30.1 us (20%)
  local copies, waits for them, and re-layouts  8.37 us (5%)
  between operations  1.6 us (1%)
    pallas_call x2, Pallas kernels, chunk_call(): pl.pallas_call(body, out_shape=out_shape, in_specs=specs, out_specs=[vm]...  42.4 us
    ppermute x9, waiting for transfers between devices, move(): lax.ppermute(array, 'dp', [(i, to(i)) for i in range(lax.axis_size('dp'))])  29.6 us
    ppermute x9, starting transfers between devices, move(): lax.ppermute(array, 'dp', [(i, to(i)) for i in range(lax.axis_size('dp'))])  13.5 us
    pallas_call x1, Pallas kernels, weight_call(): pl.pallas_call(lambda *refs: weight_kernel(deep, *refs), grid=(4,), out_s...  10.8 us
    ppermute x1, waiting for transfers between devices, second_stage(): lax.ppermute(send_a, 'mp', cross)  8.19 us
    pallas_call x5, Pallas kernels, sum_call(): pl.pallas_call(kernel, out_shape=out_shape, in_specs=[vm] * len(operands)...  7.84 us
    all_to_all x1, starting transfers between devices, on_device(): lax.all_to_all(outgoing, 'dp', split_axis=0, concat_axis=0, tiled=True)  5.54 us
    pallas_call x1, Pallas kernels, pick_call(): pl.pallas_call(pick_kernel, out_shape=jax.ShapeDtypeStruct((SEGS, MAXLEN,...  4.31 us
  transfers between devices with their start and end apart: 17, of which 11 were waited for; matrix products, arithmetic and copies ran while one was open for 2% of the time, Pallas kernels for 28%

profile of v3, /device:TPU:0, one launch (start us, length us, event | category | flops | bytes accessed | tf_op | source)
XLA Modules:
  0.0 152.1 jit_solution(2988655683288491575)
XLA Ops:
  1.3 0.7 reshape.24.refs_6_
  2.0 2.3 %copy.19 = bf16[192,8,2,384]{3,1,2,0:T(8,128)(2,1)S(1)} copy(bf16[192,8,2,384]{3,2,1,0:T(2,128)(2,1)} %bitcast.7) | data formatting | bytes 4718592
  4.3 0.8 copy-done.6
  5.1 20.5 %chunk0.1 = (bf16[864,768]{1,0:T(8,128)(2,1)}, bf16[864,384]{1,0:T(8,128)(2,1)S(1)}, f32[104,384]{1,0:T(8,128)S(1)}, f32[768,384]{1,0:T(8,128)S(1)}, bf16[768,38...) custom-call(s32[1,32]{1,0:T(1,128)S(1)} %copy-done.4, bf16[1536,1536]{1,0:T(8,128)(2,1)S(1)} %copy-done.6, ...), custom_call_target="tpu_custom_call" | custom-call | flops 20000000000 | bytes 20000000 | tf_op jit(solution)/shard_map/chunk0/pallas_call | solution.py:267
  25.7 0.8 copy-done.3
  26.4 31.6 %conditional.4 = (bf16[768,384]{1,0:T(8,128)(2,1)}, bf16[768,384]{1,0:T(8,128)(2,1)}, bf16[768,384]{1,0:T(8,128)(2,1)}, bf16[768,768]{1,0:T(8,128)(2,1)}, bf16[7...) conditional(s32[]{:T(128)} %bitcast, () %tuple.42, ...), branch_computations={%region_0.0_spmd, %region_1.0_spmd} | conditional | flops 20000000000 | bytes 27520456 | solution.py:536
  26.4 2.0 %collective-permute-start = (bf16[768,384]{1,0:T(8,128)(2,1)}, bf16[768,384]{1,0:T(8,128)(2,1)}, u32[]{:S(2)}, u32[]{:S(2)}) collective-permute-start(bf16[768,384]{1,0:T(8,128)(2,1)} %get-tuple-element.76), channel_id=1, source_target_pairs={{0,1},{1,2},{2,3},{3,0},{4,5},{5,6},{6,7},{7,4},{8,9},{9,10},{10,1... | collective-permute-start | bytes 1769480 | tf_op jit(solution)/shard_map/cond/branch_1_fun/ppermute | solution.py:576
  28.4 3.6 %collective-permute-start.1 = (bf16[768,384]{1,0:T(8,128)(2,1)}, bf16[768,384]{1,0:T(8,128)(2,1)}, u32[]{:S(2)}, u32[]{:S(2)}) collective-permute-start(bf16[768,384]{1,0:T(8,128)(2,1)} %get-tuple-element.77), channel_id=1, source_target_pairs={{0,2},{1,3},{2,0},{3,1},{4,6},{5,7},{6,4},{7,5},{8,10},{9,11},{10,... | collective-permute-start | bytes 1769480 | tf_op jit(solution)/shard_map/cond/branch_1_fun/ppermute | solution.py:577
  32.0 1.0 collective-permute-start.2
  33.0 0.9 slice.14.refs_11_
  33.9 22.0 %chunk768.1 = (bf16[768,768]{1,0:T(8,128)(2,1)}, bf16[768,384]{1,0:T(8,128)(2,1)}, f32[32,384]{1,0:T(8,128)}, bf16[384,768]{1,0:T(8,128)(2,1)}, bf16[384,768]{1,...) custom-call(s32[1,32]{1,0:T(1,128)S(1)} %get-tuple-element.79.refs_0_, ...), custom_call_target="tpu_custom_call" | custom-call | flops 20000000000 | bytes 20000000 | tf_op jit(solution)/shard_map/cond/branch_1_fun/chunk768/pallas_call | solution.py:267
  55.9 2.1 %collective-permute-done.1 = bf16[768,384]{1,0:T(8,128)(2,1)} collective-permute-done((bf16[768,384]{1,0:T(8,128)(2,1)}, bf16[768,384]{1,0:T(8,128)(2,1)}, u32[]{:S(2)}, u32[]{:S(2)}) %collective-permute-start.1) | collective-permute-done | bytes 589856 | tf_op jit(solution)/shard_map/cond/branch_1_fun/ppermute | solution.py:577
  58.0 18.1 %conditional.5 = (bf16[384,768]{1,0:T(8,128)(2,1)}, bf16[384,768]{1,0:T(8,128)(2,1)}, f32[32,384]{1,0:T(8,128)}, f32[16,48,1152]{2,1,0:T(8,128)S(1)}, bf16[16,48,1152]{2,1,0:T(8,128)(2,1)S(1)}) conditional(s32[]{:T(128)} %bitcast, () %tuple.41, (bf16[384,768]{1,0:T(8,128)(2,1)}, bf16[384,768]{1,0:T(8,128)(2,1)}, f32[32,384]{1,0:T(8,128)}, ...), branch_computations={%region_2.0_spmd, %region_3.0_spmd} | conditional | flops 11000000512 | bytes 24915360 | solution.py:536
  58.0 1.1 collective-permute-start.3
  59.2 1.7 %collective-permute-start.4 = (bf16[384,768]{1,0:T(8,128)(2,1)}, bf16[384,768]{1,0:T(8,128)(2,1)}, u32[]{:S(2)}, u32[]{:S(2)}) collective-permute-start(bf16[384,768]{1,0:T(8,128)(2,1)} %get-tuple-element.101), channel_id=1, source_target_pairs={{0,3},{1,2},{2,1},{3,0},{4,7},{5,6},{6,5},{7,4},{8,11},{9,10},{10,... | collective-permute-start | bytes 1769480 | tf_op jit(solution)/shard_map/cond/branch_1_fun/ppermute | solution.py:600
  60.8 10.8 %weight.1 = (f32[16,48,1152]{2,1,0:T(8,128)S(1)}, bf16[16,48,1152]{2,1,0:T(8,128)(2,1)S(1)}) custom-call(bf16[1536,1536]{1,0:T(8,128)(2,1)} %get-tuple-element.103.refs_0_, bf16[1536,1536]{1,0:T(8,128)(2,1)} %get-tuple-element.104.refs_1_, bf16[864,768]{1,0:T(8,128)(2,1)} %get-tuple-element.105.refs_2_, bf16[768,768]{1,0:T(8,128)(2,1)} %get-tuple-element.106.refs_3_, ...), custom_call_target="tpu_custom_call" | custom-call | flops 11000000512 | bytes 20000000 | tf_op jit(solution)/shard_map/cond/branch_1_fun/weight/pallas_call | solution.py:395
  71.6 2.4 %collective-permute-done.3 = bf16[384,768]{1,0:T(8,128)(2,1)} collective-permute-done((bf16[384,768]{1,0:T(8,128)(2,1)}, bf16[384,768]{1,0:T(8,128)(2,1)}, u32[]{:S(2)}, u32[]{:S(2)}) %collective-permute-start.3) | collective-permute-done | bytes 589856 | tf_op jit(solution)/shard_map/cond/branch_1_fun/ppermute | solution.py:599
  74.1 2.1 %collective-permute-done.4 = bf16[384,768]{1,0:T(8,128)(2,1)} collective-permute-done((bf16[384,768]{1,0:T(8,128)(2,1)}, bf16[384,768]{1,0:T(8,128)(2,1)}, u32[]{:S(2)}, u32[]{:S(2)}) %collective-permute-start.4) | collective-permute-done | bytes 589856 | tf_op jit(solution)/shard_map/cond/branch_1_fun/ppermute | solution.py:600
  76.1 3.3 %fold.1 = (bf16[768,384]{1,0:T(8,128)(2,1)}, f32[768,384]{1,0:T(8,128)}, bf16[384,384]{1,0:T(8,128)(2,1)S(1)}, bf16[384,384]{1,0:T(8,128)(2,1)S(1)}) custom-call(f32[768,384]{1,0:T(8,128)S(1)} %get-tuple-element.195.keep0, bf16[768,384]{1,0:T(8,128)(2,1)} %get-tuple-element.196.near0, bf16[768,384]{1,0:T(8,128)(2,1)} %get-tuple-element.197.far0, ...), custom_call_target="tpu_custom_call" | custom-call | flops 1000000 | bytes 60000000 | tf_op jit(solution)/shard_map/fold/pallas_call | solution.py:499
  79.5 0.3 collective-permute-done.12.got
  79.8 1.1 core_sum.1
  81.0 16.8 %conditional.6 = (bf16[384,384]{1,0:T(8,128)(2,1)}, bf16[384,384]{1,0:T(8,128)(2,1)}, bf16[8,48,640]{2,1,0:T(8,128)(2,1)}, bf16[10,48,512]{2,1,0:T(8,128)(2,1)}) conditional(s32[]{:T(128)} %bitcast, () %tuple.45, (bf16[384,384]{1,0:T(8,128)(2,1)S(1)}, bf16[384,384]{1,0:T(8,128)(2,1)S(1)}, bf16[8,48,640]{2,1,0:T(8,128)(2,1)S(1)}, ...), branch_computations={%region_4.0_spmd, %region_5.0_spmd} | conditional | bytes 6291648 | solution.py:536
  81.0 1.6 %collective-permute-start.8 = (bf16[8,48,640]{2,1,0:T(8,128)(2,1)S(1)}, bf16[8,48,640]{2,1,0:T(8,128)(2,1)}, u32[]{:S(2)}, u32[]{:S(2)}) collective-permute-start(bf16[8,48,640]{2,1,0:T(8,128)(2,1)S(1)} %get-tuple-element.113), channel_id=1, source_target_pairs={{0,32},{4,36},{8,40},{12,44},{16,48},{20,52},{24,56},{28,60},{32,0... | collective-permute-start | bytes 1474568 | tf_op jit(solution)/shard_map/cond/branch_1_fun/ppermute | solution.py:527
  82.6 3.8 %collective-permute-start.9 = (bf16[10,48,512]{2,1,0:T(8,128)(2,1)S(1)}, bf16[10,48,512]{2,1,0:T(8,128)(2,1)}, u32[]{:S(2)}, u32[]{:S(2)}) collective-permute-start(bf16[10,48,512]{2,1,0:T(8,128)(2,1)S(1)} %get-tuple-element.114), channel_id=1, source_target_pairs={{0,8},{4,12},{8,0},{12,4},{16,24},{20,28},{24,16},{28,20},{32,40},... | collective-permute-start | bytes 1474568 | tf_op jit(solution)/shard_map/cond/branch_1_fun/ppermute | solution.py:527
  86.4 1.6 %collective-permute-start.6 = (bf16[384,384]{1,0:T(8,128)(2,1)S(1)}, bf16[384,384]{1,0:T(8,128)(2,1)}, u32[]{:S(2)}, u32[]{:S(2)}) collective-permute-start(bf16[384,384]{1,0:T(8,128)(2,1)S(1)} %get-tuple-element.111), channel_id=1, source_target_pairs={{0,3},{1,2},{2,1},{3,0},{4,7},{5,6},{6,5},{7,4},{8,11},{9,10},{10,... | collective-permute-start | bytes 884744 | tf_op jit(solution)/shard_map/cond/branch_1_fun/ppermute | solution.py:606
  88.0 8.2 %collective-permute-done.6 = bf16[384,384]{1,0:T(8,128)(2,1)} collective-permute-done((bf16[384,384]{1,0:T(8,128)(2,1)S(1)}, bf16[384,384]{1,0:T(8,128)(2,1)}, u32[]{:S(2)}, u32[]{:S(2)}) %collective-permute-start.6) | collective-permute-done | bytes 294944 | tf_op jit(solution)/shard_map/cond/branch_1_fun/ppermute | solution.py:606
  96.2 0.2 collective-permute-done.7
  96.4 1.4 collective-permute-done.9
  97.8 1.5 half_sum.1
  99.3 0.1 copy-done.2
  99.5 8.4 %conditional.7 = (bf16[4,48,640]{2,1,0:T(8,128)(2,1)}, bf16[6,48,512]{2,1,0:T(8,128)(2,1)}, bf16[32,72,384]{2,1,0:T(8,128)(2,1)}) conditional(s32[]{:T(128)} %bitcast, () %tuple.40, (bf16[4,48,640]{2,1,0:T(8,128)(2,1)S(1)}, bf16[6,48,512]{2,1,0:T(8,128)(2,1)S(1)}, s32[1,32]{1,0:T(1,128)S(1)}, s32[1,32]{1,0:T(1,128)S(1)}, ...), branch_computations={%region_6.0_spmd, %region_7.0_spmd} | conditional | flops 1000000 | bytes 2310174 | solution.py:536
  99.5 0.4 collective-permute-start.11
  99.8 1.7 %collective-permute-start.10 = (bf16[4,48,640]{2,1,0:T(8,128)(2,1)S(1)}, bf16[4,48,640]{2,1,0:T(8,128)(2,1)}, u32[]{:S(2)}, u32[]{:S(2)}) collective-permute-start(bf16[4,48,640]{2,1,0:T(8,128)(2,1)S(1)} %get-tuple-element.115), channel_id=1, source_target_pairs={{0,8},{4,12},{8,0},{12,4},{16,24},{20,28},{24,16},{28,20},{32,40},... | collective-permute-start | bytes 737288 | tf_op jit(solution)/shard_map/cond/branch_1_fun/ppermute | solution.py:527
  101.6 4.3 %pick.1 = bf16[32,72,384]{2,1,0:T(8,128)(2,1)} custom-call(s32[1,32]{1,0:T(1,128)S(1)} %get-tuple-element.117.len_ref, s32[1,32]{1,0:T(1,128)S(1)} %get-tuple-element.229.owner_ref, bf16[768,384]{1,0:T(8,128)(2,1)S(1)} %get-tuple-element.119.held0, f32[768,384]{1,0:T(8,128)S(1)} %get-tuple-element.120.part, bf16[384,384]{1,0:T(8,128)(2,1)} %get-tuple-element.121.last_a, ...), custom_call_target="tpu_custom_call" | custom-call | flops 1000000 | bytes 100000 | tf_op jit(solution)/shard_map/cond/branch_1_fun/pick/pallas_call | solution.py:332
  105.9 1.3 collective-permute-done.10
  107.2 0.6 collective-permute-done.11
  107.8 5.5 %all-to-all-start = ((bf16[32,72,384]{2,1,0:T(8,128)(2,1)}), bf16[32,72,384]{2,1,0:T(8,128)(2,1)S(1)}, u32[]{:S(2)}, u32[]{:S(2)}) async-start(bf16[32,72,384]{2,1,0:T(8,128)(2,1)} %get-tuple-element.215), calls=%async_computation | async-start | bytes 3538944 | tf_op jit(solution)/shard_map/all_to_all | solution.py:643
  113.4 1.2 square_sum.1
  114.6 3.1 %collective-permute-start.13 = (bf16[48,1920]{1,0:T(8,128)(2,1)S(1)}, bf16[48,1920]{1,0:T(8,128)(2,1)S(1)}, u32[]{:S(2)}, u32[]{:S(2)}) collective-permute-start(bf16[48,1920]{1,0:T(8,128)(2,1)S(1)} %get-tuple-element.223), channel_id=1, source_target_pairs={{0,96},{4,100},{8,104},{12,108},{16,112},{20,116},{24,120},{28,124... | collective-permute-start | bytes 552968 | tf_op jit(solution)/shard_map/ppermute | solution.py:527
  117.7 2.7 %collective-permute-start.14 = (bf16[48,1920]{1,0:T(8,128)(2,1)S(1)}, bf16[48,1920]{1,0:T(8,128)(2,1)S(1)}, u32[]{:S(2)}, u32[]{:S(2)}) collective-permute-start(bf16[48,1920]{1,0:T(8,128)(2,1)S(1)} %get-tuple-element.224), channel_id=1, source_target_pairs={{0,24},{4,28},{8,16},{12,20},{16,8},{20,12},{24,0},{28,4},{32,56},... | collective-permute-start | bytes 552968 | tf_op jit(solution)/shard_map/ppermute | solution.py:527
  120.4 0.1 collective-permute-start.15
  120.6 20.3 %collective-permute-done.13.refs_2_ = bf16[48,1920]{1,0:T(8,128)(2,1)S(1)} collective-permute-done((bf16[48,1920]{1,0:T(8,128)(2,1)S(1)}, bf16[48,1920]{1,0:T(8,128)(2,1)S(1)}, u32[]{:S(2)}, u32[]{:S(2)}) %collective-permute-start.13) | collective-permute-done | bytes 184352 | tf_op jit(solution)/shard_map/ppermute | solution.py:527
  140.9 5.6 %collective-permute-done.15.refs_4_ = bf16[48,1920]{1,0:T(8,128)(2,1)S(1)} collective-permute-done((bf16[48,1920]{1,0:T(8,128)(2,1)S(1)}, bf16[48,1920]{1,0:T(8,128)(2,1)S(1)}, u32[]{:S(2)}, u32[]{:S(2)}) %collective-permute-start.15) | collective-permute-done | bytes 184352 | tf_op jit(solution)/shard_map/ppermute | solution.py:527
  146.5 0.7 last_sum.1
  147.2 0.7 reshape.25
  147.9 1.3 slice_reduce_fusion
  149.2 0.6 slice_bitcast_fusion
  149.9 2.0 %order.1 = bf16[32,72,384]{2,1,0:T(8,128)(2,1)} custom-call(s32[1,32]{1,0:T(1,128)S(1)} %copy-done, bf16[32,72,384]{2,1,0:T(8,128)(2,1)S(1)} %all-to-all-done.src), custom_call_target="tpu_custom_call" | custom-call | flops 1000000 | bytes 100000 | tf_op jit(solution)/shard_map/order/pallas_call | solution.py:355
  (37 shorter events, 0.2 us)
Async XLA Ops:
  2.0 2.3 %copy-start.4 = (s32[1,32]{1,0:T(1,128)S(1)}, s32[1,32]{1,0:T(1,128)}, u32[]{:S(2)}) copy-start(s32[1,32]{1,0:T(1,128)} %refs_0_.1) | copy-start | bytes 388
  2.0 3.1 %copy-start.6 = (bf16[1536,1536]{1,0:T(8,128)(2,1)S(1)}, bf16[1536,1536]{1,0:T(8,128)(2,1)}, u32[]{:S(2)}) copy-start(bf16[1536,1536]{1,0:T(8,128)(2,1)} %refs_1_.1) | copy-start | bytes 14155780
  2.0 23.6 %slice-start = ((s8[4718592]{0:T(1024)(128)(4,1)}), s8[4194304]{0:T(1024)(128)(4,1)S(1)}, s32[]{:S(2)}) async-start(s8[4718592]{0:T(1024)(128)(4,1)} %bitcast.12), calls=%async_computation.1 | async-start | bytes 8388608
  5.0 20.6 %slice-start.1 = ((s8[4718592]{0:T(1024)(128)(4,1)}), s8[524288]{0:T(1024)(128)(4,1)S(1)}, s32[]{:S(2)}) async-start(s8[4718592]{0:T(1024)(128)(4,1)} %bitcast.12), calls=%async_computation.2 | async-start | bytes 1048576
  5.0 20.6 %copy-start.7 = (f32[31,384]{1,0:T(8,128)S(1)}, f32[31,384]{1,0:T(8,128)}, u32[]{:S(2)}) copy-start(f32[31,384]{1,0:T(8,128)} %refs_5_.1) | copy-start | bytes 142852
  5.0 20.6 %copy-start.8 = (f32[96,240]{1,0:T(8,128)S(1)}, f32[96,240]{1,0:T(8,128)}, u32[]{:S(2)}) copy-start(f32[96,240]{1,0:T(8,128)} %constant.18.clone.refs_7_) | copy-start | bytes 276484
  5.0 20.6 %copy-start.9 = (bf16[80,288]{1,0:T(8,128)(2,1)S(1)}, bf16[80,288]{1,0:T(8,128)(2,1)}, u32[]{:S(2)}) copy-start(bf16[80,288]{1,0:T(8,128)(2,1)} %constant.15.clone.refs_8_) | copy-start | bytes 138244
  5.0 20.6 %copy-start.10 = (f32[96,31]{1,0:T(8,128)S(1)}, f32[96,31]{1,0:T(8,128)}, u32[]{:S(2)}) copy-start(f32[96,31]{1,0:T(8,128)} %constant.23.clone.refs_9_) | copy-start | bytes 35716
  5.1 20.6 %copy-start.11 = (f32[31,96]{1,0:T(8,128)S(1)}, f32[31,96]{1,0:T(8,128)}, u32[]{:S(2)}) copy-start(f32[31,96]{1,0:T(8,128)} %constant.24.clone.refs_10_) | copy-start | bytes 35716
  25.6 0.8 copy-start.3
  26.4 29.5 %collective-permute-start = (bf16[768,384]{1,0:T(8,128)(2,1)}, bf16[768,384]{1,0:T(8,128)(2,1)}, u32[]{:S(2)}, u32[]{:S(2)}) collective-permute-start(bf16[768,384]{1,0:T(8,128)(2,1)} %get-tuple-element.76), channel_id=1, source_target_pairs={{0,1},{1,2},{2,3},{3,0},{4,5},{5,6},{6,7},{7,4},{8,9},{9,10},{10,1... | collective-permute-start | bytes 1769480 | tf_op jit(solution)/shard_map/cond/branch_1_fun/ppermute | solution.py:576
  28.4 29.6 %collective-permute-start.1 = (bf16[768,384]{1,0:T(8,128)(2,1)}, bf16[768,384]{1,0:T(8,128)(2,1)}, u32[]{:S(2)}, u32[]{:S(2)}) collective-permute-start(bf16[768,384]{1,0:T(8,128)(2,1)} %get-tuple-element.77), channel_id=1, source_target_pairs={{0,2},{1,3},{2,0},{3,1},{4,6},{5,7},{6,4},{7,5},{8,10},{9,11},{10,... | collective-permute-start | bytes 1769480 | tf_op jit(solution)/shard_map/cond/branch_1_fun/ppermute | solution.py:577
  32.0 26.0 %collective-permute-start.2 = (bf16[768,384]{1,0:T(8,128)(2,1)}, bf16[768,384]{1,0:T(8,128)(2,1)}, u32[]{:S(2)}, u32[]{:S(2)}) collective-permute-start(bf16[768,384]{1,0:T(8,128)(2,1)} %get-tuple-element.78), channel_id=1, source_target_pairs={{0,3},{1,0},{2,1},{3,2},{4,7},{5,4},{6,5},{7,6},{8,11},{9,8},{10,9... | collective-permute-start | bytes 1769480 | tf_op jit(solution)/shard_map/cond/branch_1_fun/ppermute | solution.py:578
  58.0 13.6 %collective-permute-start.5 = (f32[32,384]{1,0:T(8,128)}, f32[32,384]{1,0:T(8,128)}, u32[]{:S(2)}, u32[]{:S(2)}) collective-permute-start(f32[32,384]{1,0:T(8,128)} %get-tuple-element.102), channel_id=1, source_target_pairs={{0,4},{4,0},{8,12},{12,8},{16,20},{20,16},{24,28},{28,24},{32,36},... | collective-permute-start | bytes 147464 | tf_op jit(solution)/shard_map/cond/branch_1_fun/ppermute | solution.py:527
  58.0 16.1 %collective-permute-start.3 = (bf16[384,768]{1,0:T(8,128)(2,1)}, bf16[384,768]{1,0:T(8,128)(2,1)}, u32[]{:S(2)}, u32[]{:S(2)}) collective-permute-start(bf16[384,768]{1,0:T(8,128)(2,1)} %get-tuple-element.100), channel_id=1, source_target_pairs={{0,1},{1,0},{2,3},{3,2},{4,5},{5,4},{6,7},{7,6},{8,9},{9,8},{10,11... | collective-permute-start | bytes 1769480 | tf_op jit(solution)/shard_map/cond/branch_1_fun/ppermute | solution.py:599
  59.2 17.0 %collective-permute-start.4 = (bf16[384,768]{1,0:T(8,128)(2,1)}, bf16[384,768]{1,0:T(8,128)(2,1)}, u32[]{:S(2)}, u32[]{:S(2)}) collective-permute-start(bf16[384,768]{1,0:T(8,128)(2,1)} %get-tuple-element.101), channel_id=1, source_target_pairs={{0,3},{1,2},{2,1},{3,0},{4,7},{5,6},{6,5},{7,4},{8,11},{9,10},{10,... | collective-permute-start | bytes 1769480 | tf_op jit(solution)/shard_map/cond/branch_1_fun/ppermute | solution.py:600
  76.1 3.7 %collective-permute-start.12 = (bf16[16,48,1152]{2,1,0:T(8,128)(2,1)S(1)}, bf16[16,48,1152]{2,1,0:T(8,128)(2,1)S(1)}, u32[]{:S(2)}, u32[]{:S(2)}) collective-permute-start(bf16[16,48,1152]{2,1,0:T(8,128)(2,1)S(1)} %get-tuple-element.190), channel_id=1, source_target_pairs={{0,4},{4,0},{8,12},{12,8},{16,20},{20,16},{24,28},{28,24},{32,36},... | collective-permute-start | bytes 5308424 | tf_op jit(solution)/shard_map/ppermute | solution.py:527
  81.0 15.4 %collective-permute-start.8 = (bf16[8,48,640]{2,1,0:T(8,128)(2,1)S(1)}, bf16[8,48,640]{2,1,0:T(8,128)(2,1)}, u32[]{:S(2)}, u32[]{:S(2)}) collective-permute-start(bf16[8,48,640]{2,1,0:T(8,128)(2,1)S(1)} %get-tuple-element.113), channel_id=1, source_target_pairs={{0,32},{4,36},{8,40},{12,44},{16,48},{20,52},{24,56},{28,60},{32,0... | collective-permute-start | bytes 1474568 | tf_op jit(solution)/shard_map/cond/branch_1_fun/ppermute | solution.py:527
  82.6 15.2 %collective-permute-start.9 = (bf16[10,48,512]{2,1,0:T(8,128)(2,1)S(1)}, bf16[10,48,512]{2,1,0:T(8,128)(2,1)}, u32[]{:S(2)}, u32[]{:S(2)}) collective-permute-start(bf16[10,48,512]{2,1,0:T(8,128)(2,1)S(1)} %get-tuple-element.114), channel_id=1, source_target_pairs={{0,8},{4,12},{8,0},{12,4},{16,24},{20,28},{24,16},{28,20},{32,40},... | collective-permute-start | bytes 1474568 | tf_op jit(solution)/shard_map/cond/branch_1_fun/ppermute | solution.py:527
  86.4 9.8 %collective-permute-start.6 = (bf16[384,384]{1,0:T(8,128)(2,1)S(1)}, bf16[384,384]{1,0:T(8,128)(2,1)}, u32[]{:S(2)}, u32[]{:S(2)}) collective-permute-start(bf16[384,384]{1,0:T(8,128)(2,1)S(1)} %get-tuple-element.111), channel_id=1, source_target_pairs={{0,3},{1,2},{2,1},{3,0},{4,7},{5,6},{6,5},{7,4},{8,11},{9,10},{10,... | collective-permute-start | bytes 884744 | tf_op jit(solution)/shard_map/cond/branch_1_fun/ppermute | solution.py:606
  88.0 8.3 %collective-permute-start.7 = (bf16[384,384]{1,0:T(8,128)(2,1)S(1)}, bf16[384,384]{1,0:T(8,128)(2,1)}, u32[]{:S(2)}, u32[]{:S(2)}) collective-permute-start(bf16[384,384]{1,0:T(8,128)(2,1)S(1)} %get-tuple-element.112), channel_id=1, source_target_pairs={{0,1},{1,0},{2,3},{3,2},{4,5},{5,4},{6,7},{7,6},{8,9},{9,8},{10,11... | collective-permute-start | bytes 884744 | tf_op jit(solution)/shard_map/cond/branch_1_fun/ppermute | solution.py:607
  97.8 1.6 %copy-start.1 = (f32[768,384]{1,0:T(8,128)S(1)}, f32[768,384]{1,0:T(8,128)}, u32[]{:S(2)}) copy-start(f32[768,384]{1,0:T(8,128)} %get-tuple-element.212) | copy-start | bytes 3538948
  97.8 1.7 %copy-start.2 = (bf16[768,384]{1,0:T(8,128)(2,1)S(1)}, bf16[768,384]{1,0:T(8,128)(2,1)}, u32[]{:S(2)}) copy-start(bf16[768,384]{1,0:T(8,128)(2,1)} %get-tuple-element.211) | copy-start | bytes 1769476
  97.8 1.7 %copy-start.5 = (s32[1,32]{1,0:T(1,128)S(1)}, s32[1,32]{1,0:T(1,128)}, u32[]{:S(2)}) copy-start(s32[1,32]{1,0:T(1,128)} %param.28) | copy-start | bytes 388
  99.5 8.4 %collective-permute-start.11 = (bf16[6,48,512]{2,1,0:T(8,128)(2,1)S(1)}, bf16[6,48,512]{2,1,0:T(8,128)(2,1)}, u32[]{:S(2)}, u32[]{:S(2)}) collective-permute-start(bf16[6,48,512]{2,1,0:T(8,128)(2,1)S(1)} %get-tuple-element.116), channel_id=1, source_target_pairs={{0,32},{4,36},{8,40},{12,44},{16,48},{20,52},{24,56},{28,60},{32,0... | collective-permute-start | bytes 884744 | tf_op jit(solution)/shard_map/cond/branch_1_fun/ppermute | solution.py:527
  99.8 7.4 %collective-permute-start.10 = (bf16[4,48,640]{2,1,0:T(8,128)(2,1)S(1)}, bf16[4,48,640]{2,1,0:T(8,128)(2,1)}, u32[]{:S(2)}, u32[]{:S(2)}) collective-permute-start(bf16[4,48,640]{2,1,0:T(8,128)(2,1)S(1)} %get-tuple-element.115), channel_id=1, source_target_pairs={{0,8},{4,12},{8,0},{12,4},{16,24},{20,28},{24,16},{28,20},{32,40},... | collective-permute-start | bytes 737288 | tf_op jit(solution)/shard_map/cond/branch_1_fun/ppermute | solution.py:527
  107.8 42.1 %all-to-all-start = ((bf16[32,72,384]{2,1,0:T(8,128)(2,1)}), bf16[32,72,384]{2,1,0:T(8,128)(2,1)S(1)}, u32[]{:S(2)}, u32[]{:S(2)}) async-start(bf16[32,72,384]{2,1,0:T(8,128)(2,1)} %get-tuple-element.215), calls=%async_computation | async-start | bytes 3538944 | tf_op jit(solution)/shard_map/all_to_all | solution.py:643
  113.4 36.5 %copy-start = (s32[1,32]{1,0:T(1,128)S(1)}, s32[1,32]{1,0:T(1,128)}, u32[]{:S(2)}) copy-start(s32[1,32]{1,0:T(1,128)} %slot_ref.1) | copy-start | bytes 388
  114.6 26.3 %collective-permute-start.13 = (bf16[48,1920]{1,0:T(8,128)(2,1)S(1)}, bf16[48,1920]{1,0:T(8,128)(2,1)S(1)}, u32[]{:S(2)}, u32[]{:S(2)}) collective-permute-start(bf16[48,1920]{1,0:T(8,128)(2,1)S(1)} %get-tuple-element.223), channel_id=1, source_target_pairs={{0,96},{4,100},{8,104},{12,108},{16,112},{20,116},{24,120},{28,124... | collective-permute-start | bytes 552968 | tf_op jit(solution)/shard_map/ppermute | solution.py:527
  117.7 23.2 %collective-permute-start.14 = (bf16[48,1920]{1,0:T(8,128)(2,1)S(1)}, bf16[48,1920]{1,0:T(8,128)(2,1)S(1)}, u32[]{:S(2)}, u32[]{:S(2)}) collective-permute-start(bf16[48,1920]{1,0:T(8,128)(2,1)S(1)} %get-tuple-element.224), channel_id=1, source_target_pairs={{0,24},{4,28},{8,16},{12,20},{16,8},{20,12},{24,0},{28,4},{32,56},... | collective-permute-start | bytes 552968 | tf_op jit(solution)/shard_map/ppermute | solution.py:527
  120.4 26.1 %collective-permute-start.15 = (bf16[48,1920]{1,0:T(8,128)(2,1)S(1)}, bf16[48,1920]{1,0:T(8,128)(2,1)S(1)}, u32[]{:S(2)}, u32[]{:S(2)}) collective-permute-start(bf16[48,1920]{1,0:T(8,128)(2,1)S(1)} %get-tuple-element.225), channel_id=1, source_target_pairs={{0,120},{4,124},{8,112},{12,116},{16,104},{20,108},{24,96},{28,100... | collective-permute-start | bytes 552968 | tf_op jit(solution)/shard_map/ppermute | solution.py:527

commit v4 on v3

--- a/solution.py
+++ b/solution.py
@@ -12,10 +12,12 @@
 MAXLEN = 72
 REACH = 15
 WIN = 80
-POINTS = 95
-HALF = 48
-FREQ = 2 * HALF
+POINTS = 87
+MAIN = 40
+EDGE = 4
+FREQ = 2 * (MAIN + EDGE)
 MARGIN = 96
+ROWS0 = 640
 SEGS = 32
 GROUP = 4
 MIB = 1024 * 1024
@@ -27,14 +29,23 @@
 
 
 def tables():
-    f = np.arange(HALF)[:, None].astype(np.float64)
-    w = np.where(f == 0, 1.0 / POINTS, 2.0 / POINTS)
-    ang = 2 * np.pi * ((f * np.arange(WIN)[None, :]) % POINTS) / POINTS
-    fwd = np.concatenate([np.cos(ang), np.sin(ang)], 0)
-    inv = np.concatenate([w * np.cos(ang), w * np.sin(ang)], 0).T
-    tang = 2 * np.pi * ((f * (np.arange(TAPS)[None, :] - REACH)) % POINTS) / POINTS
-    taps = np.concatenate([np.cos(tang), np.sin(tang)], 0)
-    back = np.concatenate([w * np.cos(tang), -w * np.sin(tang)], 0).T
+    f = np.arange(MAIN + EDGE)[:, None]
+    scale = np.where(f == 0, 1.0 / POINTS, 2.0 / POINTS)
+
+    def waves(at, edge_sign):
+        ang = 2 * np.pi * ((f * at[None, :]) % POINTS) / POINTS
+        cos, sin = np.cos(ang), np.sin(ang)
+        return cos[:MAIN], sin[:MAIN], cos[MAIN:], edge_sign * sin[MAIN:]
+
+    rows = np.arange(WIN)
+    shift = np.arange(TAPS) - REACH
+    fwd = np.concatenate(waves(rows, 1), 0)
+    weight = np.concatenate([scale[:MAIN]] * 2 + [scale[MAIN:]] * 2, 0)
+    inv = (weight * fwd).T
+    c, s, c4, s4 = waves(shift, 1)
+    taps = np.concatenate([c, s, c4, c4, s4, -s4], 0)
+    main, edge = scale[:MAIN], scale[MAIN:]
+    back = np.concatenate([main * c, -main * s, edge * c4, edge * c4, -edge * s4, edge * s4], 0).T
 
     def split(table):
         high = table.astype(BF16).astype(np.float32)
@@ -42,8 +53,8 @@
         return np.concatenate([high, low, high], 1)
 
     return (
-        jnp.asarray(split(fwd), F32),
-        jnp.asarray(split(inv), BF16),
+        jnp.asarray(split(fwd), BF16),
+        jnp.asarray(split(inv)[:, : 2 * FREQ + 2 * MAIN], BF16),
         jnp.asarray(taps, F32),
         jnp.asarray(back, F32),
     )
@@ -54,24 +65,28 @@
     return base, start - base
 
 
-def pieces(x):
-    high = x.astype(BF16)
-    low = (x - high.astype(F32)).astype(BF16)
-    return jnp.concatenate([high, high, low], 0)
-
-
-def chunk_kernel(first, rows, load, last, halves, *refs):
+def pieces(x, rows):
+    high = x.astype(BF16).astype(F32)
+    return jnp.concatenate([high, high, (x - high)[:rows]], 0).astype(BF16)
+
+
+def turned(x):
+    return jnp.concatenate([x[EDGE:], x[:EDGE]], 0)
+
+
+def chunk_kernel(first, rows, load, blocks, last, halves, *refs):
     (len_ref, frames_hbm, gout_hbm, w_ref, wout_ref, taps_ref, bias_ref,
      fwd_ref, inv_ref, tap_table_ref, back_table_ref) = refs[:11]
     refs = refs[11:]
     if first:
-        gp_prev, act_prev, sum_prev = refs[:3]
+        gp_prev_hbm, act_prev_hbm, sum_prev = refs[:3]
         refs = refs[3:]
+        gp_prev, act_prev, tail_sem = refs[-3:]
+        refs = refs[:-3]
     gp_ref, act_ref, sum_ref = refs[:3]
     outs = refs[3 : 3 + len(halves)]
     fr, go, gsig, gated, gsw, conv, gc, spec, kf, acc, f_sem, g_sem = refs[3 + len(halves) :]
     ch = wout_ref.shape[0]
-    blocks = 3
     block = load // blocks
 
     def copy(hbm, vmem, sem, i):
@@ -79,13 +94,21 @@
         dst = pl.ds(pl.multiple_of(i * block, 16), block)
         return pltpu.make_async_copy(hbm.at[src], vmem.at[dst], sem.at[i])
 
+    if first:
+        at = pl.ds(gp_prev_hbm.shape[0] - MARGIN, MARGIN)
+        tails = [
+            pltpu.make_async_copy(gp_prev_hbm.at[at], gp_prev, tail_sem.at[0]),
+            pltpu.make_async_copy(act_prev_hbm.at[at], act_prev, tail_sem.at[1]),
+        ]
+        for tail in tails:
+            tail.start()
     for i in range(blocks):
         copy(frames_hbm, fr, f_sem, i).start()
         copy(gout_hbm, go, g_sem, i).start()
 
-    tail = pl.ds(load, WIN)
-    gated[tail, :] = jnp.zeros((WIN, ch), F32)
-    gc[tail, :] = jnp.zeros((WIN, ch), F32)
+    beyond = pl.ds(load, WIN)
+    gated[beyond, :] = jnp.zeros((WIN, ch), F32)
+    gc[beyond, :] = jnp.zeros((WIN, ch), F32)
     conv[...] = jnp.zeros_like(conv)
     kf[...] = jnp.dot(
         tap_table_ref[...], taps_ref[...],
@@ -115,19 +138,23 @@
 
     lax.fori_loop(0, blocks, project, 0)
 
-    lane = lax.rem(lax.broadcasted_iota(jnp.int32, (FREQ, 3 * WIN), 1), WIN)
-    row8 = lax.broadcasted_iota(jnp.int32, (8, ch), 0)
-
-    def spectrum(src, base, off, length):
-        masked = jnp.where((lane >= off) & (lane < off + length), fwd_ref[...], 0.0)
-        return jnp.dot(
-            masked.astype(BF16), pieces(src[pl.ds(base, WIN), :]), preferred_element_type=F32
-        )
-
-    def inverse(real, imag):
-        return jnp.dot(
-            inv_ref[...], pieces(jnp.concatenate([real, imag], 0)), preferred_element_type=F32
-        )
+    row = lax.broadcasted_iota(jnp.int32, (WIN, ch), 0)
+    row8 = row[:8]
+
+    def spectra(src, places):
+        parts = []
+        for base, off, length in places:
+            x = src[pl.ds(base, WIN), :]
+            parts.append(pieces(jnp.where((row >= off) & (row < off + length), x, 0.0), WIN))
+        both = jnp.dot(fwd_ref[...], jnp.concatenate(parts, 1), preferred_element_type=F32)
+        return [both[:, j * ch : (j + 1) * ch] for j in range(len(places))]
+
+    def inverses(specs):
+        parts = [pieces(jnp.concatenate(p, 0), 2 * MAIN) for p in specs]
+        both = jnp.dot(inv_ref[...], jnp.concatenate(parts, 1), preferred_element_type=F32)
+        return [both[:, j * ch : (j + 1) * ch] for j in range(len(specs))]
+
+    main, sine, edge = slice(0, MAIN), slice(MAIN, 2 * MAIN), slice(2 * MAIN, FREQ)
 
     def put(out, base, off):
         head = pl.ds(base, 8)
@@ -151,19 +178,21 @@
         k, start = state
         places, start = group_of(start, k)
         results = []
-        kc, ks = kf[:HALF], kf[HALF:]
-        for j, (base, off, length) in enumerate(places):
-            s = spectrum(gated, base, off, length)
-            spec[k - k0 + j] = s
-            gr, gi = s[:HALF], s[HALF:]
-            results.append(inverse(kc * gr + ks * gi, kc * gi - ks * gr))
+        kc, ks, ke, kt = kf[main], kf[sine], kf[edge], kf[FREQ:]
+        for j in range(0, GROUP, 2):
+            specs = []
+            for i, s in enumerate(spectra(gated, places[j : j + 2])):
+                spec[k - k0 + j + i] = s
+                gr, gi, ge = s[main], s[sine], s[edge]
+                specs.append((kc * gr + ks * gi, kc * gi - ks * gr, ke * ge + kt * turned(ge)))
+            results += inverses(specs)
         for (base, off, length), out in zip(places, results):
             put(out, base, off)
         return k + GROUP, start
 
     lax.while_loop(more, forward, (k0, s0))
 
-    bias = bias_ref[...]
+    bias = bias_ref[...].reshape(1, ch)
 
     def swish(i, carry):
         at = pl.ds(pl.multiple_of(i * block, 16), block)
@@ -179,22 +208,23 @@
         k, start = state
         places, start = group_of(start, k)
         results = []
-        kc, ks = kf[:HALF], kf[HALF:]
-        real = jnp.zeros((HALF, ch), F32)
-        imag = jnp.zeros((HALF, ch), F32)
-        plain = jnp.zeros((8, ch), F32)
-        for j, (base, off, length) in enumerate(places):
-            s = spectrum(gc, base, off, length)
-            cr, ci = s[:HALF], s[HALF:]
-            g = spec[k - k0 + j]
-            gr, gi = g[:HALF], g[HALF:]
-            results.append(inverse(kc * cr - ks * ci, kc * ci + ks * cr))
-            real += gr * cr + gi * ci
-            imag += gr * ci - gi * cr
-            plain += s[:8]
-        acc[:HALF, :] += real
-        acc[HALF:FREQ, :] += imag
-        acc[FREQ:, :] += plain
+        kc, ks, ke, kt = kf[main], kf[sine], kf[edge], kf[FREQ:]
+        sums = [jnp.zeros((n, ch), F32) for n in (MAIN, MAIN, 8, 8, 8)]
+        for j in range(0, GROUP, 2):
+            specs = []
+            for i, s in enumerate(spectra(gc, places[j : j + 2])):
+                cr, ci, ce = s[main], s[sine], s[edge]
+                g = spec[k - k0 + j + i]
+                gr, gi, ge = g[main], g[sine], g[edge]
+                swapped = turned(ce)
+                specs.append((kc * cr - ks * ci, kc * ci + ks * cr, ke * ce - kt * swapped))
+                terms = (gr * cr + gi * ci, gr * ci - gi * cr, ge * ce, ge * swapped, s[:8])
+                sums = [total + term for total, term in zip(sums, terms)]
+            results += inverses(specs)
+        at = 0
+        for total in sums:
+            acc[at : at + total.shape[0], :] += total
+            at += total.shape[0]
         for (base, off, length), out in zip(places, results):
             put(out, base, off)
         return k + GROUP, start
@@ -212,6 +242,8 @@
     lax.fori_loop(0, blocks, project_back, 0)
 
     if first:
+        for tail in tails:
+            tail.wait()
         head = pl.ds(0, MARGIN)
         from_prev = lax.broadcasted_iota(jnp.int32, (MARGIN, 1), 0) < s0
         gp_ref[head, :] = jnp.where(
@@ -231,11 +263,11 @@
 
     if last:
         taps_grad = jnp.dot(
-            back_table_ref[...], acc[:FREQ, :],
+            back_table_ref[...], acc[: FREQ + 8, :],
             precision=lax.Precision.HIGHEST, preferred_element_type=F32,
         )
         sum_ref[:TAPS, :] = taps_grad
-        sum_ref[TAPS:, :] = acc[FREQ : FREQ + 1, :]
+        sum_ref[TAPS:, :] = acc[FREQ + 8 : FREQ + 9, :]
     else:
         sum_ref[...] = acc[...]
 
@@ -245,24 +277,23 @@
     ch = w_out.shape[0]
     last = first + rows == total
     load = rows if last else rows + MARGIN
+    blocks = next(n for n in range(-(-load // 384), load) if load % (16 * n) == 0)
     vm = pl.BlockSpec(memory_space=pltpu.VMEM)
     hbm = pl.BlockSpec(memory_space=pl.ANY)
     sm = pl.BlockSpec(memory_space=pltpu.SMEM)
     operands = [lengths, frames, grad_out, w_flat, w_out, taps, bias, *consts]
     specs = [sm, hbm, hbm] + [vm] * 8
     if first:
-        gp_prev, act_prev, sum_prev = prev
-        at = gp_prev.shape[0] - MARGIN
-        operands += [gp_prev[at:], act_prev[at:], sum_prev]
-        specs += [vm] * 3
+        operands += prev
+        specs += [hbm, hbm, vm]
 
     def body(*refs):
-        chunk_kernel(first, rows, load, last, [h[:3] for h in halves], *refs)
+        chunk_kernel(first, rows, load, blocks, last, [h[:3] for h in halves], *refs)
 
     out_shape = [
         jax.ShapeDtypeStruct((load, 2 * ch), BF16),
         jax.ShapeDtypeStruct((load, ch), BF16),
-        jax.ShapeDtypeStruct((TAPS + 1 if last else FREQ + 8, ch), F32),
+        jax.ShapeDtypeStruct((TAPS + 1 if last else FREQ + 16, ch), F32),
     ] + [jax.ShapeDtypeStruct((size, len(picks) * ch), dtype) for _, size, picks, dtype in halves]
     return pl.pallas_call(
         body,
@@ -278,34 +309,56 @@
             pltpu.VMEM((load + WIN, ch), F32),
             pltpu.VMEM((load + WIN, ch), F32),
             pltpu.VMEM((SEGS + GROUP, FREQ, ch), F32),
-            pltpu.VMEM((FREQ, ch), F32),
             pltpu.VMEM((FREQ + 8, ch), F32),
-            pltpu.SemaphoreType.DMA((3,)),
-            pltpu.SemaphoreType.DMA((3,)),
-        ],
-        compiler_params=pltpu.CompilerParams(vmem_limit_bytes=48 * MIB),
+            pltpu.VMEM((FREQ + 16, ch), F32),
+            pltpu.SemaphoreType.DMA((blocks,)),
+            pltpu.SemaphoreType.DMA((blocks,)),
+        ] + ([
+            pltpu.VMEM((MARGIN, 2 * ch), BF16),
+            pltpu.VMEM((MARGIN, ch), BF16),
+            pltpu.SemaphoreType.DMA((2,)),
+        ] if first else []),
+        compiler_params=pltpu.CompilerParams(vmem_limit_bytes=40 * MIB),
         cost_estimate=pl.CostEstimate(flops=2 * 10**10, bytes_accessed=2 * 10**7, transcendentals=0),
         name="chunk%d" % first,
     )(*operands)
 
 
-def fold_kernel(keep0, near0, far0, back0, keep_a, keep_b, first_a, first_b, held_ref, part_ref, out_a, out_b):
-    half, ch = out_a.shape
+def zero_sum_kernel(keep0, near0, far0, back0, after, held_ref):
     held_ref[...] = (
         keep0[...] + near0[...].astype(F32) + far0[...].astype(F32) + back0[...].astype(F32)
     ).astype(BF16)
-    for at, keep, one, out in ((0, keep_a, first_a, out_a), (half, keep_b, first_b, out_b)):
-        out[...] = (keep[:, ch:] + one[:, ch:].astype(F32)).astype(BF16)
-        part_ref[at : at + half, :] = keep[:, :ch] + one[:, :ch].astype(F32)
-
-
-def pick_kernel(len_ref, owner_ref, held0, part, last_a, last_b, out_ref, held):
+
+
+def pass_kernel(keep_a, keep_b, first_a, first_b, out_a, out_b):
+    out_a[...] = (keep_a[...] + first_a[...].astype(F32)).astype(BF16)
+    out_b[...] = (keep_b[...] + first_b[...].astype(F32)).astype(BF16)
+
+
+def pass_call(keep_a, keep_b, first_a, first_b):
+    half, ch = keep_a.shape[0], keep_a.shape[1] // 2
+    out = jax.ShapeDtypeStruct((half, ch), BF16)
+    return pl.pallas_call(
+        pass_kernel,
+        grid=(1,),
+        out_shape=(out, out),
+        in_specs=[pl.BlockSpec((half, ch), lambda i: (0, 1))] * 4,
+        out_specs=[pl.BlockSpec((half, ch), lambda i: (0, 0))] * 2,
+        compiler_params=pltpu.CompilerParams(vmem_limit_bytes=16 * MIB),
+        cost_estimate=TINY,
+        name="pass",
+    )(keep_a, keep_b, first_a, first_b)
+
+
+def pick_kernel(
+    len_ref, owner_ref, held0, keep_a, keep_b, first_a, first_b, last_a, last_b, out_ref, held
+):
     rows0, ch = held0.shape
     half = last_a.shape[0]
     rows = rows0 + 2 * half
     held[pl.ds(0, rows0), :] = held0[...]
-    for at, two in ((0, last_a), (half, last_b)):
-        held[pl.ds(rows0 + at, half), :] = (part[at : at + half, :] + two[...].astype(F32)).astype(BF16)
+    for at, keep, one, two in ((rows0, keep_a, first_a, last_a), (rows0 + half, keep_b, first_b, last_b)):
+        held[pl.ds(at, half), :] = (keep[...] + one[...].astype(F32) + two[...].astype(F32)).astype(BF16)
     held[pl.ds(rows, MARGIN), :] = jnp.zeros((MARGIN, ch), BF16)
     row = lax.broadcasted_iota(jnp.int32, (MAXLEN, MARGIN), 0)
     lane = lax.broadcasted_iota(jnp.int32, (MAXLEN, MARGIN), 1)
@@ -325,20 +378,22 @@
     lax.fori_loop(0, SEGS // GROUP, pick, jnp.int32(0))
 
 
-def pick_call(lengths, owners, rows, *parts):
-    ch = parts[-1].shape[1]
-    vm = pl.BlockSpec(memory_space=pltpu.VMEM)
+def pick_call(lengths, owners, held0, keep_a, keep_b, first_a, first_b, last_a, last_b):
+    rows0, ch = held0.shape
+    half = last_a.shape[0]
     sm = pl.BlockSpec(memory_space=pltpu.SMEM)
+    part = pl.BlockSpec((half, ch), lambda i: (0, 0))
     return pl.pallas_call(
         pick_kernel,
+        grid=(1,),
         out_shape=jax.ShapeDtypeStruct((SEGS, MAXLEN, ch), BF16),
-        in_specs=[sm, sm] + [vm] * len(parts),
-        out_specs=vm,
-        scratch_shapes=[pltpu.VMEM((rows + MARGIN, ch), BF16)],
-        compiler_params=pltpu.CompilerParams(vmem_limit_bytes=40 * MIB),
+        in_specs=[sm, sm, pl.BlockSpec((rows0, ch), lambda i: (0, 0))] + [part] * 6,
+        out_specs=pl.BlockSpec((SEGS, MAXLEN, ch), lambda i: (0, 0, 0)),
+        scratch_shapes=[pltpu.VMEM((rows0 + 2 * half + MARGIN, ch), BF16)],
+        compiler_params=pltpu.CompilerParams(vmem_limit_bytes=24 * MIB),
         cost_estimate=TINY,
         name="pick",
-    )(lengths, owners, *parts)
+    )(lengths, owners, held0, keep_a, keep_b, first_a, first_b, last_a, last_b)
 
 
 def order_kernel(slot_ref, src, dst, sem):
@@ -364,45 +419,77 @@
     )(slots, received)
 
 
-def weight_kernel(deep, frames_ref, gout_ref, gp0, gp1, act0, act1, keep_ref, send_ref, held):
-    step = pl.program_id(0) * 4
+COLS = 4
+PARTS = 4
+
+
+def weight_kernel(
+    deep, frames_hbm, gout_hbm, gp0_hbm, gp1_hbm, act0_hbm, act1_hbm, keep_ref, send_ref,
+    fr, go, gp, act, held, f_sem, g_sem, p_sem,
+):
     core = lax.rem(lax.axis_index("dp"), 2)
-    total, cols = frames_ref.shape
-    rows1 = gp1.shape[0]
+    total, width = frames_hbm.shape
+    cols = width // COLS
+    rows1 = gp1_hbm.shape[0]
     rows0 = total - rows1
-    wide = gp0.shape[1]
-
-    def both(left, right0, right1):
-        one = lax.dot_general(left[:rows0, :], right0[:rows0, :], TN, preferred_element_type=F32)
-        return one + lax.dot_general(left[rows0:, :], right1[...], TN, preferred_element_type=F32)
-
-    held[:, :wide] = both(frames_ref, gp0, gp1)
-    held[:, wide:] = both(gout_ref, act0, act1)
-    for j in range(cols // (2 * deep)):
-        own = pl.ds(pl.multiple_of((2 * j + core) * deep, 16), deep)
-        other = pl.ds(pl.multiple_of((2 * j + 1 - core) * deep, 16), deep)
-        keep_ref[step + j] = held[own, :]
-        send_ref[step + j] = held[other, :].astype(BF16)
+    wide = gp.shape[1]
+
+    def read(hbm, vmem, sem):
+        step = total // PARTS
+        return [
+            pltpu.make_async_copy(hbm.at[pl.ds(i * step, step)], vmem.at[pl.ds(i * step, step)], sem.at[i])
+            for i in range(PARTS)
+        ]
+
+    def pair(one, two, out, at):
+        return [
+            pltpu.make_async_copy(one.at[pl.ds(0, rows0)], out.at[pl.ds(0, rows0)], p_sem.at[at]),
+            pltpu.make_async_copy(two, out.at[pl.ds(rows0, rows1)], p_sem.at[at + 1]),
+        ]
+
+    first = pair(act0_hbm, act1_hbm, act, 0) + read(gout_hbm, go, g_sem)
+    second = pair(gp0_hbm, gp1_hbm, gp, 2) + read(frames_hbm, fr, f_sem)
+    for copy in first + second:
+        copy.start()
+    pairs = cols // (2 * deep)
+    for copies, left, right, at in ((first, go, act, slice(wide, None)), (second, fr, gp, slice(0, wide))):
+        for copy in copies:
+            copy.wait()
+        for j in range(COLS):
+            held[j % 2, :, at] = lax.dot_general(
+                left[:, j * cols : (j + 1) * cols], right[...], TN, preferred_element_type=F32
+            )
+            for i in range(pairs):
+                own = pl.ds(pl.multiple_of((2 * i + core) * deep, 16), deep)
+                other = pl.ds(pl.multiple_of((2 * i + 1 - core) * deep, 16), deep)
+                keep_ref[j * pairs + i, :, at] = held[j % 2, own, at]
+                send_ref[j * pairs + i, :, at] = held[j % 2, other, at].astype(BF16)
 
 
 def weight_call(deep, frames, grad_out, gp0, gp1, act0, act1):
     total, width = frames.shape
-    wide = gp0.shape[1] + act0.shape[1]
-    cols = width // 4
+    ch = act0.shape[1]
     pairs = width // (2 * deep)
     vm = pl.BlockSpec(memory_space=pltpu.VMEM)
-    tall = pl.BlockSpec((total, cols), lambda i: (0, i))
     return pl.pallas_call(
         lambda *refs: weight_kernel(deep, *refs),
-        grid=(4,),
         out_shape=(
-            jax.ShapeDtypeStruct((pairs, deep, wide), F32),
-            jax.ShapeDtypeStruct((pairs, deep, wide), BF16),
+            jax.ShapeDtypeStruct((pairs, deep, 3 * ch), F32),
+            jax.ShapeDtypeStruct((pairs, deep, 3 * ch), BF16),
         ),
-        in_specs=[tall, tall, vm, vm, vm, vm],
+        in_specs=[pl.BlockSpec(memory_space=pl.ANY)] * 6,
         out_specs=(vm, vm),
-        scratch_shapes=[pltpu.VMEM((cols, wide), F32)],
-        compiler_params=pltpu.CompilerParams(vmem_limit_bytes=48 * MIB),
+        scratch_shapes=[
+            pltpu.VMEM((total, width), BF16),
+            pltpu.VMEM((total, width), BF16),
+            pltpu.VMEM((total, 2 * ch), BF16),
+            pltpu.VMEM((total, ch), BF16),
+            pltpu.VMEM((2, width // COLS, 3 * ch), F32),
+            pltpu.SemaphoreType.DMA((PARTS,)),
+            pltpu.SemaphoreType.DMA((PARTS,)),
+            pltpu.SemaphoreType.DMA((4,)),
+        ],
+        compiler_params=pltpu.CompilerParams(vmem_limit_bytes=40 * MIB),
         cost_estimate=pl.CostEstimate(flops=11 * 10**9, bytes_accessed=2 * 10**7, transcendentals=0),
         name="weight",
     )(frames, grad_out, gp0, gp1, act0, act1)
@@ -484,27 +571,31 @@
         out[:taps, 4 * ch :] = low
 
 
-def last_sum_kernel(scale, own, small, r1, r2, r3, w_out, small_out):
+def last_sum_kernel(scale, own, small, r1, r2, r3, after, w_in_out, w_out_out, kernel_out, bias_out):
     taps, ch = small.shape
     total, small_total = own[...], small[...]
     for r in (r1, r2, r3):
         total = total + r[:, : 3 * ch].astype(F32)
         small_total = small_total + r[:taps, 3 * ch : 4 * ch].astype(F32) + r[:taps, 4 * ch :].astype(F32)
-    w_out[...] = total * scale
-    small_out[...] = small_total * scale
-
-
-def sum_call(kernel, name, cost, out_shape, *operands):
+    total, small_total = total * scale, small_total * scale
+    w_in_out[:, 0, :] = total[:, :ch]
+    w_in_out[:, 1, :] = total[:, ch : 2 * ch]
+    w_out_out[...] = total[:, 2 * ch :]
+    kernel_out[...] = small_total[:TAPS]
+    bias_out[...] = small_total[TAPS:].reshape(ch)
+
+
+def sum_call(kernel, name, cost, out_shape, *operands, after=()):
     vm = pl.BlockSpec(memory_space=pltpu.VMEM)
     return pl.pallas_call(
         kernel,
         out_shape=out_shape,
-        in_specs=[vm] * len(operands),
+        in_specs=[vm] * len(operands) + [pl.BlockSpec(memory_space=pl.ANY)] * len(after),
         out_specs=[vm] * len(out_shape),
-        compiler_params=pltpu.CompilerParams(vmem_limit_bytes=32 * MIB),
+        compiler_params=pltpu.CompilerParams(vmem_limit_bytes=24 * MIB),
         cost_estimate=cost,
         name=name,
-    )(*operands)
+    )(*operands, *after)
 
 
 def halves(n, deep, wide, small):
@@ -546,9 +637,8 @@
     deep = width // count_dev
     w_flat = w_in.reshape(width, 2 * ch)
     consts = tables()
-    shared = (seg_lengths, frames, grad_out, w_flat, w_out, conv_kernel, conv_bias.reshape(1, ch), consts)
-    half = rows // 2
-    quarter = half // 2
+    shared = (seg_lengths, frames, grad_out, w_flat, w_out, conv_kernel, conv_bias, consts)
+    quarter = (rows - ROWS0) // 2
 
     def turn(d):
         return lambda m: (m + d) % 4
@@ -560,8 +650,8 @@
         return far(near(m))
 
     gp0, act0, sum0, keep0, near0, far0, back0 = chunk_call(
-        0, half,
-        [(0, half, [turn(d)], F32 if d == 0 else BF16) for d in range(4)],
+        0, ROWS0,
+        [(0, ROWS0, [turn(d)], F32 if d == 0 else BF16) for d in range(4)],
         None, *shared,
     )
 
@@ -577,7 +667,7 @@
             lax.ppermute(far0, "mp", ring(2)),
             lax.ppermute(back0, "mp", ring(3)),
             *chunk_call(
-                half, half,
+                ROWS0, rows - ROWS0,
                 [
                     (0, quarter, [near, other], BF16),
                     (quarter, quarter, [far, other], BF16),
@@ -595,72 +685,70 @@
     cross = [(i, 3 - i) for i in range(4)]
     first_a = lax.ppermute(send_a, "mp", pair)
     first_b = lax.ppermute(send_b, "mp", cross)
-    def first_stage(frames, grad_out, gp0, gp1, act0, act1, small, send_a, send_b):
+    wide = 3 * ch
+
+    def weight_stage(frames, grad_out, gp0, gp1, act0, act1, small, keep0, near0, far0, back0):
+        small_got = move(small)
+        keep, send = weight_call(deep, frames, grad_out, gp0, gp1, act0, act1)
+        got = move(send)
+        (held0,) = sum_call(
+            zero_sum_kernel, "zero_sum", TINY, [jax.ShapeDtypeStruct(keep0.shape, BF16)],
+            keep0, near0, far0, back0, after=(keep,),
+        )
+        sums = sum_call(
+            core_sum_kernel, "core_sum", TINY, halves(8, deep, wide, small), keep, got, small, small_got
+        )
+        return held0, *sums
+
+    def first_stage(send_a, send_b, *operands):
         first_a = lax.ppermute(send_a, "mp", pair)
         first_b = lax.ppermute(send_b, "mp", cross)
-        small_got = move(small)
-        return first_a, first_b, small_got, *weight_call(deep, frames, grad_out, gp0, gp1, act0, act1)
-
-    def second_stage(send_a, send_b, send_x, send_y):
-        return (
-            lax.ppermute(send_a, "mp", cross),
-            lax.ppermute(send_b, "mp", pair),
-            move(send_x, fx=near),
-            move(send_y, fy=near),
-        )
-
-    def third_stage(lengths, owners, held0, part, last_a, last_b, send_x, send_y):
-        return (
-            move(send_x, fy=near),
-            move(send_y, fx=near),
-            pick_call(lengths, owners, rows, held0, part, last_a, last_b),
-        )
-
-    first_a, first_b, small_got, keep, send = together(
-        live, first_stage, frames, grad_out, gp0, gp1, act0, act1, small, send_a, send_b
-    )
-    got = move(send)
-    held0, part, send_a, send_b = sum_call(
-        fold_kernel, "fold", LONG,
-        [
-            jax.ShapeDtypeStruct((half, ch), BF16),
-            jax.ShapeDtypeStruct((half, ch), F32),
-            jax.ShapeDtypeStruct((quarter, ch), BF16),
-            jax.ShapeDtypeStruct((quarter, ch), BF16),
-        ],
-        keep0, near0, far0, back0, keep_a, keep_b, first_a, first_b,
-    )
+        return first_a, first_b, *together(live, weight_stage, *operands)
+
+    def last_stage(send_a, send_b):
+        return lax.ppermute(send_a, "mp", cross), lax.ppermute(send_b, "mp", pair)
+
+    def second_stage(send_x, send_y, *operands):
+        got_x, got_y = move(send_x, fx=near), move(send_y, fy=near)
+        return got_x, got_y, *together(live, last_stage, *operands)
+
+    def third_stage(send_x, send_y, *operands):
+        got_x, got_y = move(send_x, fy=near), move(send_y, fx=near)
+        return got_x, got_y, pick_call(*operands)
+
+    first_a, first_b, held0, own_x, own_y, send_x, send_y, small = together(
+        live, first_stage, send_a, send_b,
+        frames, grad_out, gp0, gp1, act0, act1, small, keep0, near0, far0, back0,
+    )
+    send_a, send_b = pass_call(keep_a, keep_b, first_a, first_b)
+    got_x, got_y, last_a, last_b = together(live, second_stage, send_x, send_y, send_a, send_b)
     own_x, own_y, send_x, send_y, small = sum_call(
-        core_sum_kernel, "core_sum", TINY, halves(8, deep, 3 * ch, small), keep, got, small, small_got
-    )
-    last_a, last_b, got_x, got_y = together(live, second_stage, send_a, send_b, send_x, send_y)
-    own_x, own_y, send_x, send_y, small = sum_call(
-        half_sum_kernel, "half_sum", TINY, halves(4, deep, 3 * ch, small), own_x, own_y, small, got_x, got_y
+        half_sum_kernel, "half_sum", TINY, halves(4, deep, wide, small), own_x, own_y, small, got_x, got_y
     )
     got_x, got_y, outgoing = together(
-        live, third_stage, seg_lengths, seg_owner, held0, part, last_a, last_b, send_x, send_y
+        live, third_stage, send_x, send_y,
+        seg_lengths, seg_owner, held0, keep_a, keep_b, first_a, first_b, last_a, last_b,
     )
     received = lax.all_to_all(outgoing, "dp", split_axis=0, concat_axis=0, tiled=True)
     dx_frames = order_call(slot_device, received)
-    wide = 3 * ch
     own, small, *sends = sum_call(
         square_sum_kernel, "square_sum", TINY,
         [jax.ShapeDtypeStruct((deep, wide), F32), jax.ShapeDtypeStruct(small.shape, F32)]
         + [jax.ShapeDtypeStruct((deep, wide + 2 * ch), BF16)] * 3,
         own_x, own_y, small, got_x, got_y,
     )
-    sums, small_sum = sum_call(
+    grad_w_in, grad_w_out, grad_kernel, grad_bias = sum_call(
         lambda *refs: last_sum_kernel(scale, *refs), "last_sum", TINY,
-        [jax.ShapeDtypeStruct((deep, wide), F32), jax.ShapeDtypeStruct(small.shape, F32)],
-        own, small, move(sends[0], fx=far), move(sends[1], fy=far), move(sends[2], fx=far, fy=far),
-    )
-    return (
-        dx_frames,
-        sums[:, : 2 * ch].reshape(deep, 2, ch),
-        sums[:, 2 * ch :].T,
-        small_sum[:TAPS],
-        small_sum[TAPS],
-    )
+        [
+            jax.ShapeDtypeStruct((deep, 2, ch), F32),
+            jax.ShapeDtypeStruct((deep, ch), F32),
+            jax.ShapeDtypeStruct((TAPS, ch), F32),
+            jax.ShapeDtypeStruct((ch,), F32),
+        ],
+        own, small, move(sends[2], fx=far, fy=far), move(sends[0], fx=far), move(sends[1], fy=far),
+        after=(dx_frames,),
+    )
+    return dx_frames, grad_w_in, grad_w_out.T, grad_kernel, grad_bias
 
 
 def solution(mesh):

time: 154 us -> 137 us (0.89)
  waiting for transfers between devices: 44.5 us -> 33.7 us
  Pallas kernels: 67.4 us -> 64.2 us
  local copies, waits for them, and re-layouts: 8.37 us -> 5.82 us
    ppermute x9, waiting for transfers between devices: 29.6 us -> 6.09 us  [move(): lax.ppermute(array, 'dp', [(i, to(i)) for i in range(lax.axis_size('dp'))])]
    all_to_all x1, waiting for transfers between devices: 0.01 us -> 18.2 us  [on_device(): lax.all_to_all(outgoing, 'dp', split_axis=0, concat_axis=0, tiled=True)]
    pallas_call x2, Pallas kernels: 42.4 us -> 36.1 us  [chunk_call(): pl.pallas_call(body, out_shape=out_shape, in_specs=specs, out_specs=[vm]...]
    pallas_call x2 -> x3, Pallas kernels: 15.1 us -> 18.1 us  [the longest x1 11.9 us: weight_call(): pl.pallas_call(lambda *refs: weight_kernel(deep, *refs), out_shape=(jax.S...]
    ppermute x1, waiting for transfers between devices: 2.45 us -> 0.01 us  [first_stage(): first_a = lax.ppermute(send_a, 'mp', pair)]
    slice x4 -> x0, local copies, waits for them, and re-layouts: 2.24 us -> none  [the longest x1 1.3 us: on_device(): small_sum[TAPS]]
    ppermute x1, waiting for transfers between devices: 2.09 us -> 0.01 us  [zeroth_stage(): lax.ppermute(far0, 'mp', ring(2))]
    ppermute x1, waiting for transfers between devices: 2.06 us -> 0.01 us  [first_stage(): first_b = lax.ppermute(send_b, 'mp', cross)]
  transfers between devices with their start and end apart: 17 -> 17, of which waited for: 11 -> 9; matrix products, arithmetic and copies ran while one was open for 2% -> 0% of each run, Pallas kernels for 28% -> 33%
where the time goes in v4:
time: 137 us; the launch traced here: 135 us
  Pallas kernels  64.2 us (47%)
  waiting for transfers between devices  33.7 us (25%)
  starting transfers between devices  30 us (22%)
  local copies, waits for them, and re-layouts  5.82 us (4%)
  between operations  1.52 us (1%)
    pallas_call x2, Pallas kernels, chunk_call(): pl.pallas_call(body, out_shape=out_shape, in_specs=specs, out_specs=[vm]...  36.1 us
    all_to_all x1, waiting for transfers between devices, on_device(): lax.all_to_all(outgoing, 'dp', split_axis=0, concat_axis=0, tiled=True)  18.2 us
    ppermute x9, starting transfers between devices, move(): lax.ppermute(array, 'dp', [(i, to(i)) for i in range(lax.axis_size('dp'))])  13.3 us
    pallas_call x1, Pallas kernels, weight_call(): pl.pallas_call(lambda *refs: weight_kernel(deep, *refs), out_shape=(jax.S...  11.9 us
    ppermute x2, waiting for transfers between devices, last_stage(): return (lax.ppermute(send_a, 'mp', cross), lax.ppermute(send_b, 'mp', pair))  9.36 us
    pallas_call x5, Pallas kernels, sum_call(): pl.pallas_call(kernel, out_shape=out_shape, in_specs=[vm] * len(operands)...  7.99 us
    all_to_all x1, starting transfers between devices, on_device(): lax.all_to_all(outgoing, 'dp', split_axis=0, concat_axis=0, tiled=True)  7.04 us
    ppermute x9, waiting for transfers between devices, move(): lax.ppermute(array, 'dp', [(i, to(i)) for i in range(lax.axis_size('dp'))])  6.09 us
  transfers between devices with their start and end apart: 17, of which 9 were waited for; matrix products, arithmetic and copies ran while one was open for 0% of the time, Pallas kernels for 33%

profile of v4, /device:TPU:0, one launch (start us, length us, event | category | flops | bytes accessed | tf_op | source)
XLA Modules:
  0.0 135.5 jit_solution(18435535868845410406)
XLA Ops:
  1.3 2.3 %copy.19 = bf16[192,8,2,384]{3,1,2,0:T(8,128)(2,1)S(1)} copy(bf16[192,8,2,384]{3,2,1,0:T(2,128)(2,1)} %bitcast.5) | data formatting | bytes 4718592
  3.6 0.7 copy-done.7
  4.4 15.5 %chunk0.1 = (bf16[736,768]{1,0:T(8,128)(2,1)S(1)}, bf16[736,384]{1,0:T(8,128)(2,1)S(1)}, f32[104,384]{1,0:T(8,128)S(1)}, f32[640,384]{1,0:T(8,128)}, bf16[640,38...) custom-call(s32[1,32]{1,0:T(1,128)S(1)} %copy-done.5, ...), custom_call_target="tpu_custom_call" | custom-call | flops 20000000000 | bytes 20000000 | tf_op jit(solution)/shard_map/chunk0/pallas_call | solution.py:298
  20.0 0.9 copy-done.15
  20.9 0.2 copy-done.16
  21.1 27.2 %conditional.6 = (bf16[640,384]{1,0:T(8,128)(2,1)}, bf16[640,384]{1,0:T(8,128)(2,1)}, bf16[640,384]{1,0:T(8,128)(2,1)}, bf16[896,768]{1,0:T(8,128)(2,1)}, bf16[8...) conditional(s32[]{:T(128)} %convert_element_type.12, () %tuple.58, ...), branch_computations={%region_0.0_spmd, %region_1.0_spmd} | conditional | flops 20000000000 | bytes 25898440 | solution.py:627
  21.1 2.0 %collective-permute-start = (bf16[640,384]{1,0:T(8,128)(2,1)S(1)}, bf16[640,384]{1,0:T(8,128)(2,1)}, u32[]{:S(2)}, u32[]{:S(2)}) collective-permute-start(bf16[640,384]{1,0:T(8,128)(2,1)S(1)} %get-tuple-element.120), channel_id=1, source_target_pairs={{0,1},{1,2},{2,3},{3,0},{4,5},{5,6},{6,7},{7,4},{8,9},{9,10},{10,1... | collective-permute-start | bytes 1474568 | tf_op jit(solution)/shard_map/cond/branch_1_fun/ppermute | solution.py:666
  23.1 3.6 %collective-permute-start.1 = (bf16[640,384]{1,0:T(8,128)(2,1)S(1)}, bf16[640,384]{1,0:T(8,128)(2,1)}, u32[]{:S(2)}, u32[]{:S(2)}) collective-permute-start(bf16[640,384]{1,0:T(8,128)(2,1)S(1)} %get-tuple-element.121), channel_id=1, source_target_pairs={{0,2},{1,3},{2,0},{3,1},{4,6},{5,7},{6,4},{7,5},{8,10},{9,11},{10,... | collective-permute-start | bytes 1474568 | tf_op jit(solution)/shard_map/cond/branch_1_fun/ppermute | solution.py:667
  26.7 1.0 collective-permute-start.2
  27.7 20.6 %chunk640.1 = (bf16[896,768]{1,0:T(8,128)(2,1)}, bf16[896,384]{1,0:T(8,128)(2,1)}, f32[32,384]{1,0:T(8,128)S(1)}, bf16[448,768]{1,0:T(8,128)(2,1)}, bf16[448,768...) custom-call(s32[1,32]{1,0:T(1,128)S(1)} %get-tuple-element.123.refs_0_, ...), custom_call_target="tpu_custom_call" | custom-call | flops 20000000000 | bytes 20000000 | tf_op jit(solution)/shard_map/cond/branch_1_fun/chunk640/pallas_call | solution.py:298
  48.3 19.1 %conditional.7 = (bf16[448,768]{1,0:T(8,128)(2,1)}, bf16[448,768]{1,0:T(8,128)(2,1)}, bf16[640,384]{1,0:T(8,128)(2,1)}, f32[8,48,640]{2,1,0:T(8,128)}, f32[8,48,...) conditional(s32[]{:T(128)} %convert_element_type.12, () %tuple.57, ...), branch_computations={%region_2.0_spmd, %region_3.0_spmd} | conditional | flops 11002001408 | bytes 36912072 | solution.py:627
  48.4 1.3 collective-permute-start.5
  49.6 0.0 collective-permute-start.6
  49.7 17.5 %conditional = (bf16[640,384]{1,0:T(8,128)(2,1)}, f32[8,48,640]{2,1,0:T(8,128)}, f32[8,48,512]{2,1,0:T(8,128)}, bf16[8,48,640]{2,1,0:T(8,128)(2,1)}, bf16[10,48,512]{2,1,0:T(8,128)(2,1)}, /*index=5*/f32[32,384]{1,0:T(8,128)}) conditional(s32[]{:T(128)} %convert_element_type.0, () %tuple.35, (bf16[1536,1536]{1,0:T(8,128)(2,1)}, ...), branch_computations={%region_4.0_spmd, %region_5.0_spmd} | conditional | flops 11002001408 | bytes 31406812 | solution.py:627
  49.7 11.9 %weight.1 = (f32[16,48,1152]{2,1,0:T(8,128)S(1)}, bf16[16,48,1152]{2,1,0:T(8,128)(2,1)S(1)}) custom-call(bf16[1536,1536]{1,0:T(8,128)(2,1)} %get-tuple-element.148.refs_0_, bf16[1536,1536]{1,0:T(8,128)(2,1)} %get-tuple-element.149.refs_1_, bf16[736,768]{1,0:T(8,128)(2,1)} %get-tuple-element.150.refs_2_, bf16[896,768]{1,0:T(8,128)(2,1)} %get-tuple-element.151.refs_3_, ...), custom_call_target="tpu_custom_call" | custom-call | flops 11000000512 | bytes 20000000 | tf_op jit(solution)/shard_map/cond/branch_1_fun/cond/branch_1_fun/weight/pallas_call | solution.py:474
  61.6 0.1 collective-permute-start.3
  61.7 0.5 collective-permute-start.4
  62.2 2.3 %zero_sum.1 = bf16[640,384]{1,0:T(8,128)(2,1)} custom-call(f32[640,384]{1,0:T(8,128)S(1)} %copy-done.4, bf16[640,384]{1,0:T(8,128)(2,1)} %get-tuple-element.145.near0, bf16[640,384]{1,0:T(8,128)(2,1)} %get-tuple-element.146.far0, bf16[640,384]{1,0:T(8,128)(2,1)} %get-tuple-element.147.back0, f32[16,48,1152]{2,1,0:T(8,128)S(1)} %get-tuple-element.154.after.keep), custom_call_target="tpu_custom_call" | custom-call | flops 1000000 | bytes 100000 | tf_op jit(solution)/shard_map/cond/branch_1_fun/cond/branch_1_fun/zero_sum/pallas_call | solution.py:590
  64.5 0.9 collective-permute-done.4.small_got
  65.5 1.7 %core_sum.1 = (f32[8,48,640]{2,1,0:T(8,128)}, f32[8,48,512]{2,1,0:T(8,128)}, bf16[8,48,640]{2,1,0:T(8,128)(2,1)}, bf16[10,48,512]{2,1,0:T(8,128)(2,1)}, f32[32,384]{1,0:T(8,128)}) custom-call(f32[16,48,1152]{2,1,0:T(8,128)S(1)} %get-tuple-element.154.after.keep, bf16[16,48,1152]{2,1,0:T(8,128)(2,1)S(1)} %collective-permute-done.3.got, ...), custom_call_target="tpu_custom_call" | custom-call | flops 1000000 | bytes 100000 | tf_op jit(solution)/shard_map/cond/branch_1_fun/cond/branch_1_fun/core_sum/pallas_call | solution.py:590
  67.4 1.3 pass.1
  68.7 16.3 %conditional.8 = (bf16[8,48,640]{2,1,0:T(8,128)(2,1)}, bf16[10,48,512]{2,1,0:T(8,128)(2,1)}, bf16[448,384]{1,0:T(8,128)(2,1)}, bf16[448,384]{1,0:T(8,128)(2,1)}) conditional(s32[]{:T(128)} %convert_element_type.12, () %tuple.61, (bf16[8,48,640]{2,1,0:T(8,128)(2,1)}, bf16[10,48,512]{2,1,0:T(8,128)(2,1)}, pred[]{:T(512)}, ...), branch_computations={%region_6.0_spmd, %region_7.0_spmd} | conditional | flops 1 | bytes 6684901 | solution.py:627
  68.7 3.0 %collective-permute-start.9 = (bf16[8,48,640]{2,1,0:T(8,128)(2,1)}, bf16[8,48,640]{2,1,0:T(8,128)(2,1)}, u32[]{:S(2)}, u32[]{:S(2)}) collective-permute-start(bf16[8,48,640]{2,1,0:T(8,128)(2,1)} %get-tuple-element.184), channel_id=1, source_target_pairs={{0,32},{4,36},{8,40},{12,44},{16,48},{20,52},{24,56},{28,60},{32,0... | collective-permute-start | bytes 1474568 | tf_op jit(solution)/shard_map/cond/branch_1_fun/ppermute | solution.py:618
  71.7 1.6 %collective-permute-start.10 = (bf16[10,48,512]{2,1,0:T(8,128)(2,1)}, bf16[10,48,512]{2,1,0:T(8,128)(2,1)}, u32[]{:S(2)}, u32[]{:S(2)}) collective-permute-start(bf16[10,48,512]{2,1,0:T(8,128)(2,1)} %get-tuple-element.185), channel_id=1, source_target_pairs={{0,8},{4,12},{8,0},{12,4},{16,24},{20,28},{24,16},{28,20},{32,40},... | collective-permute-start | bytes 1474568 | tf_op jit(solution)/shard_map/cond/branch_1_fun/ppermute | solution.py:618
  73.3 11.1 %conditional.1 = (bf16[448,384]{1,0:T(8,128)(2,1)}, bf16[448,384]{1,0:T(8,128)(2,1)}) conditional(s32[]{:T(128)} %convert_element_type.1, () %tuple.41, (bf16[448,384]{1,0:T(8,128)(2,1)S(1)}, bf16[448,384]{1,0:T(8,128)(2,1)S(1)}) %tuple.42), branch_computations={%region_8.0_spmd, %region_9.0_spmd} | conditional | bytes 2752608 | solution.py:627
  73.3 1.8 %collective-permute-start.7 = (bf16[448,384]{1,0:T(8,128)(2,1)S(1)}, bf16[448,384]{1,0:T(8,128)(2,1)}, u32[]{:S(2)}, u32[]{:S(2)}) collective-permute-start(bf16[448,384]{1,0:T(8,128)(2,1)S(1)} %get-tuple-element.182), channel_id=1, source_target_pairs={{0,3},{1,2},{2,1},{3,0},{4,7},{5,6},{6,5},{7,4},{8,11},{9,10},{10,... | collective-permute-start | bytes 1032200 | tf_op jit(solution)/shard_map/cond/branch_1_fun/cond/branch_1_fun/ppermute | solution.py:709
  75.1 9.1 %collective-permute-done.7 = bf16[448,384]{1,0:T(8,128)(2,1)} collective-permute-done((bf16[448,384]{1,0:T(8,128)(2,1)S(1)}, bf16[448,384]{1,0:T(8,128)(2,1)}, u32[]{:S(2)}, u32[]{:S(2)}) %collective-permute-start.7) | collective-permute-done | bytes 344096 | tf_op jit(solution)/shard_map/cond/branch_1_fun/cond/branch_1_fun/ppermute | solution.py:709
  84.1 0.3 collective-permute-done.8
  84.4 0.6 collective-permute-done.10
  85.0 2.0 %half_sum.1 = (f32[4,48,640]{2,1,0:T(8,128)S(1)}, f32[4,48,512]{2,1,0:T(8,128)S(1)}, bf16[4,48,640]{2,1,0:T(8,128)(2,1)S(1)}, bf16[6,48,512]{2,1,0:T(8,128)(2,1)S(1)}, f32[32,384]{1,0:T(8,128)S(1)}) custom-call(f32[8,48,640]{2,1,0:T(8,128)} %get-tuple-element.270.own_x, f32[8,48,512]{2,1,0:T(8,128)} %get-tuple-element.271.own_y, ...), custom_call_target="tpu_custom_call" | custom-call | flops 1000000 | bytes 100000 | tf_op jit(solution)/shard_map/half_sum/pallas_call | solution.py:590
  87.0 0.2 copy-done.3
  87.2 8.0 %conditional.9 = (bf16[4,48,640]{2,1,0:T(8,128)(2,1)}, bf16[6,48,512]{2,1,0:T(8,128)(2,1)}, bf16[32,72,384]{2,1,0:T(8,128)(2,1)}) conditional(s32[]{:T(128)} %convert_element_type.12, () %tuple.56, (bf16[4,48,640]{2,1,0:T(8,128)(2,1)S(1)}, bf16[6,48,512]{2,1,0:T(8,128)(2,1)S(1)}, s32[1,32]{1,0:T(1,128)S(1)}, s32[1,32]{1,0:T(1,128)S(1)}, ...), branch_computations={%region_10.0_spmd, %region_11.0_spmd} | conditional | flops 1000000 | bytes 2310174 | solution.py:627
  87.2 0.4 collective-permute-start.12
  87.6 1.7 %collective-permute-start.11 = (bf16[4,48,640]{2,1,0:T(8,128)(2,1)S(1)}, bf16[4,48,640]{2,1,0:T(8,128)(2,1)}, u32[]{:S(2)}, u32[]{:S(2)}) collective-permute-start(bf16[4,48,640]{2,1,0:T(8,128)(2,1)S(1)} %get-tuple-element.191), channel_id=1, source_target_pairs={{0,8},{4,12},{8,0},{12,4},{16,24},{20,28},{24,16},{28,20},{32,40},... | collective-permute-start | bytes 737288 | tf_op jit(solution)/shard_map/cond/branch_1_fun/ppermute | solution.py:618
  89.3 4.9 %pick.1 = bf16[32,72,384]{2,1,0:T(8,128)(2,1)} custom-call(s32[1,32]{1,0:T(1,128)S(1)} %get-tuple-element.193.len_ref, s32[1,32]{1,0:T(1,128)S(1)} %get-tuple-element.304.owner_ref, bf16[640,384]{1,0:T(8,128)(2,1)} %get-tuple-element.195.held0, f32[448,768]{1,0:T(8,128)S(1)} %get-tuple-element.196.keep_a, f32[448,768]{1,0:T(8,128)S(1)} %get-tuple-element.197.keep_b, ...), custom_call_target="tpu_custom_call" | custom-call | flops 1000000 | bytes 100000 | tf_op jit(solution)/shard_map/cond/branch_1_fun/pick/pallas_call | solution.py:386
  94.2 0.4 collective-permute-done.11
  94.6 0.6 collective-permute-done.12
  95.2 7.0 %all-to-all-start = ((bf16[32,72,384]{2,1,0:T(8,128)(2,1)}), bf16[32,72,384]{2,1,0:T(8,128)(2,1)S(1)}, u32[]{:S(2)}, u32[]{:S(2)}) async-start(bf16[32,72,384]{2,1,0:T(8,128)(2,1)} %get-tuple-element.288), calls=%async_computation | async-start | bytes 3538944 | tf_op jit(solution)/shard_map/all_to_all | solution.py:732
  102.2 1.2 square_sum.1
  103.4 5.3 %collective-permute-start.13 = (bf16[48,1920]{1,0:T(8,128)(2,1)S(1)}, bf16[48,1920]{1,0:T(8,128)(2,1)S(1)}, u32[]{:S(2)}, u32[]{:S(2)}) collective-permute-start(bf16[48,1920]{1,0:T(8,128)(2,1)S(1)} %get-tuple-element.296), channel_id=1, source_target_pairs={{0,120},{4,124},{8,112},{12,116},{16,104},{20,108},{24,96},{28,100... | collective-permute-start | bytes 552968 | tf_op jit(solution)/shard_map/ppermute | solution.py:618
  108.7 0.5 collective-permute-start.14
  109.2 0.2 collective-permute-start.15
  109.4 18.2 %all-to-all-done.src = bf16[32,72,384]{2,1,0:T(8,128)(2,1)S(1)} async-done(((bf16[32,72,384]{2,1,0:T(8,128)(2,1)}), bf16[32,72,384]{2,1,0:T(8,128)(2,1)S(1)}, u32[]{:S(2)}, u32[]{:S(2)}) %all-to-all-start) | async-done | bytes 1769504 | tf_op jit(solution)/shard_map/all_to_all | solution.py:732
  127.6 2.0 %order.1.refs_5_ = bf16[32,72,384]{2,1,0:T(8,128)(2,1)} custom-call(s32[1,32]{1,0:T(1,128)S(1)} %copy-done.1, bf16[32,72,384]{2,1,0:T(8,128)(2,1)S(1)} %all-to-all-done.src), custom_call_target="tpu_custom_call" | custom-call | flops 1000000 | bytes 100000 | tf_op jit(solution)/shard_map/order/pallas_call | solution.py:410
  129.7 2.1 %collective-permute-done.13.refs_2_ = bf16[48,1920]{1,0:T(8,128)(2,1)S(1)} collective-permute-done((bf16[48,1920]{1,0:T(8,128)(2,1)S(1)}, bf16[48,1920]{1,0:T(8,128)(2,1)S(1)}, u32[]{:S(2)}, u32[]{:S(2)}) %collective-permute-start.13) | collective-permute-done | bytes 184352 | tf_op jit(solution)/shard_map/ppermute | solution.py:618
  131.8 1.5 %collective-permute-done.14.refs_3_ = bf16[48,1920]{1,0:T(8,128)(2,1)S(1)} collective-permute-done((bf16[48,1920]{1,0:T(8,128)(2,1)S(1)}, bf16[48,1920]{1,0:T(8,128)(2,1)S(1)}, u32[]{:S(2)}, u32[]{:S(2)}) %collective-permute-start.14) | collective-permute-done | bytes 184352 | tf_op jit(solution)/shard_map/ppermute | solution.py:618
  133.2 1.5 %copy-done = bf16[32,72,384]{2,1,0:T(8,128)(2,1)S(1)} copy-done((bf16[32,72,384]{2,1,0:T(8,128)(2,1)S(1)}, bf16[32,72,384]{2,1,0:T(8,128)(2,1)}, u32[]{:S(2)}) %copy-start) | copy-done | bytes 1769496
  134.7 0.8 last_sum.1
  (43 shorter events, 0.1 us)
Async XLA Ops:
  1.3 2.3 %copy-start.5 = (s32[1,32]{1,0:T(1,128)S(1)}, s32[1,32]{1,0:T(1,128)}, u32[]{:S(2)}) copy-start(s32[1,32]{1,0:T(1,128)} %refs_0_.1) | copy-start | bytes 388
  1.3 3.1 %copy-start.7 = (bf16[1536,1536]{1,0:T(8,128)(2,1)S(1)}, bf16[1536,1536]{1,0:T(8,128)(2,1)}, u32[]{:S(2)}) copy-start(bf16[1536,1536]{1,0:T(8,128)(2,1)} %refs_1_.1) | copy-start | bytes 14155780
  1.3 18.6 %slice-start = ((s8[4718592]{0:T(1024)(128)(4,1)}), s8[4194304]{0:T(1024)(128)(4,1)S(1)}, s32[]{:S(2)}) async-start(s8[4718592]{0:T(1024)(128)(4,1)} %bitcast.9), calls=%async_computation.1 | async-start | bytes 8388608
  4.3 15.6 %slice-start.1 = ((s8[4718592]{0:T(1024)(128)(4,1)}), s8[524288]{0:T(1024)(128)(4,1)S(1)}, s32[]{:S(2)}) async-start(s8[4718592]{0:T(1024)(128)(4,1)} %bitcast.9), calls=%async_computation.2 | async-start | bytes 1048576
  4.3 15.6 %copy-start.8 = (bf16[384,1536]{1,0:T(8,128)(2,1)S(1)}, bf16[384,1536]{1,0:T(8,128)(2,1)}, u32[]{:S(2)}) copy-start(bf16[384,1536]{1,0:T(8,128)(2,1)} %refs_4_.1) | copy-start | bytes 3538948
  4.3 15.6 %copy-start.9 = (f32[31,384]{1,0:T(8,128)S(1)}, f32[31,384]{1,0:T(8,128)}, u32[]{:S(2)}) copy-start(f32[31,384]{1,0:T(8,128)} %refs_5_.1) | copy-start | bytes 142852
  4.4 15.6 %copy-start.10 = (f32[384]{0:T(512)S(1)}, f32[384]{0:T(512)}, u32[]{:S(2)}) copy-start(f32[384]{0:T(512)} %refs_6_.1) | copy-start | bytes 4612
  4.4 15.6 %copy-start.11 = (f32[96,31]{1,0:T(8,128)S(1)}, f32[96,31]{1,0:T(8,128)}, u32[]{:S(2)}) copy-start(f32[96,31]{1,0:T(8,128)} %constant.21.clone.refs_9_) | copy-start | bytes 35716
  4.4 15.6 %copy-start.12 = (bf16[88,240]{1,0:T(8,128)(2,1)S(1)}, bf16[88,240]{1,0:T(8,128)(2,1)}, u32[]{:S(2)}) copy-start(bf16[88,240]{1,0:T(8,128)(2,1)} %constant.17.clone.refs_7_) | copy-start | bytes 126724
  4.4 15.6 %copy-start.13 = (bf16[80,256]{1,0:T(8,128)(2,1)S(1)}, bf16[80,256]{1,0:T(8,128)(2,1)}, u32[]{:S(2)}) copy-start(bf16[80,256]{1,0:T(8,128)(2,1)} %constant.19.clone.refs_8_) | copy-start | bytes 122884
  4.4 15.6 %copy-start.14 = (f32[31,96]{1,0:T(8,128)S(1)}, f32[31,96]{1,0:T(8,128)}, u32[]{:S(2)}) copy-start(f32[31,96]{1,0:T(8,128)} %constant.31.clone.refs_10_) | copy-start | bytes 35716
  19.9 1.0 copy-start.15
  19.9 1.2 copy-start.16
  21.1 27.1 %collective-permute-start = (bf16[640,384]{1,0:T(8,128)(2,1)S(1)}, bf16[640,384]{1,0:T(8,128)(2,1)}, u32[]{:S(2)}, u32[]{:S(2)}) collective-permute-start(bf16[640,384]{1,0:T(8,128)(2,1)S(1)} %get-tuple-element.120), channel_id=1, source_target_pairs={{0,1},{1,2},{2,3},{3,0},{4,5},{5,6},{6,7},{7,4},{8,9},{9,10},{10,1... | collective-permute-start | bytes 1474568 | tf_op jit(solution)/shard_map/cond/branch_1_fun/ppermute | solution.py:666
  23.1 25.2 %collective-permute-start.1 = (bf16[640,384]{1,0:T(8,128)(2,1)S(1)}, bf16[640,384]{1,0:T(8,128)(2,1)}, u32[]{:S(2)}, u32[]{:S(2)}) collective-permute-start(bf16[640,384]{1,0:T(8,128)(2,1)S(1)} %get-tuple-element.121), channel_id=1, source_target_pairs={{0,2},{1,3},{2,0},{3,1},{4,6},{5,7},{6,4},{7,5},{8,10},{9,11},{10,... | collective-permute-start | bytes 1474568 | tf_op jit(solution)/shard_map/cond/branch_1_fun/ppermute | solution.py:667
  26.7 21.6 %collective-permute-start.2 = (bf16[640,384]{1,0:T(8,128)(2,1)S(1)}, bf16[640,384]{1,0:T(8,128)(2,1)}, u32[]{:S(2)}, u32[]{:S(2)}) collective-permute-start(bf16[640,384]{1,0:T(8,128)(2,1)S(1)} %get-tuple-element.122), channel_id=1, source_target_pairs={{0,3},{1,0},{2,1},{3,2},{4,7},{5,4},{6,5},{7,6},{8,11},{9,8},{10,9... | collective-permute-start | bytes 1474568 | tf_op jit(solution)/shard_map/cond/branch_1_fun/ppermute | solution.py:668
  48.3 19.1 %copy-start.2 = (f32[448,768]{1,0:T(8,128)}, f32[448,768]{1,0:T(8,128)S(1)}, u32[]{:S(2)}) copy-start(f32[448,768]{1,0:T(8,128)S(1)} %get-tuple-element.275.keep_a) | copy-start | bytes 4128772
  48.4 18.8 %collective-permute-start.5 = (bf16[448,768]{1,0:T(8,128)(2,1)}, bf16[448,768]{1,0:T(8,128)(2,1)}, u32[]{:S(2)}, u32[]{:S(2)}) collective-permute-start(bf16[448,768]{1,0:T(8,128)(2,1)} %get-tuple-element.162), channel_id=1, source_target_pairs={{0,1},{1,0},{2,3},{3,2},{4,5},{5,4},{6,7},{7,6},{8,9},{9,8},{10,11... | collective-permute-start | bytes 2064392 | tf_op jit(solution)/shard_map/cond/branch_1_fun/ppermute | solution.py:704
  49.6 17.5 %collective-permute-start.6 = (bf16[448,768]{1,0:T(8,128)(2,1)S(1)}, bf16[448,768]{1,0:T(8,128)(2,1)}, u32[]{:S(2)}, u32[]{:S(2)}) collective-permute-start(bf16[448,768]{1,0:T(8,128)(2,1)S(1)} %get-tuple-element.163), channel_id=1, source_target_pairs={{0,3},{1,2},{2,1},{3,0},{4,7},{5,6},{6,5},{7,4},{8,11},{9,10},{10,... | collective-permute-start | bytes 2064392 | tf_op jit(solution)/shard_map/cond/branch_1_fun/ppermute | solution.py:705
  49.7 12.5 %copy-start.4 = (f32[640,384]{1,0:T(8,128)S(1)}, f32[640,384]{1,0:T(8,128)}, u32[]{:S(2)}) copy-start(f32[640,384]{1,0:T(8,128)} %get-tuple-element.144.keep0) | copy-start | bytes 2949124 | tf_op jit(solution)/shard_map/cond/branch_1_fun/cond
  61.6 3.8 %collective-permute-start.3 = (bf16[16,48,1152]{2,1,0:T(8,128)(2,1)S(1)}, bf16[16,48,1152]{2,1,0:T(8,128)(2,1)S(1)}, u32[]{:S(2)}, u32[]{:S(2)}) collective-permute-start(bf16[16,48,1152]{2,1,0:T(8,128)(2,1)S(1)} %get-tuple-element.155), channel_id=1, source_target_pairs={{0,4},{4,0},{8,12},{12,8},{16,20},{20,16},{24,28},{28,24},{32,36},... | collective-permute-start | bytes 5308424 | tf_op jit(solution)/shard_map/cond/branch_1_fun/cond/branch_1_fun/ppermute | solution.py:618
  61.7 3.7 %collective-permute-start.4 = (f32[32,384]{1,0:T(8,128)S(1)}, f32[32,384]{1,0:T(8,128)S(1)}, u32[]{:S(2)}, u32[]{:S(2)}) collective-permute-start(f32[32,384]{1,0:T(8,128)S(1)} %get-tuple-element.156.small), channel_id=1, source_target_pairs={{0,4},{4,0},{8,12},{12,8},{16,20},{20,16},{24,28},{28,24},{32,36},... | collective-permute-start | bytes 147464 | tf_op jit(solution)/shard_map/cond/branch_1_fun/cond/branch_1_fun/ppermute | solution.py:618
  68.7 15.7 %collective-permute-start.9 = (bf16[8,48,640]{2,1,0:T(8,128)(2,1)}, bf16[8,48,640]{2,1,0:T(8,128)(2,1)}, u32[]{:S(2)}, u32[]{:S(2)}) collective-permute-start(bf16[8,48,640]{2,1,0:T(8,128)(2,1)} %get-tuple-element.184), channel_id=1, source_target_pairs={{0,32},{4,36},{8,40},{12,44},{16,48},{20,52},{24,56},{28,60},{32,0... | collective-permute-start | bytes 1474568 | tf_op jit(solution)/shard_map/cond/branch_1_fun/ppermute | solution.py:618
  71.7 13.3 %collective-permute-start.10 = (bf16[10,48,512]{2,1,0:T(8,128)(2,1)}, bf16[10,48,512]{2,1,0:T(8,128)(2,1)}, u32[]{:S(2)}, u32[]{:S(2)}) collective-permute-start(bf16[10,48,512]{2,1,0:T(8,128)(2,1)} %get-tuple-element.185), channel_id=1, source_target_pairs={{0,8},{4,12},{8,0},{12,4},{16,24},{20,28},{24,16},{28,20},{32,40},... | collective-permute-start | bytes 1474568 | tf_op jit(solution)/shard_map/cond/branch_1_fun/ppermute | solution.py:618
  73.3 10.9 %collective-permute-start.7 = (bf16[448,384]{1,0:T(8,128)(2,1)S(1)}, bf16[448,384]{1,0:T(8,128)(2,1)}, u32[]{:S(2)}, u32[]{:S(2)}) collective-permute-start(bf16[448,384]{1,0:T(8,128)(2,1)S(1)} %get-tuple-element.182), channel_id=1, source_target_pairs={{0,3},{1,2},{2,1},{3,0},{4,7},{5,6},{6,5},{7,4},{8,11},{9,10},{10,... | collective-permute-start | bytes 1032200 | tf_op jit(solution)/shard_map/cond/branch_1_fun/cond/branch_1_fun/ppermute | solution.py:709
  75.1 9.4 %collective-permute-start.8 = (bf16[448,384]{1,0:T(8,128)(2,1)S(1)}, bf16[448,384]{1,0:T(8,128)(2,1)}, u32[]{:S(2)}, u32[]{:S(2)}) collective-permute-start(bf16[448,384]{1,0:T(8,128)(2,1)S(1)} %get-tuple-element.183), channel_id=1, source_target_pairs={{0,1},{1,0},{2,3},{3,2},{4,5},{5,4},{6,7},{7,6},{8,9},{9,8},{10,11... | collective-permute-start | bytes 1032200 | tf_op jit(solution)/shard_map/cond/branch_1_fun/cond/branch_1_fun/ppermute | solution.py:709
  85.0 2.2 %copy-start.3 = (f32[448,768]{1,0:T(8,128)S(1)}, f32[448,768]{1,0:T(8,128)}, u32[]{:S(2)}) copy-start(f32[448,768]{1,0:T(8,128)} %copy-done.2) | copy-start | bytes 4128772
  85.0 2.2 %copy-start.6 = (s32[1,32]{1,0:T(1,128)S(1)}, s32[1,32]{1,0:T(1,128)}, u32[]{:S(2)}) copy-start(s32[1,32]{1,0:T(1,128)} %param.32) | copy-start | bytes 388
  87.2 8.0 %collective-permute-start.12 = (bf16[6,48,512]{2,1,0:T(8,128)(2,1)S(1)}, bf16[6,48,512]{2,1,0:T(8,128)(2,1)}, u32[]{:S(2)}, u32[]{:S(2)}) collective-permute-start(bf16[6,48,512]{2,1,0:T(8,128)(2,1)S(1)} %get-tuple-element.192), channel_id=1, source_target_pairs={{0,32},{4,36},{8,40},{12,44},{16,48},{20,52},{24,56},{28,60},{32,0... | collective-permute-start | bytes 884744 | tf_op jit(solution)/shard_map/cond/branch_1_fun/ppermute | solution.py:618
  87.6 7.0 %collective-permute-start.11 = (bf16[4,48,640]{2,1,0:T(8,128)(2,1)S(1)}, bf16[4,48,640]{2,1,0:T(8,128)(2,1)}, u32[]{:S(2)}, u32[]{:S(2)}) collective-permute-start(bf16[4,48,640]{2,1,0:T(8,128)(2,1)S(1)} %get-tuple-element.191), channel_id=1, source_target_pairs={{0,8},{4,12},{8,0},{12,4},{16,24},{20,28},{24,16},{28,20},{32,40},... | collective-permute-start | bytes 737288 | tf_op jit(solution)/shard_map/cond/branch_1_fun/ppermute | solution.py:618
  95.2 32.4 %copy-start.1 = (s32[1,32]{1,0:T(1,128)S(1)}, s32[1,32]{1,0:T(1,128)}, u32[]{:S(2)}) copy-start(s32[1,32]{1,0:T(1,128)} %slot_ref.1) | copy-start | bytes 388
  95.2 32.4 %all-to-all-start = ((bf16[32,72,384]{2,1,0:T(8,128)(2,1)}), bf16[32,72,384]{2,1,0:T(8,128)(2,1)S(1)}, u32[]{:S(2)}, u32[]{:S(2)}) async-start(bf16[32,72,384]{2,1,0:T(8,128)(2,1)} %get-tuple-element.288), calls=%async_computation | async-start | bytes 3538944 | tf_op jit(solution)/shard_map/all_to_all | solution.py:732
  103.4 28.4 %collective-permute-start.13 = (bf16[48,1920]{1,0:T(8,128)(2,1)S(1)}, bf16[48,1920]{1,0:T(8,128)(2,1)S(1)}, u32[]{:S(2)}, u32[]{:S(2)}) collective-permute-start(bf16[48,1920]{1,0:T(8,128)(2,1)S(1)} %get-tuple-element.296), channel_id=1, source_target_pairs={{0,120},{4,124},{8,112},{12,116},{16,104},{20,108},{24,96},{28,100... | collective-permute-start | bytes 552968 | tf_op jit(solution)/shard_map/ppermute | solution.py:618
  108.7 24.5 %collective-permute-start.14 = (bf16[48,1920]{1,0:T(8,128)(2,1)S(1)}, bf16[48,1920]{1,0:T(8,128)(2,1)S(1)}, u32[]{:S(2)}, u32[]{:S(2)}) collective-permute-start(bf16[48,1920]{1,0:T(8,128)(2,1)S(1)} %get-tuple-element.297), channel_id=1, source_target_pairs={{0,96},{4,100},{8,104},{12,108},{16,112},{20,116},{24,120},{28,124... | collective-permute-start | bytes 552968 | tf_op jit(solution)/shard_map/ppermute | solution.py:618
  109.2 24.1 %collective-permute-start.15 = (bf16[48,1920]{1,0:T(8,128)(2,1)S(1)}, bf16[48,1920]{1,0:T(8,128)(2,1)S(1)}, u32[]{:S(2)}, u32[]{:S(2)}) collective-permute-start(bf16[48,1920]{1,0:T(8,128)(2,1)S(1)} %get-tuple-element.298), channel_id=1, source_target_pairs={{0,24},{4,28},{8,16},{12,20},{16,8},{20,12},{24,0},{28,4},{32,56},... | collective-permute-start | bytes 552968 | tf_op jit(solution)/shard_map/ppermute | solution.py:618
  133.2 1.5 %copy-start = (bf16[32,72,384]{2,1,0:T(8,128)(2,1)S(1)}, bf16[32,72,384]{2,1,0:T(8,128)(2,1)}, u32[]{:S(2)}) copy-start(bf16[32,72,384]{2,1,0:T(8,128)(2,1)} %order.1.refs_5_) | copy-start | bytes 5308420

commit v5 on v4

--- a/solution.py
+++ b/solution.py
@@ -17,9 +17,10 @@
 EDGE = 4
 FREQ = 2 * (MAIN + EDGE)
 MARGIN = 96
-ROWS0 = 640
+ROWS0 = 576
 SEGS = 32
-GROUP = 4
+GROUP = 5
+PICKS = 8
 MIB = 1024 * 1024
 TINY = pl.CostEstimate(flops=10**6, bytes_accessed=10**5, transcendentals=0)
 LONG = pl.CostEstimate(flops=10**6, bytes_accessed=6 * 10**7, transcendentals=0)
@@ -65,9 +66,16 @@
     return base, start - base
 
 
-def pieces(x, rows):
+def pieces(x):
+    high = x.astype(BF16)
+    return jnp.concatenate([high, high, (x - high.astype(F32)).astype(BF16)], 0)
+
+
+def uneven_pieces(x, rows):
     high = x.astype(BF16).astype(F32)
-    return jnp.concatenate([high, high, (x - high)[:rows]], 0).astype(BF16)
+    return jnp.concatenate(
+        [jnp.concatenate([high, high], 0).astype(BF16), (x - high)[:rows].astype(BF16)], 0
+    )
 
 
 def turned(x):
@@ -138,19 +146,21 @@
 
     lax.fori_loop(0, blocks, project, 0)
 
-    row = lax.broadcasted_iota(jnp.int32, (WIN, ch), 0)
-    row8 = row[:8]
+    row = lax.broadcasted_iota(jnp.int32, (WIN, 128), 0)
+    row8 = lax.broadcasted_iota(jnp.int32, (8, ch), 0)
 
     def spectra(src, places):
         parts = []
         for base, off, length in places:
-            x = src[pl.ds(base, WIN), :]
-            parts.append(pieces(jnp.where((row >= off) & (row < off + length), x, 0.0), WIN))
+            keep = (row >= off) & (row < off + length)
+            for lane in range(0, ch, 128):
+                x = src[pl.ds(base, WIN), lane : lane + 128]
+                parts.append(pieces(jnp.where(keep, x, 0.0)))
         both = jnp.dot(fwd_ref[...], jnp.concatenate(parts, 1), preferred_element_type=F32)
         return [both[:, j * ch : (j + 1) * ch] for j in range(len(places))]
 
     def inverses(specs):
-        parts = [pieces(jnp.concatenate(p, 0), 2 * MAIN) for p in specs]
+        parts = [uneven_pieces(jnp.concatenate(p, 0), 2 * MAIN) for p in specs]
         both = jnp.dot(inv_ref[...], jnp.concatenate(parts, 1), preferred_element_type=F32)
         return [both[:, j * ch : (j + 1) * ch] for j in range(len(specs))]
 
@@ -177,15 +187,13 @@
     def forward(state):
         k, start = state
         places, start = group_of(start, k)
-        results = []
         kc, ks, ke, kt = kf[main], kf[sine], kf[edge], kf[FREQ:]
-        for j in range(0, GROUP, 2):
-            specs = []
-            for i, s in enumerate(spectra(gated, places[j : j + 2])):
-                spec[k - k0 + j + i] = s
-                gr, gi, ge = s[main], s[sine], s[edge]
-                specs.append((kc * gr + ks * gi, kc * gi - ks * gr, ke * ge + kt * turned(ge)))
-            results += inverses(specs)
+        specs = []
+        for i, s in enumerate(spectra(gated, places)):
+            spec[k - k0 + i] = s
+            gr, gi, ge = s[main], s[sine], s[edge]
+            specs.append((kc * gr + ks * gi, kc * gi - ks * gr, ke * ge + kt * turned(ge)))
+        results = inverses(specs)
         for (base, off, length), out in zip(places, results):
             put(out, base, off)
         return k + GROUP, start
@@ -207,20 +215,18 @@
     def backward(state):
         k, start = state
         places, start = group_of(start, k)
-        results = []
         kc, ks, ke, kt = kf[main], kf[sine], kf[edge], kf[FREQ:]
         sums = [jnp.zeros((n, ch), F32) for n in (MAIN, MAIN, 8, 8, 8)]
-        for j in range(0, GROUP, 2):
-            specs = []
-            for i, s in enumerate(spectra(gc, places[j : j + 2])):
-                cr, ci, ce = s[main], s[sine], s[edge]
-                g = spec[k - k0 + j + i]
-                gr, gi, ge = g[main], g[sine], g[edge]
-                swapped = turned(ce)
-                specs.append((kc * cr - ks * ci, kc * ci + ks * cr, ke * ce - kt * swapped))
-                terms = (gr * cr + gi * ci, gr * ci - gi * cr, ge * ce, ge * swapped, s[:8])
-                sums = [total + term for total, term in zip(sums, terms)]
-            results += inverses(specs)
+        specs = []
+        for i, s in enumerate(spectra(gc, places)):
+            cr, ci, ce = s[main], s[sine], s[edge]
+            g = spec[k - k0 + i]
+            gr, gi, ge = g[main], g[sine], g[edge]
+            swapped = turned(ce)
+            specs.append((kc * cr - ks * ci, kc * ci + ks * cr, ke * ce - kt * swapped))
+            terms = (gr * cr + gi * ci, gr * ci - gi * cr, ge * ce, ge * swapped, s[:8])
+            sums = [total + term for total, term in zip(sums, terms)]
+        results = inverses(specs)
         at = 0
         for total in sums:
             acc[at : at + total.shape[0], :] += total
@@ -277,7 +283,7 @@
     ch = w_out.shape[0]
     last = first + rows == total
     load = rows if last else rows + MARGIN
-    blocks = next(n for n in range(-(-load // 384), load) if load % (16 * n) == 0)
+    blocks = next(n for n in range(-(-load // 480), load) if load % (16 * n) == 0)
     vm = pl.BlockSpec(memory_space=pltpu.VMEM)
     hbm = pl.BlockSpec(memory_space=pl.ANY)
     sm = pl.BlockSpec(memory_space=pltpu.SMEM)
@@ -364,8 +370,8 @@
     lane = lax.broadcasted_iota(jnp.int32, (MAXLEN, MARGIN), 1)
 
     def pick(i, start):
-        for j in range(GROUP):
-            k = i * GROUP + j
+        for j in range(PICKS):
+            k = i * PICKS + j
             length = len_ref[0, k]
             base, off = aligned(start, 16)
             hot = jnp.where((lane == row + off) & (row < length), 1.0, 0.0).astype(BF16)
@@ -375,7 +381,7 @@
             start = start + length
         return start
 
-    lax.fori_loop(0, SEGS // GROUP, pick, jnp.int32(0))
+    lax.fori_loop(0, SEGS // PICKS, pick, jnp.int32(0))
 
 
 def pick_call(lengths, owners, held0, keep_a, keep_b, first_a, first_b, last_a, last_b):
@@ -396,7 +402,7 @@
     )(lengths, owners, held0, keep_a, keep_b, first_a, first_b, last_a, last_b)
 
 
-def order_kernel(slot_ref, src, dst, sem):
+def order_kernel(slot_ref, src, dst, done_ref, sem):
     def copy(u):
         return pltpu.make_async_copy(src.at[slot_ref[0, u]], dst.at[u], sem.at[u])
 
@@ -404,14 +410,18 @@
         copy(u).start()
     for u in range(SEGS):
         copy(u).wait()
+    done_ref[...] = jnp.zeros_like(done_ref)
 
 
 def order_call(slots, received):
     return pl.pallas_call(
         order_kernel,
-        out_shape=jax.ShapeDtypeStruct(received.shape, received.dtype),
+        out_shape=(
+            jax.ShapeDtypeStruct(received.shape, received.dtype),
+            jax.ShapeDtypeStruct((8, 128), F32),
+        ),
         in_specs=[pl.BlockSpec(memory_space=pltpu.SMEM), pl.BlockSpec(memory_space=pltpu.VMEM)],
-        out_specs=pl.BlockSpec(memory_space=pl.ANY),
+        out_specs=(pl.BlockSpec(memory_space=pl.ANY), pl.BlockSpec(memory_space=pltpu.VMEM)),
         scratch_shapes=[pltpu.SemaphoreType.DMA((SEGS,))],
         compiler_params=pltpu.CompilerParams(vmem_limit_bytes=16 * MIB),
         cost_estimate=TINY,
@@ -730,7 +740,7 @@
         seg_lengths, seg_owner, held0, keep_a, keep_b, first_a, first_b, last_a, last_b,
     )
     received = lax.all_to_all(outgoing, "dp", split_axis=0, concat_axis=0, tiled=True)
-    dx_frames = order_call(slot_device, received)
+    dx_frames, done = order_call(slot_device, received)
     own, small, *sends = sum_call(
         square_sum_kernel, "square_sum", TINY,
         [jax.ShapeDtypeStruct((deep, wide), F32), jax.ShapeDtypeStruct(small.shape, F32)]
@@ -746,7 +756,7 @@
             jax.ShapeDtypeStruct((ch,), F32),
         ],
         own, small, move(sends[2], fx=far, fy=far), move(sends[0], fx=far), move(sends[1], fy=far),
-        after=(dx_frames,),
+        after=(done,),
     )
     return dx_frames, grad_w_in, grad_w_out.T, grad_kernel, grad_bias
 

time: 137 us -> 131 us (0.956)
  Pallas kernels: 64.2 us -> 59.9 us
  local copies, waits for them, and re-layouts: 5.82 us -> 4.29 us
    pallas_call x2, Pallas kernels: 36.1 us -> 31.7 us  [chunk_call(): pl.pallas_call(body, out_shape=out_shape, in_specs=specs, out_specs=[vm]...]
    ppermute x1, starting transfers between devices: 0.04 us -> 1.64 us  [first_stage(): first_b = lax.ppermute(send_b, 'mp', cross)]
    unnamed x37 -> x35, local copies, waits for them, and re-layouts: 5.82 us -> 4.29 us
    ppermute x9, starting transfers between devices: 13.3 us -> 11.8 us  [move(): lax.ppermute(array, 'dp', [(i, to(i)) for i in range(lax.axis_size('dp'))])]
  transfers between devices with their start and end apart: 17 -> 17, of which waited for: 9 -> 9; matrix products, arithmetic and copies ran while one was open for 0% -> 0% of each run, Pallas kernels for 33% -> 32%
where the time goes in v5:
time: 131 us; the launch traced here: 130 us
  Pallas kernels  59.9 us (46%)
  waiting for transfers between devices  34.6 us (26%)
  starting transfers between devices  30 us (23%)
  local copies, waits for them, and re-layouts  4.29 us (3%)
  between operations  1.52 us (1%)
    pallas_call x2, Pallas kernels, chunk_call(): pl.pallas_call(body, out_shape=out_shape, in_specs=specs, out_specs=[vm]...  31.7 us
    all_to_all x1, waiting for transfers between devices, on_device(): lax.all_to_all(outgoing, 'dp', split_axis=0, concat_axis=0, tiled=True)  18.2 us
    pallas_call x1, Pallas kernels, weight_call(): pl.pallas_call(lambda *refs: weight_kernel(deep, *refs), out_shape=(jax.S...  11.9 us
    ppermute x9, starting transfers between devices, move(): lax.ppermute(array, 'dp', [(i, to(i)) for i in range(lax.axis_size('dp'))])  11.8 us
    ppermute x2, waiting for transfers between devices, last_stage(): return (lax.ppermute(send_a, 'mp', cross), lax.ppermute(send_b, 'mp', pair))  9.99 us
    pallas_call x5, Pallas kernels, sum_call(): pl.pallas_call(kernel, out_shape=out_shape, in_specs=[vm] * len(operands)...  7.96 us
    all_to_all x1, starting transfers between devices, on_device(): lax.all_to_all(outgoing, 'dp', split_axis=0, concat_axis=0, tiled=True)  7.18 us
    ppermute x9, waiting for transfers between devices, move(): lax.ppermute(array, 'dp', [(i, to(i)) for i in range(lax.axis_size('dp'))])  6.14 us
  transfers between devices with their start and end apart: 17, of which 9 were waited for; matrix products, arithmetic and copies ran while one was open for 0% of the time, Pallas kernels for 32%

profile of v5, /device:TPU:0, one launch (start us, length us, event | category | flops | bytes accessed | tf_op | source)
XLA Modules:
  0.0 130.4 jit_solution(18390645829261578623)
XLA Ops:
  1.3 2.3 %copy.19 = bf16[192,8,2,384]{3,1,2,0:T(8,128)(2,1)S(1)} copy(bf16[192,8,2,384]{3,2,1,0:T(2,128)(2,1)} %bitcast.5) | data formatting | bytes 4718592
  3.6 0.7 copy-done.6
  4.4 13.5 %chunk0.1 = (bf16[672,768]{1,0:T(8,128)(2,1)S(1)}, bf16[672,384]{1,0:T(8,128)(2,1)S(1)}, f32[104,384]{1,0:T(8,128)S(1)}, f32[576,384]{1,0:T(8,128)}, bf16[576,38...) custom-call(s32[1,32]{1,0:T(1,128)S(1)} %copy-done.4, ...), custom_call_target="tpu_custom_call" | custom-call | flops 20000000000 | bytes 20000000 | tf_op jit(solution)/shard_map/chunk0/pallas_call | solution.py:304
  18.0 0.8 copy-done.14
  18.9 0.2 copy-done.15
  19.0 25.1 %conditional.6 = (bf16[576,384]{1,0:T(8,128)(2,1)}, bf16[576,384]{1,0:T(8,128)(2,1)}, bf16[576,384]{1,0:T(8,128)(2,1)}, bf16[960,768]{1,0:T(8,128)(2,1)}, bf16[9...) conditional(s32[]{:T(128)} %convert_element_type.12, () %tuple.58, ...), branch_computations={%region_0.0_spmd, %region_1.0_spmd} | conditional | flops 20000000000 | bytes 25308616 | solution.py:637
  19.0 2.0 %collective-permute-start = (bf16[576,384]{1,0:T(8,128)(2,1)S(1)}, bf16[576,384]{1,0:T(8,128)(2,1)}, u32[]{:S(2)}, u32[]{:S(2)}) collective-permute-start(bf16[576,384]{1,0:T(8,128)(2,1)S(1)} %get-tuple-element.120), channel_id=1, source_target_pairs={{0,1},{1,2},{2,3},{3,0},{4,5},{5,6},{6,7},{7,4},{8,9},{9,10},{10,1... | collective-permute-start | bytes 1327112 | tf_op jit(solution)/shard_map/cond/branch_1_fun/ppermute | solution.py:676
  21.0 3.6 %collective-permute-start.1 = (bf16[576,384]{1,0:T(8,128)(2,1)S(1)}, bf16[576,384]{1,0:T(8,128)(2,1)}, u32[]{:S(2)}, u32[]{:S(2)}) collective-permute-start(bf16[576,384]{1,0:T(8,128)(2,1)S(1)} %get-tuple-element.121), channel_id=1, source_target_pairs={{0,2},{1,3},{2,0},{3,1},{4,6},{5,7},{6,4},{7,5},{8,10},{9,11},{10,... | collective-permute-start | bytes 1327112 | tf_op jit(solution)/shard_map/cond/branch_1_fun/ppermute | solution.py:677
  24.6 1.0 collective-permute-start.2
  25.6 18.2 %chunk576.1 = (bf16[960,768]{1,0:T(8,128)(2,1)}, bf16[960,384]{1,0:T(8,128)(2,1)}, f32[32,384]{1,0:T(8,128)S(1)}, bf16[480,768]{1,0:T(8,128)(2,1)}, bf16[480,768...) custom-call(s32[1,32]{1,0:T(1,128)S(1)} %get-tuple-element.123.refs_0_, ...), custom_call_target="tpu_custom_call" | custom-call | flops 20000000000 | bytes 20000000 | tf_op jit(solution)/shard_map/cond/branch_1_fun/chunk576/pallas_call | solution.py:304
  43.9 0.2 collective-permute-done.1
  44.1 20.3 %conditional.7 = (bf16[480,768]{1,0:T(8,128)(2,1)}, bf16[480,768]{1,0:T(8,128)(2,1)}, bf16[576,384]{1,0:T(8,128)(2,1)}, f32[8,48,640]{2,1,0:T(8,128)}, f32[8,48,...) conditional(s32[]{:T(128)} %convert_element_type.12, () %tuple.57, ...), branch_computations={%region_2.0_spmd, %region_3.0_spmd} | conditional | flops 11002001408 | bytes 36912072 | solution.py:637
  44.2 1.1 collective-permute-start.5
  45.3 1.6 %collective-permute-start.6 = (bf16[480,768]{1,0:T(8,128)(2,1)}, bf16[480,768]{1,0:T(8,128)(2,1)}, u32[]{:S(2)}, u32[]{:S(2)}) collective-permute-start(bf16[480,768]{1,0:T(8,128)(2,1)} %get-tuple-element.163), channel_id=1, source_target_pairs={{0,3},{1,2},{2,1},{3,0},{4,7},{5,6},{6,5},{7,4},{8,11},{9,10},{10,... | collective-permute-start | bytes 2211848 | tf_op jit(solution)/shard_map/cond/branch_1_fun/ppermute | solution.py:715
  46.9 17.5 %conditional = (bf16[576,384]{1,0:T(8,128)(2,1)}, f32[8,48,640]{2,1,0:T(8,128)}, f32[8,48,512]{2,1,0:T(8,128)}, bf16[8,48,640]{2,1,0:T(8,128)(2,1)}, bf16[10,48,512]{2,1,0:T(8,128)(2,1)}, /*index=5*/f32[32,384]{1,0:T(8,128)}) conditional(s32[]{:T(128)} %convert_element_type.0, () %tuple.35, (bf16[1536,1536]{1,0:T(8,128)(2,1)}, ...), branch_computations={%region_4.0_spmd, %region_5.0_spmd} | conditional | flops 11002001408 | bytes 31013596 | solution.py:637
  46.9 11.9 %weight.1 = (f32[16,48,1152]{2,1,0:T(8,128)S(1)}, bf16[16,48,1152]{2,1,0:T(8,128)(2,1)S(1)}) custom-call(bf16[1536,1536]{1,0:T(8,128)(2,1)} %get-tuple-element.148.refs_0_, bf16[1536,1536]{1,0:T(8,128)(2,1)} %get-tuple-element.149.refs_1_, bf16[672,768]{1,0:T(8,128)(2,1)} %get-tuple-element.150.refs_2_, bf16[960,768]{1,0:T(8,128)(2,1)} %get-tuple-element.151.refs_3_, ...), custom_call_target="tpu_custom_call" | custom-call | flops 11000000512 | bytes 20000000 | tf_op jit(solution)/shard_map/cond/branch_1_fun/cond/branch_1_fun/weight/pallas_call | solution.py:484
  58.8 0.1 collective-permute-start.3
  58.9 0.5 collective-permute-start.4
  59.4 2.2 %zero_sum.1 = bf16[576,384]{1,0:T(8,128)(2,1)} custom-call(f32[576,384]{1,0:T(8,128)S(1)} %copy-done.3, bf16[576,384]{1,0:T(8,128)(2,1)} %get-tuple-element.145.near0, bf16[576,384]{1,0:T(8,128)(2,1)} %get-tuple-element.146.far0, bf16[576,384]{1,0:T(8,128)(2,1)} %get-tuple-element.147.back0, f32[16,48,1152]{2,1,0:T(8,128)S(1)} %get-tuple-element.154.after.keep), custom_call_target="tpu_custom_call" | custom-call | flops 1000000 | bytes 100000 | tf_op jit(solution)/shard_map/cond/branch_1_fun/cond/branch_1_fun/zero_sum/pallas_call | solution.py:600
  61.6 1.0 collective-permute-done.4.small_got
  62.6 1.7 %core_sum.1 = (f32[8,48,640]{2,1,0:T(8,128)}, f32[8,48,512]{2,1,0:T(8,128)}, bf16[8,48,640]{2,1,0:T(8,128)(2,1)}, bf16[10,48,512]{2,1,0:T(8,128)(2,1)}, f32[32,384]{1,0:T(8,128)}) custom-call(f32[16,48,1152]{2,1,0:T(8,128)S(1)} %get-tuple-element.154.after.keep, bf16[16,48,1152]{2,1,0:T(8,128)(2,1)S(1)} %collective-permute-done.3.got, ...), custom_call_target="tpu_custom_call" | custom-call | flops 1000000 | bytes 100000 | tf_op jit(solution)/shard_map/cond/branch_1_fun/cond/branch_1_fun/core_sum/pallas_call | solution.py:600
  64.4 0.0 collective-permute-done.6
  64.4 2.0 %pass.1 = (bf16[480,384]{1,0:T(8,128)(2,1)S(1)}, bf16[480,384]{1,0:T(8,128)(2,1)}) custom-call(f32[480,768]{1,0:T(8,128)S(1)} %get-tuple-element.277.keep_a, f32[480,768]{1,0:T(8,128)S(1)} %get-tuple-element.278.keep_b, bf16[480,768]{1,0:T(8,128)(2,1)} %get-tuple-element.279.first_a, bf16[480,768]{1,0:T(8,128)(2,1)} %get-tuple-element.280.first_b), custom_call_target="tpu_custom_call" | custom-call | flops 1000000 | bytes 100000 | tf_op jit(solution)/shard_map/pass/pallas_call | solution.py:347
  66.4 14.8 %conditional.8 = (bf16[8,48,640]{2,1,0:T(8,128)(2,1)}, bf16[10,48,512]{2,1,0:T(8,128)(2,1)}, bf16[480,384]{1,0:T(8,128)(2,1)}, bf16[480,384]{1,0:T(8,128)(2,1)}) conditional(s32[]{:T(128)} %convert_element_type.12, () %tuple.61, (bf16[8,48,640]{2,1,0:T(8,128)(2,1)}, bf16[10,48,512]{2,1,0:T(8,128)(2,1)}, pred[]{:T(512)}, ...), branch_computations={%region_6.0_spmd, %region_7.0_spmd} | conditional | flops 1 | bytes 6881509 | solution.py:637
  66.4 1.5 %collective-permute-start.9 = (bf16[8,48,640]{2,1,0:T(8,128)(2,1)}, bf16[8,48,640]{2,1,0:T(8,128)(2,1)}, u32[]{:S(2)}, u32[]{:S(2)}) collective-permute-start(bf16[8,48,640]{2,1,0:T(8,128)(2,1)} %get-tuple-element.184), channel_id=1, source_target_pairs={{0,32},{4,36},{8,40},{12,44},{16,48},{20,52},{24,56},{28,60},{32,0... | collective-permute-start | bytes 1474568 | tf_op jit(solution)/shard_map/cond/branch_1_fun/ppermute | solution.py:628
  67.9 1.6 %collective-permute-start.10 = (bf16[10,48,512]{2,1,0:T(8,128)(2,1)}, bf16[10,48,512]{2,1,0:T(8,128)(2,1)}, u32[]{:S(2)}, u32[]{:S(2)}) collective-permute-start(bf16[10,48,512]{2,1,0:T(8,128)(2,1)} %get-tuple-element.185), channel_id=1, source_target_pairs={{0,8},{4,12},{8,0},{12,4},{16,24},{20,28},{24,16},{28,20},{32,40},... | collective-permute-start | bytes 1474568 | tf_op jit(solution)/shard_map/cond/branch_1_fun/ppermute | solution.py:628
  69.5 11.7 %conditional.1 = (bf16[480,384]{1,0:T(8,128)(2,1)}, bf16[480,384]{1,0:T(8,128)(2,1)}) conditional(s32[]{:T(128)} %convert_element_type.1, () %tuple.41, (bf16[480,384]{1,0:T(8,128)(2,1)S(1)}, bf16[480,384]{1,0:T(8,128)(2,1)}) %tuple.42), branch_computations={%region_8.0_spmd, %region_9.0_spmd} | conditional | bytes 2949216 | solution.py:637
  69.5 1.7 %collective-permute-start.7 = (bf16[480,384]{1,0:T(8,128)(2,1)S(1)}, bf16[480,384]{1,0:T(8,128)(2,1)}, u32[]{:S(2)}, u32[]{:S(2)}) collective-permute-start(bf16[480,384]{1,0:T(8,128)(2,1)S(1)} %get-tuple-element.182), channel_id=1, source_target_pairs={{0,3},{1,2},{2,1},{3,0},{4,7},{5,6},{6,5},{7,4},{8,11},{9,10},{10,... | collective-permute-start | bytes 1105928 | tf_op jit(solution)/shard_map/cond/branch_1_fun/cond/branch_1_fun/ppermute | solution.py:719
  71.2 9.7 %collective-permute-done.7 = bf16[480,384]{1,0:T(8,128)(2,1)} collective-permute-done((bf16[480,384]{1,0:T(8,128)(2,1)S(1)}, bf16[480,384]{1,0:T(8,128)(2,1)}, u32[]{:S(2)}, u32[]{:S(2)}) %collective-permute-start.7) | collective-permute-done | bytes 368672 | tf_op jit(solution)/shard_map/cond/branch_1_fun/cond/branch_1_fun/ppermute | solution.py:719
  80.9 0.3 collective-permute-done.8
  81.2 2.0 %half_sum.1 = (f32[4,48,640]{2,1,0:T(8,128)S(1)}, f32[4,48,512]{2,1,0:T(8,128)S(1)}, bf16[4,48,640]{2,1,0:T(8,128)(2,1)S(1)}, bf16[6,48,512]{2,1,0:T(8,128)(2,1)S(1)}, f32[32,384]{1,0:T(8,128)S(1)}) custom-call(f32[8,48,640]{2,1,0:T(8,128)} %get-tuple-element.272.own_x, f32[8,48,512]{2,1,0:T(8,128)} %get-tuple-element.273.own_y, ...), custom_call_target="tpu_custom_call" | custom-call | flops 1000000 | bytes 100000 | tf_op jit(solution)/shard_map/half_sum/pallas_call | solution.py:600
  83.3 0.2 copy-done.2
  83.4 8.0 %conditional.9 = (bf16[4,48,640]{2,1,0:T(8,128)(2,1)}, bf16[6,48,512]{2,1,0:T(8,128)(2,1)}, bf16[32,72,384]{2,1,0:T(8,128)(2,1)}) conditional(s32[]{:T(128)} %convert_element_type.12, () %tuple.56, (bf16[4,48,640]{2,1,0:T(8,128)(2,1)S(1)}, bf16[6,48,512]{2,1,0:T(8,128)(2,1)S(1)}, s32[1,32]{1,0:T(1,128)S(1)}, s32[1,32]{1,0:T(1,128)S(1)}, ...), branch_computations={%region_10.0_spmd, %region_11.0_spmd} | conditional | flops 1000000 | bytes 2310174 | solution.py:637
  83.4 0.6 collective-permute-start.12
  84.0 1.6 %collective-permute-start.11 = (bf16[4,48,640]{2,1,0:T(8,128)(2,1)S(1)}, bf16[4,48,640]{2,1,0:T(8,128)(2,1)}, u32[]{:S(2)}, u32[]{:S(2)}) collective-permute-start(bf16[4,48,640]{2,1,0:T(8,128)(2,1)S(1)} %get-tuple-element.191), channel_id=1, source_target_pairs={{0,8},{4,12},{8,0},{12,4},{16,24},{20,28},{24,16},{28,20},{32,40},... | collective-permute-start | bytes 737288 | tf_op jit(solution)/shard_map/cond/branch_1_fun/ppermute | solution.py:628
  85.6 4.3 %pick.1 = bf16[32,72,384]{2,1,0:T(8,128)(2,1)} custom-call(s32[1,32]{1,0:T(1,128)S(1)} %get-tuple-element.193.len_ref, s32[1,32]{1,0:T(1,128)S(1)} %get-tuple-element.308.owner_ref, bf16[576,384]{1,0:T(8,128)(2,1)} %get-tuple-element.195.held0, f32[480,768]{1,0:T(8,128)S(1)} %get-tuple-element.196.keep_a, f32[480,768]{1,0:T(8,128)S(1)} %get-tuple-element.197.keep_b, ...), custom_call_target="tpu_custom_call" | custom-call | flops 1000000 | bytes 100000 | tf_op jit(solution)/shard_map/cond/branch_1_fun/pick/pallas_call | solution.py:392
  89.9 0.8 collective-permute-done.11
  90.7 0.7 collective-permute-done.12
  91.4 7.2 %all-to-all-start = ((bf16[32,72,384]{2,1,0:T(8,128)(2,1)}), bf16[32,72,384]{2,1,0:T(8,128)(2,1)S(1)}, u32[]{:S(2)}, u32[]{:S(2)}) async-start(bf16[32,72,384]{2,1,0:T(8,128)(2,1)} %get-tuple-element.290), calls=%async_computation | async-start | bytes 3538944 | tf_op jit(solution)/shard_map/all_to_all | solution.py:742
  98.6 1.2 square_sum.1
  99.8 5.3 %collective-permute-start.13 = (bf16[48,1920]{1,0:T(8,128)(2,1)S(1)}, bf16[48,1920]{1,0:T(8,128)(2,1)S(1)}, u32[]{:S(2)}, u32[]{:S(2)}) collective-permute-start(bf16[48,1920]{1,0:T(8,128)(2,1)S(1)} %get-tuple-element.299), channel_id=1, source_target_pairs={{0,120},{4,124},{8,112},{12,116},{16,104},{20,108},{24,96},{28,100... | collective-permute-start | bytes 552968 | tf_op jit(solution)/shard_map/ppermute | solution.py:628
  105.1 0.5 collective-permute-start.14
  105.5 0.2 collective-permute-start.15
  105.8 18.2 %all-to-all-done.src = bf16[32,72,384]{2,1,0:T(8,128)(2,1)S(1)} async-done(((bf16[32,72,384]{2,1,0:T(8,128)(2,1)}), bf16[32,72,384]{2,1,0:T(8,128)(2,1)S(1)}, u32[]{:S(2)}, u32[]{:S(2)}) %all-to-all-start) | async-done | bytes 1769504 | tf_op jit(solution)/shard_map/all_to_all | solution.py:742
  124.0 2.0 %order.1 = (bf16[32,72,384]{2,1,0:T(8,128)(2,1)}, f32[8,128]{1,0:T(8,128)S(1)}) custom-call(s32[1,32]{1,0:T(1,128)S(1)} %copy-done, bf16[32,72,384]{2,1,0:T(8,128)(2,1)S(1)} %all-to-all-done.src), custom_call_target="tpu_custom_call" | custom-call | flops 1000000 | bytes 100000 | tf_op jit(solution)/shard_map/order/pallas_call | solution.py:417
  126.0 2.1 %collective-permute-done.13.refs_2_ = bf16[48,1920]{1,0:T(8,128)(2,1)S(1)} collective-permute-done((bf16[48,1920]{1,0:T(8,128)(2,1)S(1)}, bf16[48,1920]{1,0:T(8,128)(2,1)S(1)}, u32[]{:S(2)}, u32[]{:S(2)}) %collective-permute-start.13) | collective-permute-done | bytes 184352 | tf_op jit(solution)/shard_map/ppermute | solution.py:628
  128.1 1.5 %collective-permute-done.14.refs_3_ = bf16[48,1920]{1,0:T(8,128)(2,1)S(1)} collective-permute-done((bf16[48,1920]{1,0:T(8,128)(2,1)S(1)}, bf16[48,1920]{1,0:T(8,128)(2,1)S(1)}, u32[]{:S(2)}, u32[]{:S(2)}) %collective-permute-start.14) | collective-permute-done | bytes 184352 | tf_op jit(solution)/shard_map/ppermute | solution.py:628
  129.6 0.8 last_sum.1
  (41 shorter events, 0.1 us)
Async XLA Ops:
  1.3 2.3 %copy-start.4 = (s32[1,32]{1,0:T(1,128)S(1)}, s32[1,32]{1,0:T(1,128)}, u32[]{:S(2)}) copy-start(s32[1,32]{1,0:T(1,128)} %refs_0_.1) | copy-start | bytes 388
  1.3 3.1 %copy-start.6 = (bf16[1536,1536]{1,0:T(8,128)(2,1)S(1)}, bf16[1536,1536]{1,0:T(8,128)(2,1)}, u32[]{:S(2)}) copy-start(bf16[1536,1536]{1,0:T(8,128)(2,1)} %refs_1_.1) | copy-start | bytes 14155780
  1.3 16.6 %slice-start = ((s8[4718592]{0:T(1024)(128)(4,1)}), s8[4194304]{0:T(1024)(128)(4,1)S(1)}, s32[]{:S(2)}) async-start(s8[4718592]{0:T(1024)(128)(4,1)} %bitcast.9), calls=%async_computation.1 | async-start | bytes 8388608
  4.3 13.6 %slice-start.1 = ((s8[4718592]{0:T(1024)(128)(4,1)}), s8[524288]{0:T(1024)(128)(4,1)S(1)}, s32[]{:S(2)}) async-start(s8[4718592]{0:T(1024)(128)(4,1)} %bitcast.9), calls=%async_computation.2 | async-start | bytes 1048576
  4.3 13.6 %copy-start.7 = (bf16[384,1536]{1,0:T(8,128)(2,1)S(1)}, bf16[384,1536]{1,0:T(8,128)(2,1)}, u32[]{:S(2)}) copy-start(bf16[384,1536]{1,0:T(8,128)(2,1)} %refs_4_.1) | copy-start | bytes 3538948
  4.3 13.6 %copy-start.8 = (f32[31,384]{1,0:T(8,128)S(1)}, f32[31,384]{1,0:T(8,128)}, u32[]{:S(2)}) copy-start(f32[31,384]{1,0:T(8,128)} %refs_5_.1) | copy-start | bytes 142852
  4.4 13.6 %copy-start.9 = (f32[384]{0:T(512)S(1)}, f32[384]{0:T(512)}, u32[]{:S(2)}) copy-start(f32[384]{0:T(512)} %refs_6_.1) | copy-start | bytes 4612
  4.4 13.6 %copy-start.10 = (f32[96,31]{1,0:T(8,128)S(1)}, f32[96,31]{1,0:T(8,128)}, u32[]{:S(2)}) copy-start(f32[96,31]{1,0:T(8,128)} %constant.21.clone.refs_9_) | copy-start | bytes 35716
  4.4 13.6 %copy-start.11 = (bf16[88,240]{1,0:T(8,128)(2,1)S(1)}, bf16[88,240]{1,0:T(8,128)(2,1)}, u32[]{:S(2)}) copy-start(bf16[88,240]{1,0:T(8,128)(2,1)} %constant.17.clone.refs_7_) | copy-start | bytes 126724
  4.4 13.6 %copy-start.12 = (bf16[80,256]{1,0:T(8,128)(2,1)S(1)}, bf16[80,256]{1,0:T(8,128)(2,1)}, u32[]{:S(2)}) copy-start(bf16[80,256]{1,0:T(8,128)(2,1)} %constant.19.clone.refs_8_) | copy-start | bytes 122884
  4.4 13.6 %copy-start.13 = (f32[31,96]{1,0:T(8,128)S(1)}, f32[31,96]{1,0:T(8,128)}, u32[]{:S(2)}) copy-start(f32[31,96]{1,0:T(8,128)} %constant.31.clone.refs_10_) | copy-start | bytes 35716
  17.9 1.0 copy-start.14
  17.9 1.1 copy-start.15
  19.0 24.8 %collective-permute-start = (bf16[576,384]{1,0:T(8,128)(2,1)S(1)}, bf16[576,384]{1,0:T(8,128)(2,1)}, u32[]{:S(2)}, u32[]{:S(2)}) collective-permute-start(bf16[576,384]{1,0:T(8,128)(2,1)S(1)} %get-tuple-element.120), channel_id=1, source_target_pairs={{0,1},{1,2},{2,3},{3,0},{4,5},{5,6},{6,7},{7,4},{8,9},{9,10},{10,1... | collective-permute-start | bytes 1327112 | tf_op jit(solution)/shard_map/cond/branch_1_fun/ppermute | solution.py:676
  21.0 23.1 %collective-permute-start.1 = (bf16[576,384]{1,0:T(8,128)(2,1)S(1)}, bf16[576,384]{1,0:T(8,128)(2,1)}, u32[]{:S(2)}, u32[]{:S(2)}) collective-permute-start(bf16[576,384]{1,0:T(8,128)(2,1)S(1)} %get-tuple-element.121), channel_id=1, source_target_pairs={{0,2},{1,3},{2,0},{3,1},{4,6},{5,7},{6,4},{7,5},{8,10},{9,11},{10,... | collective-permute-start | bytes 1327112 | tf_op jit(solution)/shard_map/cond/branch_1_fun/ppermute | solution.py:677
  24.6 19.5 %collective-permute-start.2 = (bf16[576,384]{1,0:T(8,128)(2,1)S(1)}, bf16[576,384]{1,0:T(8,128)(2,1)}, u32[]{:S(2)}, u32[]{:S(2)}) collective-permute-start(bf16[576,384]{1,0:T(8,128)(2,1)S(1)} %get-tuple-element.122), channel_id=1, source_target_pairs={{0,3},{1,0},{2,1},{3,2},{4,7},{5,4},{6,5},{7,6},{8,11},{9,8},{10,9... | collective-permute-start | bytes 1327112 | tf_op jit(solution)/shard_map/cond/branch_1_fun/ppermute | solution.py:678
  44.1 20.3 %copy-start.1 = (f32[480,768]{1,0:T(8,128)}, f32[480,768]{1,0:T(8,128)S(1)}, u32[]{:S(2)}) copy-start(f32[480,768]{1,0:T(8,128)S(1)} %get-tuple-element.277.keep_a) | copy-start | bytes 4423684
  44.2 20.2 %collective-permute-start.5 = (bf16[480,768]{1,0:T(8,128)(2,1)}, bf16[480,768]{1,0:T(8,128)(2,1)}, u32[]{:S(2)}, u32[]{:S(2)}) collective-permute-start(bf16[480,768]{1,0:T(8,128)(2,1)} %get-tuple-element.162), channel_id=1, source_target_pairs={{0,1},{1,0},{2,3},{3,2},{4,5},{5,4},{6,7},{7,6},{8,9},{9,8},{10,11... | collective-permute-start | bytes 2211848 | tf_op jit(solution)/shard_map/cond/branch_1_fun/ppermute | solution.py:714
  45.3 19.1 %collective-permute-start.6 = (bf16[480,768]{1,0:T(8,128)(2,1)}, bf16[480,768]{1,0:T(8,128)(2,1)}, u32[]{:S(2)}, u32[]{:S(2)}) collective-permute-start(bf16[480,768]{1,0:T(8,128)(2,1)} %get-tuple-element.163), channel_id=1, source_target_pairs={{0,3},{1,2},{2,1},{3,0},{4,7},{5,6},{6,5},{7,4},{8,11},{9,10},{10,... | collective-permute-start | bytes 2211848 | tf_op jit(solution)/shard_map/cond/branch_1_fun/ppermute | solution.py:715
  46.9 12.5 %copy-start.3 = (f32[576,384]{1,0:T(8,128)S(1)}, f32[576,384]{1,0:T(8,128)}, u32[]{:S(2)}) copy-start(f32[576,384]{1,0:T(8,128)} %get-tuple-element.144.keep0) | copy-start | bytes 2654212 | tf_op jit(solution)/shard_map/cond/branch_1_fun/cond
  58.8 3.8 %collective-permute-start.3 = (bf16[16,48,1152]{2,1,0:T(8,128)(2,1)S(1)}, bf16[16,48,1152]{2,1,0:T(8,128)(2,1)S(1)}, u32[]{:S(2)}, u32[]{:S(2)}) collective-permute-start(bf16[16,48,1152]{2,1,0:T(8,128)(2,1)S(1)} %get-tuple-element.155), channel_id=1, source_target_pairs={{0,4},{4,0},{8,12},{12,8},{16,20},{20,16},{24,28},{28,24},{32,36},... | collective-permute-start | bytes 5308424 | tf_op jit(solution)/shard_map/cond/branch_1_fun/cond/branch_1_fun/ppermute | solution.py:628
  58.9 3.7 %collective-permute-start.4 = (f32[32,384]{1,0:T(8,128)S(1)}, f32[32,384]{1,0:T(8,128)S(1)}, u32[]{:S(2)}, u32[]{:S(2)}) collective-permute-start(f32[32,384]{1,0:T(8,128)S(1)} %get-tuple-element.156.small), channel_id=1, source_target_pairs={{0,4},{4,0},{8,12},{12,8},{16,20},{20,16},{24,28},{28,24},{32,36},... | collective-permute-start | bytes 147464 | tf_op jit(solution)/shard_map/cond/branch_1_fun/cond/branch_1_fun/ppermute | solution.py:628
  66.4 14.8 %collective-permute-start.9 = (bf16[8,48,640]{2,1,0:T(8,128)(2,1)}, bf16[8,48,640]{2,1,0:T(8,128)(2,1)}, u32[]{:S(2)}, u32[]{:S(2)}) collective-permute-start(bf16[8,48,640]{2,1,0:T(8,128)(2,1)} %get-tuple-element.184), channel_id=1, source_target_pairs={{0,32},{4,36},{8,40},{12,44},{16,48},{20,52},{24,56},{28,60},{32,0... | collective-permute-start | bytes 1474568 | tf_op jit(solution)/shard_map/cond/branch_1_fun/ppermute | solution.py:628
  67.9 13.3 %collective-permute-start.10 = (bf16[10,48,512]{2,1,0:T(8,128)(2,1)}, bf16[10,48,512]{2,1,0:T(8,128)(2,1)}, u32[]{:S(2)}, u32[]{:S(2)}) collective-permute-start(bf16[10,48,512]{2,1,0:T(8,128)(2,1)} %get-tuple-element.185), channel_id=1, source_target_pairs={{0,8},{4,12},{8,0},{12,4},{16,24},{20,28},{24,16},{28,20},{32,40},... | collective-permute-start | bytes 1474568 | tf_op jit(solution)/shard_map/cond/branch_1_fun/ppermute | solution.py:628
  69.5 11.4 %collective-permute-start.7 = (bf16[480,384]{1,0:T(8,128)(2,1)S(1)}, bf16[480,384]{1,0:T(8,128)(2,1)}, u32[]{:S(2)}, u32[]{:S(2)}) collective-permute-start(bf16[480,384]{1,0:T(8,128)(2,1)S(1)} %get-tuple-element.182), channel_id=1, source_target_pairs={{0,3},{1,2},{2,1},{3,0},{4,7},{5,6},{6,5},{7,4},{8,11},{9,10},{10,... | collective-permute-start | bytes 1105928 | tf_op jit(solution)/shard_map/cond/branch_1_fun/cond/branch_1_fun/ppermute | solution.py:719
  71.2 10.0 %collective-permute-start.8 = (bf16[480,384]{1,0:T(8,128)(2,1)}, bf16[480,384]{1,0:T(8,128)(2,1)}, u32[]{:S(2)}, u32[]{:S(2)}) collective-permute-start(bf16[480,384]{1,0:T(8,128)(2,1)} %get-tuple-element.183), channel_id=1, source_target_pairs={{0,1},{1,0},{2,3},{3,2},{4,5},{5,4},{6,7},{7,6},{8,9},{9,8},{10,11... | collective-permute-start | bytes 1105928 | tf_op jit(solution)/shard_map/cond/branch_1_fun/cond/branch_1_fun/ppermute | solution.py:719
  81.2 2.2 %copy-start.2 = (f32[480,768]{1,0:T(8,128)S(1)}, f32[480,768]{1,0:T(8,128)}, u32[]{:S(2)}) copy-start(f32[480,768]{1,0:T(8,128)} %copy-done.1) | copy-start | bytes 4423684
  81.2 2.2 %copy-start.5 = (s32[1,32]{1,0:T(1,128)S(1)}, s32[1,32]{1,0:T(1,128)}, u32[]{:S(2)}) copy-start(s32[1,32]{1,0:T(1,128)} %param.32) | copy-start | bytes 388
  83.4 8.0 %collective-permute-start.12 = (bf16[6,48,512]{2,1,0:T(8,128)(2,1)S(1)}, bf16[6,48,512]{2,1,0:T(8,128)(2,1)}, u32[]{:S(2)}, u32[]{:S(2)}) collective-permute-start(bf16[6,48,512]{2,1,0:T(8,128)(2,1)S(1)} %get-tuple-element.192), channel_id=1, source_target_pairs={{0,32},{4,36},{8,40},{12,44},{16,48},{20,52},{24,56},{28,60},{32,0... | collective-permute-start | bytes 884744 | tf_op jit(solution)/shard_map/cond/branch_1_fun/ppermute | solution.py:628
  84.0 6.7 %collective-permute-start.11 = (bf16[4,48,640]{2,1,0:T(8,128)(2,1)S(1)}, bf16[4,48,640]{2,1,0:T(8,128)(2,1)}, u32[]{:S(2)}, u32[]{:S(2)}) collective-permute-start(bf16[4,48,640]{2,1,0:T(8,128)(2,1)S(1)} %get-tuple-element.191), channel_id=1, source_target_pairs={{0,8},{4,12},{8,0},{12,4},{16,24},{20,28},{24,16},{28,20},{32,40},... | collective-permute-start | bytes 737288 | tf_op jit(solution)/shard_map/cond/branch_1_fun/ppermute | solution.py:628
  91.4 32.6 %copy-start = (s32[1,32]{1,0:T(1,128)S(1)}, s32[1,32]{1,0:T(1,128)}, u32[]{:S(2)}) copy-start(s32[1,32]{1,0:T(1,128)} %slot_ref.1) | copy-start | bytes 388
  91.4 32.6 %all-to-all-start = ((bf16[32,72,384]{2,1,0:T(8,128)(2,1)}), bf16[32,72,384]{2,1,0:T(8,128)(2,1)S(1)}, u32[]{:S(2)}, u32[]{:S(2)}) async-start(bf16[32,72,384]{2,1,0:T(8,128)(2,1)} %get-tuple-element.290), calls=%async_computation | async-start | bytes 3538944 | tf_op jit(solution)/shard_map/all_to_all | solution.py:742
  99.8 28.4 %collective-permute-start.13 = (bf16[48,1920]{1,0:T(8,128)(2,1)S(1)}, bf16[48,1920]{1,0:T(8,128)(2,1)S(1)}, u32[]{:S(2)}, u32[]{:S(2)}) collective-permute-start(bf16[48,1920]{1,0:T(8,128)(2,1)S(1)} %get-tuple-element.299), channel_id=1, source_target_pairs={{0,120},{4,124},{8,112},{12,116},{16,104},{20,108},{24,96},{28,100... | collective-permute-start | bytes 552968 | tf_op jit(solution)/shard_map/ppermute | solution.py:628
  105.1 24.5 %collective-permute-start.14 = (bf16[48,1920]{1,0:T(8,128)(2,1)S(1)}, bf16[48,1920]{1,0:T(8,128)(2,1)S(1)}, u32[]{:S(2)}, u32[]{:S(2)}) collective-permute-start(bf16[48,1920]{1,0:T(8,128)(2,1)S(1)} %get-tuple-element.300), channel_id=1, source_target_pairs={{0,96},{4,100},{8,104},{12,108},{16,112},{20,116},{24,120},{28,124... | collective-permute-start | bytes 552968 | tf_op jit(solution)/shard_map/ppermute | solution.py:628
  105.5 24.1 %collective-permute-start.15 = (bf16[48,1920]{1,0:T(8,128)(2,1)S(1)}, bf16[48,1920]{1,0:T(8,128)(2,1)S(1)}, u32[]{:S(2)}, u32[]{:S(2)}) collective-permute-start(bf16[48,1920]{1,0:T(8,128)(2,1)S(1)} %get-tuple-element.301), channel_id=1, source_target_pairs={{0,24},{4,28},{8,16},{12,20},{16,8},{20,12},{24,0},{28,4},{32,56},... | collective-permute-start | bytes 552968 | tf_op jit(solution)/shard_map/ppermute | solution.py:628

commit v6 on v5

--- a/solution.py
+++ b/solution.py
@@ -430,7 +430,7 @@
 
 
 COLS = 4
-PARTS = 4
+PARTS = 1
 
 
 def weight_kernel(
@@ -462,18 +462,32 @@
     for copy in first + second:
         copy.start()
     pairs = cols // (2 * deep)
-    for copies, left, right, at in ((first, go, act, slice(wide, None)), (second, fr, gp, slice(0, wide))):
-        for copy in copies:
-            copy.wait()
+    step = total // PARTS
+
+    def share(j, at):
+        for i in range(pairs):
+            own = pl.ds(pl.multiple_of(j * cols + (2 * i + core) * deep, 16), deep)
+            other = pl.ds(pl.multiple_of(j * cols + (2 * i + 1 - core) * deep, 16), deep)
+            keep_ref[j * pairs + i, :, at] = held[own, at]
+            send_ref[j * pairs + i, :, at] = held[other, at].astype(BF16)
+
+    out_cols, in_cols = slice(wide, None), slice(0, wide)
+    for copy in first[:2]:
+        copy.wait()
+    for p in range(PARTS):
+        first[2 + p].wait()
+        rows = slice(p * step, (p + 1) * step)
         for j in range(COLS):
-            held[j % 2, :, at] = lax.dot_general(
-                left[:, j * cols : (j + 1) * cols], right[...], TN, preferred_element_type=F32
-            )
-            for i in range(pairs):
-                own = pl.ds(pl.multiple_of((2 * i + core) * deep, 16), deep)
-                other = pl.ds(pl.multiple_of((2 * i + 1 - core) * deep, 16), deep)
-                keep_ref[j * pairs + i, :, at] = held[j % 2, own, at]
-                send_ref[j * pairs + i, :, at] = held[j % 2, other, at].astype(BF16)
+            here = slice(j * cols, (j + 1) * cols)
+            term = lax.dot_general(go[rows, here], act[rows, :], TN, preferred_element_type=F32)
+            held[here, out_cols] = term if p == 0 else held[here, out_cols] + term
+    for copy in second:
+        copy.wait()
+    for j in range(COLS):
+        here = slice(j * cols, (j + 1) * cols)
+        held[here, in_cols] = lax.dot_general(fr[:, here], gp[...], TN, preferred_element_type=F32)
+        share(j, out_cols)
+        share(j, in_cols)
 
 
 def weight_call(deep, frames, grad_out, gp0, gp1, act0, act1):
@@ -494,7 +508,7 @@
             pltpu.VMEM((total, width), BF16),
             pltpu.VMEM((total, 2 * ch), BF16),
             pltpu.VMEM((total, ch), BF16),
-            pltpu.VMEM((2, width // COLS, 3 * ch), F32),
+            pltpu.VMEM((width, 3 * ch), F32),
             pltpu.SemaphoreType.DMA((PARTS,)),
             pltpu.SemaphoreType.DMA((PARTS,)),
             pltpu.SemaphoreType.DMA((4,)),
@@ -688,8 +702,8 @@
             ),
         )
 
-    near0, far0, back0, gp1, act1, small, send_a, send_b, keep_a, keep_b = together(
-        live, zeroth_stage, near0, far0, back0, gp0, act0, sum0, *shared[:7], *consts
+    near0, far0, back0, gp1, act1, small, send_a, send_b, keep_a, keep_b = zeroth_stage(
+        near0, far0, back0, gp0, act0, sum0, *shared[:7], *consts
     )
     pair = [(i, i ^ 1) for i in range(4)]
     cross = [(i, 3 - i) for i in range(4)]
@@ -710,28 +724,26 @@
         )
         return held0, *sums
 
-    def first_stage(send_a, send_b, *operands):
+    def last_stage(send_a, send_b):
+        return lax.ppermute(send_a, "mp", cross), lax.ppermute(send_b, "mp", pair)
+
+    def first_stage(send_a, send_b, keep_a, keep_b, *operands):
         first_a = lax.ppermute(send_a, "mp", pair)
         first_b = lax.ppermute(send_b, "mp", cross)
-        return first_a, first_b, *together(live, weight_stage, *operands)
-
-    def last_stage(send_a, send_b):
-        return lax.ppermute(send_a, "mp", cross), lax.ppermute(send_b, "mp", pair)
-
-    def second_stage(send_x, send_y, *operands):
+        held0, own_x, own_y, send_x, send_y, small = together(live, weight_stage, *operands)
         got_x, got_y = move(send_x, fx=near), move(send_y, fy=near)
-        return got_x, got_y, *together(live, last_stage, *operands)
+        send_a, send_b = pass_call(keep_a, keep_b, first_a, first_b)
+        last_a, last_b = together(live, last_stage, send_a, send_b)
+        return first_a, first_b, held0, own_x, own_y, small, got_x, got_y, last_a, last_b
 
     def third_stage(send_x, send_y, *operands):
         got_x, got_y = move(send_x, fy=near), move(send_y, fx=near)
         return got_x, got_y, pick_call(*operands)
 
-    first_a, first_b, held0, own_x, own_y, send_x, send_y, small = together(
-        live, first_stage, send_a, send_b,
+    first_a, first_b, held0, own_x, own_y, small, got_x, got_y, last_a, last_b = first_stage(
+        send_a, send_b, keep_a, keep_b,
         frames, grad_out, gp0, gp1, act0, act1, small, keep0, near0, far0, back0,
     )
-    send_a, send_b = pass_call(keep_a, keep_b, first_a, first_b)
-    got_x, got_y, last_a, last_b = together(live, second_stage, send_x, send_y, send_a, send_b)
     own_x, own_y, send_x, send_y, small = sum_call(
         half_sum_kernel, "half_sum", TINY, halves(4, deep, wide, small), own_x, own_y, small, got_x, got_y
     )

time: 131 us -> 124 us (0.947)
  Pallas kernels: 59.9 us -> 51.8 us
  waiting for transfers between devices: 34.6 us -> 38.8 us
  starting transfers between devices: 30 us -> 27.8 us
    ppermute x9, waiting for transfers between devices: 6.14 us -> 9.96 us  [move(): lax.ppermute(array, 'dp', [(i, to(i)) for i in range(lax.axis_size('dp'))])]
    pallas_call x5, Pallas kernels: 7.96 us -> 5.03 us  [sum_call(): pl.pallas_call(kernel, out_shape=out_shape, in_specs=[vm] * len(operands)...]
    pallas_call x1, Pallas kernels: 11.9 us -> 9.11 us  [weight_call(): pl.pallas_call(lambda *refs: weight_kernel(deep, *refs), out_shape=(jax.S...]
    ppermute x1, starting transfers between devices: 1.64 us -> 0.1 us  [first_stage(): first_b = lax.ppermute(send_b, 'mp', cross)]
    unnamed x35 -> x37, local copies, waits for them, and re-layouts: 4.29 us -> 3.79 us
  transfers between devices with their start and end apart: 17 -> 17, of which waited for: 9 -> 9; matrix products, arithmetic and copies ran while one was open for 0% -> 0% of each run, Pallas kernels for 32% -> 30%
where the time goes in v6:
time: 124 us; the launch traced here: 123 us
  Pallas kernels  51.8 us (42%)
  waiting for transfers between devices  38.8 us (31%)
  starting transfers between devices  27.8 us (22%)
  local copies, waits for them, and re-layouts  3.79 us (3%)
    pallas_call x2, Pallas kernels, chunk_call(): pl.pallas_call(body, out_shape=out_shape, in_specs=specs, out_specs=[vm]...  30.9 us
    all_to_all x1, waiting for transfers between devices, on_device(): lax.all_to_all(outgoing, 'dp', split_axis=0, concat_axis=0, tiled=True)  18.2 us
    ppermute x9, starting transfers between devices, move(): lax.ppermute(array, 'dp', [(i, to(i)) for i in range(lax.axis_size('dp'))])  10.6 us
    ppermute x9, waiting for transfers between devices, move(): lax.ppermute(array, 'dp', [(i, to(i)) for i in range(lax.axis_size('dp'))])  9.96 us
    ppermute x2, waiting for transfers between devices, last_stage(): return (lax.ppermute(send_a, 'mp', cross), lax.ppermute(send_b, 'mp', pair))  9.89 us
    pallas_call x1, Pallas kernels, weight_call(): pl.pallas_call(lambda *refs: weight_kernel(deep, *refs), out_shape=(jax.S...  9.11 us
    all_to_all x1, starting transfers between devices, on_device(): lax.all_to_all(outgoing, 'dp', split_axis=0, concat_axis=0, tiled=True)  6.88 us
    pallas_call x5, Pallas kernels, sum_call(): pl.pallas_call(kernel, out_shape=out_shape, in_specs=[vm] * len(operands)...  5.03 us
  transfers between devices with their start and end apart: 17, of which 9 were waited for; matrix products, arithmetic and copies ran while one was open for 0% of the time, Pallas kernels for 30%

profile of v6, /device:TPU:0, one launch (start us, length us, event | category | flops | bytes accessed | tf_op | source)
XLA Modules:
  0.0 123.3 jit_solution(14397301801082213380)
XLA Ops:
  0.7 0.0 copy-start.4
  0.7 0.0 slice-start
  0.7 0.0 slice-start.2
  0.7 2.3 %copy.19 = bf16[192,8,2,384]{3,1,2,0:T(8,128)(2,1)S(1)} copy(bf16[192,8,2,384]{3,2,1,0:T(2,128)(2,1)} %bitcast.7) | data formatting | bytes 4718592
  3.1 0.0 slice-start.1
  3.1 0.0 slice-start.3
  3.1 12.8 %chunk0.1 = (bf16[672,768]{1,0:T(8,128)(2,1)S(1)}, bf16[672,384]{1,0:T(8,128)(2,1)S(1)}, f32[104,384]{1,0:T(8,128)S(1)}, f32[576,384]{1,0:T(8,128)S(1)}, bf16[57...) custom-call(s32[1,32]{1,0:T(1,128)S(1)} %copy-done.12, ...), custom_call_target="tpu_custom_call" | custom-call | flops 20000000000 | bytes 20000000 | tf_op jit(solution)/shard_map/chunk0/pallas_call | solution.py:304
  16.0 2.1 %collective-permute-start.6 = (bf16[576,384]{1,0:T(8,128)(2,1)S(1)}, bf16[576,384]{1,0:T(8,128)(2,1)S(1)}, u32[]{:S(2)}, u32[]{:S(2)}) collective-permute-start(bf16[576,384]{1,0:T(8,128)(2,1)S(1)} %get-tuple-element.131), channel_id=1, source_target_pairs={{0,1},{1,2},{2,3},{3,0},{4,5},{5,6},{6,7},{7,4},{8,9},{9,10},{10,1... | collective-permute-start | bytes 1327112 | tf_op jit(solution)/shard_map/ppermute | solution.py:690
  18.0 3.6 %collective-permute-start.7 = (bf16[576,384]{1,0:T(8,128)(2,1)S(1)}, bf16[576,384]{1,0:T(8,128)(2,1)S(1)}, u32[]{:S(2)}, u32[]{:S(2)}) collective-permute-start(bf16[576,384]{1,0:T(8,128)(2,1)S(1)} %get-tuple-element.132), channel_id=1, source_target_pairs={{0,2},{1,3},{2,0},{3,1},{4,6},{5,7},{6,4},{7,5},{8,10},{9,11},{10,... | collective-permute-start | bytes 1327112 | tf_op jit(solution)/shard_map/ppermute | solution.py:691
  21.6 1.0 collective-permute-start.8
  22.7 18.1 %chunk576.1 = (bf16[960,768]{1,0:T(8,128)(2,1)S(1)}, bf16[960,384]{1,0:T(8,128)(2,1)S(1)}, f32[32,384]{1,0:T(8,128)S(1)}, bf16[480,768]{1,0:T(8,128)(2,1)S(1)}, ...) custom-call(s32[1,32]{1,0:T(1,128)S(1)} %copy-done.12, bf16[1536,1536]{1,0:T(8,128)(2,1)S(1)} %bitcast.10, ...), custom_call_target="tpu_custom_call" | custom-call | flops 20000000000 | bytes 20000000 | tf_op jit(solution)/shard_map/chunk576/pallas_call | solution.py:304
  40.8 1.1 collective-permute-start.11
  41.9 0.1 collective-permute-start.12
  42.0 14.4 %conditional.3 = (bf16[576,384]{1,0:T(8,128)(2,1)S(1)}, f32[8,48,640]{2,1,0:T(8,128)S(1)}, f32[8,48,512]{2,1,0:T(8,128)}, bf16[8,48,640]{2,1,0:T(8,128)(2,1)}, b...) conditional(s32[]{:T(128)} %bitcast, () %tuple.32, (bf16[1536,1536]{1,0:T(8,128)(2,1)S(1)}, ...), branch_computations={%region_0.0_spmd, %region_1.0_spmd} | conditional | flops 11002001408 | bytes 27474624 | solution.py:651
  42.1 9.1 %weight.1 = (f32[16,48,1152]{2,1,0:T(8,128)S(1)}, bf16[16,48,1152]{2,1,0:T(8,128)(2,1)S(1)}) custom-call(bf16[1536,1536]{1,0:T(8,128)(2,1)S(1)} %get-tuple-element.52.refs_0_, bf16[1536,1536]{1,0:T(8,128)(2,1)S(1)} %get-tuple-element.53.refs_1_, bf16[672,768]{1,0:T(8,128)(2,1)S(1)} %get-tuple-element.54.refs_2_, ...), custom_call_target="tpu_custom_call" | custom-call | flops 11000000512 | bytes 20000000 | tf_op jit(solution)/shard_map/cond/branch_1_fun/weight/pallas_call | solution.py:498
  51.2 0.1 collective-permute-start
  51.3 0.5 collective-permute-start.1
  51.8 0.2 zero_sum.1
  52.0 3.1 %collective-permute-done.1.small_got = f32[32,384]{1,0:T(8,128)S(1)} collective-permute-done((f32[32,384]{1,0:T(8,128)S(1)}, f32[32,384]{1,0:T(8,128)S(1)}, u32[]{:S(2)}, u32[]{:S(2)}) %collective-permute-start.1) | collective-permute-done | bytes 49184 | tf_op jit(solution)/shard_map/cond/branch_1_fun/ppermute | solution.py:642
  55.0 1.4 %core_sum.1 = (f32[8,48,640]{2,1,0:T(8,128)S(1)}, f32[8,48,512]{2,1,0:T(8,128)}, bf16[8,48,640]{2,1,0:T(8,128)(2,1)}, bf16[10,48,512]{2,1,0:T(8,128)(2,1)}, f32[32,384]{1,0:T(8,128)S(1)}) custom-call(f32[16,48,1152]{2,1,0:T(8,128)S(1)} %get-tuple-element.58.after.keep, bf16[16,48,1152]{2,1,0:T(8,128)(2,1)S(1)} %collective-permute-done.got, ...), custom_call_target="tpu_custom_call" | custom-call | flops 1000000 | bytes 100000 | tf_op jit(solution)/shard_map/cond/branch_1_fun/core_sum/pallas_call | solution.py:614
  56.4 1.5 %collective-permute-start.9 = (bf16[8,48,640]{2,1,0:T(8,128)(2,1)}, bf16[8,48,640]{2,1,0:T(8,128)(2,1)S(1)}, u32[]{:S(2)}, u32[]{:S(2)}) collective-permute-start(bf16[8,48,640]{2,1,0:T(8,128)(2,1)} %get-tuple-element.138), channel_id=1, source_target_pairs={{0,32},{4,36},{8,40},{12,44},{16,48},{20,52},{24,56},{28,60},{32,0... | collective-permute-start | bytes 1474568 | tf_op jit(solution)/shard_map/ppermute | solution.py:642
  57.9 1.6 %collective-permute-start.10 = (bf16[10,48,512]{2,1,0:T(8,128)(2,1)}, bf16[10,48,512]{2,1,0:T(8,128)(2,1)S(1)}, u32[]{:S(2)}, u32[]{:S(2)}) collective-permute-start(bf16[10,48,512]{2,1,0:T(8,128)(2,1)} %get-tuple-element.139), channel_id=1, source_target_pairs={{0,8},{4,12},{8,0},{12,4},{16,24},{20,28},{24,16},{28,20},{32,40},... | collective-permute-start | bytes 1474568 | tf_op jit(solution)/shard_map/ppermute | solution.py:642
  59.5 0.8 collective-permute-done.12.first_b
  60.3 1.7 %pass.1 = (bf16[480,384]{1,0:T(8,128)(2,1)S(1)}, bf16[480,384]{1,0:T(8,128)(2,1)S(1)}) custom-call(f32[480,768]{1,0:T(8,128)} %get-tuple-element.143.keep_a, f32[480,768]{1,0:T(8,128)} %get-tuple-element.144.keep_b, bf16[480,768]{1,0:T(8,128)(2,1)} %collective-permute-done.11.first_a, bf16[480,768]{1,0:T(8,128)(2,1)} %collective-permute-done.12.first_b), custom_call_target="tpu_custom_call" | custom-call | flops 1000000 | bytes 100000 | tf_op jit(solution)/shard_map/pass/pallas_call | solution.py:347
  62.0 12.4 %conditional.4 = (bf16[480,384]{1,0:T(8,128)(2,1)}, bf16[480,384]{1,0:T(8,128)(2,1)}) conditional(s32[]{:T(128)} %bitcast, () %tuple.34, (bf16[480,384]{1,0:T(8,128)(2,1)S(1)}, bf16[480,384]{1,0:T(8,128)(2,1)S(1)}) %pass.1), branch_computations={%region_2.0_spmd, %region_3.0_spmd} | conditional | bytes 2949216 | solution.py:651
  62.0 2.5 %collective-permute-start.2 = (bf16[480,384]{1,0:T(8,128)(2,1)S(1)}, bf16[480,384]{1,0:T(8,128)(2,1)}, u32[]{:S(2)}, u32[]{:S(2)}) collective-permute-start(bf16[480,384]{1,0:T(8,128)(2,1)S(1)} %get-tuple-element.66), channel_id=1, source_target_pairs={{0,3},{1,2},{2,1},{3,0},{4,7},{5,6},{6,5},{7,4},{8,11},{9,10},{10,... | collective-permute-start | bytes 1105928 | tf_op jit(solution)/shard_map/cond/branch_1_fun/ppermute | solution.py:728
  64.5 8.4 %collective-permute-done.2 = bf16[480,384]{1,0:T(8,128)(2,1)} collective-permute-done((bf16[480,384]{1,0:T(8,128)(2,1)S(1)}, bf16[480,384]{1,0:T(8,128)(2,1)}, u32[]{:S(2)}, u32[]{:S(2)}) %collective-permute-start.2) | collective-permute-done | bytes 368672 | tf_op jit(solution)/shard_map/cond/branch_1_fun/ppermute | solution.py:728
  72.9 1.5 %collective-permute-done.3 = bf16[480,384]{1,0:T(8,128)(2,1)} collective-permute-done((bf16[480,384]{1,0:T(8,128)(2,1)S(1)}, bf16[480,384]{1,0:T(8,128)(2,1)}, u32[]{:S(2)}, u32[]{:S(2)}) %collective-permute-start.3) | collective-permute-done | bytes 368672 | tf_op jit(solution)/shard_map/cond/branch_1_fun/ppermute | solution.py:728
  74.4 1.5 %half_sum.1 = (f32[4,48,640]{2,1,0:T(8,128)S(1)}, f32[4,48,512]{2,1,0:T(8,128)S(1)}, bf16[4,48,640]{2,1,0:T(8,128)(2,1)S(1)}, bf16[6,48,512]{2,1,0:T(8,128)(2,1)S(1)}, f32[32,384]{1,0:T(8,128)S(1)}) custom-call(f32[8,48,640]{2,1,0:T(8,128)S(1)} %get-tuple-element.135.own_x, f32[8,48,512]{2,1,0:T(8,128)} %get-tuple-element.136.own_y, ...), custom_call_target="tpu_custom_call" | custom-call | flops 1000000 | bytes 100000 | tf_op jit(solution)/shard_map/half_sum/pallas_call | solution.py:614
  75.9 0.1 copy-done.9
  76.0 0.1 copy-done.11
  76.1 7.4 %conditional.5 = (bf16[4,48,640]{2,1,0:T(8,128)(2,1)}, bf16[6,48,512]{2,1,0:T(8,128)(2,1)}, bf16[32,72,384]{2,1,0:T(8,128)(2,1)S(1)}) conditional(s32[]{:T(128)} %bitcast, () %tuple.31, (bf16[4,48,640]{2,1,0:T(8,128)(2,1)S(1)}, bf16[6,48,512]{2,1,0:T(8,128)(2,1)S(1)}, s32[1,32]{1,0:T(1,128)S(1)}, s32[1,32]{1,0:T(1,128)S(1)}, ...), branch_computations={%region_4.0_spmd, %region_5.0_spmd} | conditional | flops 1000000 | bytes 2310174 | solution.py:651
  76.1 0.6 collective-permute-start.5
  76.6 0.4 collective-permute-start.4
  77.0 3.1 %pick.1 = bf16[32,72,384]{2,1,0:T(8,128)(2,1)S(1)} custom-call(s32[1,32]{1,0:T(1,128)S(1)} %get-tuple-element.70.len_ref, s32[1,32]{1,0:T(1,128)S(1)} %get-tuple-element.167.owner_ref, bf16[576,384]{1,0:T(8,128)(2,1)S(1)} %get-tuple-element.72.held0, f32[480,768]{1,0:T(8,128)S(1)} %get-tuple-element.73.keep_a, f32[480,768]{1,0:T(8,128)} %get-tuple-element.74.keep_b, ...), custom_call_target="tpu_custom_call" | custom-call | flops 1000000 | bytes 100000 | tf_op jit(solution)/shard_map/cond/branch_1_fun/pick/pallas_call | solution.py:392
  80.2 2.8 %collective-permute-done.4 = bf16[4,48,640]{2,1,0:T(8,128)(2,1)} collective-permute-done((bf16[4,48,640]{2,1,0:T(8,128)(2,1)S(1)}, bf16[4,48,640]{2,1,0:T(8,128)(2,1)}, u32[]{:S(2)}, u32[]{:S(2)}) %collective-permute-start.4) | collective-permute-done | bytes 245792 | tf_op jit(solution)/shard_map/cond/branch_1_fun/ppermute | solution.py:642
  82.9 0.5 collective-permute-done.5
  83.5 1.2 copy-done.8
  84.7 6.9 %all-to-all-start = ((bf16[32,72,384]{2,1,0:T(8,128)(2,1)}), bf16[32,72,384]{2,1,0:T(8,128)(2,1)S(1)}, u32[]{:S(2)}, u32[]{:S(2)}) async-start(bf16[32,72,384]{2,1,0:T(8,128)(2,1)} %copy-done.8), calls=%async_computation | async-start | bytes 3538944 | tf_op jit(solution)/shard_map/all_to_all | solution.py:754
  91.6 1.2 square_sum.1
  92.7 5.3 %collective-permute-start.13 = (bf16[48,1920]{1,0:T(8,128)(2,1)S(1)}, bf16[48,1920]{1,0:T(8,128)(2,1)S(1)}, u32[]{:S(2)}, u32[]{:S(2)}) collective-permute-start(bf16[48,1920]{1,0:T(8,128)(2,1)S(1)} %get-tuple-element.158), channel_id=1, source_target_pairs={{0,120},{4,124},{8,112},{12,116},{16,104},{20,108},{24,96},{28,100... | collective-permute-start | bytes 552968 | tf_op jit(solution)/shard_map/ppermute | solution.py:642
  98.0 0.5 collective-permute-start.14
  98.5 0.2 collective-permute-start.15
  98.7 18.2 %all-to-all-done.src = bf16[32,72,384]{2,1,0:T(8,128)(2,1)S(1)} async-done(((bf16[32,72,384]{2,1,0:T(8,128)(2,1)}), bf16[32,72,384]{2,1,0:T(8,128)(2,1)S(1)}, u32[]{:S(2)}, u32[]{:S(2)}) %all-to-all-start) | async-done | bytes 1769504 | tf_op jit(solution)/shard_map/all_to_all | solution.py:754
  116.9 2.0 %order.1 = (bf16[32,72,384]{2,1,0:T(8,128)(2,1)}, f32[8,128]{1,0:T(8,128)S(1)}) custom-call(s32[1,32]{1,0:T(1,128)S(1)} %copy-done, bf16[32,72,384]{2,1,0:T(8,128)(2,1)S(1)} %all-to-all-done.src), custom_call_target="tpu_custom_call" | custom-call | flops 1000000 | bytes 100000 | tf_op jit(solution)/shard_map/order/pallas_call | solution.py:417
  119.0 2.1 %collective-permute-done.13.refs_2_ = bf16[48,1920]{1,0:T(8,128)(2,1)S(1)} collective-permute-done((bf16[48,1920]{1,0:T(8,128)(2,1)S(1)}, bf16[48,1920]{1,0:T(8,128)(2,1)S(1)}, u32[]{:S(2)}, u32[]{:S(2)}) %collective-permute-start.13) | collective-permute-done | bytes 184352 | tf_op jit(solution)/shard_map/ppermute | solution.py:642
  121.1 1.5 %collective-permute-done.14.refs_3_ = bf16[48,1920]{1,0:T(8,128)(2,1)S(1)} collective-permute-done((bf16[48,1920]{1,0:T(8,128)(2,1)S(1)}, bf16[48,1920]{1,0:T(8,128)(2,1)S(1)}, u32[]{:S(2)}, u32[]{:S(2)}) %collective-permute-start.14) | collective-permute-done | bytes 184352 | tf_op jit(solution)/shard_map/ppermute | solution.py:642
  122.6 0.8 last_sum.1
  (39 shorter events, 0.1 us)
Async XLA Ops:
  0.6 2.4 %copy-start.1 = (bf16[384,1536]{1,0:T(8,128)(2,1)S(1)}, bf16[384,1536]{1,0:T(8,128)(2,1)}, u32[]{:S(2)}) copy-start(bf16[384,1536]{1,0:T(8,128)(2,1)} %refs_4_.3) | copy-start | bytes 3538948
  0.6 2.4 %copy-start.2 = (f32[31,384]{1,0:T(8,128)S(1)}, f32[31,384]{1,0:T(8,128)}, u32[]{:S(2)}) copy-start(f32[31,384]{1,0:T(8,128)} %refs_5_.3) | copy-start | bytes 142852
  0.7 2.4 %copy-start.3 = (f32[384]{0:T(512)S(1)}, f32[384]{0:T(512)}, u32[]{:S(2)}) copy-start(f32[384]{0:T(512)} %refs_6_.3) | copy-start | bytes 4612
  0.7 2.4 %copy-start.4 = (f32[96,31]{1,0:T(8,128)S(1)}, f32[96,31]{1,0:T(8,128)}, u32[]{:S(2)}) copy-start(f32[96,31]{1,0:T(8,128)} %constant.19.clone.refs_9_) | copy-start | bytes 35716
  0.7 2.4 %copy-start.5 = (bf16[88,240]{1,0:T(8,128)(2,1)S(1)}, bf16[88,240]{1,0:T(8,128)(2,1)}, u32[]{:S(2)}) copy-start(bf16[88,240]{1,0:T(8,128)(2,1)} %constant.9.clone.refs_7_) | copy-start | bytes 126724
  0.7 2.4 %copy-start.6 = (bf16[80,256]{1,0:T(8,128)(2,1)S(1)}, bf16[80,256]{1,0:T(8,128)(2,1)}, u32[]{:S(2)}) copy-start(bf16[80,256]{1,0:T(8,128)(2,1)} %constant.17.clone.refs_8_) | copy-start | bytes 122884
  0.7 2.4 %copy-start.7 = (f32[31,96]{1,0:T(8,128)S(1)}, f32[31,96]{1,0:T(8,128)}, u32[]{:S(2)}) copy-start(f32[31,96]{1,0:T(8,128)} %constant.20.clone.refs_10_) | copy-start | bytes 35716
  0.7 2.4 %copy-start.12 = (s32[1,32]{1,0:T(1,128)S(1)}, s32[1,32]{1,0:T(1,128)}, u32[]{:S(2)}) copy-start(s32[1,32]{1,0:T(1,128)} %refs_0_.3) | copy-start | bytes 388
  0.7 21.9 %slice-start = ((s8[4718592]{0:T(1024)(128)(4,1)}), s8[4194304]{0:T(1024)(128)(4,1)S(1)}, s32[]{:S(2)}) async-start(s8[4718592]{0:T(1024)(128)(4,1)} %bitcast.9), calls=%async_computation.1 | async-start | bytes 8388608
  0.7 21.9 %slice-start.2 = ((s8[4718592]{0:T(1024)(128)(4,1)}), s8[4194304]{0:T(1024)(128)(4,1)S(1)}, s32[]{:S(2)}) async-start(s8[4718592]{0:T(1024)(128)(4,1)} %bitcast.11), calls=%async_computation.3 | async-start | bytes 8388608
  3.1 19.5 %slice-start.1 = ((s8[4718592]{0:T(1024)(128)(4,1)}), s8[524288]{0:T(1024)(128)(4,1)S(1)}, s32[]{:S(2)}) async-start(s8[4718592]{0:T(1024)(128)(4,1)} %bitcast.9), calls=%async_computation.2 | async-start | bytes 1048576
  3.1 19.5 %slice-start.3 = ((s8[4718592]{0:T(1024)(128)(4,1)}), s8[524288]{0:T(1024)(128)(4,1)S(1)}, s32[]{:S(2)}) async-start(s8[4718592]{0:T(1024)(128)(4,1)} %bitcast.11), calls=%async_computation.4 | async-start | bytes 1048576
  16.0 26.1 %collective-permute-start.6 = (bf16[576,384]{1,0:T(8,128)(2,1)S(1)}, bf16[576,384]{1,0:T(8,128)(2,1)S(1)}, u32[]{:S(2)}, u32[]{:S(2)}) collective-permute-start(bf16[576,384]{1,0:T(8,128)(2,1)S(1)} %get-tuple-element.131), channel_id=1, source_target_pairs={{0,1},{1,2},{2,3},{3,0},{4,5},{5,6},{6,7},{7,4},{8,9},{9,10},{10,1... | collective-permute-start | bytes 1327112 | tf_op jit(solution)/shard_map/ppermute | solution.py:690
  18.0 24.0 %collective-permute-start.7 = (bf16[576,384]{1,0:T(8,128)(2,1)S(1)}, bf16[576,384]{1,0:T(8,128)(2,1)S(1)}, u32[]{:S(2)}, u32[]{:S(2)}) collective-permute-start(bf16[576,384]{1,0:T(8,128)(2,1)S(1)} %get-tuple-element.132), channel_id=1, source_target_pairs={{0,2},{1,3},{2,0},{3,1},{4,6},{5,7},{6,4},{7,5},{8,10},{9,11},{10,... | collective-permute-start | bytes 1327112 | tf_op jit(solution)/shard_map/ppermute | solution.py:691
  21.6 20.4 %collective-permute-start.8 = (bf16[576,384]{1,0:T(8,128)(2,1)S(1)}, bf16[576,384]{1,0:T(8,128)(2,1)S(1)}, u32[]{:S(2)}, u32[]{:S(2)}) collective-permute-start(bf16[576,384]{1,0:T(8,128)(2,1)S(1)} %get-tuple-element.133), channel_id=1, source_target_pairs={{0,3},{1,0},{2,1},{3,2},{4,7},{5,4},{6,5},{7,6},{8,11},{9,8},{10,9... | collective-permute-start | bytes 1327112 | tf_op jit(solution)/shard_map/ppermute | solution.py:692
  40.8 18.8 %collective-permute-start.11 = (bf16[480,768]{1,0:T(8,128)(2,1)S(1)}, bf16[480,768]{1,0:T(8,128)(2,1)}, u32[]{:S(2)}, u32[]{:S(2)}) collective-permute-start(bf16[480,768]{1,0:T(8,128)(2,1)S(1)} %get-tuple-element.145), channel_id=1, source_target_pairs={{0,1},{1,0},{2,3},{3,2},{4,5},{5,4},{6,7},{7,6},{8,9},{9,8},{10,11... | collective-permute-start | bytes 2211848 | tf_op jit(solution)/shard_map/ppermute | solution.py:731
  41.9 18.4 %collective-permute-start.12 = (bf16[480,768]{1,0:T(8,128)(2,1)S(1)}, bf16[480,768]{1,0:T(8,128)(2,1)}, u32[]{:S(2)}, u32[]{:S(2)}) collective-permute-start(bf16[480,768]{1,0:T(8,128)(2,1)S(1)} %get-tuple-element.146), channel_id=1, source_target_pairs={{0,3},{1,2},{2,1},{3,0},{4,7},{5,6},{6,5},{7,4},{8,11},{9,10},{10,... | collective-permute-start | bytes 2211848 | tf_op jit(solution)/shard_map/ppermute | solution.py:732
  51.2 3.8 %collective-permute-start = (bf16[16,48,1152]{2,1,0:T(8,128)(2,1)S(1)}, bf16[16,48,1152]{2,1,0:T(8,128)(2,1)S(1)}, u32[]{:S(2)}, u32[]{:S(2)}) collective-permute-start(bf16[16,48,1152]{2,1,0:T(8,128)(2,1)S(1)} %get-tuple-element.59), channel_id=1, source_target_pairs={{0,4},{4,0},{8,12},{12,8},{16,20},{20,16},{24,28},{28,24},{32,36},... | collective-permute-start | bytes 5308424 | tf_op jit(solution)/shard_map/cond/branch_1_fun/ppermute | solution.py:642
  51.3 3.7 %collective-permute-start.1 = (f32[32,384]{1,0:T(8,128)S(1)}, f32[32,384]{1,0:T(8,128)S(1)}, u32[]{:S(2)}, u32[]{:S(2)}) collective-permute-start(f32[32,384]{1,0:T(8,128)S(1)} %get-tuple-element.60.small), channel_id=1, source_target_pairs={{0,4},{4,0},{8,12},{12,8},{16,20},{20,16},{24,28},{28,24},{32,36},... | collective-permute-start | bytes 147464 | tf_op jit(solution)/shard_map/cond/branch_1_fun/ppermute | solution.py:642
  56.4 5.5 %copy-start.10 = (bf16[576,384]{1,0:T(8,128)(2,1)}, bf16[576,384]{1,0:T(8,128)(2,1)S(1)}, u32[]{:S(2)}) copy-start(bf16[576,384]{1,0:T(8,128)(2,1)S(1)} %get-tuple-element.142) | copy-start | bytes 1327108
  56.4 17.9 %collective-permute-start.9 = (bf16[8,48,640]{2,1,0:T(8,128)(2,1)}, bf16[8,48,640]{2,1,0:T(8,128)(2,1)S(1)}, u32[]{:S(2)}, u32[]{:S(2)}) collective-permute-start(bf16[8,48,640]{2,1,0:T(8,128)(2,1)} %get-tuple-element.138), channel_id=1, source_target_pairs={{0,32},{4,36},{8,40},{12,44},{16,48},{20,52},{24,56},{28,60},{32,0... | collective-permute-start | bytes 1474568 | tf_op jit(solution)/shard_map/ppermute | solution.py:642
  57.9 16.5 %collective-permute-start.10 = (bf16[10,48,512]{2,1,0:T(8,128)(2,1)}, bf16[10,48,512]{2,1,0:T(8,128)(2,1)S(1)}, u32[]{:S(2)}, u32[]{:S(2)}) collective-permute-start(bf16[10,48,512]{2,1,0:T(8,128)(2,1)} %get-tuple-element.139), channel_id=1, source_target_pairs={{0,8},{4,12},{8,0},{12,4},{16,24},{20,28},{24,16},{28,20},{32,40},... | collective-permute-start | bytes 1474568 | tf_op jit(solution)/shard_map/ppermute | solution.py:642
  62.0 13.9 %copy-start.13 = (s32[1,32]{1,0:T(1,128)S(1)}, s32[1,32]{1,0:T(1,128)}, u32[]{:S(2)}) copy-start(s32[1,32]{1,0:T(1,128)} %param.26) | copy-start | bytes 388
  62.0 10.9 %collective-permute-start.2 = (bf16[480,384]{1,0:T(8,128)(2,1)S(1)}, bf16[480,384]{1,0:T(8,128)(2,1)}, u32[]{:S(2)}, u32[]{:S(2)}) collective-permute-start(bf16[480,384]{1,0:T(8,128)(2,1)S(1)} %get-tuple-element.66), channel_id=1, source_target_pairs={{0,3},{1,2},{2,1},{3,0},{4,7},{5,6},{6,5},{7,4},{8,11},{9,10},{10,... | collective-permute-start | bytes 1105928 | tf_op jit(solution)/shard_map/cond/branch_1_fun/ppermute | solution.py:728
  64.5 9.9 %collective-permute-start.3 = (bf16[480,384]{1,0:T(8,128)(2,1)S(1)}, bf16[480,384]{1,0:T(8,128)(2,1)}, u32[]{:S(2)}, u32[]{:S(2)}) collective-permute-start(bf16[480,384]{1,0:T(8,128)(2,1)S(1)} %get-tuple-element.67), channel_id=1, source_target_pairs={{0,1},{1,0},{2,3},{3,2},{4,5},{5,4},{6,7},{7,6},{8,9},{9,8},{10,11... | collective-permute-start | bytes 1105928 | tf_op jit(solution)/shard_map/cond/branch_1_fun/ppermute | solution.py:728
  74.4 1.6 %copy-start.9 = (f32[480,768]{1,0:T(8,128)S(1)}, f32[480,768]{1,0:T(8,128)}, u32[]{:S(2)}) copy-start(f32[480,768]{1,0:T(8,128)} %get-tuple-element.143.keep_a) | copy-start | bytes 4423684
  74.4 1.7 %copy-start.11 = (bf16[576,384]{1,0:T(8,128)(2,1)S(1)}, bf16[576,384]{1,0:T(8,128)(2,1)}, u32[]{:S(2)}) copy-start(bf16[576,384]{1,0:T(8,128)(2,1)} %copy-done.10) | copy-start | bytes 1327108
  76.1 7.4 %collective-permute-start.5 = (bf16[6,48,512]{2,1,0:T(8,128)(2,1)S(1)}, bf16[6,48,512]{2,1,0:T(8,128)(2,1)}, u32[]{:S(2)}, u32[]{:S(2)}) collective-permute-start(bf16[6,48,512]{2,1,0:T(8,128)(2,1)S(1)} %get-tuple-element.69), channel_id=1, source_target_pairs={{0,32},{4,36},{8,40},{12,44},{16,48},{20,52},{24,56},{28,60},{32,0... | collective-permute-start | bytes 884744 | tf_op jit(solution)/shard_map/cond/branch_1_fun/ppermute | solution.py:642
  76.6 6.3 %collective-permute-start.4 = (bf16[4,48,640]{2,1,0:T(8,128)(2,1)S(1)}, bf16[4,48,640]{2,1,0:T(8,128)(2,1)}, u32[]{:S(2)}, u32[]{:S(2)}) collective-permute-start(bf16[4,48,640]{2,1,0:T(8,128)(2,1)S(1)} %get-tuple-element.68), channel_id=1, source_target_pairs={{0,8},{4,12},{8,0},{12,4},{16,24},{20,28},{24,16},{28,20},{32,40},... | collective-permute-start | bytes 737288 | tf_op jit(solution)/shard_map/cond/branch_1_fun/ppermute | solution.py:642
  83.5 1.2 copy-start.8
  84.7 32.3 %copy-start = (s32[1,32]{1,0:T(1,128)S(1)}, s32[1,32]{1,0:T(1,128)}, u32[]{:S(2)}) copy-start(s32[1,32]{1,0:T(1,128)} %slot_ref.1) | copy-start | bytes 388
  84.7 32.3 %all-to-all-start = ((bf16[32,72,384]{2,1,0:T(8,128)(2,1)}), bf16[32,72,384]{2,1,0:T(8,128)(2,1)S(1)}, u32[]{:S(2)}, u32[]{:S(2)}) async-start(bf16[32,72,384]{2,1,0:T(8,128)(2,1)} %copy-done.8), calls=%async_computation | async-start | bytes 3538944 | tf_op jit(solution)/shard_map/all_to_all | solution.py:754
  92.7 28.4 %collective-permute-start.13 = (bf16[48,1920]{1,0:T(8,128)(2,1)S(1)}, bf16[48,1920]{1,0:T(8,128)(2,1)S(1)}, u32[]{:S(2)}, u32[]{:S(2)}) collective-permute-start(bf16[48,1920]{1,0:T(8,128)(2,1)S(1)} %get-tuple-element.158), channel_id=1, source_target_pairs={{0,120},{4,124},{8,112},{12,116},{16,104},{20,108},{24,96},{28,100... | collective-permute-start | bytes 552968 | tf_op jit(solution)/shard_map/ppermute | solution.py:642
  98.0 24.5 %collective-permute-start.14 = (bf16[48,1920]{1,0:T(8,128)(2,1)S(1)}, bf16[48,1920]{1,0:T(8,128)(2,1)S(1)}, u32[]{:S(2)}, u32[]{:S(2)}) collective-permute-start(bf16[48,1920]{1,0:T(8,128)(2,1)S(1)} %get-tuple-element.159), channel_id=1, source_target_pairs={{0,96},{4,100},{8,104},{12,108},{16,112},{20,116},{24,120},{28,124... | collective-permute-start | bytes 552968 | tf_op jit(solution)/shard_map/ppermute | solution.py:642
  98.5 24.1 %collective-permute-start.15 = (bf16[48,1920]{1,0:T(8,128)(2,1)S(1)}, bf16[48,1920]{1,0:T(8,128)(2,1)S(1)}, u32[]{:S(2)}, u32[]{:S(2)}) collective-permute-start(bf16[48,1920]{1,0:T(8,128)(2,1)S(1)} %get-tuple-element.160), channel_id=1, source_target_pairs={{0,24},{4,28},{8,16},{12,20},{16,8},{20,12},{24,0},{28,4},{32,56},... | collective-permute-start | bytes 552968 | tf_op jit(solution)/shard_map/ppermute | solution.py:642

commit v7 on v6

--- a/solution.py
+++ b/solution.py
@@ -651,8 +651,8 @@
     return lax.cond(live, stage, never, *operands)
 
 
-def on_device(
-    frames, grad_out, w_in, conv_kernel, conv_bias, w_out, seg_lengths, seg_owner, slot_device
+def until_owners(
+    frames, grad_out, w_in, conv_kernel, conv_bias, w_out, seg_lengths, seg_owner
 ):
     count_dev = lax.axis_size("dp")
     rows, width = frames.shape
@@ -733,7 +733,7 @@
         held0, own_x, own_y, send_x, send_y, small = together(live, weight_stage, *operands)
         got_x, got_y = move(send_x, fx=near), move(send_y, fy=near)
         send_a, send_b = pass_call(keep_a, keep_b, first_a, first_b)
-        last_a, last_b = together(live, last_stage, send_a, send_b)
+        last_a, last_b = last_stage(send_a, send_b)
         return first_a, first_b, held0, own_x, own_y, small, got_x, got_y, last_a, last_b
 
     def third_stage(send_x, send_y, *operands):
@@ -747,9 +747,24 @@
     own_x, own_y, send_x, send_y, small = sum_call(
         half_sum_kernel, "half_sum", TINY, halves(4, deep, wide, small), own_x, own_y, small, got_x, got_y
     )
-    got_x, got_y, outgoing = together(
-        live, third_stage, send_x, send_y,
+    got_x, got_y, outgoing = third_stage(
+        send_x, send_y,
         seg_lengths, seg_owner, held0, keep_a, keep_b, first_a, first_b, last_a, last_b,
+    )
+    return outgoing, own_x, own_y, small, got_x, got_y
+
+
+def on_device(
+    frames, grad_out, w_in, conv_kernel, conv_bias, w_out, seg_lengths, seg_owner, slot_device
+):
+    rows, width = frames.shape
+    ch = w_out.shape[0]
+    count_dev = lax.axis_size("dp")
+    scale = 1.0 / math.sqrt(rows * count_dev)
+    deep, wide = width // count_dev, 3 * ch
+    outgoing, own_x, own_y, small, got_x, got_y = together(
+        seg_lengths[0, 0] > 0, until_owners,
+        frames, grad_out, w_in, conv_kernel, conv_bias, w_out, seg_lengths, seg_owner,
     )
     received = lax.all_to_all(outgoing, "dp", split_axis=0, concat_axis=0, tiled=True)
     dx_frames, done = order_call(slot_device, received)

time: 124 us -> 121 us (0.976)
  waiting for transfers between devices: 38.8 us -> 36.7 us
  local copies, waits for them, and re-layouts: 3.79 us -> 2.38 us
    ppermute x2, waiting for transfers between devices: 9.89 us -> 1.22 us  [last_stage(): return (lax.ppermute(send_a, 'mp', cross), lax.ppermute(send_b, 'mp', pair))]
    ppermute x9, waiting for transfers between devices: 9.96 us -> 13.8 us  [move(): lax.ppermute(array, 'dp', [(i, to(i)) for i in range(lax.axis_size('dp'))])]
    unnamed x37 -> x4, local copies, waits for them, and re-layouts: 3.79 us -> 0.01 us
    cond x0 -> x27, local copies, waits for them, and re-layouts: none -> 2.38 us
    ppermute x2, starting transfers between devices: 2.47 us -> 0.45 us  [last_stage(): return (lax.ppermute(send_a, 'mp', cross), lax.ppermute(send_b, 'mp', pair))]
    ppermute x1, waiting for transfers between devices: 0.01 us -> 1.6 us  [first_stage(): first_a = lax.ppermute(send_a, 'mp', pair)]
    pallas_call x5, Pallas kernels: 5.03 us -> 3.7 us  [sum_call(): pl.pallas_call(kernel, out_shape=out_shape, in_specs=[vm] * len(operands)...]
  transfers between devices with their start and end apart: 17 -> 17, of which waited for: 9 -> 10; matrix products, arithmetic and copies ran while one was open for 0% -> 0% of each run, Pallas kernels for 30% -> 31%
where the time goes in v7:
time: 121 us; the launch traced here: 119 us
  Pallas kernels  51.6 us (43%)
  waiting for transfers between devices  36.7 us (30%)
  starting transfers between devices  27.2 us (22%)
  local copies, waits for them, and re-layouts  2.38 us (2%)
  between operations  1.32 us (1%)
    pallas_call x2, Pallas kernels, chunk_call(): pl.pallas_call(body, out_shape=out_shape, in_specs=specs, out_specs=[vm]...  31.8 us
    all_to_all x1, waiting for transfers between devices, on_device(): lax.all_to_all(outgoing, 'dp', split_axis=0, concat_axis=0, tiled=True)  18.1 us
    ppermute x9, waiting for transfers between devices, move(): lax.ppermute(array, 'dp', [(i, to(i)) for i in range(lax.axis_size('dp'))])  13.8 us
    ppermute x9, starting transfers between devices, move(): lax.ppermute(array, 'dp', [(i, to(i)) for i in range(lax.axis_size('dp'))])  11.6 us
    pallas_call x1, Pallas kernels, weight_call(): pl.pallas_call(lambda *refs: weight_kernel(deep, *refs), out_shape=(jax.S...  8.79 us
    all_to_all x1, starting transfers between devices, on_device(): lax.all_to_all(outgoing, 'dp', split_axis=0, concat_axis=0, tiled=True)  7.03 us
    pallas_call x1, Pallas kernels, pick_call(): pl.pallas_call(pick_kernel, grid=(1,), out_shape=jax.ShapeDtypeStruct((SE...  3.97 us
    pallas_call x5, Pallas kernels, sum_call(): pl.pallas_call(kernel, out_shape=out_shape, in_specs=[vm] * len(operands)...  3.7 us
  transfers between devices with their start and end apart: 17, of which 10 were waited for; matrix products, arithmetic and copies ran while one was open for 0% of the time, Pallas kernels for 31%

profile of v7, /device:TPU:0, one launch (start us, length us, event | category | flops | bytes accessed | tf_op | source)
XLA Modules:
  0.0 119.5 jit_solution(4619309885578107677)
XLA Ops:
  1.3 79.4 %conditional.2 = (bf16[32,72,384]{2,1,0:T(8,128)(2,1)}, f32[4,48,640]{2,1,0:T(8,128)}, f32[4,48,512]{2,1,0:T(8,128)}, f32[32,384]{1,0:T(8,128)S(1)}, bf16[4,48,6...) conditional(s32[]{:T(128)} %bitcast.1, () %tuple.24, (s32[1,32]{1,0:T(1,128)}, bf16[1536,2,384]{2,1,0:T(2,128)(2,1)}, ...), branch_computations={%region_0.0_spmd, %region_1.0_spmd} | conditional | flops 51004997632 | bytes 126400592 | solution.py:651
  1.3 0.0 copy-start.1
  1.3 0.0 copy-start.2
  1.3 0.0 copy-start.3
  1.3 0.0 copy-start.4
  1.4 0.0 slice-start
  1.4 0.0 slice-start.2
  1.4 2.3 %copy.29 = bf16[192,8,2,384]{3,1,2,0:T(8,128)(2,1)S(1)} copy(bf16[192,8,2,384]{3,2,1,0:T(2,128)(2,1)} %bitcast.9) | data formatting | bytes 4718592 | tf_op jit(solution)/shard_map/cond
  3.7 0.0 slice-start.1
  3.7 0.0 slice-start.3
  3.8 14.0 %chunk0.1 = (bf16[672,768]{1,0:T(8,128)(2,1)}, bf16[672,384]{1,0:T(8,128)(2,1)S(1)}, f32[104,384]{1,0:T(8,128)S(1)}, f32[576,384]{1,0:T(8,128)S(1)}, bf16[576,38...) custom-call(s32[1,32]{1,0:T(1,128)S(1)} %copy-done.6, ...), custom_call_target="tpu_custom_call" | custom-call | flops 20000000000 | bytes 20000000 | tf_op jit(solution)/shard_map/cond/branch_1_fun/chunk0/pallas_call | solution.py:304
  17.8 2.1 %collective-permute-start.2 = (bf16[576,384]{1,0:T(8,128)(2,1)S(1)}, bf16[576,384]{1,0:T(8,128)(2,1)S(1)}, u32[]{:S(2)}, u32[]{:S(2)}) collective-permute-start(bf16[576,384]{1,0:T(8,128)(2,1)S(1)} %get-tuple-element.82), channel_id=1, source_target_pairs={{0,1},{1,2},{2,3},{3,0},{4,5},{5,6},{6,7},{7,4},{8,9},{9,10},{10,1... | collective-permute-start | bytes 1327112 | tf_op jit(solution)/shard_map/cond/branch_1_fun/ppermute | solution.py:690
  19.8 3.6 %collective-permute-start.3 = (bf16[576,384]{1,0:T(8,128)(2,1)S(1)}, bf16[576,384]{1,0:T(8,128)(2,1)S(1)}, u32[]{:S(2)}, u32[]{:S(2)}) collective-permute-start(bf16[576,384]{1,0:T(8,128)(2,1)S(1)} %get-tuple-element.83), channel_id=1, source_target_pairs={{0,2},{1,3},{2,0},{3,1},{4,6},{5,7},{6,4},{7,5},{8,10},{9,11},{10,... | collective-permute-start | bytes 1327112 | tf_op jit(solution)/shard_map/cond/branch_1_fun/ppermute | solution.py:691
  23.4 1.0 collective-permute-start.4
  24.5 17.8 %chunk576.1 = (bf16[960,768]{1,0:T(8,128)(2,1)}, bf16[960,384]{1,0:T(8,128)(2,1)}, f32[32,384]{1,0:T(8,128)S(1)}, bf16[480,768]{1,0:T(8,128)(2,1)}, bf16[480,768...) custom-call(s32[1,32]{1,0:T(1,128)S(1)} %copy-done.6, bf16[1536,1536]{1,0:T(8,128)(2,1)S(1)} %bitcast.13, ...), custom_call_target="tpu_custom_call" | custom-call | flops 20000000000 | bytes 20000000 | tf_op jit(solution)/shard_map/cond/branch_1_fun/chunk576/pallas_call | solution.py:304
  42.3 1.3 %collective-permute-start.5 = (bf16[480,768]{1,0:T(8,128)(2,1)}, bf16[480,768]{1,0:T(8,128)(2,1)}, u32[]{:S(2)}, u32[]{:S(2)}) collective-permute-start(bf16[480,768]{1,0:T(8,128)(2,1)} %get-tuple-element.89), channel_id=1, source_target_pairs={{0,1},{1,0},{2,3},{3,2},{4,5},{5,4},{6,7},{7,6},{8,9},{9,8},{10,11... | collective-permute-start | bytes 2211848 | tf_op jit(solution)/shard_map/cond/branch_1_fun/ppermute | solution.py:731
  43.6 0.1 collective-permute-start.6
  43.8 13.0 %conditional = (bf16[576,384]{1,0:T(8,128)(2,1)S(1)}, f32[8,48,640]{2,1,0:T(8,128)S(1)}, f32[8,48,512]{2,1,0:T(8,128)S(1)}, bf16[8,48,640]{2,1,0:T(8,128)(2,1)S(...) conditional(s32[]{:T(128)} %bitcast, () %tuple.17, (bf16[1536,1536]{1,0:T(8,128)(2,1)S(1)}, ...), branch_computations={%region_2.0_spmd, %region_3.0_spmd} | conditional | flops 11002001408 | bytes 27474624 | solution.py:651
  43.8 8.8 %weight.1 = (f32[16,48,1152]{2,1,0:T(8,128)S(1)}, bf16[16,48,1152]{2,1,0:T(8,128)(2,1)S(1)}) custom-call(bf16[1536,1536]{1,0:T(8,128)(2,1)S(1)} %get-tuple-element.50.refs_0_, bf16[1536,1536]{1,0:T(8,128)(2,1)S(1)} %get-tuple-element.51.refs_1_, bf16[672,768]{1,0:T(8,128)(2,1)} %get-tuple-element.52.refs_2_, bf16[960,768]{1,0:T(8,128)(2,1)} %get-tuple-element.53.refs_3_, ...), custom_call_target="tpu_custom_call" | custom-call | flops 11000000512 | bytes 20000000 | tf_op jit(solution)/shard_map/cond/branch_1_fun/cond/branch_1_fun/weight/pallas_call | solution.py:498
  52.6 0.1 collective-permute-start
  52.7 0.5 collective-permute-start.1
  53.2 0.2 zero_sum.1
  53.4 3.1 %collective-permute-done.1.small_got = f32[32,384]{1,0:T(8,128)S(1)} collective-permute-done((f32[32,384]{1,0:T(8,128)S(1)}, f32[32,384]{1,0:T(8,128)S(1)}, u32[]{:S(2)}, u32[]{:S(2)}) %collective-permute-start.1) | collective-permute-done | bytes 49184 | tf_op jit(solution)/shard_map/cond/branch_1_fun/cond/branch_1_fun/ppermute | solution.py:642
  56.5 0.3 core_sum.1
  56.8 1.7 %collective-permute-start.10 = (bf16[10,48,512]{2,1,0:T(8,128)(2,1)S(1)}, bf16[10,48,512]{2,1,0:T(8,128)(2,1)S(1)}, u32[]{:S(2)}, u32[]{:S(2)}) collective-permute-start(bf16[10,48,512]{2,1,0:T(8,128)(2,1)S(1)} %get-tuple-element.97), channel_id=1, source_target_pairs={{0,8},{4,12},{8,0},{12,4},{16,24},{20,28},{24,16},{28,20},{32,40},... | collective-permute-start | bytes 1474568 | tf_op jit(solution)/shard_map/cond/branch_1_fun/ppermute | solution.py:642
  58.4 1.5 %collective-permute-start.9 = (bf16[8,48,640]{2,1,0:T(8,128)(2,1)S(1)}, bf16[8,48,640]{2,1,0:T(8,128)(2,1)S(1)}, u32[]{:S(2)}, u32[]{:S(2)}) collective-permute-start(bf16[8,48,640]{2,1,0:T(8,128)(2,1)S(1)} %get-tuple-element.96), channel_id=1, source_target_pairs={{0,32},{4,36},{8,40},{12,44},{16,48},{20,52},{24,56},{28,60},{32,0... | collective-permute-start | bytes 1474568 | tf_op jit(solution)/shard_map/cond/branch_1_fun/ppermute | solution.py:642
  59.9 1.6 %collective-permute-done.5.first_a = bf16[480,768]{1,0:T(8,128)(2,1)} collective-permute-done((bf16[480,768]{1,0:T(8,128)(2,1)}, bf16[480,768]{1,0:T(8,128)(2,1)}, u32[]{:S(2)}, u32[]{:S(2)}) %collective-permute-start.5) | collective-permute-done | bytes 737312 | tf_op jit(solution)/shard_map/cond/branch_1_fun/ppermute | solution.py:731
  61.5 2.0 %collective-permute-done.6.first_b = bf16[480,768]{1,0:T(8,128)(2,1)} collective-permute-done((bf16[480,768]{1,0:T(8,128)(2,1)}, bf16[480,768]{1,0:T(8,128)(2,1)}, u32[]{:S(2)}, u32[]{:S(2)}) %collective-permute-start.6) | collective-permute-done | bytes 737312 | tf_op jit(solution)/shard_map/cond/branch_1_fun/ppermute | solution.py:732
  63.5 1.3 %pass.1 = (bf16[480,384]{1,0:T(8,128)(2,1)S(1)}, bf16[480,384]{1,0:T(8,128)(2,1)S(1)}) custom-call(f32[480,768]{1,0:T(8,128)S(1)} %get-tuple-element.87.keep_a, f32[480,768]{1,0:T(8,128)S(1)} %get-tuple-element.88.keep_b, bf16[480,768]{1,0:T(8,128)(2,1)} %collective-permute-done.5.first_a, bf16[480,768]{1,0:T(8,128)(2,1)} %collective-permute-done.6.first_b), custom_call_target="tpu_custom_call" | custom-call | flops 1000000 | bytes 100000 | tf_op jit(solution)/shard_map/cond/branch_1_fun/pass/pallas_call | solution.py:347
  64.8 0.5 collective-permute-start.7
  65.3 4.9 %collective-permute-done.10.got_y = bf16[10,48,512]{2,1,0:T(8,128)(2,1)S(1)} collective-permute-done((bf16[10,48,512]{2,1,0:T(8,128)(2,1)S(1)}, bf16[10,48,512]{2,1,0:T(8,128)(2,1)S(1)}, u32[]{:S(2)}, u32[]{:S(2)}) %collective-permute-start.10) | collective-permute-done | bytes 491552 | tf_op jit(solution)/shard_map/cond/branch_1_fun/ppermute | solution.py:642
  70.1 1.3 %collective-permute-done.9.got_x = bf16[8,48,640]{2,1,0:T(8,128)(2,1)S(1)} collective-permute-done((bf16[8,48,640]{2,1,0:T(8,128)(2,1)S(1)}, bf16[8,48,640]{2,1,0:T(8,128)(2,1)S(1)}, u32[]{:S(2)}, u32[]{:S(2)}) %collective-permute-start.9) | collective-permute-done | bytes 491552 | tf_op jit(solution)/shard_map/cond/branch_1_fun/ppermute | solution.py:642
  71.4 1.1 half_sum.1
  72.5 1.5 %collective-permute-start.12 = (bf16[6,48,512]{2,1,0:T(8,128)(2,1)S(1)}, bf16[6,48,512]{2,1,0:T(8,128)(2,1)}, u32[]{:S(2)}, u32[]{:S(2)}) collective-permute-start(bf16[6,48,512]{2,1,0:T(8,128)(2,1)S(1)} %get-tuple-element.102), channel_id=1, source_target_pairs={{0,32},{4,36},{8,40},{12,44},{16,48},{20,52},{24,56},{28,60},{32,0... | collective-permute-start | bytes 884744 | tf_op jit(solution)/shard_map/cond/branch_1_fun/ppermute | solution.py:642
  74.0 0.5 collective-permute-start.11
  74.5 1.2 %collective-permute-done.7.last_a = bf16[480,384]{1,0:T(8,128)(2,1)S(1)} collective-permute-done((bf16[480,384]{1,0:T(8,128)(2,1)S(1)}, bf16[480,384]{1,0:T(8,128)(2,1)S(1)}, u32[]{:S(2)}, u32[]{:S(2)}) %collective-permute-start.7) | collective-permute-done | bytes 368672 | tf_op jit(solution)/shard_map/cond/branch_1_fun/ppermute | solution.py:728
  75.7 4.0 %pick.1 = bf16[32,72,384]{2,1,0:T(8,128)(2,1)} custom-call(s32[1,32]{1,0:T(1,128)S(1)} %copy-done.6, s32[1,32]{1,0:T(1,128)S(1)} %copy-done.7, bf16[576,384]{1,0:T(8,128)(2,1)S(1)} %get-tuple-element.86.held0, f32[480,768]{1,0:T(8,128)S(1)} %get-tuple-element.87.keep_a, f32[480,768]{1,0:T(8,128)S(1)} %get-tuple-element.88.keep_b, ...), custom_call_target="tpu_custom_call" | custom-call | flops 1000000 | bytes 100000 | tf_op jit(solution)/shard_map/cond/branch_1_fun/pick/pallas_call | solution.py:392
  79.7 1.0 collective-permute-done.11
  80.7 7.0 %all-to-all-start = ((bf16[32,72,384]{2,1,0:T(8,128)(2,1)}), bf16[32,72,384]{2,1,0:T(8,128)(2,1)S(1)}, u32[]{:S(2)}, u32[]{:S(2)}) async-start(bf16[32,72,384]{2,1,0:T(8,128)(2,1)} %get-tuple-element.125), calls=%async_computation | async-start | bytes 3538944 | tf_op jit(solution)/shard_map/all_to_all | solution.py:769
  87.7 1.3 %square_sum.1 = (f32[48,1152]{1,0:T(8,128)S(1)}, f32[32,384]{1,0:T(8,128)S(1)}, bf16[48,1920]{1,0:T(8,128)(2,1)S(1)}, bf16[48,1920]{1,0:T(8,128)(2,1)S(1)}, bf16[48,1920]{1,0:T(8,128)(2,1)S(1)}) custom-call(f32[4,48,640]{2,1,0:T(8,128)S(1)} %copy-done.5, f32[4,48,512]{2,1,0:T(8,128)} %get-tuple-element.128.own_y, f32[32,384]{1,0:T(8,128)S(1)} %get-tuple-element.129.small, ...), custom_call_target="tpu_custom_call" | custom-call | flops 1000000 | bytes 100000 | tf_op jit(solution)/shard_map/square_sum/pallas_call | solution.py:614
  89.1 5.3 %collective-permute-start.13 = (bf16[48,1920]{1,0:T(8,128)(2,1)S(1)}, bf16[48,1920]{1,0:T(8,128)(2,1)S(1)}, u32[]{:S(2)}, u32[]{:S(2)}) collective-permute-start(bf16[48,1920]{1,0:T(8,128)(2,1)S(1)} %get-tuple-element.134), channel_id=1, source_target_pairs={{0,120},{4,124},{8,112},{12,116},{16,104},{20,108},{24,96},{28,100... | collective-permute-start | bytes 552968 | tf_op jit(solution)/shard_map/ppermute | solution.py:642
  94.3 0.5 collective-permute-start.14
  94.8 0.2 collective-permute-start.15
  95.1 18.1 %all-to-all-done.src = bf16[32,72,384]{2,1,0:T(8,128)(2,1)S(1)} async-done(((bf16[32,72,384]{2,1,0:T(8,128)(2,1)}), bf16[32,72,384]{2,1,0:T(8,128)(2,1)S(1)}, u32[]{:S(2)}, u32[]{:S(2)}) %all-to-all-start) | async-done | bytes 1769504 | tf_op jit(solution)/shard_map/all_to_all | solution.py:769
  113.1 2.0 %order.1 = (bf16[32,72,384]{2,1,0:T(8,128)(2,1)}, f32[8,128]{1,0:T(8,128)S(1)}) custom-call(s32[1,32]{1,0:T(1,128)S(1)} %copy-done, bf16[32,72,384]{2,1,0:T(8,128)(2,1)S(1)} %all-to-all-done.src), custom_call_target="tpu_custom_call" | custom-call | flops 1000000 | bytes 100000 | tf_op jit(solution)/shard_map/order/pallas_call | solution.py:417
  115.1 2.1 %collective-permute-done.13.refs_2_ = bf16[48,1920]{1,0:T(8,128)(2,1)S(1)} collective-permute-done((bf16[48,1920]{1,0:T(8,128)(2,1)S(1)}, bf16[48,1920]{1,0:T(8,128)(2,1)S(1)}, u32[]{:S(2)}, u32[]{:S(2)}) %collective-permute-start.13) | collective-permute-done | bytes 184352 | tf_op jit(solution)/shard_map/ppermute | solution.py:642
  117.3 1.5 %collective-permute-done.14.refs_3_ = bf16[48,1920]{1,0:T(8,128)(2,1)S(1)} collective-permute-done((bf16[48,1920]{1,0:T(8,128)(2,1)S(1)}, bf16[48,1920]{1,0:T(8,128)(2,1)S(1)}, u32[]{:S(2)}, u32[]{:S(2)}) %collective-permute-start.14) | collective-permute-done | bytes 184352 | tf_op jit(solution)/shard_map/ppermute | solution.py:642
  118.7 0.8 last_sum.1
  (32 shorter events, 0.1 us)
Async XLA Ops:
  1.3 2.4 %copy-start.1 = (f32[96,31]{1,0:T(8,128)S(1)}, f32[96,31]{1,0:T(8,128)}, u32[]{:S(2)}) copy-start(f32[96,31]{1,0:T(8,128)} %constant.20.clone.1.refs_9_) | copy-start | bytes 35716 | tf_op jit(solution)/shard_map/cond
  1.3 2.4 %copy-start.2 = (bf16[88,240]{1,0:T(8,128)(2,1)S(1)}, bf16[88,240]{1,0:T(8,128)(2,1)}, u32[]{:S(2)}) copy-start(bf16[88,240]{1,0:T(8,128)(2,1)} %constant.18.clone.1.refs_7_) | copy-start | bytes 126724 | tf_op jit(solution)/shard_map/cond
  1.3 2.4 %copy-start.3 = (bf16[80,256]{1,0:T(8,128)(2,1)S(1)}, bf16[80,256]{1,0:T(8,128)(2,1)}, u32[]{:S(2)}) copy-start(bf16[80,256]{1,0:T(8,128)(2,1)} %constant.19.clone.1.refs_8_) | copy-start | bytes 122884 | tf_op jit(solution)/shard_map/cond
  1.3 2.4 %copy-start.4 = (f32[31,96]{1,0:T(8,128)S(1)}, f32[31,96]{1,0:T(8,128)}, u32[]{:S(2)}) copy-start(f32[31,96]{1,0:T(8,128)} %constant.21.clone.1.refs_10_) | copy-start | bytes 35716 | tf_op jit(solution)/shard_map/cond
  1.3 2.4 %copy-start.6 = (s32[1,32]{1,0:T(1,128)S(1)}, s32[1,32]{1,0:T(1,128)}, u32[]{:S(2)}) copy-start(s32[1,32]{1,0:T(1,128)} %get-tuple-element.64.refs_0_.len_ref) | copy-start | bytes 388 | tf_op jit(solution)/shard_map/cond
  1.4 23.1 %slice-start = ((s8[4718592]{0:T(1024)(128)(4,1)}), s8[4194304]{0:T(1024)(128)(4,1)S(1)}, s32[]{:S(2)}) async-start(s8[4718592]{0:T(1024)(128)(4,1)} %bitcast.12), calls=%async_computation.1 | async-start | bytes 8388608 | tf_op jit(solution)/shard_map/cond
  1.4 23.1 %slice-start.2 = ((s8[4718592]{0:T(1024)(128)(4,1)}), s8[4194304]{0:T(1024)(128)(4,1)S(1)}, s32[]{:S(2)}) async-start(s8[4718592]{0:T(1024)(128)(4,1)} %bitcast.14), calls=%async_computation.3 | async-start | bytes 8388608 | tf_op jit(solution)/shard_map/cond
  3.7 20.7 %slice-start.1 = ((s8[4718592]{0:T(1024)(128)(4,1)}), s8[524288]{0:T(1024)(128)(4,1)S(1)}, s32[]{:S(2)}) async-start(s8[4718592]{0:T(1024)(128)(4,1)} %bitcast.12), calls=%async_computation.2 | async-start | bytes 1048576 | tf_op jit(solution)/shard_map/cond
  3.7 20.7 %slice-start.3 = ((s8[4718592]{0:T(1024)(128)(4,1)}), s8[524288]{0:T(1024)(128)(4,1)S(1)}, s32[]{:S(2)}) async-start(s8[4718592]{0:T(1024)(128)(4,1)} %bitcast.14), calls=%async_computation.4 | async-start | bytes 1048576 | tf_op jit(solution)/shard_map/cond
  3.8 20.7 %copy-start.8 = (bf16[384,1536]{1,0:T(8,128)(2,1)S(1)}, bf16[384,1536]{1,0:T(8,128)(2,1)}, u32[]{:S(2)}) copy-start(bf16[384,1536]{1,0:T(8,128)(2,1)} %get-tuple-element.156.refs_4_) | copy-start | bytes 3538948 | tf_op jit(solution)/shard_map/cond
  3.8 20.7 %copy-start.9 = (f32[31,384]{1,0:T(8,128)S(1)}, f32[31,384]{1,0:T(8,128)}, u32[]{:S(2)}) copy-start(f32[31,384]{1,0:T(8,128)} %get-tuple-element.157.refs_5_) | copy-start | bytes 142852 | tf_op jit(solution)/shard_map/cond
  3.8 20.7 %copy-start.10 = (f32[384]{0:T(512)S(1)}, f32[384]{0:T(512)}, u32[]{:S(2)}) copy-start(f32[384]{0:T(512)} %get-tuple-element.158.refs_6_) | copy-start | bytes 4612 | tf_op jit(solution)/shard_map/cond
  17.8 26.0 %collective-permute-start.2 = (bf16[576,384]{1,0:T(8,128)(2,1)S(1)}, bf16[576,384]{1,0:T(8,128)(2,1)S(1)}, u32[]{:S(2)}, u32[]{:S(2)}) collective-permute-start(bf16[576,384]{1,0:T(8,128)(2,1)S(1)} %get-tuple-element.82), channel_id=1, source_target_pairs={{0,1},{1,2},{2,3},{3,0},{4,5},{5,6},{6,7},{7,4},{8,9},{9,10},{10,1... | collective-permute-start | bytes 1327112 | tf_op jit(solution)/shard_map/cond/branch_1_fun/ppermute | solution.py:690
  19.8 23.9 %collective-permute-start.3 = (bf16[576,384]{1,0:T(8,128)(2,1)S(1)}, bf16[576,384]{1,0:T(8,128)(2,1)S(1)}, u32[]{:S(2)}, u32[]{:S(2)}) collective-permute-start(bf16[576,384]{1,0:T(8,128)(2,1)S(1)} %get-tuple-element.83), channel_id=1, source_target_pairs={{0,2},{1,3},{2,0},{3,1},{4,6},{5,7},{6,4},{7,5},{8,10},{9,11},{10,... | collective-permute-start | bytes 1327112 | tf_op jit(solution)/shard_map/cond/branch_1_fun/ppermute | solution.py:691
  23.4 20.4 %collective-permute-start.4 = (bf16[576,384]{1,0:T(8,128)(2,1)S(1)}, bf16[576,384]{1,0:T(8,128)(2,1)S(1)}, u32[]{:S(2)}, u32[]{:S(2)}) collective-permute-start(bf16[576,384]{1,0:T(8,128)(2,1)S(1)} %get-tuple-element.84), channel_id=1, source_target_pairs={{0,3},{1,0},{2,1},{3,2},{4,7},{5,4},{6,5},{7,6},{8,11},{9,8},{10,9... | collective-permute-start | bytes 1327112 | tf_op jit(solution)/shard_map/cond/branch_1_fun/ppermute | solution.py:692
  42.3 19.2 %collective-permute-start.5 = (bf16[480,768]{1,0:T(8,128)(2,1)}, bf16[480,768]{1,0:T(8,128)(2,1)}, u32[]{:S(2)}, u32[]{:S(2)}) collective-permute-start(bf16[480,768]{1,0:T(8,128)(2,1)} %get-tuple-element.89), channel_id=1, source_target_pairs={{0,1},{1,0},{2,3},{3,2},{4,5},{5,4},{6,7},{7,6},{8,9},{9,8},{10,11... | collective-permute-start | bytes 2211848 | tf_op jit(solution)/shard_map/cond/branch_1_fun/ppermute | solution.py:731
  43.6 19.9 %collective-permute-start.6 = (bf16[480,768]{1,0:T(8,128)(2,1)}, bf16[480,768]{1,0:T(8,128)(2,1)}, u32[]{:S(2)}, u32[]{:S(2)}) collective-permute-start(bf16[480,768]{1,0:T(8,128)(2,1)} %get-tuple-element.90), channel_id=1, source_target_pairs={{0,3},{1,2},{2,1},{3,0},{4,7},{5,6},{6,5},{7,4},{8,11},{9,10},{10,... | collective-permute-start | bytes 2211848 | tf_op jit(solution)/shard_map/cond/branch_1_fun/ppermute | solution.py:732
  52.6 3.8 %collective-permute-start = (bf16[16,48,1152]{2,1,0:T(8,128)(2,1)S(1)}, bf16[16,48,1152]{2,1,0:T(8,128)(2,1)S(1)}, u32[]{:S(2)}, u32[]{:S(2)}) collective-permute-start(bf16[16,48,1152]{2,1,0:T(8,128)(2,1)S(1)} %get-tuple-element.57), channel_id=1, source_target_pairs={{0,4},{4,0},{8,12},{12,8},{16,20},{20,16},{24,28},{28,24},{32,36},... | collective-permute-start | bytes 5308424 | tf_op jit(solution)/shard_map/cond/branch_1_fun/cond/branch_1_fun/ppermute | solution.py:642
  52.7 3.7 %collective-permute-start.1 = (f32[32,384]{1,0:T(8,128)S(1)}, f32[32,384]{1,0:T(8,128)S(1)}, u32[]{:S(2)}, u32[]{:S(2)}) collective-permute-start(f32[32,384]{1,0:T(8,128)S(1)} %get-tuple-element.58.small), channel_id=1, source_target_pairs={{0,4},{4,0},{8,12},{12,8},{16,20},{20,16},{24,28},{28,24},{32,36},... | collective-permute-start | bytes 147464 | tf_op jit(solution)/shard_map/cond/branch_1_fun/cond/branch_1_fun/ppermute | solution.py:642
  56.8 13.3 %collective-permute-start.10 = (bf16[10,48,512]{2,1,0:T(8,128)(2,1)S(1)}, bf16[10,48,512]{2,1,0:T(8,128)(2,1)S(1)}, u32[]{:S(2)}, u32[]{:S(2)}) collective-permute-start(bf16[10,48,512]{2,1,0:T(8,128)(2,1)S(1)} %get-tuple-element.97), channel_id=1, source_target_pairs={{0,8},{4,12},{8,0},{12,4},{16,24},{20,28},{24,16},{28,20},{32,40},... | collective-permute-start | bytes 1474568 | tf_op jit(solution)/shard_map/cond/branch_1_fun/ppermute | solution.py:642
  58.4 13.0 %collective-permute-start.9 = (bf16[8,48,640]{2,1,0:T(8,128)(2,1)S(1)}, bf16[8,48,640]{2,1,0:T(8,128)(2,1)S(1)}, u32[]{:S(2)}, u32[]{:S(2)}) collective-permute-start(bf16[8,48,640]{2,1,0:T(8,128)(2,1)S(1)} %get-tuple-element.96), channel_id=1, source_target_pairs={{0,32},{4,36},{8,40},{12,44},{16,48},{20,52},{24,56},{28,60},{32,0... | collective-permute-start | bytes 1474568 | tf_op jit(solution)/shard_map/cond/branch_1_fun/ppermute | solution.py:642
  64.8 10.9 %copy-start.7 = (s32[1,32]{1,0:T(1,128)S(1)}, s32[1,32]{1,0:T(1,128)}, u32[]{:S(2)}) copy-start(s32[1,32]{1,0:T(1,128)} %get-tuple-element.163.owner_ref) | copy-start | bytes 388 | tf_op jit(solution)/shard_map/cond
  64.8 10.9 %collective-permute-start.7 = (bf16[480,384]{1,0:T(8,128)(2,1)S(1)}, bf16[480,384]{1,0:T(8,128)(2,1)S(1)}, u32[]{:S(2)}, u32[]{:S(2)}) collective-permute-start(bf16[480,384]{1,0:T(8,128)(2,1)S(1)} %get-tuple-element.91), channel_id=1, source_target_pairs={{0,3},{1,2},{2,1},{3,0},{4,7},{5,6},{6,5},{7,4},{8,11},{9,10},{10,... | collective-permute-start | bytes 1105928 | tf_op jit(solution)/shard_map/cond/branch_1_fun/ppermute | solution.py:728
  65.3 10.4 %collective-permute-start.8 = (bf16[480,384]{1,0:T(8,128)(2,1)S(1)}, bf16[480,384]{1,0:T(8,128)(2,1)S(1)}, u32[]{:S(2)}, u32[]{:S(2)}) collective-permute-start(bf16[480,384]{1,0:T(8,128)(2,1)S(1)} %get-tuple-element.92), channel_id=1, source_target_pairs={{0,1},{1,0},{2,3},{3,2},{4,5},{5,4},{6,7},{7,6},{8,9},{9,8},{10,11... | collective-permute-start | bytes 1105928 | tf_op jit(solution)/shard_map/cond/branch_1_fun/ppermute | solution.py:728
  72.5 8.2 %collective-permute-start.12 = (bf16[6,48,512]{2,1,0:T(8,128)(2,1)S(1)}, bf16[6,48,512]{2,1,0:T(8,128)(2,1)}, u32[]{:S(2)}, u32[]{:S(2)}) collective-permute-start(bf16[6,48,512]{2,1,0:T(8,128)(2,1)S(1)} %get-tuple-element.102), channel_id=1, source_target_pairs={{0,32},{4,36},{8,40},{12,44},{16,48},{20,52},{24,56},{28,60},{32,0... | collective-permute-start | bytes 884744 | tf_op jit(solution)/shard_map/cond/branch_1_fun/ppermute | solution.py:642
  74.0 6.7 %collective-permute-start.11 = (bf16[4,48,640]{2,1,0:T(8,128)(2,1)S(1)}, bf16[4,48,640]{2,1,0:T(8,128)(2,1)}, u32[]{:S(2)}, u32[]{:S(2)}) collective-permute-start(bf16[4,48,640]{2,1,0:T(8,128)(2,1)S(1)} %get-tuple-element.101), channel_id=1, source_target_pairs={{0,8},{4,12},{8,0},{12,4},{16,24},{20,28},{24,16},{28,20},{32,40},... | collective-permute-start | bytes 737288 | tf_op jit(solution)/shard_map/cond/branch_1_fun/ppermute | solution.py:642
  80.7 7.1 %copy-start.5 = (f32[4,48,640]{2,1,0:T(8,128)S(1)}, f32[4,48,640]{2,1,0:T(8,128)}, u32[]{:S(2)}) copy-start(f32[4,48,640]{2,1,0:T(8,128)} %get-tuple-element.127.own_x) | copy-start | bytes 1474564
  80.7 32.4 %copy-start = (s32[1,32]{1,0:T(1,128)S(1)}, s32[1,32]{1,0:T(1,128)}, u32[]{:S(2)}) copy-start(s32[1,32]{1,0:T(1,128)} %slot_ref.1) | copy-start | bytes 388
  80.7 32.4 %all-to-all-start = ((bf16[32,72,384]{2,1,0:T(8,128)(2,1)}), bf16[32,72,384]{2,1,0:T(8,128)(2,1)S(1)}, u32[]{:S(2)}, u32[]{:S(2)}) async-start(bf16[32,72,384]{2,1,0:T(8,128)(2,1)} %get-tuple-element.125), calls=%async_computation | async-start | bytes 3538944 | tf_op jit(solution)/shard_map/all_to_all | solution.py:769
  89.1 28.2 %collective-permute-start.13 = (bf16[48,1920]{1,0:T(8,128)(2,1)S(1)}, bf16[48,1920]{1,0:T(8,128)(2,1)S(1)}, u32[]{:S(2)}, u32[]{:S(2)}) collective-permute-start(bf16[48,1920]{1,0:T(8,128)(2,1)S(1)} %get-tuple-element.134), channel_id=1, source_target_pairs={{0,120},{4,124},{8,112},{12,116},{16,104},{20,108},{24,96},{28,100... | collective-permute-start | bytes 552968 | tf_op jit(solution)/shard_map/ppermute | solution.py:642
  94.3 24.4 %collective-permute-start.14 = (bf16[48,1920]{1,0:T(8,128)(2,1)S(1)}, bf16[48,1920]{1,0:T(8,128)(2,1)S(1)}, u32[]{:S(2)}, u32[]{:S(2)}) collective-permute-start(bf16[48,1920]{1,0:T(8,128)(2,1)S(1)} %get-tuple-element.135), channel_id=1, source_target_pairs={{0,96},{4,100},{8,104},{12,108},{16,112},{20,116},{24,120},{28,124... | collective-permute-start | bytes 552968 | tf_op jit(solution)/shard_map/ppermute | solution.py:642
  94.8 23.9 %collective-permute-start.15 = (bf16[48,1920]{1,0:T(8,128)(2,1)S(1)}, bf16[48,1920]{1,0:T(8,128)(2,1)S(1)}, u32[]{:S(2)}, u32[]{:S(2)}) collective-permute-start(bf16[48,1920]{1,0:T(8,128)(2,1)S(1)} %get-tuple-element.136), channel_id=1, source_target_pairs={{0,24},{4,28},{8,16},{12,20},{16,8},{20,12},{24,0},{28,4},{32,56},... | collective-permute-start | bytes 552968 | tf_op jit(solution)/shard_map/ppermute | solution.py:642

commit v8 on v7

--- a/solution.py
+++ b/solution.py
@@ -17,7 +17,7 @@
 EDGE = 4
 FREQ = 2 * (MAIN + EDGE)
 MARGIN = 96
-ROWS0 = 576
+ROWS0 = 608
 SEGS = 32
 GROUP = 5
 PICKS = 8
@@ -468,7 +468,7 @@
         for i in range(pairs):
             own = pl.ds(pl.multiple_of(j * cols + (2 * i + core) * deep, 16), deep)
             other = pl.ds(pl.multiple_of(j * cols + (2 * i + 1 - core) * deep, 16), deep)
-            keep_ref[j * pairs + i, :, at] = held[own, at]
+            keep_ref[j * pairs + i, :, at] = held[own, at].astype(BF16)
             send_ref[j * pairs + i, :, at] = held[other, at].astype(BF16)
 
     out_cols, in_cols = slice(wide, None), slice(0, wide)
@@ -498,7 +498,7 @@
     return pl.pallas_call(
         lambda *refs: weight_kernel(deep, *refs),
         out_shape=(
-            jax.ShapeDtypeStruct((pairs, deep, 3 * ch), F32),
+            jax.ShapeDtypeStruct((pairs, deep, 3 * ch), BF16),
             jax.ShapeDtypeStruct((pairs, deep, 3 * ch), BF16),
         ),
         in_specs=[pl.BlockSpec(memory_space=pl.ANY)] * 6,
@@ -561,7 +561,7 @@
         for j in range(4):
             for where, out, slot in ((a, outs[i], 0), (far(a), outs[i], 4), (near(a), outs[2 + i], 0), (far(near(a)), outs[2 + i], 4)):
                 at = where * 4 + j if x_first else j * 4 + where
-                total = keep[at, :, cols] + got[at, :, cols].astype(F32)
+                total = keep[at, :, cols].astype(F32) + got[at, :, cols].astype(F32)
                 out[slot + j] = total.astype(out.dtype)
     put_small(outs[3], 8, small_total)
 

time: 121 us -> 122 us (level)
  starting transfers between devices: 27.2 us -> 29.5 us
    ppermute x2, starting transfers between devices: 0.45 us -> 2.83 us  [last_stage(): return (lax.ppermute(send_a, 'mp', cross), lax.ppermute(send_b, 'mp', pair))]
    ppermute x9, waiting for transfers between devices: 13.8 us -> 16.2 us  [move(): lax.ppermute(array, 'dp', [(i, to(i)) for i in range(lax.axis_size('dp'))])]
    ppermute x1, waiting for transfers between devices: 0.01 us -> 2.15 us  [zeroth_stage(): lax.ppermute(far0, 'mp', ring(2))]
    ppermute x1, waiting for transfers between devices: 1.95 us -> 0.01 us  [first_stage(): first_b = lax.ppermute(send_b, 'mp', cross)]
    ppermute x1, waiting for transfers between devices: 1.6 us -> 0.01 us  [first_stage(): first_a = lax.ppermute(send_a, 'mp', pair)]
  transfers between devices with their start and end apart: 17 -> 17, of which waited for: 10 -> 8; matrix products, arithmetic and copies ran while one was open for 0% -> 0% of each run, Pallas kernels for 31% -> 29%
where the time goes in v8:
time: 122 us; the launch traced here: 120 us
  Pallas kernels  50.4 us (41%)
  waiting for transfers between devices  36.4 us (30%)
  starting transfers between devices  29.5 us (24%)
  local copies, waits for them, and re-layouts  2.38 us (2%)
  between operations  1.32 us (1%)
    pallas_call x2, Pallas kernels, chunk_call(): pl.pallas_call(body, out_shape=out_shape, in_specs=specs, out_specs=[vm]...  31 us
    all_to_all x1, waiting for transfers between devices, on_device(): lax.all_to_all(outgoing, 'dp', split_axis=0, concat_axis=0, tiled=True)  18.1 us
    ppermute x9, waiting for transfers between devices, move(): lax.ppermute(array, 'dp', [(i, to(i)) for i in range(lax.axis_size('dp'))])  16.2 us
    ppermute x9, starting transfers between devices, move(): lax.ppermute(array, 'dp', [(i, to(i)) for i in range(lax.axis_size('dp'))])  11.7 us
    pallas_call x1, Pallas kernels, weight_call(): pl.pallas_call(lambda *refs: weight_kernel(deep, *refs), out_shape=(jax.S...  8.44 us
    all_to_all x1, starting transfers between devices, on_device(): lax.all_to_all(outgoing, 'dp', split_axis=0, concat_axis=0, tiled=True)  6.99 us
    pallas_call x1, Pallas kernels, pick_call(): pl.pallas_call(pick_kernel, grid=(1,), out_shape=jax.ShapeDtypeStruct((SE...  3.95 us
    pallas_call x5, Pallas kernels, sum_call(): pl.pallas_call(kernel, out_shape=out_shape, in_specs=[vm] * len(operands)...  3.79 us
  transfers between devices with their start and end apart: 17, of which 8 were waited for; matrix products, arithmetic and copies ran while one was open for 0% of the time, Pallas kernels for 29%

profile of v8, /device:TPU:0, one launch (start us, length us, event | category | flops | bytes accessed | tf_op | source)
XLA Modules:
  0.0 120.4 jit_solution(4524852832416653232)
XLA Ops:
  1.3 80.4 %conditional.2 = (bf16[32,72,384]{2,1,0:T(8,128)(2,1)}, f32[4,48,640]{2,1,0:T(8,128)}, f32[4,48,512]{2,1,0:T(8,128)}, f32[32,384]{1,0:T(8,128)S(1)}, bf16[4,48,6...) conditional(s32[]{:T(128)} %bitcast.1, () %tuple.24, (s32[1,32]{1,0:T(1,128)}, bf16[1536,2,384]{2,1,0:T(2,128)(2,1)}, ...), branch_computations={%region_0.0_spmd, %region_1.0_spmd} | conditional | flops 51004997632 | bytes 126400592 | solution.py:651
  1.3 0.0 copy-start.1
  1.3 0.0 copy-start.2
  1.3 0.0 copy-start.3
  1.3 0.0 copy-start.4
  1.4 0.0 slice-start
  1.4 0.0 slice-start.2
  1.4 2.3 %copy.29 = bf16[192,8,2,384]{3,1,2,0:T(8,128)(2,1)S(1)} copy(bf16[192,8,2,384]{3,2,1,0:T(2,128)(2,1)} %bitcast.9) | data formatting | bytes 4718592 | tf_op jit(solution)/shard_map/cond
  3.7 0.0 slice-start.1
  3.7 0.0 slice-start.3
  3.8 0.0 copy-start.9
  3.8 14.3 %chunk0.1 = (bf16[704,768]{1,0:T(8,128)(2,1)}, bf16[704,384]{1,0:T(8,128)(2,1)}, f32[104,384]{1,0:T(8,128)S(1)}, f32[608,384]{1,0:T(8,128)S(1)}, bf16[608,384]{1...) custom-call(s32[1,32]{1,0:T(1,128)S(1)} %copy-done.6, ...), custom_call_target="tpu_custom_call" | custom-call | flops 20000000000 | bytes 20000000 | tf_op jit(solution)/shard_map/cond/branch_1_fun/chunk0/pallas_call | solution.py:304
  18.1 2.1 %collective-permute-start.2 = (bf16[608,384]{1,0:T(8,128)(2,1)S(1)}, bf16[608,384]{1,0:T(8,128)(2,1)S(1)}, u32[]{:S(2)}, u32[]{:S(2)}) collective-permute-start(bf16[608,384]{1,0:T(8,128)(2,1)S(1)} %get-tuple-element.82), channel_id=1, source_target_pairs={{0,1},{1,2},{2,3},{3,0},{4,5},{5,6},{6,7},{7,4},{8,9},{9,10},{10,1... | collective-permute-start | bytes 1400840 | tf_op jit(solution)/shard_map/cond/branch_1_fun/ppermute | solution.py:690
  20.2 3.6 %collective-permute-start.3 = (bf16[608,384]{1,0:T(8,128)(2,1)S(1)}, bf16[608,384]{1,0:T(8,128)(2,1)S(1)}, u32[]{:S(2)}, u32[]{:S(2)}) collective-permute-start(bf16[608,384]{1,0:T(8,128)(2,1)S(1)} %get-tuple-element.83), channel_id=1, source_target_pairs={{0,2},{1,3},{2,0},{3,1},{4,6},{5,7},{6,4},{7,5},{8,10},{9,11},{10,... | collective-permute-start | bytes 1400840 | tf_op jit(solution)/shard_map/cond/branch_1_fun/ppermute | solution.py:691
  23.8 1.0 collective-permute-start.4
  24.9 16.6 %chunk608.1 = (bf16[928,768]{1,0:T(8,128)(2,1)S(1)}, bf16[928,384]{1,0:T(8,128)(2,1)S(1)}, f32[32,384]{1,0:T(8,128)S(1)}, bf16[464,768]{1,0:T(8,128)(2,1)}, bf16...) custom-call(s32[1,32]{1,0:T(1,128)S(1)} %copy-done.6, bf16[1536,1536]{1,0:T(8,128)(2,1)S(1)} %bitcast.13, ...), custom_call_target="tpu_custom_call" | custom-call | flops 20000000000 | bytes 20000000 | tf_op jit(solution)/shard_map/cond/branch_1_fun/chunk608/pallas_call | solution.py:304
  41.5 1.3 %collective-permute-start.5 = (bf16[464,768]{1,0:T(8,128)(2,1)}, bf16[464,768]{1,0:T(8,128)(2,1)}, u32[]{:S(2)}, u32[]{:S(2)}) collective-permute-start(bf16[464,768]{1,0:T(8,128)(2,1)} %get-tuple-element.89), channel_id=1, source_target_pairs={{0,1},{1,0},{2,3},{3,2},{4,5},{5,4},{6,7},{7,6},{8,9},{9,8},{10,11... | collective-permute-start | bytes 2138120 | tf_op jit(solution)/shard_map/cond/branch_1_fun/ppermute | solution.py:731
  42.8 0.1 collective-permute-start.6
  42.9 2.2 %collective-permute-done.3 = bf16[608,384]{1,0:T(8,128)(2,1)S(1)} collective-permute-done((bf16[608,384]{1,0:T(8,128)(2,1)S(1)}, bf16[608,384]{1,0:T(8,128)(2,1)S(1)}, u32[]{:S(2)}, u32[]{:S(2)}) %collective-permute-start.3) | collective-permute-done | bytes 466976 | tf_op jit(solution)/shard_map/cond/branch_1_fun/ppermute | solution.py:691
  45.1 12.7 %conditional = (bf16[608,384]{1,0:T(8,128)(2,1)S(1)}, f32[8,48,640]{2,1,0:T(8,128)S(1)}, f32[8,48,512]{2,1,0:T(8,128)S(1)}, bf16[8,48,640]{2,1,0:T(8,128)(2,1)S(...) conditional(s32[]{:T(128)} %bitcast, () %tuple.17, (bf16[1536,1536]{1,0:T(8,128)(2,1)S(1)}, ...), branch_computations={%region_2.0_spmd, %region_3.0_spmd} | conditional | flops 11002001408 | bytes 27474624 | solution.py:651
  45.1 8.4 %weight.1 = (bf16[16,48,1152]{2,1,0:T(8,128)(2,1)S(1)}, bf16[16,48,1152]{2,1,0:T(8,128)(2,1)S(1)}) custom-call(bf16[1536,1536]{1,0:T(8,128)(2,1)S(1)} %get-tuple-element.50.refs_0_, bf16[1536,1536]{1,0:T(8,128)(2,1)S(1)} %get-tuple-element.51.refs_1_, bf16[704,768]{1,0:T(8,128)(2,1)} %get-tuple-element.52.refs_2_, ...), custom_call_target="tpu_custom_call" | custom-call | flops 11000000512 | bytes 20000000 | tf_op jit(solution)/shard_map/cond/branch_1_fun/cond/branch_1_fun/weight/pallas_call | solution.py:498
  53.5 0.1 collective-permute-start
  53.6 0.5 collective-permute-start.1
  54.1 0.2 zero_sum.1
  54.3 3.0 %collective-permute-done.1.small_got = f32[32,384]{1,0:T(8,128)S(1)} collective-permute-done((f32[32,384]{1,0:T(8,128)S(1)}, f32[32,384]{1,0:T(8,128)S(1)}, u32[]{:S(2)}, u32[]{:S(2)}) %collective-permute-start.1) | collective-permute-done | bytes 49184 | tf_op jit(solution)/shard_map/cond/branch_1_fun/cond/branch_1_fun/ppermute | solution.py:642
  57.4 0.4 core_sum.1
  57.8 1.6 %collective-permute-start.10 = (bf16[10,48,512]{2,1,0:T(8,128)(2,1)S(1)}, bf16[10,48,512]{2,1,0:T(8,128)(2,1)S(1)}, u32[]{:S(2)}, u32[]{:S(2)}) collective-permute-start(bf16[10,48,512]{2,1,0:T(8,128)(2,1)S(1)} %get-tuple-element.97), channel_id=1, source_target_pairs={{0,8},{4,12},{8,0},{12,4},{16,24},{20,28},{24,16},{28,20},{32,40},... | collective-permute-start | bytes 1474568 | tf_op jit(solution)/shard_map/cond/branch_1_fun/ppermute | solution.py:642
  59.4 1.5 %collective-permute-start.9 = (bf16[8,48,640]{2,1,0:T(8,128)(2,1)S(1)}, bf16[8,48,640]{2,1,0:T(8,128)(2,1)S(1)}, u32[]{:S(2)}, u32[]{:S(2)}) collective-permute-start(bf16[8,48,640]{2,1,0:T(8,128)(2,1)S(1)} %get-tuple-element.96), channel_id=1, source_target_pairs={{0,32},{4,36},{8,40},{12,44},{16,48},{20,52},{24,56},{28,60},{32,0... | collective-permute-start | bytes 1474568 | tf_op jit(solution)/shard_map/cond/branch_1_fun/ppermute | solution.py:642
  60.9 1.3 %pass.1 = (bf16[464,384]{1,0:T(8,128)(2,1)S(1)}, bf16[464,384]{1,0:T(8,128)(2,1)S(1)}) custom-call(f32[464,768]{1,0:T(8,128)S(1)} %get-tuple-element.87.keep_a, f32[464,768]{1,0:T(8,128)S(1)} %get-tuple-element.88.keep_b, bf16[464,768]{1,0:T(8,128)(2,1)} %collective-permute-done.5.first_a, bf16[464,768]{1,0:T(8,128)(2,1)} %collective-permute-done.6.first_b), custom_call_target="tpu_custom_call" | custom-call | flops 1000000 | bytes 100000 | tf_op jit(solution)/shard_map/cond/branch_1_fun/pass/pallas_call | solution.py:347
  62.2 1.5 %collective-permute-start.7 = (bf16[464,384]{1,0:T(8,128)(2,1)S(1)}, bf16[464,384]{1,0:T(8,128)(2,1)S(1)}, u32[]{:S(2)}, u32[]{:S(2)}) collective-permute-start(bf16[464,384]{1,0:T(8,128)(2,1)S(1)} %get-tuple-element.91), channel_id=1, source_target_pairs={{0,3},{1,2},{2,1},{3,0},{4,7},{5,6},{6,5},{7,4},{8,11},{9,10},{10,... | collective-permute-start | bytes 1069064 | tf_op jit(solution)/shard_map/cond/branch_1_fun/ppermute | solution.py:728
  63.7 1.3 %collective-permute-start.8 = (bf16[464,384]{1,0:T(8,128)(2,1)S(1)}, bf16[464,384]{1,0:T(8,128)(2,1)S(1)}, u32[]{:S(2)}, u32[]{:S(2)}) collective-permute-start(bf16[464,384]{1,0:T(8,128)(2,1)S(1)} %get-tuple-element.92), channel_id=1, source_target_pairs={{0,1},{1,0},{2,3},{3,2},{4,5},{5,4},{6,7},{7,6},{8,9},{9,8},{10,11... | collective-permute-start | bytes 1069064 | tf_op jit(solution)/shard_map/cond/branch_1_fun/ppermute | solution.py:728
  65.1 6.0 %collective-permute-done.10.got_y = bf16[10,48,512]{2,1,0:T(8,128)(2,1)S(1)} collective-permute-done((bf16[10,48,512]{2,1,0:T(8,128)(2,1)S(1)}, bf16[10,48,512]{2,1,0:T(8,128)(2,1)S(1)}, u32[]{:S(2)}, u32[]{:S(2)}) %collective-permute-start.10) | collective-permute-done | bytes 491552 | tf_op jit(solution)/shard_map/cond/branch_1_fun/ppermute | solution.py:642
  71.1 1.3 %collective-permute-done.9.got_x = bf16[8,48,640]{2,1,0:T(8,128)(2,1)S(1)} collective-permute-done((bf16[8,48,640]{2,1,0:T(8,128)(2,1)S(1)}, bf16[8,48,640]{2,1,0:T(8,128)(2,1)S(1)}, u32[]{:S(2)}, u32[]{:S(2)}) %collective-permute-start.9) | collective-permute-done | bytes 491552 | tf_op jit(solution)/shard_map/cond/branch_1_fun/ppermute | solution.py:642
  72.4 1.1 half_sum.1
  73.4 1.5 %collective-permute-start.12 = (bf16[6,48,512]{2,1,0:T(8,128)(2,1)S(1)}, bf16[6,48,512]{2,1,0:T(8,128)(2,1)}, u32[]{:S(2)}, u32[]{:S(2)}) collective-permute-start(bf16[6,48,512]{2,1,0:T(8,128)(2,1)S(1)} %get-tuple-element.102), channel_id=1, source_target_pairs={{0,32},{4,36},{8,40},{12,44},{16,48},{20,52},{24,56},{28,60},{32,0... | collective-permute-start | bytes 884744 | tf_op jit(solution)/shard_map/cond/branch_1_fun/ppermute | solution.py:642
  75.0 0.5 collective-permute-start.11
  75.4 3.9 %pick.1 = bf16[32,72,384]{2,1,0:T(8,128)(2,1)} custom-call(s32[1,32]{1,0:T(1,128)S(1)} %copy-done.6, s32[1,32]{1,0:T(1,128)S(1)} %copy-done.7, bf16[608,384]{1,0:T(8,128)(2,1)S(1)} %get-tuple-element.86.held0, f32[464,768]{1,0:T(8,128)S(1)} %get-tuple-element.87.keep_a, f32[464,768]{1,0:T(8,128)S(1)} %get-tuple-element.88.keep_b, ...), custom_call_target="tpu_custom_call" | custom-call | flops 1000000 | bytes 100000 | tf_op jit(solution)/shard_map/cond/branch_1_fun/pick/pallas_call | solution.py:392
  79.4 2.3 %collective-permute-done.11 = bf16[4,48,640]{2,1,0:T(8,128)(2,1)} collective-permute-done((bf16[4,48,640]{2,1,0:T(8,128)(2,1)S(1)}, bf16[4,48,640]{2,1,0:T(8,128)(2,1)}, u32[]{:S(2)}, u32[]{:S(2)}) %collective-permute-start.11) | collective-permute-done | bytes 245792 | tf_op jit(solution)/shard_map/cond/branch_1_fun/ppermute | solution.py:642
  81.7 7.0 %all-to-all-start = ((bf16[32,72,384]{2,1,0:T(8,128)(2,1)}), bf16[32,72,384]{2,1,0:T(8,128)(2,1)S(1)}, u32[]{:S(2)}, u32[]{:S(2)}) async-start(bf16[32,72,384]{2,1,0:T(8,128)(2,1)} %get-tuple-element.125), calls=%async_computation | async-start | bytes 3538944 | tf_op jit(solution)/shard_map/all_to_all | solution.py:769
  88.7 1.3 %square_sum.1 = (f32[48,1152]{1,0:T(8,128)S(1)}, f32[32,384]{1,0:T(8,128)S(1)}, bf16[48,1920]{1,0:T(8,128)(2,1)S(1)}, bf16[48,1920]{1,0:T(8,128)(2,1)S(1)}, bf16[48,1920]{1,0:T(8,128)(2,1)S(1)}) custom-call(f32[4,48,640]{2,1,0:T(8,128)S(1)} %copy-done.5, f32[4,48,512]{2,1,0:T(8,128)} %get-tuple-element.128.own_y, f32[32,384]{1,0:T(8,128)S(1)} %get-tuple-element.129.small, ...), custom_call_target="tpu_custom_call" | custom-call | flops 1000000 | bytes 100000 | tf_op jit(solution)/shard_map/square_sum/pallas_call | solution.py:614
  90.0 5.3 %collective-permute-start.13 = (bf16[48,1920]{1,0:T(8,128)(2,1)S(1)}, bf16[48,1920]{1,0:T(8,128)(2,1)S(1)}, u32[]{:S(2)}, u32[]{:S(2)}) collective-permute-start(bf16[48,1920]{1,0:T(8,128)(2,1)S(1)} %get-tuple-element.134), channel_id=1, source_target_pairs={{0,120},{4,124},{8,112},{12,116},{16,104},{20,108},{24,96},{28,100... | collective-permute-start | bytes 552968 | tf_op jit(solution)/shard_map/ppermute | solution.py:642
  95.3 0.5 collective-permute-start.14
  95.7 0.2 collective-permute-start.15
  96.0 18.1 %all-to-all-done.src = bf16[32,72,384]{2,1,0:T(8,128)(2,1)S(1)} async-done(((bf16[32,72,384]{2,1,0:T(8,128)(2,1)}), bf16[32,72,384]{2,1,0:T(8,128)(2,1)S(1)}, u32[]{:S(2)}, u32[]{:S(2)}) %all-to-all-start) | async-done | bytes 1769504 | tf_op jit(solution)/shard_map/all_to_all | solution.py:769
  114.0 2.0 %order.1 = (bf16[32,72,384]{2,1,0:T(8,128)(2,1)}, f32[8,128]{1,0:T(8,128)S(1)}) custom-call(s32[1,32]{1,0:T(1,128)S(1)} %copy-done, bf16[32,72,384]{2,1,0:T(8,128)(2,1)S(1)} %all-to-all-done.src), custom_call_target="tpu_custom_call" | custom-call | flops 1000000 | bytes 100000 | tf_op jit(solution)/shard_map/order/pallas_call | solution.py:417
  116.1 2.1 %collective-permute-done.13.refs_2_ = bf16[48,1920]{1,0:T(8,128)(2,1)S(1)} collective-permute-done((bf16[48,1920]{1,0:T(8,128)(2,1)S(1)}, bf16[48,1920]{1,0:T(8,128)(2,1)S(1)}, u32[]{:S(2)}, u32[]{:S(2)}) %collective-permute-start.13) | collective-permute-done | bytes 184352 | tf_op jit(solution)/shard_map/ppermute | solution.py:642
  118.2 1.5 %collective-permute-done.14.refs_3_ = bf16[48,1920]{1,0:T(8,128)(2,1)S(1)} collective-permute-done((bf16[48,1920]{1,0:T(8,128)(2,1)S(1)}, bf16[48,1920]{1,0:T(8,128)(2,1)S(1)}, u32[]{:S(2)}, u32[]{:S(2)}) %collective-permute-start.14) | collective-permute-done | bytes 184352 | tf_op jit(solution)/shard_map/ppermute | solution.py:642
  119.7 0.8 last_sum.1
  (32 shorter events, 0.1 us)
Async XLA Ops:
  1.3 2.4 %copy-start.1 = (f32[96,31]{1,0:T(8,128)S(1)}, f32[96,31]{1,0:T(8,128)}, u32[]{:S(2)}) copy-start(f32[96,31]{1,0:T(8,128)} %constant.20.clone.1.refs_9_) | copy-start | bytes 35716 | tf_op jit(solution)/shard_map/cond
  1.3 2.4 %copy-start.2 = (bf16[88,240]{1,0:T(8,128)(2,1)S(1)}, bf16[88,240]{1,0:T(8,128)(2,1)}, u32[]{:S(2)}) copy-start(bf16[88,240]{1,0:T(8,128)(2,1)} %constant.18.clone.1.refs_7_) | copy-start | bytes 126724 | tf_op jit(solution)/shard_map/cond
  1.3 2.4 %copy-start.3 = (bf16[80,256]{1,0:T(8,128)(2,1)S(1)}, bf16[80,256]{1,0:T(8,128)(2,1)}, u32[]{:S(2)}) copy-start(bf16[80,256]{1,0:T(8,128)(2,1)} %constant.19.clone.1.refs_8_) | copy-start | bytes 122884 | tf_op jit(solution)/shard_map/cond
  1.3 2.4 %copy-start.4 = (f32[31,96]{1,0:T(8,128)S(1)}, f32[31,96]{1,0:T(8,128)}, u32[]{:S(2)}) copy-start(f32[31,96]{1,0:T(8,128)} %constant.21.clone.1.refs_10_) | copy-start | bytes 35716 | tf_op jit(solution)/shard_map/cond
  1.3 2.4 %copy-start.6 = (s32[1,32]{1,0:T(1,128)S(1)}, s32[1,32]{1,0:T(1,128)}, u32[]{:S(2)}) copy-start(s32[1,32]{1,0:T(1,128)} %get-tuple-element.64.refs_0_.len_ref) | copy-start | bytes 388 | tf_op jit(solution)/shard_map/cond
  1.4 23.4 %slice-start = ((s8[4718592]{0:T(1024)(128)(4,1)}), s8[4194304]{0:T(1024)(128)(4,1)S(1)}, s32[]{:S(2)}) async-start(s8[4718592]{0:T(1024)(128)(4,1)} %bitcast.12), calls=%async_computation.1 | async-start | bytes 8388608 | tf_op jit(solution)/shard_map/cond
  1.4 23.4 %slice-start.2 = ((s8[4718592]{0:T(1024)(128)(4,1)}), s8[4194304]{0:T(1024)(128)(4,1)S(1)}, s32[]{:S(2)}) async-start(s8[4718592]{0:T(1024)(128)(4,1)} %bitcast.14), calls=%async_computation.3 | async-start | bytes 8388608 | tf_op jit(solution)/shard_map/cond
  3.7 21.1 %slice-start.1 = ((s8[4718592]{0:T(1024)(128)(4,1)}), s8[524288]{0:T(1024)(128)(4,1)S(1)}, s32[]{:S(2)}) async-start(s8[4718592]{0:T(1024)(128)(4,1)} %bitcast.12), calls=%async_computation.2 | async-start | bytes 1048576 | tf_op jit(solution)/shard_map/cond
  3.7 21.1 %slice-start.3 = ((s8[4718592]{0:T(1024)(128)(4,1)}), s8[524288]{0:T(1024)(128)(4,1)S(1)}, s32[]{:S(2)}) async-start(s8[4718592]{0:T(1024)(128)(4,1)} %bitcast.14), calls=%async_computation.4 | async-start | bytes 1048576 | tf_op jit(solution)/shard_map/cond
  3.8 21.1 %copy-start.8 = (bf16[384,1536]{1,0:T(8,128)(2,1)S(1)}, bf16[384,1536]{1,0:T(8,128)(2,1)}, u32[]{:S(2)}) copy-start(bf16[384,1536]{1,0:T(8,128)(2,1)} %get-tuple-element.156.refs_4_) | copy-start | bytes 3538948 | tf_op jit(solution)/shard_map/cond
  3.8 21.1 %copy-start.9 = (f32[31,384]{1,0:T(8,128)S(1)}, f32[31,384]{1,0:T(8,128)}, u32[]{:S(2)}) copy-start(f32[31,384]{1,0:T(8,128)} %get-tuple-element.157.refs_5_) | copy-start | bytes 142852 | tf_op jit(solution)/shard_map/cond
  3.8 21.0 %copy-start.10 = (f32[384]{0:T(512)S(1)}, f32[384]{0:T(512)}, u32[]{:S(2)}) copy-start(f32[384]{0:T(512)} %get-tuple-element.158.refs_6_) | copy-start | bytes 4612 | tf_op jit(solution)/shard_map/cond
  18.1 24.8 %collective-permute-start.2 = (bf16[608,384]{1,0:T(8,128)(2,1)S(1)}, bf16[608,384]{1,0:T(8,128)(2,1)S(1)}, u32[]{:S(2)}, u32[]{:S(2)}) collective-permute-start(bf16[608,384]{1,0:T(8,128)(2,1)S(1)} %get-tuple-element.82), channel_id=1, source_target_pairs={{0,1},{1,2},{2,3},{3,0},{4,5},{5,6},{6,7},{7,4},{8,9},{9,10},{10,1... | collective-permute-start | bytes 1400840 | tf_op jit(solution)/shard_map/cond/branch_1_fun/ppermute | solution.py:690
  20.2 24.9 %collective-permute-start.3 = (bf16[608,384]{1,0:T(8,128)(2,1)S(1)}, bf16[608,384]{1,0:T(8,128)(2,1)S(1)}, u32[]{:S(2)}, u32[]{:S(2)}) collective-permute-start(bf16[608,384]{1,0:T(8,128)(2,1)S(1)} %get-tuple-element.83), channel_id=1, source_target_pairs={{0,2},{1,3},{2,0},{3,1},{4,6},{5,7},{6,4},{7,5},{8,10},{9,11},{10,... | collective-permute-start | bytes 1400840 | tf_op jit(solution)/shard_map/cond/branch_1_fun/ppermute | solution.py:691
  23.8 21.3 %collective-permute-start.4 = (bf16[608,384]{1,0:T(8,128)(2,1)S(1)}, bf16[608,384]{1,0:T(8,128)(2,1)S(1)}, u32[]{:S(2)}, u32[]{:S(2)}) collective-permute-start(bf16[608,384]{1,0:T(8,128)(2,1)S(1)} %get-tuple-element.84), channel_id=1, source_target_pairs={{0,3},{1,0},{2,1},{3,2},{4,7},{5,4},{6,5},{7,6},{8,11},{9,8},{10,9... | collective-permute-start | bytes 1400840 | tf_op jit(solution)/shard_map/cond/branch_1_fun/ppermute | solution.py:692
  41.5 19.4 %collective-permute-start.5 = (bf16[464,768]{1,0:T(8,128)(2,1)}, bf16[464,768]{1,0:T(8,128)(2,1)}, u32[]{:S(2)}, u32[]{:S(2)}) collective-permute-start(bf16[464,768]{1,0:T(8,128)(2,1)} %get-tuple-element.89), channel_id=1, source_target_pairs={{0,1},{1,0},{2,3},{3,2},{4,5},{5,4},{6,7},{7,6},{8,9},{9,8},{10,11... | collective-permute-start | bytes 2138120 | tf_op jit(solution)/shard_map/cond/branch_1_fun/ppermute | solution.py:731
  42.8 18.2 %collective-permute-start.6 = (bf16[464,768]{1,0:T(8,128)(2,1)}, bf16[464,768]{1,0:T(8,128)(2,1)}, u32[]{:S(2)}, u32[]{:S(2)}) collective-permute-start(bf16[464,768]{1,0:T(8,128)(2,1)} %get-tuple-element.90), channel_id=1, source_target_pairs={{0,3},{1,2},{2,1},{3,0},{4,7},{5,6},{6,5},{7,4},{8,11},{9,10},{10,... | collective-permute-start | bytes 2138120 | tf_op jit(solution)/shard_map/cond/branch_1_fun/ppermute | solution.py:732
  53.5 3.8 %collective-permute-start = (bf16[16,48,1152]{2,1,0:T(8,128)(2,1)S(1)}, bf16[16,48,1152]{2,1,0:T(8,128)(2,1)S(1)}, u32[]{:S(2)}, u32[]{:S(2)}) collective-permute-start(bf16[16,48,1152]{2,1,0:T(8,128)(2,1)S(1)} %get-tuple-element.57), channel_id=1, source_target_pairs={{0,4},{4,0},{8,12},{12,8},{16,20},{20,16},{24,28},{28,24},{32,36},... | collective-permute-start | bytes 5308424 | tf_op jit(solution)/shard_map/cond/branch_1_fun/cond/branch_1_fun/ppermute | solution.py:642
  53.6 3.7 %collective-permute-start.1 = (f32[32,384]{1,0:T(8,128)S(1)}, f32[32,384]{1,0:T(8,128)S(1)}, u32[]{:S(2)}, u32[]{:S(2)}) collective-permute-start(f32[32,384]{1,0:T(8,128)S(1)} %get-tuple-element.58.small), channel_id=1, source_target_pairs={{0,4},{4,0},{8,12},{12,8},{16,20},{20,16},{24,28},{28,24},{32,36},... | collective-permute-start | bytes 147464 | tf_op jit(solution)/shard_map/cond/branch_1_fun/cond/branch_1_fun/ppermute | solution.py:642
  57.8 13.3 %collective-permute-start.10 = (bf16[10,48,512]{2,1,0:T(8,128)(2,1)S(1)}, bf16[10,48,512]{2,1,0:T(8,128)(2,1)S(1)}, u32[]{:S(2)}, u32[]{:S(2)}) collective-permute-start(bf16[10,48,512]{2,1,0:T(8,128)(2,1)S(1)} %get-tuple-element.97), channel_id=1, source_target_pairs={{0,8},{4,12},{8,0},{12,4},{16,24},{20,28},{24,16},{28,20},{32,40},... | collective-permute-start | bytes 1474568 | tf_op jit(solution)/shard_map/cond/branch_1_fun/ppermute | solution.py:642
  59.4 13.0 %collective-permute-start.9 = (bf16[8,48,640]{2,1,0:T(8,128)(2,1)S(1)}, bf16[8,48,640]{2,1,0:T(8,128)(2,1)S(1)}, u32[]{:S(2)}, u32[]{:S(2)}) collective-permute-start(bf16[8,48,640]{2,1,0:T(8,128)(2,1)S(1)} %get-tuple-element.96), channel_id=1, source_target_pairs={{0,32},{4,36},{8,40},{12,44},{16,48},{20,52},{24,56},{28,60},{32,0... | collective-permute-start | bytes 1474568 | tf_op jit(solution)/shard_map/cond/branch_1_fun/ppermute | solution.py:642
  62.2 13.2 %copy-start.7 = (s32[1,32]{1,0:T(1,128)S(1)}, s32[1,32]{1,0:T(1,128)}, u32[]{:S(2)}) copy-start(s32[1,32]{1,0:T(1,128)} %get-tuple-element.163.owner_ref) | copy-start | bytes 388 | tf_op jit(solution)/shard_map/cond
  62.2 13.2 %collective-permute-start.7 = (bf16[464,384]{1,0:T(8,128)(2,1)S(1)}, bf16[464,384]{1,0:T(8,128)(2,1)S(1)}, u32[]{:S(2)}, u32[]{:S(2)}) collective-permute-start(bf16[464,384]{1,0:T(8,128)(2,1)S(1)} %get-tuple-element.91), channel_id=1, source_target_pairs={{0,3},{1,2},{2,1},{3,0},{4,7},{5,6},{6,5},{7,4},{8,11},{9,10},{10,... | collective-permute-start | bytes 1069064 | tf_op jit(solution)/shard_map/cond/branch_1_fun/ppermute | solution.py:728
  63.7 11.7 %collective-permute-start.8 = (bf16[464,384]{1,0:T(8,128)(2,1)S(1)}, bf16[464,384]{1,0:T(8,128)(2,1)S(1)}, u32[]{:S(2)}, u32[]{:S(2)}) collective-permute-start(bf16[464,384]{1,0:T(8,128)(2,1)S(1)} %get-tuple-element.92), channel_id=1, source_target_pairs={{0,1},{1,0},{2,3},{3,2},{4,5},{5,4},{6,7},{7,6},{8,9},{9,8},{10,11... | collective-permute-start | bytes 1069064 | tf_op jit(solution)/shard_map/cond/branch_1_fun/ppermute | solution.py:728
  73.4 8.2 %collective-permute-start.12 = (bf16[6,48,512]{2,1,0:T(8,128)(2,1)S(1)}, bf16[6,48,512]{2,1,0:T(8,128)(2,1)}, u32[]{:S(2)}, u32[]{:S(2)}) collective-permute-start(bf16[6,48,512]{2,1,0:T(8,128)(2,1)S(1)} %get-tuple-element.102), channel_id=1, source_target_pairs={{0,32},{4,36},{8,40},{12,44},{16,48},{20,52},{24,56},{28,60},{32,0... | collective-permute-start | bytes 884744 | tf_op jit(solution)/shard_map/cond/branch_1_fun/ppermute | solution.py:642
  75.0 6.7 %collective-permute-start.11 = (bf16[4,48,640]{2,1,0:T(8,128)(2,1)S(1)}, bf16[4,48,640]{2,1,0:T(8,128)(2,1)}, u32[]{:S(2)}, u32[]{:S(2)}) collective-permute-start(bf16[4,48,640]{2,1,0:T(8,128)(2,1)S(1)} %get-tuple-element.101), channel_id=1, source_target_pairs={{0,8},{4,12},{8,0},{12,4},{16,24},{20,28},{24,16},{28,20},{32,40},... | collective-permute-start | bytes 737288 | tf_op jit(solution)/shard_map/cond/branch_1_fun/ppermute | solution.py:642
  81.6 7.0 %copy-start.5 = (f32[4,48,640]{2,1,0:T(8,128)S(1)}, f32[4,48,640]{2,1,0:T(8,128)}, u32[]{:S(2)}) copy-start(f32[4,48,640]{2,1,0:T(8,128)} %get-tuple-element.127.own_x) | copy-start | bytes 1474564
  81.6 32.4 %copy-start = (s32[1,32]{1,0:T(1,128)S(1)}, s32[1,32]{1,0:T(1,128)}, u32[]{:S(2)}) copy-start(s32[1,32]{1,0:T(1,128)} %slot_ref.1) | copy-start | bytes 388
  81.7 32.4 %all-to-all-start = ((bf16[32,72,384]{2,1,0:T(8,128)(2,1)}), bf16[32,72,384]{2,1,0:T(8,128)(2,1)S(1)}, u32[]{:S(2)}, u32[]{:S(2)}) async-start(bf16[32,72,384]{2,1,0:T(8,128)(2,1)} %get-tuple-element.125), calls=%async_computation | async-start | bytes 3538944 | tf_op jit(solution)/shard_map/all_to_all | solution.py:769
  90.0 28.2 %collective-permute-start.13 = (bf16[48,1920]{1,0:T(8,128)(2,1)S(1)}, bf16[48,1920]{1,0:T(8,128)(2,1)S(1)}, u32[]{:S(2)}, u32[]{:S(2)}) collective-permute-start(bf16[48,1920]{1,0:T(8,128)(2,1)S(1)} %get-tuple-element.134), channel_id=1, source_target_pairs={{0,120},{4,124},{8,112},{12,116},{16,104},{20,108},{24,96},{28,100... | collective-permute-start | bytes 552968 | tf_op jit(solution)/shard_map/ppermute | solution.py:642
  95.3 24.4 %collective-permute-start.14 = (bf16[48,1920]{1,0:T(8,128)(2,1)S(1)}, bf16[48,1920]{1,0:T(8,128)(2,1)S(1)}, u32[]{:S(2)}, u32[]{:S(2)}) collective-permute-start(bf16[48,1920]{1,0:T(8,128)(2,1)S(1)} %get-tuple-element.135), channel_id=1, source_target_pairs={{0,96},{4,100},{8,104},{12,108},{16,112},{20,116},{24,120},{28,124... | collective-permute-start | bytes 552968 | tf_op jit(solution)/shard_map/ppermute | solution.py:642
  95.7 23.9 %collective-permute-start.15 = (bf16[48,1920]{1,0:T(8,128)(2,1)S(1)}, bf16[48,1920]{1,0:T(8,128)(2,1)S(1)}, u32[]{:S(2)}, u32[]{:S(2)}) collective-permute-start(bf16[48,1920]{1,0:T(8,128)(2,1)S(1)} %get-tuple-element.136), channel_id=1, source_target_pairs={{0,24},{4,28},{8,16},{12,20},{16,8},{20,12},{24,0},{28,4},{32,56},... | collective-permute-start | bytes 552968 | tf_op jit(solution)/shard_map/ppermute | solution.py:642
